TPU v7x, 256 devices: a whole 4x4x8 slice. The times are simulated.
256 devices in a mesh: gx: 8 (over y, core), gy: 32 (over x, z).
Axes of the slice: x: 4, y: 4, z: 8, core: 2. Of those that a mesh axis runs over, the one named last changes fastest.
Arguments:
- features: bfloat16 [131072, 128], P(('gx', 'gy')), may hold values from -6 to 6
- point_slab: int32 [131072, 1], P(('gx', 'gy')), may hold values from 0 to 31; in each aligned block of 512 rows (0 to 511, 512 to 1023, ...) at most 48 rows name the same one
- base_cell: int32 [131072], P(('gx', 'gy')), may hold values from 0 to 366, as said below
- nearest: int32 [131072], P(('gx', 'gy')), may hold values from 0 to 7
- offsets: bfloat16 [3, 131072], P(None, ('gx', 'gy')), may hold values from 0 to 1
- conv_weight: bfloat16 [27, 128, 128], replicated, may hold values from -0.109375 to 0.109375
- mlp_weight: bfloat16 [128, 128], replicated, may hold values from -0.5 to 0.5
- cotangent: bfloat16 [131072, 128], P(('gx', 'gy')), may hold values from -6 to 6
Outputs:
- output: bfloat16 [131072, 128], P(('gx', 'gy'))
- grad_features: bfloat16 [131072, 128], P(('gx', 'gy'))
- grad_conv: float32 [27, 128, 128], replicated
- grad_mlp: float32 [128, 128], replicated
Inputs may be any that keep to these rules, and one draw needn't show every extreme that they name: `point_slab`: in the rows of one device at most 48 points name the same slab, a bound that some block reaches of them. `base_cell`: each entry is (a * 8 + b) * 16 + c with a < 3, b < 7, c < 15.
All inputs are finite; a program needn't handle non-finite values.
Results may differ from a plain program's by a relative error of at most 0.0058.
Values may be sent and summed in bfloat16 or wider, within the bound.
No kernel may reach another device: no remote copies, remote signals or barrier semaphores. Data moves between devices by JAX's collectives and lax.ppermute only.
A program may use at most 64 MiB of HBM per device.

v0:
```python
import math

import jax
import jax.numpy as jnp
from jax import lax
from jax.sharding import PartitionSpec as P

VX_DEV = 4
VY_DEV = 8
Z = 16


def padded_2(cells, sides, width):
    for axis, dim in sides:
        count = lax.axis_size(axis)
        ends = count - 1
        head = lax.slice_in_dim(cells, 0, width, axis=dim)
        tail = lax.slice_in_dim(cells, cells.shape[dim] - width, cells.shape[dim], axis=dim)
        cells = jnp.concatenate(
            [
                lax.ppermute(tail, axis, [(i, (i + 1) % count) for i in range(ends)]),
                cells,
                lax.ppermute(head, axis, [((i + 1) % count, i) for i in range(ends)]),
            ],
            axis=dim,
        )
    return cells


def sigmoid_slope(pre_act):
    sigmoid_value = jax.nn.sigmoid(pre_act)
    return sigmoid_value * (1.0 + pre_act * (1.0 - sigmoid_value))


def convolve(padded, kernel_stack, block_shape, flipped):
    x_cells, y_cells, z_cells = block_shape
    channels = padded.shape[3]
    accumulated = jnp.zeros((x_cells * y_cells * z_cells, kernel_stack.shape[2]), jnp.float32)
    for offset in range(27):
        x_shift = offset // 9
        y_shift = offset // 3 % 3
        z_shift = offset % 3
        if flipped:
            starts = (2 - x_shift, 2 - y_shift, 2 - z_shift)
            kernel = kernel_stack[offset].T
        else:
            starts = (x_shift, y_shift, z_shift)
            kernel = kernel_stack[offset]
        window = lax.slice(
            padded,
            (starts[0], starts[1], starts[2], 0),
            (starts[0] + x_cells, starts[1] + y_cells, starts[2] + z_cells, channels),
        )
        accumulated = accumulated + jnp.dot(
            window.reshape(-1, channels), kernel, preferred_element_type=jnp.float32
        )
    return accumulated


def weight_gradient(padded, grad_hidden, block_shape):
    x_cells, y_cells, z_cells = block_shape
    channels = padded.shape[3]
    pieces = []
    for offset in range(27):
        x_shift = offset // 9
        y_shift = offset // 3 % 3
        z_shift = offset % 3
        window = lax.slice(
            padded,
            (x_shift, y_shift, z_shift, 0),
            (x_shift + x_cells, y_shift + y_cells, z_shift + z_cells, channels),
        )
        pieces.append(
            lax.dot_general(
                window.reshape(-1, channels),
                grad_hidden,
                (((0,), (0,)), ((), ())),
                preferred_element_type=jnp.float32,
            )
        )
    return jnp.stack(pieces)


def trilinear(offsets, base_cell, plane_cells, z_cells):
    fraction = offsets.astype(jnp.float32)
    weights = []
    corners = []
    for corner in range(8):
        x_bit = corner // 4
        y_bit = corner // 2 % 2
        z_bit = corner % 2
        factor = fraction[0] if x_bit else 1.0 - fraction[0]
        factor = factor * (fraction[1] if y_bit else 1.0 - fraction[1])
        factor = factor * (fraction[2] if z_bit else 1.0 - fraction[2])
        weights.append(factor)
        corners.append(base_cell + x_bit * plane_cells + y_bit * z_cells + z_bit)
    return (weights, corners)


def body(features, point_slab, base_cell, nearest, offsets, conv_weight, mlp_weight, cotangent):
    gy_count = lax.axis_size("gy")
    gx_count = lax.axis_size("gx")
    local_points = features.shape[0]
    channels = features.shape[1]
    capacity = 3 * local_points // gy_count
    slot_count = gy_count * capacity
    plane_cells = VY_DEV * Z
    cells_dev = VX_DEV * plane_cells
    block_shape = (VX_DEV, VY_DEV, Z)
    block_rows = min(512, slot_count)
    block_total = -(-slot_count // block_rows)
    padded_slots = block_total * block_rows
    extra_slots = padded_slots - slot_count
    cell_iota = jnp.arange(cells_dev, dtype=jnp.int32)
    target = point_slab[:, 0]
    matches = (target[:, None] == jnp.arange(gy_count, dtype=jnp.int32)[None, :]).astype(jnp.int32)
    before = jnp.cumsum(matches, axis=0) - matches
    position = target * capacity + jnp.sum(before * matches, axis=1)
    own_cell = base_cell + nearest // 4 * plane_cells + nearest // 2 % 2 * Z + nearest % 2

    def pack_rows(row_values):
        blank_rows = jnp.zeros((slot_count, row_values.shape[1]), row_values.dtype)
        return (
            blank_rows.at[position].set(row_values).reshape(gy_count, capacity, row_values.shape[1])
        )

    def pack_lanes(lane_values, fill_value):
        blank_lanes = jnp.full((lane_values.shape[0], slot_count), fill_value, lane_values.dtype)
        filled = blank_lanes.at[:, position].set(lane_values)
        return filled.reshape(lane_values.shape[0], gy_count, capacity).transpose(1, 0, 2)

    def slot_blocks(values, fill_value):
        tail = jnp.full((extra_slots,) + values.shape[1:], fill_value, values.dtype)
        whole = jnp.concatenate([values, tail], axis=0)
        return whole.reshape((block_total, block_rows) + values.shape[1:])

    cell_lists = jnp.concatenate(
        [pack_lanes(own_cell[None, :], cells_dev), pack_lanes(base_cell[None, :], 0)], axis=1
    )
    packed_offsets = pack_lanes(offsets, jnp.zeros((), offsets.dtype))
    sent_rows, sent_cells, sent_offsets = (
        lax.all_to_all(pack_rows(features), "gy", split_axis=0, concat_axis=0, tiled=True),
        lax.all_to_all(cell_lists, "gy", split_axis=0, concat_axis=0, tiled=True),
        lax.all_to_all(packed_offsets, "gy", split_axis=0, concat_axis=0, tiled=True),
    )
    rows_in = sent_rows.reshape(slot_count, channels)
    cells_in = sent_cells[:, 0, :].reshape(slot_count)
    bases_in = sent_cells[:, 1, :].reshape(slot_count)
    fraction_in = sent_offsets.transpose(1, 0, 2).reshape(3, slot_count)
    cell_blocks = slot_blocks(cells_in, cells_dev)
    base_blocks = slot_blocks(bases_in, 0)
    fraction_blocks = slot_blocks(fraction_in.T, jnp.zeros((), fraction_in.dtype))

    def corner_matrix(base_block, fraction_block):
        weights, corners = trilinear(fraction_block.T, base_block, plane_cells, Z)
        matrix = jnp.zeros((base_block.shape[0], cells_dev), jnp.float32)
        for corner in range(8):
            matrix = matrix + jnp.where(
                corners[corner][:, None] == cell_iota[None, :], weights[corner][:, None], 0.0
            )
        return matrix.astype(jnp.bfloat16)

    def add_block(carry, inputs):
        cell_block, row_block = inputs
        onehot = (cell_block[:, None] == cell_iota[None, :]).astype(jnp.bfloat16)
        sums_now = carry[0] + lax.dot_general(
            onehot, row_block, (((0,), (0,)), ((), ())), preferred_element_type=jnp.float32
        )
        counts_now = carry[1] + jnp.sum(onehot, axis=0, dtype=jnp.float32)
        return ((sums_now, counts_now), None)

    start_sums = (
        jnp.zeros((cells_dev, channels), jnp.float32),
        jnp.zeros((cells_dev,), jnp.float32),
    )
    (voxel_sums, counts), _ = lax.scan(
        add_block, start_sums, (cell_blocks, slot_blocks(rows_in, 0.0))
    )
    divisor = jnp.maximum(counts, 1.0)
    voxels = (voxel_sums / divisor[:, None]).astype(jnp.bfloat16)
    voxels = voxels.reshape(VX_DEV, VY_DEV, Z, channels)
    with_rim = padded_2(voxels, (("gx", 0), ("gy", 1)), 1)
    padded = jnp.pad(with_rim, ((0, 0), (0, 0), (1, 1), (0, 0)))
    hidden = convolve(padded, conv_weight, block_shape, False)
    conv_out = jax.nn.silu(hidden).astype(jnp.bfloat16)

    def sample_block(carry, inputs):
        base_block, fraction_block = inputs
        matrix = corner_matrix(base_block, fraction_block)
        return (carry, jnp.dot(matrix, conv_out, preferred_element_type=jnp.float32))

    _, sampled_blocks = lax.scan(
        sample_block, jnp.zeros((), jnp.float32), (base_blocks, fraction_blocks)
    )
    sampled = sampled_blocks.reshape(padded_slots, channels)[:slot_count]
    sampled = sampled.astype(jnp.bfloat16).reshape(gy_count, capacity, channels)
    divisor_ext = jnp.concatenate([divisor, jnp.ones((1,), jnp.float32)], axis=0)
    pre_mlp = jnp.dot(features, mlp_weight, preferred_element_type=jnp.float32)
    upstream = cotangent.astype(jnp.float32)
    grad_pre = (upstream * sigmoid_slope(pre_mlp)).astype(jnp.bfloat16)
    sampled_back = lax.all_to_all(sampled, "gy", split_axis=0, concat_axis=0, tiled=True)
    grad_rows = lax.all_to_all(pack_rows(cotangent), "gy", split_axis=0, concat_axis=0, tiled=True)
    grad_blocks = slot_blocks(grad_rows.reshape(slot_count, channels), 0.0)

    def spread_block(carry, inputs):
        base_block, fraction_block, grad_block = inputs
        matrix = corner_matrix(base_block, fraction_block)
        return (
            carry
            + lax.dot_general(
                matrix, grad_block, (((0,), (0,)), ((), ())), preferred_element_type=jnp.float32
            ),
            None,
        )

    grad_conv_out, _ = lax.scan(
        spread_block,
        jnp.zeros((cells_dev, channels), jnp.float32),
        (base_blocks, fraction_blocks, grad_blocks),
    )
    grad_hidden = (grad_conv_out * sigmoid_slope(hidden)).astype(jnp.bfloat16)
    local_conv = weight_gradient(padded, grad_hidden, block_shape)
    grad_rim = padded_2(grad_hidden.reshape(VX_DEV, VY_DEV, Z, channels), (("gx", 0), ("gy", 1)), 1)
    grad_padded = jnp.pad(grad_rim, ((0, 0), (0, 0), (1, 1), (0, 0)))
    grad_voxels = convolve(grad_padded, conv_weight, block_shape, True)
    extended = jnp.concatenate([grad_voxels, jnp.zeros((1, channels), jnp.float32)], axis=0)
    from_voxels = (extended[cells_in] / divisor_ext[cells_in][:, None]).astype(jnp.bfloat16)
    from_voxels, local_conv = (from_voxels.reshape(gy_count, capacity, channels), local_conv)
    voxel_back = lax.all_to_all(from_voxels, "gy", split_axis=0, concat_axis=0, tiled=True)
    sampled_points = sampled_back.reshape(slot_count, channels)[position]
    output = (sampled_points.astype(jnp.float32) + jax.nn.silu(pre_mlp)).astype(jnp.bfloat16)
    local_mlp = lax.dot_general(
        features, grad_pre, (((0,), (0,)), ((), ())), preferred_element_type=jnp.float32
    )
    conv_total, mlp_total = lax.psum((local_conv, local_mlp), ("gx", "gy"))
    cells_all = cells_dev * gx_count * gy_count
    points_all = local_points * gx_count * gy_count
    grad_conv = conv_total * (1.0 / math.sqrt(cells_all))
    grad_mlp = mlp_total * (1.0 / math.sqrt(points_all))
    voxel_points = voxel_back.reshape(slot_count, channels)[position]
    grad_features = (
        jnp.dot(grad_pre, mlp_weight.T, preferred_element_type=jnp.float32)
        + voxel_points.astype(jnp.float32)
    ).astype(jnp.bfloat16)
    return (output, grad_features, grad_conv, grad_mlp)


def solution(mesh):
    in_specs = (
        P(("gx", "gy"), None),
        P(("gx", "gy"), None),
        P(("gx", "gy")),
        P(("gx", "gy")),
        P(None, ("gx", "gy")),
        P(),
        P(),
        P(("gx", "gy"), None),
    )
    out_specs = (P(("gx", "gy"), None), P(("gx", "gy"), None), P(), P())
    return jax.shard_map(body, mesh=mesh, in_specs=in_specs, out_specs=out_specs, check_vma=False)
```

profile of v0, /device:TPU:1, one launch (start us, length us, event | category | flops | bytes accessed | tf_op | source)
XLA Modules:
  0.0 450.2 jit_solution(10816852394261739822)
XLA Ops:
  14.4 11.9 %all-to-all-start.1 = ((bf16[32,3,48]{2,1,0:T(4,128)(2,1)}), bf16[32,3,48]{2,1,0:T(4,128)(2,1)S(1)}, u32[]{:S(2)}, u32[]{:S(2)}) async-start(bf16[32,3,48]{2,1,0:T(4,128)(2,1)} %bitcast.7), calls=%async_computation.1 | async-start | bytes 65536 | tf_op jit(solution)/shard_map/all_to_all | solution.py:144
  35.1 7.1 %all-to-all-start = ((s32[32,2,48]{2,1,0:T(2,128)}), s32[32,2,48]{2,1,0:T(2,128)S(1)}, u32[]{:S(2)}, u32[]{:S(2)}) async-start(s32[32,2,48]{2,1,0:T(2,128)} %pad_add_fusion), calls=%async_computation | async-start | bytes 65536 | tf_op jit(solution)/shard_map/all_to_all | solution.py:143
  42.2 2.9 scatter_custom_fusion.3
  45.0 5.9 %all-to-all-done = s32[32,2,48]{2,1,0:T(2,128)S(1)} async-done(((s32[32,2,48]{2,1,0:T(2,128)}), s32[32,2,48]{2,1,0:T(2,128)S(1)}, u32[]{:S(2)}, u32[]{:S(2)}) %all-to-all-start) | async-done | bytes 12320 | tf_op jit(solution)/shard_map/all_to_all | solution.py:143
  50.9 3.9 all-to-all-start.2
  58.2 6.8 %all-to-all-done.2 = bf16[32,48,128]{2,1,0:T(8,128)(2,1)S(1)} async-done(((bf16[32,48,128]{2,1,0:T(8,128)(2,1)}), bf16[32,48,128]{2,1,0:T(8,128)(2,1)S(1)}, u32[]{:S(2)}, u32[]{:S(2)}) %all-to-all-start.2) | async-done | bytes 393248 | tf_op jit(solution)/shard_map/all_to_all | solution.py:142
  65.1 6.8 %all-to-all-start.4 = ((bf16[32,48,128]{2,1,0:T(8,128)(2,1)}), bf16[32,48,128]{2,1,0:T(8,128)(2,1)S(1)}, u32[]{:S(2)}, u32[]{:S(2)}) async-start(bf16[32,48,128]{2,1,0:T(8,128)(2,1)} %bitcast.72), calls=%async_computation.4 | async-start | bytes 786432 | tf_op jit(solution)/shard_map/all_to_all | solution.py:202
  74.5 6.7 %collective-permute-start = (bf16[1,8,16,128]{3,2,1,0:T(8,128)(2,1)S(1)}, bf16[1,8,16,128]{3,2,1,0:T(8,128)(2,1)S(1)}, u32[]{:S(2)}, u32[]{:S(2)}) collective-permute-start(bf16[1,8,16,128]{3,2,1,0:T(8,128)(2,1)S(1)} %bitcast.633), channel_id=1, source_target_pairs={{0,32},{32,64},{64,96},{96,128},{128,160},{160,192},{192,224},{1,3... | collective-permute-start | bytes 98312 | tf_op jit(solution)/shard_map/ppermute | solution.py:21
  83.3 5.6 %while.47 = (s32[]{:T(128)}, f32[512,128]{1,0:T(8,128)S(1)}, s32[3,512]{1,0:T(4,128)S(1)}, bf16[3,512,3]{1,2,0:T(4,128)(2,1)S(1)}, bf16[3,512,128]{2,1,0:T(8,128)(2,1)S(1)}, /*index=5*/s32[]{:T(128)}, s32[]{:T(128)}) while((s32[]{:T(128)}, f32[512,128]{1,0:T(8,128)S(1)}, s32[3,512]{1,0:T(4,128)S(1)}, ...), condition=%wide.region_14.15_spmd.clone.clone, body=%wide.region_13.14_spmd.clone.clone.sunk | while | flops 73544192 | bytes 752739 | solution.py:216
  88.9 5.9 %gather_fusion.2 = f32[1536]{0:T(1024)S(1)} fusion(f32[513]{0:T(1024)S(1)} %pad_maximum_fusion.12, s32[2048]{0:T(1024)S(1)} %pad_clamp_fusion), kind=kCustom, calls=%fused_computation.2 | custom fusion | bytes 18432 | tf_op jit(solution)/shard_map/gather | solution.py:227
  94.9 3.4 collective-permute-start.2
  99.7 3.2 collective-permute-done.3
  116.8 8.9 %while.45 = (s32[]{:T(128)}, bf16[3,512,128]{2,1,0:T(8,128)(2,1)S(1)}, s32[3,512]{1,0:T(4,128)S(1)}, bf16[3,512,3]{1,2,0:T(4,128)(2,1)S(1)}, bf16[512,128]{1,0:T(8,128)(2,1)}, /*index=5*/s32[]{:T(128)}) while((s32[]{:T(128)}, bf16[3,512,128]{2,1,0:T(8,128)(2,1)S(1)}, s32[3,512]{1,0:T(4,128)S(1)}, ...), condition=%wide.region_11.12_spmd.clone.clone, body=%wide.region_10.11_spmd.clone.clone.sunk | while | flops 73413120 | bytes 490577 | solution.py:192
  116.9 2.9 fusion.365
  119.9 2.9 fusion.365
  122.9 2.9 fusion.365
  125.8 9.4 %collective-permute-start.4 = (bf16[1,8,16,128]{3,2,1,0:T(8,128)(2,1)S(1)}, bf16[1,8,16,128]{3,2,1,0:T(8,128)(2,1)S(1)}, u32[]{:S(2)}, u32[]{:S(2)}) collective-permute-start(bf16[1,8,16,128]{3,2,1,0:T(8,128)(2,1)S(1)} %bitcast.631), channel_id=1, source_target_pairs={{0,32},{32,64},{64,96},{96,128},{128,160},{160,192},{192,224},{1,3... | collective-permute-start | bytes 98312 | tf_op jit(solution)/shard_map/ppermute | solution.py:21
  137.4 6.0 %all-to-all-start.3 = ((bf16[32,48,128]{2,1,0:T(8,128)(2,1)}), bf16[32,48,128]{2,1,0:T(8,128)(2,1)S(1)}, u32[]{:S(2)}, u32[]{:S(2)}) async-start(bf16[32,48,128]{2,1,0:T(8,128)(2,1)} %bitcast.612), calls=%async_computation.3 | async-start | bytes 786432 | tf_op jit(solution)/shard_map/all_to_all | solution.py:201
  143.5 3.1 collective-permute-start.6
  149.3 3.7 collective-permute-done.7
  162.7 8.3 %all-to-all-start.5 = ((bf16[32,48,128]{2,1,0:T(8,128)(2,1)}), bf16[32,48,128]{2,1,0:T(8,128)(2,1)S(1)}, u32[]{:S(2)}, u32[]{:S(2)}) async-start(bf16[32,48,128]{2,1,0:T(8,128)(2,1)} %divide_convert_fusion), calls=%async_computation.5 | async-start | bytes 786432 | tf_op jit(solution)/shard_map/all_to_all | solution.py:229
  174.2 10.0 %all-to-all-done.5 = bf16[32,48,128]{2,1,0:T(8,128)(2,1)S(1)} async-done(((bf16[32,48,128]{2,1,0:T(8,128)(2,1)}), bf16[32,48,128]{2,1,0:T(8,128)(2,1)S(1)}, u32[]{:S(2)}, u32[]{:S(2)}) %all-to-all-start.5) | async-done | bytes 393248 | tf_op jit(solution)/shard_map/all_to_all | solution.py:229
  186.4 253.3 %all-reduce.6.cloned.1.call-done = (f32[27,128,128]{2,1,0:T(8,128)}, f32[128,128]{0,1:T(8,128)}) async-done(((f32[27,128,128]{2,1,0:T(8,128)}, f32[128,128]{0,1:T(8,128)}), (f32[27,128,128]{2,1,0:T(8,128)}, f32[128,128]{0,1:T(8,128)})) %all-reduce.6.cloned.1.call-update) | async-done | bytes 1835024 | tf_op jit(solution)/shard_map/psum | solution.py:235
  439.7 3.0 broadcast_multiply_fusion
  (217 shorter events, 67.3 us)
Async XLA Ops:
  7.2 165.2 %copy-start = (bf16[128,128]{1,0:T(8,128)(2,1)S(1)}, bf16[128,128]{1,0:T(8,128)(2,1)}, u32[]{:S(2)}) copy-start(bf16[128,128]{1,0:T(8,128)(2,1)} %param.20) | copy-start | bytes 98308
  14.4 20.6 %all-to-all-start.1 = ((bf16[32,3,48]{2,1,0:T(4,128)(2,1)}), bf16[32,3,48]{2,1,0:T(4,128)(2,1)S(1)}, u32[]{:S(2)}, u32[]{:S(2)}) async-start(bf16[32,3,48]{2,1,0:T(4,128)(2,1)} %bitcast.7), calls=%async_computation.1 | async-start | bytes 65536 | tf_op jit(solution)/shard_map/all_to_all | solution.py:144
  35.1 15.9 %all-to-all-start = ((s32[32,2,48]{2,1,0:T(2,128)}), s32[32,2,48]{2,1,0:T(2,128)S(1)}, u32[]{:S(2)}, u32[]{:S(2)}) async-start(s32[32,2,48]{2,1,0:T(2,128)} %pad_add_fusion), calls=%async_computation | async-start | bytes 65536 | tf_op jit(solution)/shard_map/all_to_all | solution.py:143
  50.9 14.1 %all-to-all-start.2 = ((bf16[32,48,128]{2,1,0:T(8,128)(2,1)}), bf16[32,48,128]{2,1,0:T(8,128)(2,1)S(1)}, u32[]{:S(2)}, u32[]{:S(2)}) async-start(bf16[32,48,128]{2,1,0:T(8,128)(2,1)} %bitcast.11), calls=%async_computation.2 | async-start | bytes 786432 | tf_op jit(solution)/shard_map/all_to_all | solution.py:142
  65.1 18.2 %all-to-all-start.4 = ((bf16[32,48,128]{2,1,0:T(8,128)(2,1)}), bf16[32,48,128]{2,1,0:T(8,128)(2,1)S(1)}, u32[]{:S(2)}, u32[]{:S(2)}) async-start(bf16[32,48,128]{2,1,0:T(8,128)(2,1)} %bitcast.72), calls=%async_computation.4 | async-start | bytes 786432 | tf_op jit(solution)/shard_map/all_to_all | solution.py:202
  74.5 20.4 %collective-permute-start = (bf16[1,8,16,128]{3,2,1,0:T(8,128)(2,1)S(1)}, bf16[1,8,16,128]{3,2,1,0:T(8,128)(2,1)S(1)}, u32[]{:S(2)}, u32[]{:S(2)}) collective-permute-start(bf16[1,8,16,128]{3,2,1,0:T(8,128)(2,1)S(1)} %bitcast.633), channel_id=1, source_target_pairs={{0,32},{32,64},{64,96},{96,128},{128,160},{160,192},{192,224},{1,3... | collective-permute-start | bytes 98312 | tf_op jit(solution)/shard_map/ppermute | solution.py:21
  81.2 13.7 %collective-permute-start.1 = (bf16[1,8,16,128]{3,2,1,0:T(8,128)(2,1)S(1)}, bf16[1,8,16,128]{3,2,1,0:T(8,128)(2,1)S(1)}, u32[]{:S(2)}, u32[]{:S(2)}) collective-permute-start(bf16[1,8,16,128]{3,2,1,0:T(8,128)(2,1)S(1)} %bitcast.632), channel_id=1, source_target_pairs={{32,0},{64,32},{96,64},{128,96},{160,128},{192,160},{224,192},{33,... | collective-permute-start | bytes 98312 | tf_op jit(solution)/shard_map/ppermute | solution.py:23
  94.9 4.8 %collective-permute-start.2 = (bf16[6,1,16,128]{3,2,1,0:T(8,128)(2,1)S(1)}, bf16[6,1,16,128]{3,2,1,0:T(8,128)(2,1)S(1)}, u32[]{:S(2)}, u32[]{:S(2)}) collective-permute-start(bf16[6,1,16,128]{3,2,1,0:T(8,128)(2,1)S(1)} %get-tuple-element.575), channel_id=1, source_target_pairs={{0,1},{1,2},{2,3},{3,4},{4,5},{5,6},{6,7},{7,8},{8,9},{9,10},{10,1... | collective-permute-start | bytes 73736 | tf_op jit(solution)/shard_map/ppermute | solution.py:21
  98.3 4.6 %collective-permute-start.3 = (bf16[6,1,16,128]{3,2,1,0:T(8,128)(2,1)S(1)}, bf16[6,1,16,128]{3,2,1,0:T(8,128)(2,1)S(1)}, u32[]{:S(2)}, u32[]{:S(2)}) collective-permute-start(bf16[6,1,16,128]{3,2,1,0:T(8,128)(2,1)S(1)} %get-tuple-element.576), channel_id=1, source_target_pairs={{1,0},{2,1},{3,2},{4,3},{5,4},{6,5},{7,6},{8,7},{9,8},{10,9},{11,1... | collective-permute-start | bytes 73736 | tf_op jit(solution)/shard_map/ppermute | solution.py:23
  103.1 1.2 copy-start.1
  116.8 9.0 %copy-start.6 = (bf16[128,128]{1,0:T(8,128)(2,1)S(1)}, bf16[128,128]{1,0:T(8,128)(2,1)}, u32[]{:S(2)}) copy-start(bf16[128,128]{1,0:T(8,128)(2,1)} %get-tuple-element.579) | copy-start | bytes 98308
  125.8 11.6 %copy-start.3 = (bf16[3,512,128]{2,1,0:T(8,128)(2,1)}, bf16[3,512,128]{2,1,0:T(8,128)(2,1)S(1)}, u32[]{:S(2)}) copy-start(bf16[3,512,128]{2,1,0:T(8,128)(2,1)S(1)} %get-tuple-element.329) | copy-start | bytes 1179652
  125.8 17.6 %collective-permute-start.4 = (bf16[1,8,16,128]{3,2,1,0:T(8,128)(2,1)S(1)}, bf16[1,8,16,128]{3,2,1,0:T(8,128)(2,1)S(1)}, u32[]{:S(2)}, u32[]{:S(2)}) collective-permute-start(bf16[1,8,16,128]{3,2,1,0:T(8,128)(2,1)S(1)} %bitcast.631), channel_id=1, source_target_pairs={{0,32},{32,64},{64,96},{96,128},{128,160},{160,192},{192,224},{1,3... | collective-permute-start | bytes 98312 | tf_op jit(solution)/shard_map/ppermute | solution.py:21
  135.2 8.2 %collective-permute-start.5 = (bf16[1,8,16,128]{3,2,1,0:T(8,128)(2,1)S(1)}, bf16[1,8,16,128]{3,2,1,0:T(8,128)(2,1)S(1)}, u32[]{:S(2)}, u32[]{:S(2)}) collective-permute-start(bf16[1,8,16,128]{3,2,1,0:T(8,128)(2,1)S(1)} %bitcast.630), channel_id=1, source_target_pairs={{32,0},{64,32},{96,64},{128,96},{160,128},{192,160},{224,192},{33,... | collective-permute-start | bytes 98312 | tf_op jit(solution)/shard_map/ppermute | solution.py:23
  137.4 15.9 %copy-start.2 = (f32[27,128,128]{2,1,0:T(8,128)}, f32[27,128,128]{2,1,0:T(8,128)S(1)}, u32[]{:S(2)}) copy-start(f32[27,128,128]{2,1,0:T(8,128)S(1)} %fusion.62) | copy-start | bytes 5308420
  137.4 25.2 %all-to-all-start.3 = ((bf16[32,48,128]{2,1,0:T(8,128)(2,1)}), bf16[32,48,128]{2,1,0:T(8,128)(2,1)S(1)}, u32[]{:S(2)}, u32[]{:S(2)}) async-start(bf16[32,48,128]{2,1,0:T(8,128)(2,1)} %bitcast.612), calls=%async_computation.3 | async-start | bytes 786432 | tf_op jit(solution)/shard_map/all_to_all | solution.py:201
  143.5 5.9 %collective-permute-start.6 = (bf16[6,1,16,128]{3,2,1,0:T(8,128)(2,1)S(1)}, bf16[6,1,16,128]{3,2,1,0:T(8,128)(2,1)S(1)}, u32[]{:S(2)}, u32[]{:S(2)}) collective-permute-start(bf16[6,1,16,128]{3,2,1,0:T(8,128)(2,1)S(1)} %get-tuple-element.571), channel_id=1, source_target_pairs={{0,1},{1,2},{2,3},{3,4},{4,5},{5,6},{6,7},{7,8},{8,9},{9,10},{10,1... | collective-permute-start | bytes 73736 | tf_op jit(solution)/shard_map/ppermute | solution.py:21
  146.6 6.4 %collective-permute-start.7 = (bf16[6,1,16,128]{3,2,1,0:T(8,128)(2,1)S(1)}, bf16[6,1,16,128]{3,2,1,0:T(8,128)(2,1)S(1)}, u32[]{:S(2)}, u32[]{:S(2)}) collective-permute-start(bf16[6,1,16,128]{3,2,1,0:T(8,128)(2,1)S(1)} %get-tuple-element.572), channel_id=1, source_target_pairs={{1,0},{2,1},{3,2},{4,3},{5,4},{6,5},{7,6},{8,7},{9,8},{10,9},{11,1... | collective-permute-start | bytes 73736 | tf_op jit(solution)/shard_map/ppermute | solution.py:23
  161.6 10.8 %copy-start.4 = (bf16[512,128]{1,0:T(8,128)(2,1)S(1)}, bf16[512,128]{1,0:T(8,128)(2,1)}, u32[]{:S(2)}) copy-start(bf16[512,128]{1,0:T(8,128)(2,1)} %param.14) | copy-start | bytes 393220
  161.6 10.8 %copy-start.7 = (bf16[512,128]{1,0:T(8,128)(2,1)S(1)}, bf16[512,128]{1,0:T(8,128)(2,1)}, u32[]{:S(2)}) copy-start(bf16[512,128]{1,0:T(8,128)(2,1)} %param.21) | copy-start | bytes 393220
  162.7 21.5 %all-to-all-start.5 = ((bf16[32,48,128]{2,1,0:T(8,128)(2,1)}), bf16[32,48,128]{2,1,0:T(8,128)(2,1)S(1)}, u32[]{:S(2)}, u32[]{:S(2)}) async-start(bf16[32,48,128]{2,1,0:T(8,128)(2,1)} %divide_convert_fusion), calls=%async_computation.5 | async-start | bytes 786432 | tf_op jit(solution)/shard_map/all_to_all | solution.py:229
  171.0 268.7 %all-reduce.6.cloned.1.call-start = ((), (), s32[]{:S(2)}) async-start(), calls=%async_computation.6 | async-start | bytes 3670016 | tf_op jit(solution)/shard_map/psum | solution.py:235
  439.7 3.0 copy-start.5
Sparse Core Ops, SparseCore 0:
  177.8 261.7 all-reduce.5
where the time goes:
time: 452 us; the launch traced here: 450 us
  waiting for transfers between devices  286 us (63%)
  starting transfers between devices  73.2 us (16%)
  matrix products  34.9 us (8%)
  local copies, waits for them, and re-layouts  29.8 us (7%)
  between operations  15.2 us (3%)
  other arithmetic  10.2 us (2%)
    psum x1, waiting for transfers between devices, body(): conv_total, mlp_total = lax.psum((local_conv, local_mlp), ('gx', 'gy'))  253 us
    ppermute x4, starting transfers between devices, padded_2(): lax.ppermute(tail, axis, [(i, (i + 1) % count) for i in range(ends)])  22.7 us
    all_to_all x1, starting transfers between devices, body(): lax.all_to_all(packed_offsets, 'gy', split_axis=0, concat_axis=0, tiled=T...  11.9 us
    dot_general x54, matrix products, convolve(): jnp.dot(window.reshape(-1, channels), kernel, preferred_element_type=jnp....  10.4 us
    all_to_all x1, waiting for transfers between devices, body(): lax.all_to_all(from_voxels, 'gy', split_axis=0, concat_axis=0, tiled=True)  9.96 us
  transfers between devices with their start and end apart: 15, of which 8 were waited for; matrix products, arithmetic and copies ran while one was open for 9% of the time, Pallas kernels for 0%

commit v1 on v0

v1 whole, which is shorter than its diff:
```python
import functools
import math

import jax
import jax.numpy as jnp
from jax import lax
from jax.experimental import pallas as pl
from jax.experimental.pallas import tpu as pltpu
from jax.sharding import Mesh, PartitionSpec as P

C = 128
VX = 4
VY = 8
Z = 16
CELLS = VX * VY * Z
PTS = 512
CAP = 48
GY = 32
SLOTS = GY * CAP
GX = 8
KINDS = 16
HALF = 14
SHARE = HALF * C // GY
SHARE_PAD = 64
BF = jnp.bfloat16
F32 = jnp.float32
VMEM = pl.BlockSpec(memory_space=pltpu.VMEM)
SMEM = pl.BlockSpec(memory_space=pltpu.SMEM)
PARAMS = pltpu.CompilerParams(vmem_limit_bytes=48 * 1024 * 1024)
LEFT = (((0,), (0,)), ((), ()))
RIGHT = (((1,), (1,)), ((), ()))


def sds(shape, dtype):
    return jax.ShapeDtypeStruct(shape, dtype)


def call(kernel, out_shape, args, scratch=(), smem=0):
    return pl.pallas_call(
        kernel,
        out_shape=out_shape,
        in_specs=[SMEM] * smem + [VMEM] * (len(args) - smem),
        out_specs=jax.tree.map(lambda _: VMEM, out_shape),
        scratch_shapes=list(scratch),
        compiler_params=PARAMS,
    )(*args)


def iota(shape, dim):
    return lax.broadcasted_iota(jnp.int32, shape, dim)


def dot(a, b, dims=(((1,), (0,)), ((), ()))):
    return lax.dot_general(a, b, dims, preferred_element_type=F32)


def onehot(mask):
    return jnp.where(mask, 1.0, 0.0).astype(BF)


def sigmoid(v):
    return 1.0 / (1.0 + jnp.exp(-v))


def pack_kernel(feat_ref, cot_ref, slab_ref, base_ref, near_ref, off_ref, sent_ref, pos_ref):
    slab = slab_ref[...]
    named = iota((GY, PTS), 0) == slab
    earlier = onehot(iota((PTS, PTS), 0) < iota((PTS, PTS), 1))
    before = dot(onehot(named), earlier)
    rank = jnp.sum(jnp.where(named, before, 0.0), axis=0, keepdims=True)
    position = slab * CAP + rank.astype(jnp.int32)
    spread = jnp.broadcast_to(position.astype(F32), (C, PTS))
    pos_ref[...] = spread.T.astype(jnp.int32)
    base = base_ref[...]
    near = near_ref[...]
    a = base // (VY * Z)
    b = base // Z % VY
    c = base % Z
    fraction = off_ref[...].astype(F32)
    rows = [a + 2, b, c, a + near // 4 + 2, b + near // 2 % 2, c + near % 2]
    meta = jnp.concatenate(
        [r.astype(F32) for r in rows] + [fraction, jnp.zeros((KINDS - 9, PTS), F32)], axis=0
    ).astype(BF)
    both = jnp.concatenate([feat_ref[...], cot_ref[...]], axis=1)
    group = 8
    for g in range(GY // group):
        span = group * CAP
        chosen = onehot(iota((span, PTS), 0) + g * span == position)
        packed = dot(chosen, both).astype(BF).reshape(group, CAP, 2 * C)
        here = pl.ds(g * group, group)
        sent_ref[here, 0:CAP, :] = packed[:, :, :C]
        sent_ref[here, CAP : 2 * CAP, :] = packed[:, :, C:]
        lanes = dot(meta, chosen, RIGHT)
        for i in range(group):
            piece = lanes[:, i * CAP : (i + 1) * CAP]
            wide = jnp.concatenate([piece, jnp.zeros((KINDS, C - CAP), F32)], axis=1)
            sent_ref[g * group + i, 2 * CAP : 2 * CAP + KINDS, :] = wide.astype(BF)


def mlp_kernel(feat_ref, cot_ref, mlp_ref, act_ref, back_ref, grad_ref):
    feat = feat_ref[...]
    weight = mlp_ref[...]
    pre = dot(feat, weight)
    s = sigmoid(pre)
    act_ref[...] = pre * s
    grad_pre = (cot_ref[...].astype(F32) * (s * (1.0 + pre * (1.0 - s)))).astype(BF)
    back_ref[...] = dot(grad_pre, weight, RIGHT)
    grad_ref[...] = dot(grad_pre, feat, LEFT)


def voxel_kernel(got_ref, vox_ref, div_ref, own_ref, meta_ref):
    meta = jnp.concatenate(
        [got_ref[t, 2 * CAP : 2 * CAP + KINDS, :].astype(F32)[:, :CAP] for t in range(GY)], axis=1
    )
    meta_ref[...] = meta
    own = ((meta[3:4] - 2.0) * (VY * Z) + meta[4:5] * Z + meta[5:6]).astype(jnp.int32)
    own_hot = onehot(iota((CELLS, SLOTS), 0) == own)
    own_ref[...] = own_hot
    rows = got_ref[:, 0:CAP, :].reshape(SLOTS, C)
    both = jnp.concatenate([rows, jnp.ones((SLOTS, C), BF)], axis=1)
    total = dot(own_hot, both)
    divisor = jnp.maximum(total[:, C:], 1.0)
    div_ref[...] = divisor
    vox_ref[...] = (total[:, :C] / divisor).astype(BF).reshape(VX, VY, Z, C)


def spread_kernel(got_ref, meta_ref, matrix_ref, grad_ref):
    meta = meta_ref[...]
    a, b, c = meta[0:1] - 2.0, meta[1:2], meta[2:3]
    fx, fy, fz = meta[6:7], meta[7:8], meta[8:9]

    def side(distance, fraction):
        return jnp.where(distance == 0.0, 1.0 - fraction, jnp.where(distance == 1.0, fraction, 0.0))

    plane = VY * Z
    place = iota((plane, SLOTS), 0)
    wy = side((place // Z).astype(F32) - b, fy)
    wz = side((place % Z).astype(F32) - c, fz)
    for x in range(VX):
        wx = side(x - a, fx)
        matrix_ref[x * plane : (x + 1) * plane, :] = ((wx * wy) * wz).astype(BF)
    cots = got_ref[:, CAP : 2 * CAP, :].reshape(SLOTS, C)
    grad_ref[...] = dot(matrix_ref[...], cots)


def assemble(wide_ref, own_ref, xlo_ref, xhi_ref, ylo_ref, yhi_ref):
    def put(x, y, block):
        nx, ny = block.shape[0], block.shape[1]
        flat = block.reshape(nx * ny * Z, C).astype(F32)
        z = iota(flat.shape, 0) % Z
        blank = jnp.zeros((8, C), F32)
        down = jnp.concatenate([blank, flat], axis=0)[7 : 7 + flat.shape[0]]
        up = jnp.concatenate([flat, blank], axis=0)[1 : 1 + flat.shape[0]]
        down = jnp.where(z == 0, 0.0, down)
        up = jnp.where(z == Z - 1, 0.0, up)
        shape = (nx, ny, Z, C)
        wide_ref[x : x + nx, y : y + ny, :, 0:C] = down.astype(BF).reshape(shape)
        wide_ref[x : x + nx, y : y + ny, :, C : 2 * C] = block
        wide_ref[x : x + nx, y : y + ny, :, 2 * C :] = up.astype(BF).reshape(shape)

    put(1, 1, own_ref[...])
    put(0, 1, xlo_ref[...])
    put(VX + 1, 1, xhi_ref[...])
    put(0, 0, ylo_ref[...])
    put(0, VY + 1, yhi_ref[...])


def window(wide_ref, x, y):
    return wide_ref[x : x + VX, y : y + VY, :, :].reshape(CELLS, 3 * C)


def conv_kernel(core_ref, vox_ref, xlo_ref, xhi_ref, ylo_ref, yhi_ref, weight_ref, matrix_ref, gout_ref,
                mlp_ref, keep_ref, send_ref, sampled_ref, hid_ref, wide_ref, all_ref):
    assemble(wide_ref, vox_ref, xlo_ref, xhi_ref, ylo_ref, yhi_ref)
    hidden = jnp.zeros((CELLS, C), F32)
    for k in range(9):
        taps = weight_ref[3 * k : 3 * k + 3].reshape(3 * C, C)
        hidden = hidden + dot(window(wide_ref, k // 3, k % 3), taps)
    s = sigmoid(hidden)
    conv_out = (hidden * s).astype(BF)
    grad = gout_ref[...] * (s * (1.0 + hidden * (1.0 - s)))
    grad_hidden = grad.astype(BF)
    hid_ref[...] = grad_hidden.reshape(VX, VY, Z, C)
    turned = grad_hidden.astype(F32).T.astype(BF)
    for k in range(9):
        part = dot(turned, window(wide_ref, k // 3, k % 3))
        for j in range(3):
            all_ref[3 * k + j] = part[:, j * C : (j + 1) * C]
    all_ref[27] = mlp_ref[...]
    core = core_ref[0]
    keep_ref[...] = all_ref[pl.ds(core * HALF, HALF)]
    send_ref[...] = all_ref[pl.ds((1 - core) * HALF, HALF)].astype(BF)
    sampled_ref[...] = dot(matrix_ref[...], conv_out, LEFT).astype(BF).reshape(GY, CAP, C)


def join_kernel(keep_ref, got_ref, sampled_ref, out_ref):
    total = (keep_ref[...] + got_ref[...].astype(F32)).reshape(GY, SHARE, C)
    blank = jnp.zeros((GY, SHARE_PAD - SHARE, C), F32)
    out_ref[:, 0:SHARE_PAD, :] = jnp.concatenate([total, blank], axis=1).astype(BF)
    out_ref[:, SHARE_PAD:, :] = sampled_ref[...]


def share_kernel(got_ref, out_ref):
    total = jnp.sum(got_ref[:, 0:SHARE_PAD, :].astype(F32), axis=0)
    out_ref[...] = jnp.broadcast_to(total.astype(BF)[None], out_ref.shape)


def back_kernel(hid_ref, xlo_ref, xhi_ref, ylo_ref, yhi_ref, weight_ref, own_ref, div_ref, from_ref, wide_ref):
    assemble(wide_ref, hid_ref, xlo_ref, xhi_ref, ylo_ref, yhi_ref)
    total = jnp.zeros((CELLS, C), F32)
    for k in range(9):
        taps = jnp.concatenate([weight_ref[3 * k + 2 - j] for j in range(3)], axis=1)
        total = total + dot(window(wide_ref, 2 - k // 3, 2 - k % 3), taps, RIGHT)
    mean = (total / div_ref[...]).astype(BF)
    from_ref[...] = dot(own_ref[...], mean, LEFT).astype(BF).reshape(GY, CAP, C)


def spread_share_kernel(got_ref, from_ref, out_ref):
    total = jnp.sum(got_ref[...].astype(F32), axis=0)
    out_ref[:, 0:SHARE_PAD, :] = jnp.broadcast_to(total.astype(BF)[None], (GY, SHARE_PAD, C))
    out_ref[:, SHARE_PAD:, :] = from_ref[...]


def unpack(pos, rows):
    chosen = jnp.concatenate(
        [onehot(iota((PTS, C), 1) + i * C == pos) for i in range(SLOTS // C)], axis=1
    )
    return dot(chosen, rows)


def points_kernel(second, pos_ref, got_ref, base_ref, out_ref):
    rows = got_ref[:, SHARE_PAD:, :].reshape(SLOTS, C)
    out_ref[...] = (unpack(pos_ref[...], rows) + base_ref[...]).astype(BF)


def weights_kernel(half_ref, conv_ref, mlp_ref):
    for o in range(27):
        conv_ref[o] = half_ref[o].astype(F32).T * (1.0 / math.sqrt(GX * GY * CELLS))
    mlp_ref[...] = half_ref[27].astype(F32).T * (1.0 / math.sqrt(GX * GY * PTS))


def halo(cells):
    up = [(i, i + 1) for i in range(GX - 1)]
    down = [(i + 1, i) for i in range(GX - 1)]
    xlo = lax.ppermute(cells[VX - 1 :], ("y", "c"), up)
    xhi = lax.ppermute(cells[:1], ("y", "c"), down)
    tail = jnp.concatenate([xlo[:, VY - 1 :], cells[:, VY - 1 :], xhi[:, VY - 1 :]], axis=0)
    head = jnp.concatenate([xlo[:, :1], cells[:, :1], xhi[:, :1]], axis=0)
    up = [(i, i + 1) for i in range(GY - 1)]
    down = [(i + 1, i) for i in range(GY - 1)]
    ylo = lax.ppermute(tail, ("x", "z"), up)
    yhi = lax.ppermute(head, ("x", "z"), down)
    return xlo, xhi, ylo, yhi


def exchange(rows):
    return lax.all_to_all(rows, ("x", "z"), split_axis=0, concat_axis=0, tiled=True)


def body(features, point_slab, base_cell, nearest, offsets, conv_weight, mlp_weight, cotangent):
    core = lax.axis_index("c").reshape(1)
    sent, position = call(
        pack_kernel,
        (sds((GY, 2 * CAP + KINDS, C), BF), sds((PTS, C), jnp.int32)),
        (features, cotangent, point_slab.reshape(1, PTS), base_cell.reshape(1, PTS), nearest.reshape(1, PTS), offsets),
    )
    got = exchange(sent)
    act, mlp_back, mlp_grad = call(
        mlp_kernel,
        (sds((PTS, C), F32), sds((PTS, C), F32), sds((C, C), F32)),
        (features, cotangent, mlp_weight),
    )
    voxels, divisor, own_hot, meta = call(
        voxel_kernel,
        (sds((VX, VY, Z, C), BF), sds((CELLS, C), F32), sds((CELLS, SLOTS), BF), sds((KINDS, SLOTS), F32)),
        (got,),
    )
    faces = halo(voxels)
    matrix, grad_out = call(
        spread_kernel, (sds((CELLS, SLOTS), BF), sds((CELLS, C), F32)), (got, meta)
    )
    wide = pltpu.VMEM((VX + 2, VY + 2, Z, 3 * C), BF)
    keep, send, sampled, grad_hidden = call(
        conv_kernel,
        (
            sds((HALF, C, C), F32),
            sds((HALF, C, C), BF),
            sds((GY, CAP, C), BF),
            sds((VX, VY, Z, C), BF),
        ),
        (core, voxels) + faces + (conv_weight, matrix, grad_out, mlp_grad),
        scratch=(wide, pltpu.VMEM((2 * HALF, C, C), F32)),
        smem=1,
    )
    arrived = lax.ppermute(send, "c", [(0, 1), (1, 0)])
    joined = call(join_kernel, sds((GY, SHARE_PAD + CAP, C), BF), (keep, arrived, sampled))
    first = exchange(joined)
    grad_faces = halo(grad_hidden)
    from_voxels = call(
        back_kernel,
        sds((GY, CAP, C), BF),
        (grad_hidden,) + grad_faces + (conv_weight, own_hot, divisor),
        scratch=(wide,),
    )
    shares = call(share_kernel, sds((4, SHARE_PAD, C), BF), (first,))
    shares = lax.all_to_all(shares, "y", split_axis=0, concat_axis=0, tiled=True)
    second_rows = call(spread_share_kernel, sds((GY, SHARE_PAD + CAP, C), BF), (shares, from_voxels))
    second = exchange(second_rows)
    output = call(
        functools.partial(points_kernel, False), sds((PTS, C), BF), (position, first, act)
    )
    half = second[:, :SHARE, :].reshape(1, HALF, C, C)
    whole = lax.all_gather(half, "c", axis=0, tiled=True).reshape(2 * HALF, C, C)
    grad_features = call(
        functools.partial(points_kernel, True), sds((PTS, C), BF), (position, second, mlp_back)
    )
    grad_conv, grad_mlp = call(weights_kernel, (sds((27, C, C), F32), sds((C, C), F32)), (whole,))
    return (output, grad_features, grad_conv, grad_mlp)


def solution(mesh):
    fine = Mesh(mesh.devices.reshape(4, 2, 4, 8), ("y", "c", "x", "z"))
    rows = ("y", "c", "x", "z")
    in_specs = (P(rows, None), P(rows, None), P(rows), P(rows), P(None, rows), P(), P(), P(rows, None))
    out_specs = (P(rows, None), P(rows, None), P(), P())
    return jax.shard_map(body, mesh=fine, in_specs=in_specs, out_specs=out_specs, check_vma=False)
```

time: 452 us -> 163 us (0.36)
  waiting for transfers between devices: 286 us -> 35 us
  blocking collectives: 0 us -> 43.2 us
  matrix products: 34.9 us -> 0 us
  starting transfers between devices: 73.2 us -> 47 us
  Pallas kernels: 0 us -> 16.1 us
  between operations: 15.2 us -> 0.98 us
  local copies, waits for them, and re-layouts: 29.8 us -> 16.9 us
  other arithmetic: 10.2 us -> 2.52 us
    psum x1 -> x0, waiting for transfers between devices: 253 us -> none  [body(): conv_total, mlp_total = lax.psum((local_conv, local_mlp), ('gx', 'gy'))]
    dot_general x93 -> x0, matrix products: 34.9 us -> none  [the longest x54 10.4 us: convolve(): jnp.dot(window.reshape(-1, channels), kernel, preferred_element_type=jnp....]
    all_to_all x0 -> x1, blocking collectives: none -> 33.7 us  [exchange(): lax.all_to_all(rows, ('x', 'z'), split_axis=0, concat_axis=0, tiled=True)]
    all_to_all x6 -> x3, starting transfers between devices: 43.9 us -> 18.8 us  [the longest x2 12.8 us: exchange(): lax.all_to_all(rows, ('x', 'z'), split_axis=0, concat_axis=0, tiled=True)]
    pallas_call x0 -> x12, Pallas kernels: none -> 16.1 us  [call(): pl.pallas_call(kernel, out_shape=out_shape, in_specs=[SMEM] * smem + [VME...]
    unnamed x18 -> x58, local copies, waits for them, and re-layouts: 2.41 us -> 15.6 us
    scatter x5 -> x0, local copies, waits for them, and re-layouts: 12.7 us -> none  [the longest x3 6.95 us: pack_lanes(): filled = blank_lanes.at[:, position].set(lane_values)]
    gather x4 -> x0, local copies, waits for them, and re-layouts: 11.1 us -> none  [the longest x1 5.85 us: body(): divisor_ext[cells_in][:, None]]
  transfers between devices with their start and end apart: 15 -> 12, of which waited for: 8 -> 6; matrix products, arithmetic and copies ran while one was open for 9% -> 2% of each run, Pallas kernels for 0% -> 3%
where the time goes in v1:
time: 163 us; the launch traced here: 162 us
  starting transfers between devices  47 us (29%)
  blocking collectives  43.2 us (27%)
  waiting for transfers between devices  35 us (21%)
  local copies, waits for them, and re-layouts  16.9 us (10%)
  Pallas kernels  16.1 us (10%)
  other arithmetic  2.52 us (2%)
    all_to_all x1, blocking collectives, exchange(): lax.all_to_all(rows, ('x', 'z'), split_axis=0, concat_axis=0, tiled=True)  33.7 us
    all_to_all x2, waiting for transfers between devices, exchange(): lax.all_to_all(rows, ('x', 'z'), split_axis=0, concat_axis=0, tiled=True)  26.8 us
    pallas_call x12, Pallas kernels, call(): pl.pallas_call(kernel, out_shape=out_shape, in_specs=[SMEM] * smem + [VME...  16.1 us
    unnamed x58, local copies, waits for them, and re-layouts  15.6 us
    all_to_all x2, starting transfers between devices, exchange(): lax.all_to_all(rows, ('x', 'z'), split_axis=0, concat_axis=0, tiled=True)  12.8 us
    ppermute x2, starting transfers between devices, halo(): xhi = lax.ppermute(cells[:1], ('y', 'c'), down)  9.46 us
    all_gather x1, blocking collectives, body(): lax.all_gather(half, 'c', axis=0, tiled=True).reshape(2 * HALF, C, C)  9.42 us
    ppermute x2, starting transfers between devices, halo(): xlo = lax.ppermute(cells[VX - 1:], ('y', 'c'), up)  8.03 us
  transfers between devices with their start and end apart: 12, of which 6 were waited for; matrix products, arithmetic and copies ran while one was open for 2% of the time, Pallas kernels for 3%

profile of v1, /device:TPU:1, one launch (start us, length us, event | category | flops | bytes accessed | tf_op | source)
XLA Modules:
  0.0 161.6 jit_solution(6381740963811930644)
XLA Ops:
  5.2 1.3 shard_map.111
  7.2 33.7 %all_to_all.20.got_ref = bf16[32,112,128]{2,1,0:T(8,128)(2,1)S(1)} all-to-all(bf16[32,112,128]{2,1,0:T(8,128)(2,1)S(1)} %get-tuple-element.22), channel_id=1, replica_groups=mesh['y'=4,'c'=2,'x'=4,'z'=8] {'x','z'}, dimensions={0} | all-to-all | bytes 1835008 | tf_op jit(solution)/shard_map/all_to_all | solution.py:257
  43.2 7.0 %collective-permute-start.1 = (bf16[1,8,16,128]{3,2,1,0:T(8,128)(2,1)S(1)}, bf16[1,8,16,128]{3,2,1,0:T(8,128)(2,1)S(1)}, u32[]{:S(2)}, u32[]{:S(2)}) collective-permute-start(bf16[1,8,16,128]{3,2,1,0:T(8,128)(2,1)S(1)} %get-tuple-element.44), channel_id=1, source_target_pairs={{32,0},{64,32},{96,64},{128,96},{160,128},{192,160},{224,192},{33,... | collective-permute-start | bytes 98312 | tf_op jit(solution)/shard_map/ppermute | solution.py:246
  50.2 3.1 %collective-permute-start = (bf16[1,8,16,128]{3,2,1,0:T(8,128)(2,1)S(1)}, bf16[1,8,16,128]{3,2,1,0:T(8,128)(2,1)S(1)}, u32[]{:S(2)}, u32[]{:S(2)}) collective-permute-start(bf16[1,8,16,128]{3,2,1,0:T(8,128)(2,1)S(1)} %get-tuple-element.45), channel_id=1, source_target_pairs={{0,32},{32,64},{64,96},{96,128},{128,160},{160,192},{192,224},{1,3... | collective-permute-start | bytes 98312 | tf_op jit(solution)/shard_map/ppermute | solution.py:245
  55.5 3.8 %collective-permute-start.2 = (bf16[6,1,16,128]{3,2,1,0:T(8,128)(2,1)}, bf16[6,1,16,128]{3,2,1,0:T(8,128)(2,1)}, u32[]{:S(2)}, u32[]{:S(2)}) collective-permute-start(bf16[6,1,16,128]{3,2,1,0:T(8,128)(2,1)} %pad_maximum_fusion), channel_id=1, source_target_pairs={{0,1},{1,2},{2,3},{3,4},{4,5},{5,6},{6,7},{7,8},{8,9},{9,10},{10,1... | collective-permute-start | bytes 73736 | tf_op jit(solution)/shard_map/ppermute | solution.py:251
  59.9 1.3 collective-permute-start.3
  66.9 3.2 %shard_map.115 = (f32[14,128,128]{2,1,0:T(8,128)S(1)}, bf16[14,128,128]{2,1,0:T(8,128)(2,1)S(1)}, bf16[32,48,128]{2,1,0:T(8,128)(2,1)S(1)}, bf16[4,8,16,128]{3,2,1,0:T(8,128)(2,1)S(1)}) custom-call(s32[1]{0:T(128)} %bitcast.3.core_ref, bf16[4,8,16,128]{3,2,1,0:T(8,128)(2,1)S(1)} %copy-done.10, bf16[1,8,16,128]{3,2,1,0:T(8,128)(2,1)S(1)} %copy-done.21, ...), custom_call_target="tpu_custom_call" | custom-call | tf_op jit(solution)/shard_map/pallas_call | solution.py:39
  70.6 1.5 collective-permute-done.4.got_ref
  73.1 5.7 %all-to-all-start.1 = ((bf16[32,112,128]{2,1,0:T(8,128)(2,1)}), bf16[32,112,128]{2,1,0:T(8,128)(2,1)S(1)}, u32[]{:S(2)}, u32[]{:S(2)}) async-start(bf16[32,112,128]{2,1,0:T(8,128)(2,1)} %shard_map.116), calls=%async_computation.1 | async-start | bytes 1835008 | tf_op jit(solution)/shard_map/all_to_all | solution.py:257
  78.8 2.5 %collective-permute-start.6 = (bf16[1,8,16,128]{3,2,1,0:T(8,128)(2,1)S(1)}, bf16[1,8,16,128]{3,2,1,0:T(8,128)(2,1)S(1)}, u32[]{:S(2)}, u32[]{:S(2)}) collective-permute-start(bf16[1,8,16,128]{3,2,1,0:T(8,128)(2,1)S(1)} %get-tuple-element.40), channel_id=1, source_target_pairs={{32,0},{64,32},{96,64},{128,96},{160,128},{192,160},{224,192},{33,... | collective-permute-start | bytes 98312 | tf_op jit(solution)/shard_map/ppermute | solution.py:246
  81.3 4.9 %collective-permute-start.5 = (bf16[1,8,16,128]{3,2,1,0:T(8,128)(2,1)S(1)}, bf16[1,8,16,128]{3,2,1,0:T(8,128)(2,1)S(1)}, u32[]{:S(2)}, u32[]{:S(2)}) collective-permute-start(bf16[1,8,16,128]{3,2,1,0:T(8,128)(2,1)S(1)} %get-tuple-element.41), channel_id=1, source_target_pairs={{0,32},{32,64},{64,96},{96,128},{128,160},{160,192},{192,224},{1,3... | collective-permute-start | bytes 98312 | tf_op jit(solution)/shard_map/ppermute | solution.py:245
  88.5 4.0 %collective-permute-start.7 = (bf16[6,1,16,128]{3,2,1,0:T(8,128)(2,1)}, bf16[6,1,16,128]{3,2,1,0:T(8,128)(2,1)}, u32[]{:S(2)}, u32[]{:S(2)}) collective-permute-start(bf16[6,1,16,128]{3,2,1,0:T(8,128)(2,1)} %pad_maximum_fusion.2), channel_id=1, source_target_pairs={{0,1},{1,2},{2,3},{3,4},{4,5},{5,6},{6,7},{7,8},{8,9},{9,10},{10,1... | collective-permute-start | bytes 73736 | tf_op jit(solution)/shard_map/ppermute | solution.py:251
  92.5 8.6 %all-to-all-done.1.got_ref = bf16[32,112,128]{2,1,0:T(8,128)(2,1)S(1)} async-done(((bf16[32,112,128]{2,1,0:T(8,128)(2,1)}), bf16[32,112,128]{2,1,0:T(8,128)(2,1)S(1)}, u32[]{:S(2)}, u32[]{:S(2)}) %all-to-all-start.1) | async-done | bytes 917536 | tf_op jit(solution)/shard_map/all_to_all | solution.py:257
  101.8 5.9 %all-to-all-start.2 = ((bf16[4,64,128]{2,1,0:T(8,128)(2,1)}), bf16[4,64,128]{2,1,0:T(8,128)(2,1)}, u32[]{:S(2)}, u32[]{:S(2)}) async-start(bf16[4,64,128]{2,1,0:T(8,128)(2,1)} %copy-done.17), calls=%async_computation.2 | async-start | bytes 131072 | tf_op jit(solution)/shard_map/all_to_all | solution.py:306
  108.4 1.3 collective-permute-start.8
  109.7 5.4 %collective-permute-done.8.yhi_ref = bf16[6,1,16,128]{3,2,1,0:T(8,128)(2,1)S(1)} collective-permute-done((bf16[6,1,16,128]{3,2,1,0:T(8,128)(2,1)S(1)}, bf16[6,1,16,128]{3,2,1,0:T(8,128)(2,1)S(1)}, u32[]{:S(2)}, u32[]{:S(2)}) %collective-permute-start.8) | collective-permute-done | bytes 24608 | tf_op jit(solution)/shard_map/ppermute | solution.py:252
  116.8 2.4 %shard_map.119.from_ref = bf16[32,48,128]{2,1,0:T(8,128)(2,1)S(1)} custom-call(bf16[4,8,16,128]{3,2,1,0:T(8,128)(2,1)S(1)} %get-tuple-element.32.hid_ref, bf16[1,8,16,128]{3,2,1,0:T(8,128)(2,1)S(1)} %copy-done.23, bf16[1,8,16,128]{3,2,1,0:T(8,128)(2,1)S(1)} %collective-permute-done.6.xhi_ref, bf16[6,1,16,128]{3,2,1,0:T(8,128)(2,1)} %collective-permute-done.7.ylo_ref, ...), custom_call_target="tpu_custom_call" | custom-call | tf_op jit(solution)/shard_map/pallas_call | solution.py:39
  120.9 1.9 %shard_map.120 = bf16[32,112,128]{2,1,0:T(8,128)(2,1)} custom-call(bf16[4,64,128]{2,1,0:T(8,128)(2,1)} %all-to-all-done.2.got_ref, bf16[32,48,128]{2,1,0:T(8,128)(2,1)S(1)} %copy-done.2), custom_call_target="tpu_custom_call" | custom-call | tf_op jit(solution)/shard_map/pallas_call | solution.py:39
  122.8 7.1 %all-to-all-start.3 = ((bf16[32,112,128]{2,1,0:T(8,128)(2,1)}), bf16[32,112,128]{2,1,0:T(8,128)(2,1)S(1)}, u32[]{:S(2)}, u32[]{:S(2)}) async-start(bf16[32,112,128]{2,1,0:T(8,128)(2,1)} %shard_map.120), calls=%async_computation.3 | async-start | bytes 1835008 | tf_op jit(solution)/shard_map/all_to_all | solution.py:257
  130.0 1.2 shard_map.117
  131.2 18.2 %all-to-all-done.3.got_ref = bf16[32,112,128]{2,1,0:T(8,128)(2,1)S(1)} async-done(((bf16[32,112,128]{2,1,0:T(8,128)(2,1)}), bf16[32,112,128]{2,1,0:T(8,128)(2,1)S(1)}, u32[]{:S(2)}, u32[]{:S(2)}) %all-to-all-start.3) | async-done | bytes 917536 | tf_op jit(solution)/shard_map/all_to_all | solution.py:257
  149.4 9.4 %all_gather.3 = bf16[2,14,128,128]{3,2,1,0:T(8,128)(2,1)S(1)} all-gather(bf16[1,14,128,128]{3,2,1,0:T(8,128)(2,1)S(1)} %bitcast.10), channel_id=1, replica_groups=mesh['y'=4,'c'=2,'x'=4,'z'=8] {'c'}, dimensions={0}, use_global_device_ids=true | all-gather | bytes 1376256 | tf_op jit(solution)/shard_map/all_gather | solution.py:313
  158.9 1.5 shard_map.122
  160.4 1.2 shard_map.121
  (85 shorter events, 24.5 us)
Async XLA Ops:
  7.2 54.1 %copy-start.6 = (bf16[512,128]{1,0:T(8,128)(2,1)S(1)}, bf16[512,128]{1,0:T(8,128)(2,1)}, u32[]{:S(2)}) copy-start(bf16[512,128]{1,0:T(8,128)(2,1)} %feat_ref.3) | copy-start | bytes 393220
  40.9 24.3 %copy-start = (bf16[27,128,128]{2,1,0:T(8,128)(2,1)S(1)}, bf16[27,128,128]{2,1,0:T(8,128)(2,1)}, u32[]{:S(2)}) copy-start(bf16[27,128,128]{2,1,0:T(8,128)(2,1)} %weight_ref.3) | copy-start | bytes 2654212
  43.2 7.0 %copy-start.9 = (bf16[4,8,16,128]{3,2,1,0:T(8,128)(2,1)}, bf16[4,8,16,128]{3,2,1,0:T(8,128)(2,1)S(1)}, u32[]{:S(2)}) copy-start(bf16[4,8,16,128]{3,2,1,0:T(8,128)(2,1)S(1)} %get-tuple-element.23.vox_ref) | copy-start | bytes 393220
  43.2 10.1 %collective-permute-start.1 = (bf16[1,8,16,128]{3,2,1,0:T(8,128)(2,1)S(1)}, bf16[1,8,16,128]{3,2,1,0:T(8,128)(2,1)S(1)}, u32[]{:S(2)}, u32[]{:S(2)}) collective-permute-start(bf16[1,8,16,128]{3,2,1,0:T(8,128)(2,1)S(1)} %get-tuple-element.44), channel_id=1, source_target_pairs={{32,0},{64,32},{96,64},{128,96},{160,128},{192,160},{224,192},{33,... | collective-permute-start | bytes 98312 | tf_op jit(solution)/shard_map/ppermute | solution.py:246
  50.2 4.1 %collective-permute-start = (bf16[1,8,16,128]{3,2,1,0:T(8,128)(2,1)S(1)}, bf16[1,8,16,128]{3,2,1,0:T(8,128)(2,1)S(1)}, u32[]{:S(2)}, u32[]{:S(2)}) collective-permute-start(bf16[1,8,16,128]{3,2,1,0:T(8,128)(2,1)S(1)} %get-tuple-element.45), channel_id=1, source_target_pairs={{0,32},{32,64},{64,96},{96,128},{128,160},{160,192},{192,224},{1,3... | collective-permute-start | bytes 98312 | tf_op jit(solution)/shard_map/ppermute | solution.py:245
  55.5 9.7 %collective-permute-start.2 = (bf16[6,1,16,128]{3,2,1,0:T(8,128)(2,1)}, bf16[6,1,16,128]{3,2,1,0:T(8,128)(2,1)}, u32[]{:S(2)}, u32[]{:S(2)}) collective-permute-start(bf16[6,1,16,128]{3,2,1,0:T(8,128)(2,1)} %pad_maximum_fusion), channel_id=1, source_target_pairs={{0,1},{1,2},{2,3},{3,4},{4,5},{5,6},{6,7},{7,8},{8,9},{9,10},{10,1... | collective-permute-start | bytes 73736 | tf_op jit(solution)/shard_map/ppermute | solution.py:251
  59.9 5.3 %collective-permute-start.3 = (bf16[6,1,16,128]{3,2,1,0:T(8,128)(2,1)}, bf16[6,1,16,128]{3,2,1,0:T(8,128)(2,1)}, u32[]{:S(2)}, u32[]{:S(2)}) collective-permute-start(bf16[6,1,16,128]{3,2,1,0:T(8,128)(2,1)} %pad_maximum_fusion.1), channel_id=1, source_target_pairs={{1,0},{2,1},{3,2},{4,3},{5,4},{6,5},{7,6},{8,7},{9,8},{10,9},{11,1... | collective-permute-start | bytes 73736 | tf_op jit(solution)/shard_map/ppermute | solution.py:252
  63.3 6.8 %copy-start.13 = (f32[512,128]{1,0:T(8,128)}, f32[512,128]{1,0:T(8,128)S(1)}, u32[]{:S(2)}) copy-start(f32[512,128]{1,0:T(8,128)S(1)} %get-tuple-element.35.base_ref) | copy-start | bytes 786436
  63.3 6.8 %copy-start.15 = (f32[512,128]{1,0:T(8,128)}, f32[512,128]{1,0:T(8,128)S(1)}, u32[]{:S(2)}) copy-start(f32[512,128]{1,0:T(8,128)S(1)} %get-tuple-element.31.base_ref) | copy-start | bytes 786436
  63.4 1.0 copy-start.19
  70.1 1.9 %collective-permute-start.4 = (bf16[14,128,128]{2,1,0:T(8,128)(2,1)S(1)}, bf16[14,128,128]{2,1,0:T(8,128)(2,1)S(1)}, u32[]{:S(2)}, u32[]{:S(2)}) collective-permute-start(bf16[14,128,128]{2,1,0:T(8,128)(2,1)S(1)} %get-tuple-element.29), channel_id=1, source_target_pairs={{0,32},{32,0},{1,33},{33,1},{2,34},{34,2},{3,35},{35,3},{4,36},{36... | collective-permute-start | bytes 1376264 | tf_op jit(solution)/shard_map/ppermute | solution.py:295
  73.1 28.0 %all-to-all-start.1 = ((bf16[32,112,128]{2,1,0:T(8,128)(2,1)}), bf16[32,112,128]{2,1,0:T(8,128)(2,1)S(1)}, u32[]{:S(2)}, u32[]{:S(2)}) async-start(bf16[32,112,128]{2,1,0:T(8,128)(2,1)} %shard_map.116), calls=%async_computation.1 | async-start | bytes 1835008 | tf_op jit(solution)/shard_map/all_to_all | solution.py:257
  78.8 7.5 %collective-permute-start.6 = (bf16[1,8,16,128]{3,2,1,0:T(8,128)(2,1)S(1)}, bf16[1,8,16,128]{3,2,1,0:T(8,128)(2,1)S(1)}, u32[]{:S(2)}, u32[]{:S(2)}) collective-permute-start(bf16[1,8,16,128]{3,2,1,0:T(8,128)(2,1)S(1)} %get-tuple-element.40), channel_id=1, source_target_pairs={{32,0},{64,32},{96,64},{128,96},{160,128},{192,160},{224,192},{33,... | collective-permute-start | bytes 98312 | tf_op jit(solution)/shard_map/ppermute | solution.py:246
  81.3 5.9 %collective-permute-start.5 = (bf16[1,8,16,128]{3,2,1,0:T(8,128)(2,1)S(1)}, bf16[1,8,16,128]{3,2,1,0:T(8,128)(2,1)S(1)}, u32[]{:S(2)}, u32[]{:S(2)}) collective-permute-start(bf16[1,8,16,128]{3,2,1,0:T(8,128)(2,1)S(1)} %get-tuple-element.41), channel_id=1, source_target_pairs={{0,32},{32,64},{64,96},{96,128},{128,160},{160,192},{192,224},{1,3... | collective-permute-start | bytes 98312 | tf_op jit(solution)/shard_map/ppermute | solution.py:245
  87.3 1.2 copy-start.22
  88.5 21.2 %collective-permute-start.7 = (bf16[6,1,16,128]{3,2,1,0:T(8,128)(2,1)}, bf16[6,1,16,128]{3,2,1,0:T(8,128)(2,1)}, u32[]{:S(2)}, u32[]{:S(2)}) collective-permute-start(bf16[6,1,16,128]{3,2,1,0:T(8,128)(2,1)} %pad_maximum_fusion.2), channel_id=1, source_target_pairs={{0,1},{1,2},{2,3},{3,4},{4,5},{5,6},{6,7},{7,8},{8,9},{9,10},{10,1... | collective-permute-start | bytes 73736 | tf_op jit(solution)/shard_map/ppermute | solution.py:251
  101.8 18.1 %all-to-all-start.2 = ((bf16[4,64,128]{2,1,0:T(8,128)(2,1)}), bf16[4,64,128]{2,1,0:T(8,128)(2,1)}, u32[]{:S(2)}, u32[]{:S(2)}) async-start(bf16[4,64,128]{2,1,0:T(8,128)(2,1)} %copy-done.17), calls=%async_computation.2 | async-start | bytes 131072 | tf_op jit(solution)/shard_map/all_to_all | solution.py:306
  108.4 6.7 %collective-permute-start.8 = (bf16[6,1,16,128]{3,2,1,0:T(8,128)(2,1)S(1)}, bf16[6,1,16,128]{3,2,1,0:T(8,128)(2,1)S(1)}, u32[]{:S(2)}, u32[]{:S(2)}) collective-permute-start(bf16[6,1,16,128]{3,2,1,0:T(8,128)(2,1)S(1)} %pad_maximum_fusion.3), channel_id=1, source_target_pairs={{1,0},{2,1},{3,2},{4,3},{5,4},{6,5},{7,6},{8,7},{9,8},{10,9},{11,1... | collective-permute-start | bytes 73736 | tf_op jit(solution)/shard_map/ppermute | solution.py:252
  115.1 1.0 copy-start.12
  119.9 1.0 copy-start.2
  120.9 9.0 %copy-start.4 = (s32[512,128]{1,0:T(8,128)S(1)}, s32[512,128]{1,0:T(8,128)}, u32[]{:S(2)}) copy-start(s32[512,128]{1,0:T(8,128)} %copy-done.3) | copy-start | bytes 786436
  120.9 9.0 %copy-start.16 = (f32[512,128]{1,0:T(8,128)S(1)}, f32[512,128]{1,0:T(8,128)}, u32[]{:S(2)}) copy-start(f32[512,128]{1,0:T(8,128)} %copy-done.15) | copy-start | bytes 786436
  122.8 26.6 %all-to-all-start.3 = ((bf16[32,112,128]{2,1,0:T(8,128)(2,1)}), bf16[32,112,128]{2,1,0:T(8,128)(2,1)S(1)}, u32[]{:S(2)}, u32[]{:S(2)}) async-start(bf16[32,112,128]{2,1,0:T(8,128)(2,1)} %shard_map.120), calls=%async_computation.3 | async-start | bytes 1835008 | tf_op jit(solution)/shard_map/all_to_all | solution.py:257
  131.2 29.2 %copy-start.14 = (f32[512,128]{1,0:T(8,128)S(1)}, f32[512,128]{1,0:T(8,128)}, u32[]{:S(2)}) copy-start(f32[512,128]{1,0:T(8,128)} %copy-done.13) | copy-start | bytes 786436
  (17 other events, 12.7 us)

commit v2 on v1

v2 whole, which is shorter than its diff:
```python
import math

import jax
import jax.numpy as jnp
from jax import lax
from jax.experimental import pallas as pl
from jax.experimental.pallas import tpu as pltpu
from jax.sharding import Mesh, PartitionSpec as P

C = 128
VX = 4
VY = 8
Z = 16
CELLS = VX * VY * Z
PTS = 512
CAP = 48
GY = 32
SLOTS = GY * CAP
GX = 8
KINDS = 8
HALF = 14
SHARE = HALF * C // GY
ROWS = CAP + SHARE
BF = jnp.bfloat16
F32 = jnp.float32
VMEM = pl.BlockSpec(memory_space=pltpu.VMEM)
SMEM = pl.BlockSpec(memory_space=pltpu.SMEM)
HBM = pl.BlockSpec(memory_space=pltpu.HBM)
LEFT = (((0,), (0,)), ((), ()))
RIGHT = (((1,), (1,)), ((), ()))


def sds(shape, dtype):
    return jax.ShapeDtypeStruct(shape, dtype)


def call(kernel, out_shape, args, scratch=(), smem=0, hbm=0, mib=12):
    return pl.pallas_call(
        kernel,
        out_shape=out_shape,
        in_specs=[SMEM] * smem + [HBM] * hbm + [VMEM] * (len(args) - smem - hbm),
        out_specs=jax.tree.map(lambda _: VMEM, out_shape),
        scratch_shapes=list(scratch),
        compiler_params=pltpu.CompilerParams(vmem_limit_bytes=mib * 1024 * 1024),
    )(*args)


def iota(shape, dim):
    return lax.broadcasted_iota(jnp.int32, shape, dim)


def dot(a, b, dims=(((1,), (0,)), ((), ()))):
    return lax.dot_general(a, b, dims, preferred_element_type=F32)


def onehot(mask):
    return jnp.where(mask, 1.0, 0.0).astype(BF)


def sigmoid(v):
    return 1.0 / (1.0 + jnp.exp(-v))


def places(slab):
    named = iota((GY, PTS), 0) == slab
    earlier = onehot(iota((PTS, PTS), 0) < iota((PTS, PTS), 1))
    before = dot(onehot(named), earlier)
    rank = jnp.sum(jnp.where(named, before, 0.0), axis=0, keepdims=True)
    return slab * CAP + rank.astype(jnp.int32)


def pack_kernel(feat_hbm, cot_hbm, slab_hbm, base_hbm, near_hbm, off_hbm, sent_ref,
                both_ref, slab_ref, base_ref, near_ref, off_ref, sems):
    moves = [
        pltpu.make_async_copy(slab_hbm, slab_ref, sems.at[0]),
        pltpu.make_async_copy(base_hbm, base_ref, sems.at[1]),
        pltpu.make_async_copy(near_hbm, near_ref, sems.at[2]),
        pltpu.make_async_copy(off_hbm, off_ref, sems.at[3]),
        pltpu.make_async_copy(feat_hbm, both_ref.at[:, 0:C], sems.at[4]),
        pltpu.make_async_copy(cot_hbm, both_ref.at[:, C : 2 * C], sems.at[5]),
    ]
    for move in moves:
        move.start()
    for move in moves:
        move.wait()
    position = places(slab_ref[...])
    base = base_ref[...]
    near = near_ref[...]
    a = base // (VY * Z)
    b = base // Z % VY
    c = base % Z
    fraction = off_ref[...].astype(F32)
    rows = [a + 2, b, c, near]
    meta = jnp.concatenate(
        [r.astype(F32) for r in rows] + [fraction, jnp.zeros((KINDS - 7, PTS), F32)], axis=0
    ).astype(BF)
    both = both_ref[...]
    group = 8
    for g in range(GY // group):
        span = group * CAP
        chosen = onehot(iota((span, PTS), 0) + g * span == position)
        packed = dot(chosen, both).astype(BF).reshape(group, CAP, 2 * C)
        here = pl.ds(g * group, group)
        sent_ref[here, 0:CAP, :] = packed[:, :, :C]
        sent_ref[here, CAP : 2 * CAP, :] = packed[:, :, C:]
        lanes = dot(meta, chosen, RIGHT)
        for i in range(group):
            piece = lanes[:, i * CAP : (i + 1) * CAP]
            wide = jnp.concatenate([piece, jnp.zeros((KINDS, C - CAP), F32)], axis=1)
            sent_ref[g * group + i, 2 * CAP : 2 * CAP + KINDS, :] = wide.astype(BF)


def slope(v, s):
    return s * (1.0 + v * (1.0 - s))


def mlp_kernel(feat_ref, cot_ref, mlp_ref, grad_ref):
    feat = feat_ref[...]
    pre = dot(feat, mlp_ref[...])
    grad_pre = (cot_ref[...].astype(F32) * slope(pre, sigmoid(pre))).astype(BF)
    grad_ref[...] = dot(grad_pre, feat, LEFT)


def arrived_meta(got_ref):
    return jnp.concatenate(
        [got_ref[t, 2 * CAP : 2 * CAP + KINDS, :].astype(F32)[:, :CAP] for t in range(GY)], axis=1
    )


def own_matrix(meta):
    near = meta[3:4].astype(jnp.int32)
    base = (meta[0:1] - 2.0) * (VY * Z) + meta[1:2] * Z + meta[2:3]
    own = base.astype(jnp.int32) + near // 4 * (VY * Z) + near // 2 % 2 * Z + near % 2
    return onehot(iota((CELLS, SLOTS), 0) == own)


def voxel_kernel(got_ref, vox_ref, lo_ref, hi_ref, div_ref, meta_ref):
    meta = arrived_meta(got_ref)
    meta_ref[...] = meta
    own_hot = own_matrix(meta)
    rows = got_ref[:, 0:CAP, :].reshape(SLOTS, C)
    both = jnp.concatenate([rows, jnp.ones((SLOTS, C), BF)], axis=1)
    total = dot(own_hot, both)
    divisor = jnp.maximum(total[:, C:], 1.0)
    div_ref[...] = divisor
    voxels = (total[:, :C] / divisor).astype(BF).reshape(VX, VY, Z, C)
    vox_ref[...] = voxels
    lo_ref[...] = voxels[:1]
    hi_ref[...] = voxels[VX - 1 :]


def spread_kernel(got_ref, meta_ref, matrix_ref, grad_ref):
    meta = meta_ref[...]
    a, b, c = meta[0:1] - 2.0, meta[1:2], meta[2:3]
    fx, fy, fz = meta[4:5], meta[5:6], meta[6:7]

    def side(distance, fraction):
        return jnp.where(distance == 0.0, 1.0 - fraction, jnp.where(distance == 1.0, fraction, 0.0))

    plane = VY * Z
    place = iota((plane, SLOTS), 0)
    wy = side((place // Z).astype(F32) - b, fy)
    wz = side((place % Z).astype(F32) - c, fz)
    for x in range(VX):
        wx = side(x - a, fx)
        matrix_ref[x * plane : (x + 1) * plane, :] = ((wx * wy) * wz).astype(BF)
    cots = got_ref[:, CAP : 2 * CAP, :].reshape(SLOTS, C)
    grad_ref[...] = dot(matrix_ref[...], cots)


def edge_kernel(xlo_ref, own_ref, xhi_ref, tail_ref, head_ref):
    for ref, y in ((tail_ref, VY - 1), (head_ref, 0)):
        ref[0] = xlo_ref[0, y : y + 1]
        ref[1 : VX + 1] = own_ref[:, y : y + 1]
        ref[VX + 1] = xhi_ref[0, y : y + 1]


def assemble(wide_ref, own_ref, xlo_ref, xhi_ref, ylo_ref, yhi_ref):
    def put(x, y, block):
        nx, ny = block.shape[0], block.shape[1]
        flat = block.reshape(nx * ny * Z, C).astype(F32)
        z = iota(flat.shape, 0) % Z
        blank = jnp.zeros((8, C), F32)
        down = jnp.concatenate([blank, flat], axis=0)[7 : 7 + flat.shape[0]]
        up = jnp.concatenate([flat, blank], axis=0)[1 : 1 + flat.shape[0]]
        down = jnp.where(z == 0, 0.0, down)
        up = jnp.where(z == Z - 1, 0.0, up)
        shape = (nx, ny, Z, C)
        wide_ref[x : x + nx, y : y + ny, :, 0:C] = down.astype(BF).reshape(shape)
        wide_ref[x : x + nx, y : y + ny, :, C : 2 * C] = block
        wide_ref[x : x + nx, y : y + ny, :, 2 * C :] = up.astype(BF).reshape(shape)

    put(1, 1, own_ref[...])
    put(0, 1, xlo_ref[...])
    put(VX + 1, 1, xhi_ref[...])
    put(0, 0, ylo_ref[...])
    put(0, VY + 1, yhi_ref[...])


def window(wide_ref, x, y):
    return wide_ref[x : x + VX, y : y + VY, :, :].reshape(CELLS, 3 * C)


def conv_kernel(core_ref, vox_ref, xlo_ref, xhi_ref, ylo_ref, yhi_ref, weight_ref, gout_ref,
                mlp_ref, keep_ref, send_ref, act_ref, hid_ref, lo_ref, hi_ref, wide_ref, all_ref):
    assemble(wide_ref, vox_ref, xlo_ref, xhi_ref, ylo_ref, yhi_ref)
    hidden = jnp.zeros((CELLS, C), F32)
    for k in range(9):
        taps = weight_ref[3 * k : 3 * k + 3].reshape(3 * C, C)
        hidden = hidden + dot(window(wide_ref, k // 3, k % 3), taps)
    s = sigmoid(hidden)
    act_ref[...] = (hidden * s).astype(BF)
    grad_hidden = (gout_ref[...] * slope(hidden, s)).astype(BF)
    shaped = grad_hidden.reshape(VX, VY, Z, C)
    hid_ref[...] = shaped
    lo_ref[...] = shaped[:1]
    hi_ref[...] = shaped[VX - 1 :]
    turned = grad_hidden.astype(F32).T.astype(BF)
    for k in range(9):
        part = dot(turned, window(wide_ref, k // 3, k % 3))
        for j in range(3):
            all_ref[3 * k + j] = part[:, j * C : (j + 1) * C]
    all_ref[27] = mlp_ref[...]
    core = core_ref[0]
    keep_ref[...] = all_ref[pl.ds(core * HALF, HALF)]
    send_ref[...] = all_ref[pl.ds((1 - core) * HALF, HALF)].astype(BF)


def sample_kernel(matrix_ref, act_ref, out_ref):
    out_ref[...] = dot(matrix_ref[...], act_ref[...], LEFT).astype(BF).reshape(GY, CAP, C)


def join_kernel(keep_ref, got_ref, filled_ref, out_ref):
    total = keep_ref[...] + got_ref[...].astype(F32)
    out_ref[:, CAP:, :] = total.reshape(GY, SHARE, C).astype(BF)
    out_ref[:, 0:CAP, :] = filled_ref[...]


def share_kernel(got_ref, out_ref):
    total = jnp.sum(got_ref[:, CAP:, :].astype(F32), axis=0)
    out_ref[...] = jnp.broadcast_to(total.astype(BF)[None], out_ref.shape)


def back_kernel(hid_ref, xlo_ref, xhi_ref, ylo_ref, yhi_ref, weight_ref, meta_ref, div_ref, out_ref, wide_ref):
    assemble(wide_ref, hid_ref, xlo_ref, xhi_ref, ylo_ref, yhi_ref)
    total = jnp.zeros((CELLS, C), F32)
    for k in range(9):
        taps = jnp.concatenate([weight_ref[3 * k + 2 - j] for j in range(3)], axis=1)
        total = total + dot(window(wide_ref, 2 - k // 3, 2 - k % 3), taps, RIGHT)
    mean = (total / div_ref[...]).astype(BF)
    out_ref[...] = dot(own_matrix(meta_ref[...]), mean, LEFT).astype(BF).reshape(GY, CAP, C)


def spread_share_kernel(got_ref, filled_ref, out_ref):
    total = jnp.sum(got_ref[...].astype(F32), axis=0)
    out_ref[:, CAP:, :] = jnp.broadcast_to(total.astype(BF)[None], (GY, SHARE, C))
    out_ref[:, 0:CAP, :] = filled_ref[...]


def unpack(pos, got_ref):
    rows = got_ref[:, 0:CAP, :].reshape(SLOTS, C)
    chosen = jnp.concatenate(
        [onehot(iota((PTS, C), 1) + i * C == pos) for i in range(SLOTS // C)], axis=1
    )
    return dot(chosen, rows)


def forward_kernel(got_ref, slab_ref, feat_ref, cot_ref, mlp_ref, out_ref, pos_ref, back_ref):
    spread = jnp.broadcast_to(places(slab_ref[...]).astype(F32), (C, PTS))
    pos = spread.T.astype(jnp.int32)
    pos_ref[...] = pos
    weight = mlp_ref[...]
    pre = dot(feat_ref[...], weight)
    s = sigmoid(pre)
    grad_pre = (cot_ref[...].astype(F32) * slope(pre, s)).astype(BF)
    back_ref[...] = dot(grad_pre, weight, RIGHT)
    sampled = unpack(pos, got_ref).astype(BF).astype(F32)
    out_ref[...] = (sampled + pre * s).astype(BF)


def take_kernel(got_ref, out_ref):
    out_ref[...] = got_ref[:, CAP:, :].astype(F32).reshape(HALF, C, C).astype(BF)


def backward_kernel(got_ref, pos_ref, back_ref, out_ref):
    out_ref[...] = (unpack(pos_ref[...], got_ref) + back_ref[...]).astype(BF)


def weights_kernel(core_ref, mine_ref, other_ref, conv_ref, mlp_ref):
    def fill(first_ref, second_ref):
        for o in range(27):
            half = first_ref[o] if o < HALF else second_ref[o - HALF]
            conv_ref[o] = half.astype(F32).T * (1.0 / math.sqrt(GX * GY * CELLS))
        mlp_ref[...] = second_ref[HALF - 1].astype(F32).T * (1.0 / math.sqrt(GX * GY * PTS))

    @pl.when(core_ref[0] == 0)
    def _():
        fill(mine_ref, other_ref)

    @pl.when(core_ref[0] == 1)
    def _():
        fill(other_ref, mine_ref)


FACE = sds((1, VY, Z, C), BF)
EDGE = sds((VX + 2, 1, Z, C), BF)


def halo(cells, lo, hi):
    up = [(i, i + 1) for i in range(GX - 1)]
    down = [(i + 1, i) for i in range(GX - 1)]
    xlo = lax.ppermute(hi, ("y", "c"), up)
    xhi = lax.ppermute(lo, ("y", "c"), down)
    tail, head = call(edge_kernel, (EDGE, EDGE), (xlo, cells, xhi), mib=2)
    up = [(i, i + 1) for i in range(GY - 1)]
    down = [(i + 1, i) for i in range(GY - 1)]
    ylo = lax.ppermute(tail, ("x", "z"), up)
    yhi = lax.ppermute(head, ("x", "z"), down)
    return xlo, xhi, ylo, yhi


def exchange(rows):
    return lax.all_to_all(rows, ("x", "z"), split_axis=0, concat_axis=0, tiled=True)


def swap(half):
    return lax.ppermute(half, "c", [(0, 1), (1, 0)])


def body(features, point_slab, base_cell, nearest, offsets, conv_weight, mlp_weight, cotangent):
    core = lax.axis_index("c").reshape(1)
    point_slab, core = lax.optimization_barrier((point_slab, core))
    slab = point_slab.reshape(1, PTS)
    line = pltpu.VMEM((1, PTS), jnp.int32)
    sent = call(
        pack_kernel,
        sds((GY, 2 * CAP + KINDS, C), BF),
        (features, cotangent, slab, base_cell.reshape(1, PTS), nearest.reshape(1, PTS), offsets),
        scratch=(
            pltpu.VMEM((PTS, 2 * C), BF),
            line,
            line,
            line,
            pltpu.VMEM((3, PTS), BF),
            pltpu.SemaphoreType.DMA((6,)),
        ),
        hbm=6,
        mib=60,
    )
    got = exchange(sent)
    mlp_grad = call(mlp_kernel, sds((C, C), F32), (features, cotangent, mlp_weight))
    got, mlp_grad = lax.optimization_barrier((got, mlp_grad))
    cells = sds((VX, VY, Z, C), BF)
    voxels, lo, hi, divisor, meta = call(
        voxel_kernel,
        (cells, FACE, FACE, sds((CELLS, C), F32), sds((KINDS, SLOTS), F32)),
        (got,),
    )
    faces = halo(voxels, lo, hi)
    matrix, grad_out = call(
        spread_kernel, (sds((CELLS, SLOTS), BF), sds((CELLS, C), F32)), (got, meta)
    )
    wide = pltpu.VMEM((VX + 2, VY + 2, Z, 3 * C), BF)
    block = sds((GY, ROWS, C), BF)
    rows = sds((GY, CAP, C), BF)
    keep, send, act, grad_hidden, lo, hi = call(
        conv_kernel,
        (sds((HALF, C, C), F32), sds((HALF, C, C), BF), sds((CELLS, C), BF), cells, FACE, FACE),
        (core, voxels) + faces + (conv_weight, grad_out, mlp_grad),
        scratch=(wide, pltpu.VMEM((2 * HALF, C, C), F32)),
        smem=1,
    )
    arrived = swap(send)
    filled = call(sample_kernel, rows, (matrix, act))
    joined = call(join_kernel, block, (keep, arrived, filled))
    first = exchange(joined)
    grad_faces = halo(grad_hidden, lo, hi)
    filled = call(
        back_kernel,
        rows,
        (grad_hidden,) + grad_faces + (conv_weight, meta, divisor),
        scratch=(wide,),
    )
    first, filled = lax.optimization_barrier((first, filled))
    shares = call(share_kernel, sds((4, SHARE, C), BF), (first,), mib=4)
    shares = lax.all_to_all(shares, "y", split_axis=0, concat_axis=0, tiled=True)
    joined = call(spread_share_kernel, block, (shares, filled))
    second = exchange(joined)
    output, position, back = call(
        forward_kernel,
        (sds((PTS, C), BF), sds((PTS, C), jnp.int32), sds((PTS, C), F32)),
        (first, slab, features, cotangent, mlp_weight),
    )
    second, back = lax.optimization_barrier((second, back))
    mine = call(take_kernel, sds((HALF, C, C), BF), (second,), mib=4)
    other = swap(mine)
    grad_features = call(backward_kernel, sds((PTS, C), BF), (second, position, back))
    grad_conv, grad_mlp = call(
        weights_kernel, (sds((27, C, C), F32), sds((C, C), F32)), (core, mine, other), smem=1
    )
    return (output, grad_features, grad_conv, grad_mlp)


def solution(mesh):
    fine = Mesh(mesh.devices.reshape(4, 2, 4, 8), ("y", "c", "x", "z"))
    rows = ("y", "c", "x", "z")
    in_specs = (P(rows, None), P(rows, None), P(rows), P(rows), P(None, rows), P(), P(), P(rows, None))
    out_specs = (P(rows, None), P(rows, None), P(), P())
    return jax.shard_map(body, mesh=fine, in_specs=in_specs, out_specs=out_specs, check_vma=False)
```

time: 163 us -> 139 us (0.85)
  blocking collectives: 43.2 us -> 8.16 us
  waiting for transfers between devices: 35 us -> 53.2 us
  local copies, waits for them, and re-layouts: 16.9 us -> 0.03 us
  starting transfers between devices: 47 us -> 59.8 us
  other arithmetic: 2.52 us -> 0 us
    all_to_all x1, blocking collectives: 33.7 us -> 8.16 us  [body(): lax.all_to_all(shares, 'y', split_axis=0, concat_axis=0, tiled=True)]
    unnamed x58 -> x10, local copies, waits for them, and re-layouts: 15.6 us -> 0.03 us
    all_to_all x2 -> x3, starting transfers between devices: 12.8 us -> 27.4 us  [exchange(): lax.all_to_all(rows, ('x', 'z'), split_axis=0, concat_axis=0, tiled=True)]
    all_to_all x2 -> x3, waiting for transfers between devices: 26.8 us -> 36.4 us  [exchange(): lax.all_to_all(rows, ('x', 'z'), split_axis=0, concat_axis=0, tiled=True)]
    all_gather x1 -> x0, blocking collectives: 9.42 us -> none  [body(): lax.all_gather(half, 'c', axis=0, tiled=True).reshape(2 * HALF, C, C)]
    all_to_all x1 -> x0, starting transfers between devices: 5.9 us -> none  [body(): lax.all_to_all(shares, 'y', split_axis=0, concat_axis=0, tiled=True)]
    ppermute x5 -> x6, starting transfers between devices: 17.9 us -> 23.4 us  [the longest x2 12.1 us: halo(): xlo = lax.ppermute(hi, ('y', 'c'), up)]
    ppermute x5 -> x6, waiting for transfers between devices: 2.88 us -> 8.28 us  [the longest x2 6.88 us: halo(): xhi = lax.ppermute(lo, ('y', 'c'), down)]
  transfers between devices with their start and end apart: 12 -> 13, of which waited for: 6 -> 9; matrix products, arithmetic and copies ran while one was open for 2% -> 0% of each run, Pallas kernels for 3% -> 5%
where the time goes in v2:
time: 139 us; the launch traced here: 138 us
  starting transfers between devices  59.8 us (43%)
  waiting for transfers between devices  53.2 us (38%)
  Pallas kernels  16 us (12%)
  blocking collectives  8.16 us (6%)
    all_to_all x3, waiting for transfers between devices, exchange(): lax.all_to_all(rows, ('x', 'z'), split_axis=0, concat_axis=0, tiled=True)  36.4 us
    all_to_all x3, starting transfers between devices, exchange(): lax.all_to_all(rows, ('x', 'z'), split_axis=0, concat_axis=0, tiled=True)  27.4 us
    pallas_call x16, Pallas kernels, call(): pl.pallas_call(kernel, out_shape=out_shape, in_specs=[SMEM] * smem + [HBM...  16 us
    ppermute x2, starting transfers between devices, halo(): xlo = lax.ppermute(hi, ('y', 'c'), up)  12.1 us
    all_to_all x1, blocking collectives, body(): lax.all_to_all(shares, 'y', split_axis=0, concat_axis=0, tiled=True)  8.16 us
    ppermute x2, starting transfers between devices, swap(): return lax.ppermute(half, 'c', [(0, 1), (1, 0)])  7.43 us
    ppermute x2, waiting for transfers between devices, halo(): xhi = lax.ppermute(lo, ('y', 'c'), down)  6.88 us
    ppermute x2, starting transfers between devices, halo(): ylo = lax.ppermute(tail, ('x', 'z'), up)  6.52 us
  transfers between devices with their start and end apart: 13, of which 9 were waited for; matrix products, arithmetic and copies ran while one was open for 0% of the time, Pallas kernels for 5%

profile of v2, /device:TPU:1, one launch (start us, length us, event | category | flops | bytes accessed | tf_op | source)
XLA Modules:
  0.0 138.1 jit_solution(15749624535841196701)
XLA Ops:
  0.7 3.3 %shard_map.111 = bf16[32,104,128]{2,1,0:T(8,128)(2,1)} custom-call(bf16[512,128]{1,0:T(8,128)(2,1)} %feat_ref.3, bf16[512,128]{1,0:T(8,128)(2,1)} %cot_ref.3, s32[1,512]{1,0:T(1,128)} %bitcast.4, s32[1,512]{1,0:T(1,128)} %bitcast.6, s32[1,512]{1,0:T(1,128)} %bitcast.7, bf16[3,512]{1,0:T(4,128)(2,1)} %off_hbm.1), custom_call_target="tpu_custom_call" | custom-call | tf_op jit(solution)/shard_map/pallas_call | solution.py:38
  4.0 12.0 %all-to-all-start = ((bf16[32,104,128]{2,1,0:T(8,128)(2,1)}), bf16[32,104,128]{2,1,0:T(8,128)(2,1)S(1)}, u32[]{:S(2)}, u32[]{:S(2)}) async-start(bf16[32,104,128]{2,1,0:T(8,128)(2,1)} %shard_map.111), calls=%async_computation | async-start | bytes 1703936 | tf_op jit(solution)/shard_map/all_to_all | solution.py:323
  16.5 19.9 %all-to-all-done.got_ref = bf16[32,104,128]{2,1,0:T(8,128)(2,1)S(1)} async-done(((bf16[32,104,128]{2,1,0:T(8,128)(2,1)}), bf16[32,104,128]{2,1,0:T(8,128)(2,1)S(1)}, u32[]{:S(2)}, u32[]{:S(2)}) %all-to-all-start) | async-done | bytes 852000 | tf_op jit(solution)/shard_map/all_to_all | solution.py:323
  37.0 8.5 %collective-permute-start = (bf16[1,8,16,128]{3,2,1,0:T(8,128)(2,1)S(1)}, bf16[1,8,16,128]{3,2,1,0:T(8,128)(2,1)S(1)}, u32[]{:S(2)}, u32[]{:S(2)}) collective-permute-start(bf16[1,8,16,128]{3,2,1,0:T(8,128)(2,1)S(1)} %get-tuple-element.38), channel_id=1, source_target_pairs={{0,32},{32,64},{64,96},{96,128},{128,160},{160,192},{192,224},{1,3... | collective-permute-start | bytes 98312 | tf_op jit(solution)/shard_map/ppermute | solution.py:312
  45.5 1.9 %collective-permute-start.1 = (bf16[1,8,16,128]{3,2,1,0:T(8,128)(2,1)S(1)}, bf16[1,8,16,128]{3,2,1,0:T(8,128)(2,1)S(1)}, u32[]{:S(2)}, u32[]{:S(2)}) collective-permute-start(bf16[1,8,16,128]{3,2,1,0:T(8,128)(2,1)S(1)} %get-tuple-element.39), channel_id=1, source_target_pairs={{32,0},{64,32},{96,64},{128,96},{160,128},{192,160},{224,192},{33,... | collective-permute-start | bytes 98312 | tf_op jit(solution)/shard_map/ppermute | solution.py:313
  47.5 3.3 %collective-permute-done.1.xhi_ref = bf16[1,8,16,128]{3,2,1,0:T(8,128)(2,1)S(1)} collective-permute-done((bf16[1,8,16,128]{3,2,1,0:T(8,128)(2,1)S(1)}, bf16[1,8,16,128]{3,2,1,0:T(8,128)(2,1)S(1)}, u32[]{:S(2)}, u32[]{:S(2)}) %collective-permute-start.1) | collective-permute-done | bytes 32800 | tf_op jit(solution)/shard_map/ppermute | solution.py:313
  50.8 3.1 %collective-permute-start.2 = (bf16[6,1,16,128]{3,2,1,0:T(8,128)(2,1)S(1)}, bf16[6,1,16,128]{3,2,1,0:T(8,128)(2,1)S(1)}, u32[]{:S(2)}, u32[]{:S(2)}) collective-permute-start(bf16[6,1,16,128]{3,2,1,0:T(8,128)(2,1)S(1)} %get-tuple-element.40), channel_id=1, source_target_pairs={{0,1},{1,2},{2,3},{3,4},{4,5},{5,6},{6,7},{7,8},{8,9},{9,10},{10,1... | collective-permute-start | bytes 73736 | tf_op jit(solution)/shard_map/ppermute | solution.py:317
  53.9 1.3 collective-permute-start.3
  56.0 2.4 %collective-permute-done.3.yhi_ref = bf16[6,1,16,128]{3,2,1,0:T(8,128)(2,1)S(1)} collective-permute-done((bf16[6,1,16,128]{3,2,1,0:T(8,128)(2,1)S(1)}, bf16[6,1,16,128]{3,2,1,0:T(8,128)(2,1)S(1)}, u32[]{:S(2)}, u32[]{:S(2)}) %collective-permute-start.3) | collective-permute-done | bytes 24608 | tf_op jit(solution)/shard_map/ppermute | solution.py:318
  58.5 2.0 %shard_map.116 = (f32[14,128,128]{2,1,0:T(8,128)S(1)}, bf16[14,128,128]{2,1,0:T(8,128)(2,1)S(1)}, bf16[512,128]{1,0:T(8,128)(2,1)S(1)}, bf16[4,8,16,128]{3,2,1,0...) custom-call(s32[1]{0:T(128)} %bitcast.core_ref, ...), custom_call_target="tpu_custom_call" | custom-call | tf_op jit(solution)/shard_map/pallas_call | solution.py:38
  63.4 6.4 %all-to-all-start.1 = ((bf16[32,104,128]{2,1,0:T(8,128)(2,1)}), bf16[32,104,128]{2,1,0:T(8,128)(2,1)S(1)}, u32[]{:S(2)}, u32[]{:S(2)}) async-start(bf16[32,104,128]{2,1,0:T(8,128)(2,1)} %shard_map.118), calls=%async_computation.1 | async-start | bytes 1703936 | tf_op jit(solution)/shard_map/all_to_all | solution.py:323
  69.8 3.6 %collective-permute-start.5 = (bf16[1,8,16,128]{3,2,1,0:T(8,128)(2,1)S(1)}, bf16[1,8,16,128]{3,2,1,0:T(8,128)(2,1)S(1)}, u32[]{:S(2)}, u32[]{:S(2)}) collective-permute-start(bf16[1,8,16,128]{3,2,1,0:T(8,128)(2,1)S(1)} %get-tuple-element.50), channel_id=1, source_target_pairs={{0,32},{32,64},{64,96},{96,128},{128,160},{160,192},{192,224},{1,3... | collective-permute-start | bytes 98312 | tf_op jit(solution)/shard_map/ppermute | solution.py:312
  73.4 1.9 %collective-permute-start.6 = (bf16[1,8,16,128]{3,2,1,0:T(8,128)(2,1)S(1)}, bf16[1,8,16,128]{3,2,1,0:T(8,128)(2,1)S(1)}, u32[]{:S(2)}, u32[]{:S(2)}) collective-permute-start(bf16[1,8,16,128]{3,2,1,0:T(8,128)(2,1)S(1)} %get-tuple-element.51), channel_id=1, source_target_pairs={{32,0},{64,32},{96,64},{128,96},{160,128},{192,160},{224,192},{33,... | collective-permute-start | bytes 98312 | tf_op jit(solution)/shard_map/ppermute | solution.py:313
  75.4 3.6 %collective-permute-done.6.xhi_ref = bf16[1,8,16,128]{3,2,1,0:T(8,128)(2,1)S(1)} collective-permute-done((bf16[1,8,16,128]{3,2,1,0:T(8,128)(2,1)S(1)}, bf16[1,8,16,128]{3,2,1,0:T(8,128)(2,1)S(1)}, u32[]{:S(2)}, u32[]{:S(2)}) %collective-permute-start.6) | collective-permute-done | bytes 32800 | tf_op jit(solution)/shard_map/ppermute | solution.py:313
  79.0 3.4 %collective-permute-start.7 = (bf16[6,1,16,128]{3,2,1,0:T(8,128)(2,1)S(1)}, bf16[6,1,16,128]{3,2,1,0:T(8,128)(2,1)S(1)}, u32[]{:S(2)}, u32[]{:S(2)}) collective-permute-start(bf16[6,1,16,128]{3,2,1,0:T(8,128)(2,1)S(1)} %get-tuple-element.52), channel_id=1, source_target_pairs={{0,1},{1,2},{2,3},{3,4},{4,5},{5,6},{6,7},{7,8},{8,9},{9,10},{10,1... | collective-permute-start | bytes 73736 | tf_op jit(solution)/shard_map/ppermute | solution.py:317
  83.7 3.1 %collective-permute-done.7.ylo_ref = bf16[6,1,16,128]{3,2,1,0:T(8,128)(2,1)S(1)} collective-permute-done((bf16[6,1,16,128]{3,2,1,0:T(8,128)(2,1)S(1)}, bf16[6,1,16,128]{3,2,1,0:T(8,128)(2,1)S(1)}, u32[]{:S(2)}, u32[]{:S(2)}) %collective-permute-start.7) | collective-permute-done | bytes 24608 | tf_op jit(solution)/shard_map/ppermute | solution.py:317
  86.8 2.9 %collective-permute-done.8.yhi_ref = bf16[6,1,16,128]{3,2,1,0:T(8,128)(2,1)S(1)} collective-permute-done((bf16[6,1,16,128]{3,2,1,0:T(8,128)(2,1)S(1)}, bf16[6,1,16,128]{3,2,1,0:T(8,128)(2,1)S(1)}, u32[]{:S(2)}, u32[]{:S(2)}) %collective-permute-start.8) | collective-permute-done | bytes 24608 | tf_op jit(solution)/shard_map/ppermute | solution.py:318
  89.7 1.7 %shard_map.120.filled_ref = bf16[32,48,128]{2,1,0:T(8,128)(2,1)S(1)} custom-call(bf16[4,8,16,128]{3,2,1,0:T(8,128)(2,1)S(1)} %get-tuple-element.49.own_ref.hid_ref, bf16[1,8,16,128]{3,2,1,0:T(8,128)(2,1)S(1)} %collective-permute-done.5.xlo_ref, bf16[1,8,16,128]{3,2,1,0:T(8,128)(2,1)S(1)} %collective-permute-done.6.xhi_ref, ...), custom_call_target="tpu_custom_call" | custom-call | tf_op jit(solution)/shard_map/pallas_call | solution.py:38
  91.6 8.2 %all_to_all.20.got_ref = bf16[4,56,128]{2,1,0:T(8,128)(2,1)S(1)} all-to-all(bf16[4,56,128]{2,1,0:T(8,128)(2,1)S(1)} %shard_map.122), channel_id=1, replica_groups=mesh['y'=4,'c'=2,'x'=4,'z'=8] {'y'}, dimensions={0} | all-to-all | bytes 114688 | tf_op jit(solution)/shard_map/all_to_all | solution.py:386
  100.7 9.0 %all-to-all-start.3 = ((bf16[32,104,128]{2,1,0:T(8,128)(2,1)}), bf16[32,104,128]{2,1,0:T(8,128)(2,1)S(1)}, u32[]{:S(2)}, u32[]{:S(2)}) async-start(bf16[32,104,128]{2,1,0:T(8,128)(2,1)} %shard_map.123), calls=%async_computation.3 | async-start | bytes 1703936 | tf_op jit(solution)/shard_map/all_to_all | solution.py:323
  109.7 1.5 %shard_map.121 = (bf16[512,128]{1,0:T(8,128)(2,1)}, s32[512,128]{1,0:T(8,128)S(1)}, f32[512,128]{1,0:T(8,128)S(1)}) custom-call(bf16[32,104,128]{2,1,0:T(8,128)(2,1)S(1)} %all-to-all-done.1.got_ref, s32[1,512]{1,0:T(1,128)S(1)} %bitcast.5, bf16[512,128]{1,0:T(8,128)(2,1)S(1)} %copy-done.1, bf16[512,128]{1,0:T(8,128)(2,1)S(1)} %copy-done.2, ...), custom_call_target="tpu_custom_call" | custom-call | tf_op jit(solution)/shard_map/pallas_call | solution.py:38
  111.2 16.5 %all-to-all-done.3.got_ref = bf16[32,104,128]{2,1,0:T(8,128)(2,1)S(1)} async-done(((bf16[32,104,128]{2,1,0:T(8,128)(2,1)}), bf16[32,104,128]{2,1,0:T(8,128)(2,1)S(1)}, u32[]{:S(2)}, u32[]{:S(2)}) %all-to-all-start.3) | async-done | bytes 852000 | tf_op jit(solution)/shard_map/all_to_all | solution.py:323
  127.8 7.3 %collective-permute-start.9 = (bf16[14,128,128]{2,1,0:T(8,128)(2,1)S(1)}, bf16[14,128,128]{2,1,0:T(8,128)(2,1)S(1)}, u32[]{:S(2)}, u32[]{:S(2)}) collective-permute-start(bf16[14,128,128]{2,1,0:T(8,128)(2,1)S(1)} %shard_map.125.mine_ref), channel_id=1, source_target_pairs={{0,32},{32,0},{1,33},{33,1},{2,34},{34,2},{3,35},{35,3},{4,36},{36... | collective-permute-start | bytes 1376264 | tf_op jit(solution)/shard_map/ppermute | solution.py:327
  136.6 1.5 %shard_map.126 = (f32[27,128,128]{2,1,0:T(8,128)}, f32[128,128]{1,0:T(8,128)}) custom-call(s32[1]{0:T(128)} %bitcast.core_ref, bf16[14,128,128]{2,1,0:T(8,128)(2,1)S(1)} %shard_map.125.mine_ref, bf16[14,128,128]{2,1,0:T(8,128)(2,1)S(1)} %collective-permute-done.9.other_ref), custom_call_target="tpu_custom_call" | custom-call | tf_op jit(solution)/shard_map/pallas_call | solution.py:38
  (29 shorter events, 8.7 us)
Async XLA Ops:
  0.6 15.4 %copy-start.2 = (bf16[512,128]{1,0:T(8,128)(2,1)S(1)}, bf16[512,128]{1,0:T(8,128)(2,1)}, u32[]{:S(2)}) copy-start(bf16[512,128]{1,0:T(8,128)(2,1)} %cot_ref.3) | copy-start | bytes 393220
  0.6 15.4 %copy-start.1 = (bf16[512,128]{1,0:T(8,128)(2,1)S(1)}, bf16[512,128]{1,0:T(8,128)(2,1)}, u32[]{:S(2)}) copy-start(bf16[512,128]{1,0:T(8,128)(2,1)} %feat_ref.3) | copy-start | bytes 393220
  0.7 15.4 %copy-start.3 = (bf16[128,128]{1,0:T(8,128)(2,1)S(1)}, bf16[128,128]{1,0:T(8,128)(2,1)}, u32[]{:S(2)}) copy-start(bf16[128,128]{1,0:T(8,128)(2,1)} %mlp_ref.3) | copy-start | bytes 98308
  4.0 54.5 %copy-start = (bf16[27,128,128]{2,1,0:T(8,128)(2,1)S(1)}, bf16[27,128,128]{2,1,0:T(8,128)(2,1)}, u32[]{:S(2)}) copy-start(bf16[27,128,128]{2,1,0:T(8,128)(2,1)} %weight_ref.3) | copy-start | bytes 2654212
  4.0 32.3 %all-to-all-start = ((bf16[32,104,128]{2,1,0:T(8,128)(2,1)}), bf16[32,104,128]{2,1,0:T(8,128)(2,1)S(1)}, u32[]{:S(2)}, u32[]{:S(2)}) async-start(bf16[32,104,128]{2,1,0:T(8,128)(2,1)} %shard_map.111), calls=%async_computation | async-start | bytes 1703936 | tf_op jit(solution)/shard_map/all_to_all | solution.py:323
  37.0 10.4 %collective-permute-start = (bf16[1,8,16,128]{3,2,1,0:T(8,128)(2,1)S(1)}, bf16[1,8,16,128]{3,2,1,0:T(8,128)(2,1)S(1)}, u32[]{:S(2)}, u32[]{:S(2)}) collective-permute-start(bf16[1,8,16,128]{3,2,1,0:T(8,128)(2,1)S(1)} %get-tuple-element.38), channel_id=1, source_target_pairs={{0,32},{32,64},{64,96},{96,128},{128,160},{160,192},{192,224},{1,3... | collective-permute-start | bytes 98312 | tf_op jit(solution)/shard_map/ppermute | solution.py:312
  45.5 5.2 %collective-permute-start.1 = (bf16[1,8,16,128]{3,2,1,0:T(8,128)(2,1)S(1)}, bf16[1,8,16,128]{3,2,1,0:T(8,128)(2,1)S(1)}, u32[]{:S(2)}, u32[]{:S(2)}) collective-permute-start(bf16[1,8,16,128]{3,2,1,0:T(8,128)(2,1)S(1)} %get-tuple-element.39), channel_id=1, source_target_pairs={{32,0},{64,32},{96,64},{128,96},{160,128},{192,160},{224,192},{33,... | collective-permute-start | bytes 98312 | tf_op jit(solution)/shard_map/ppermute | solution.py:313
  50.8 5.3 %collective-permute-start.2 = (bf16[6,1,16,128]{3,2,1,0:T(8,128)(2,1)S(1)}, bf16[6,1,16,128]{3,2,1,0:T(8,128)(2,1)S(1)}, u32[]{:S(2)}, u32[]{:S(2)}) collective-permute-start(bf16[6,1,16,128]{3,2,1,0:T(8,128)(2,1)S(1)} %get-tuple-element.40), channel_id=1, source_target_pairs={{0,1},{1,2},{2,3},{3,4},{4,5},{5,6},{6,7},{7,8},{8,9},{9,10},{10,1... | collective-permute-start | bytes 73736 | tf_op jit(solution)/shard_map/ppermute | solution.py:317
  53.9 4.6 %collective-permute-start.3 = (bf16[6,1,16,128]{3,2,1,0:T(8,128)(2,1)S(1)}, bf16[6,1,16,128]{3,2,1,0:T(8,128)(2,1)S(1)}, u32[]{:S(2)}, u32[]{:S(2)}) collective-permute-start(bf16[6,1,16,128]{3,2,1,0:T(8,128)(2,1)S(1)} %get-tuple-element.41), channel_id=1, source_target_pairs={{1,0},{2,1},{3,2},{4,3},{5,4},{6,5},{7,6},{8,7},{9,8},{10,9},{11,1... | collective-permute-start | bytes 73736 | tf_op jit(solution)/shard_map/ppermute | solution.py:318
  60.5 1.9 %collective-permute-start.4 = (bf16[14,128,128]{2,1,0:T(8,128)(2,1)S(1)}, bf16[14,128,128]{2,1,0:T(8,128)(2,1)S(1)}, u32[]{:S(2)}, u32[]{:S(2)}) collective-permute-start(bf16[14,128,128]{2,1,0:T(8,128)(2,1)S(1)} %get-tuple-element.46), channel_id=1, source_target_pairs={{0,32},{32,0},{1,33},{33,1},{2,34},{34,2},{3,35},{35,3},{4,36},{36... | collective-permute-start | bytes 1376264 | tf_op jit(solution)/shard_map/ppermute | solution.py:327
  63.4 28.1 %all-to-all-start.1 = ((bf16[32,104,128]{2,1,0:T(8,128)(2,1)}), bf16[32,104,128]{2,1,0:T(8,128)(2,1)S(1)}, u32[]{:S(2)}, u32[]{:S(2)}) async-start(bf16[32,104,128]{2,1,0:T(8,128)(2,1)} %shard_map.118), calls=%async_computation.1 | async-start | bytes 1703936 | tf_op jit(solution)/shard_map/all_to_all | solution.py:323
  69.8 5.6 %collective-permute-start.5 = (bf16[1,8,16,128]{3,2,1,0:T(8,128)(2,1)S(1)}, bf16[1,8,16,128]{3,2,1,0:T(8,128)(2,1)S(1)}, u32[]{:S(2)}, u32[]{:S(2)}) collective-permute-start(bf16[1,8,16,128]{3,2,1,0:T(8,128)(2,1)S(1)} %get-tuple-element.50), channel_id=1, source_target_pairs={{0,32},{32,64},{64,96},{96,128},{128,160},{160,192},{192,224},{1,3... | collective-permute-start | bytes 98312 | tf_op jit(solution)/shard_map/ppermute | solution.py:312
  73.4 5.5 %collective-permute-start.6 = (bf16[1,8,16,128]{3,2,1,0:T(8,128)(2,1)S(1)}, bf16[1,8,16,128]{3,2,1,0:T(8,128)(2,1)S(1)}, u32[]{:S(2)}, u32[]{:S(2)}) collective-permute-start(bf16[1,8,16,128]{3,2,1,0:T(8,128)(2,1)S(1)} %get-tuple-element.51), channel_id=1, source_target_pairs={{32,0},{64,32},{96,64},{128,96},{160,128},{192,160},{224,192},{33,... | collective-permute-start | bytes 98312 | tf_op jit(solution)/shard_map/ppermute | solution.py:313
  79.0 7.9 %collective-permute-start.7 = (bf16[6,1,16,128]{3,2,1,0:T(8,128)(2,1)S(1)}, bf16[6,1,16,128]{3,2,1,0:T(8,128)(2,1)S(1)}, u32[]{:S(2)}, u32[]{:S(2)}) collective-permute-start(bf16[6,1,16,128]{3,2,1,0:T(8,128)(2,1)S(1)} %get-tuple-element.52), channel_id=1, source_target_pairs={{0,1},{1,2},{2,3},{3,4},{4,5},{5,6},{6,7},{7,8},{8,9},{9,10},{10,1... | collective-permute-start | bytes 73736 | tf_op jit(solution)/shard_map/ppermute | solution.py:317
  82.4 7.4 %collective-permute-start.8 = (bf16[6,1,16,128]{3,2,1,0:T(8,128)(2,1)S(1)}, bf16[6,1,16,128]{3,2,1,0:T(8,128)(2,1)S(1)}, u32[]{:S(2)}, u32[]{:S(2)}) collective-permute-start(bf16[6,1,16,128]{3,2,1,0:T(8,128)(2,1)S(1)} %get-tuple-element.53), channel_id=1, source_target_pairs={{1,0},{2,1},{3,2},{4,3},{5,4},{6,5},{7,6},{8,7},{9,8},{10,9},{11,1... | collective-permute-start | bytes 73736 | tf_op jit(solution)/shard_map/ppermute | solution.py:318
  91.6 18.1 %copy-start.4 = (s32[512,1]{0,1:T(1,128)S(1)}, s32[512,1]{0,1:T(1,128)}, u32[]{:S(2)}) copy-start(s32[512,1]{0,1:T(1,128)} %param.9) | copy-start | bytes 6148
  100.7 27.0 %all-to-all-start.3 = ((bf16[32,104,128]{2,1,0:T(8,128)(2,1)}), bf16[32,104,128]{2,1,0:T(8,128)(2,1)S(1)}, u32[]{:S(2)}, u32[]{:S(2)}) async-start(bf16[32,104,128]{2,1,0:T(8,128)(2,1)} %shard_map.123), calls=%async_computation.3 | async-start | bytes 1703936 | tf_op jit(solution)/shard_map/all_to_all | solution.py:323
  127.8 8.8 %collective-permute-start.9 = (bf16[14,128,128]{2,1,0:T(8,128)(2,1)S(1)}, bf16[14,128,128]{2,1,0:T(8,128)(2,1)S(1)}, u32[]{:S(2)}, u32[]{:S(2)}) collective-permute-start(bf16[14,128,128]{2,1,0:T(8,128)(2,1)S(1)} %shard_map.125.mine_ref), channel_id=1, source_target_pairs={{0,32},{32,0},{1,33},{33,1},{2,34},{34,2},{3,35},{35,3},{4,36},{36... | collective-permute-start | bytes 1376264 | tf_op jit(solution)/shard_map/ppermute | solution.py:327

commit v3 on v2

--- a/solution.py
+++ b/solution.py
@@ -34,12 +34,12 @@
     return jax.ShapeDtypeStruct(shape, dtype)
 
 
-def call(kernel, out_shape, args, scratch=(), smem=0, hbm=0, mib=12):
+def call(kernel, out_shape, args, scratch=(), smem=0, hbm=0, mib=12, out=VMEM):
     return pl.pallas_call(
         kernel,
         out_shape=out_shape,
         in_specs=[SMEM] * smem + [HBM] * hbm + [VMEM] * (len(args) - smem - hbm),
-        out_specs=jax.tree.map(lambda _: VMEM, out_shape),
+        out_specs=jax.tree.map(lambda _: out, out_shape),
         scratch_shapes=list(scratch),
         compiler_params=pltpu.CompilerParams(vmem_limit_bytes=mib * 1024 * 1024),
     )(*args)
@@ -69,8 +69,8 @@
     return slab * CAP + rank.astype(jnp.int32)
 
 
-def pack_kernel(feat_hbm, cot_hbm, slab_hbm, base_hbm, near_hbm, off_hbm, sent_ref,
-                both_ref, slab_ref, base_ref, near_ref, off_ref, sems):
+def pack_kernel(feat_hbm, cot_hbm, slab_hbm, base_hbm, near_hbm, off_hbm, sent_hbm,
+                both_ref, slab_ref, base_ref, near_ref, off_ref, sent_ref, sems, out_sems):
     moves = [
         pltpu.make_async_copy(slab_hbm, slab_ref, sems.at[0]),
         pltpu.make_async_copy(base_hbm, base_ref, sems.at[1]),
@@ -81,7 +81,7 @@
     ]
     for move in moves:
         move.start()
-    for move in moves:
+    for move in moves[:4]:
         move.wait()
     position = places(slab_ref[...])
     base = base_ref[...]
@@ -94,8 +94,11 @@
     meta = jnp.concatenate(
         [r.astype(F32) for r in rows] + [fraction, jnp.zeros((KINDS - 7, PTS), F32)], axis=0
     ).astype(BF)
+    moves[4].wait()
+    moves[5].wait()
     both = both_ref[...]
     group = 8
+    sends = []
     for g in range(GY // group):
         span = group * CAP
         chosen = onehot(iota((span, PTS), 0) + g * span == position)
@@ -108,6 +111,10 @@
             piece = lanes[:, i * CAP : (i + 1) * CAP]
             wide = jnp.concatenate([piece, jnp.zeros((KINDS, C - CAP), F32)], axis=1)
             sent_ref[g * group + i, 2 * CAP : 2 * CAP + KINDS, :] = wide.astype(BF)
+        sends.append(pltpu.make_async_copy(sent_ref.at[here], sent_hbm.at[here], out_sems.at[g]))
+        sends[g].start()
+    for send in sends:
+        send.wait()
 
 
 def slope(v, s):
@@ -134,7 +141,7 @@
     return onehot(iota((CELLS, SLOTS), 0) == own)
 
 
-def voxel_kernel(got_ref, vox_ref, lo_ref, hi_ref, div_ref, meta_ref):
+def voxel_kernel(core_ref, got_ref, vox_ref, near_ref, far_ref, div_ref, meta_ref):
     meta = arrived_meta(got_ref)
     meta_ref[...] = meta
     own_hot = own_matrix(meta)
@@ -143,10 +150,10 @@
     total = dot(own_hot, both)
     divisor = jnp.maximum(total[:, C:], 1.0)
     div_ref[...] = divisor
-    voxels = (total[:, :C] / divisor).astype(BF).reshape(VX, VY, Z, C)
-    vox_ref[...] = voxels
-    lo_ref[...] = voxels[:1]
-    hi_ref[...] = voxels[VX - 1 :]
+    vox_ref[...] = (total[:, :C] / divisor).astype(BF).reshape(VX, VY, Z, C)
+    core = core_ref[0]
+    near_ref[...] = vox_ref[pl.ds((VX - 1) * (1 - core), 1)]
+    far_ref[...] = vox_ref[pl.ds((VX - 1) * core, 1)]
 
 
 def spread_kernel(got_ref, meta_ref, matrix_ref, grad_ref):
@@ -168,14 +175,15 @@
     grad_ref[...] = dot(matrix_ref[...], cots)
 
 
-def edge_kernel(xlo_ref, own_ref, xhi_ref, tail_ref, head_ref):
+def edge_kernel(core_ref, near_ref, own_ref, far_ref, tail_ref, head_ref):
+    core = core_ref[0]
     for ref, y in ((tail_ref, VY - 1), (head_ref, 0)):
-        ref[0] = xlo_ref[0, y : y + 1]
+        ref[pl.ds((VX + 1) * (1 - core), 1)] = near_ref[:, y : y + 1]
         ref[1 : VX + 1] = own_ref[:, y : y + 1]
-        ref[VX + 1] = xhi_ref[0, y : y + 1]
-
-
-def assemble(wide_ref, own_ref, xlo_ref, xhi_ref, ylo_ref, yhi_ref):
+        ref[pl.ds((VX + 1) * core, 1)] = far_ref[:, y : y + 1]
+
+
+def assemble(core, wide_ref, own_ref, near_ref, far_ref, ylo_ref, yhi_ref):
     def put(x, y, block):
         nx, ny = block.shape[0], block.shape[1]
         flat = block.reshape(nx * ny * Z, C).astype(F32)
@@ -186,13 +194,14 @@
         down = jnp.where(z == 0, 0.0, down)
         up = jnp.where(z == Z - 1, 0.0, up)
         shape = (nx, ny, Z, C)
-        wide_ref[x : x + nx, y : y + ny, :, 0:C] = down.astype(BF).reshape(shape)
-        wide_ref[x : x + nx, y : y + ny, :, C : 2 * C] = block
-        wide_ref[x : x + nx, y : y + ny, :, 2 * C :] = up.astype(BF).reshape(shape)
+        planes = pl.ds(x, nx)
+        wide_ref[planes, y : y + ny, :, 0:C] = down.astype(BF).reshape(shape)
+        wide_ref[planes, y : y + ny, :, C : 2 * C] = block
+        wide_ref[planes, y : y + ny, :, 2 * C :] = up.astype(BF).reshape(shape)
 
     put(1, 1, own_ref[...])
-    put(0, 1, xlo_ref[...])
-    put(VX + 1, 1, xhi_ref[...])
+    put((VX + 1) * (1 - core), 1, near_ref[...])
+    put((VX + 1) * core, 1, far_ref[...])
     put(0, 0, ylo_ref[...])
     put(0, VY + 1, yhi_ref[...])
 
@@ -201,9 +210,10 @@
     return wide_ref[x : x + VX, y : y + VY, :, :].reshape(CELLS, 3 * C)
 
 
-def conv_kernel(core_ref, vox_ref, xlo_ref, xhi_ref, ylo_ref, yhi_ref, weight_ref, gout_ref,
-                mlp_ref, keep_ref, send_ref, act_ref, hid_ref, lo_ref, hi_ref, wide_ref, all_ref):
-    assemble(wide_ref, vox_ref, xlo_ref, xhi_ref, ylo_ref, yhi_ref)
+def conv_kernel(core_ref, vox_ref, near_ref, far_ref, ylo_ref, yhi_ref, weight_ref, gout_ref,
+                mlp_ref, keep_ref, send_ref, act_ref, hid_ref, in_ref, out_ref, wide_ref, all_ref):
+    core = core_ref[0]
+    assemble(core, wide_ref, vox_ref, near_ref, far_ref, ylo_ref, yhi_ref)
     hidden = jnp.zeros((CELLS, C), F32)
     for k in range(9):
         taps = weight_ref[3 * k : 3 * k + 3].reshape(3 * C, C)
@@ -211,17 +221,15 @@
     s = sigmoid(hidden)
     act_ref[...] = (hidden * s).astype(BF)
     grad_hidden = (gout_ref[...] * slope(hidden, s)).astype(BF)
-    shaped = grad_hidden.reshape(VX, VY, Z, C)
-    hid_ref[...] = shaped
-    lo_ref[...] = shaped[:1]
-    hi_ref[...] = shaped[VX - 1 :]
+    hid_ref[...] = grad_hidden.reshape(VX, VY, Z, C)
+    in_ref[...] = hid_ref[pl.ds((VX - 1) * (1 - core), 1)]
+    out_ref[...] = hid_ref[pl.ds((VX - 1) * core, 1)]
     turned = grad_hidden.astype(F32).T.astype(BF)
     for k in range(9):
         part = dot(turned, window(wide_ref, k // 3, k % 3))
         for j in range(3):
             all_ref[3 * k + j] = part[:, j * C : (j + 1) * C]
     all_ref[27] = mlp_ref[...]
-    core = core_ref[0]
     keep_ref[...] = all_ref[pl.ds(core * HALF, HALF)]
     send_ref[...] = all_ref[pl.ds((1 - core) * HALF, HALF)].astype(BF)
 
@@ -241,8 +249,8 @@
     out_ref[...] = jnp.broadcast_to(total.astype(BF)[None], out_ref.shape)
 
 
-def back_kernel(hid_ref, xlo_ref, xhi_ref, ylo_ref, yhi_ref, weight_ref, meta_ref, div_ref, out_ref, wide_ref):
-    assemble(wide_ref, hid_ref, xlo_ref, xhi_ref, ylo_ref, yhi_ref)
+def back_kernel(core_ref, hid_ref, near_ref, far_ref, ylo_ref, yhi_ref, weight_ref, meta_ref, div_ref, out_ref, wide_ref):
+    assemble(core_ref[0], wide_ref, hid_ref, near_ref, far_ref, ylo_ref, yhi_ref)
     total = jnp.zeros((CELLS, C), F32)
     for k in range(9):
         taps = jnp.concatenate([weight_ref[3 * k + 2 - j] for j in range(3)], axis=1)
@@ -306,17 +314,16 @@
 EDGE = sds((VX + 2, 1, Z, C), BF)
 
 
-def halo(cells, lo, hi):
-    up = [(i, i + 1) for i in range(GX - 1)]
-    down = [(i + 1, i) for i in range(GX - 1)]
-    xlo = lax.ppermute(hi, ("y", "c"), up)
-    xhi = lax.ppermute(lo, ("y", "c"), down)
-    tail, head = call(edge_kernel, (EDGE, EDGE), (xlo, cells, xhi), mib=2)
+def chips(face):
+    pairs = [(i, i + 1) for i in range(1, GX - 1, 2)]
+    return lax.ppermute(face, ("y", "c"), pairs + [(j, i) for i, j in pairs])
+
+
+def edges(core, near, cells, far):
+    tail, head = call(edge_kernel, (EDGE, EDGE), (core, near, cells, far), smem=1, mib=2)
     up = [(i, i + 1) for i in range(GY - 1)]
     down = [(i + 1, i) for i in range(GY - 1)]
-    ylo = lax.ppermute(tail, ("x", "z"), up)
-    yhi = lax.ppermute(head, ("x", "z"), down)
-    return xlo, xhi, ylo, yhi
+    return lax.ppermute(tail, ("x", "z"), up), lax.ppermute(head, ("x", "z"), down)
 
 
 def exchange(rows):
@@ -342,28 +349,33 @@
             line,
             line,
             pltpu.VMEM((3, PTS), BF),
+            pltpu.VMEM((GY, 2 * CAP + KINDS, C), BF),
             pltpu.SemaphoreType.DMA((6,)),
+            pltpu.SemaphoreType.DMA((4,)),
         ),
         hbm=6,
         mib=60,
+        out=HBM,
     )
     got = exchange(sent)
     mlp_grad = call(mlp_kernel, sds((C, C), F32), (features, cotangent, mlp_weight))
     got, mlp_grad = lax.optimization_barrier((got, mlp_grad))
     cells = sds((VX, VY, Z, C), BF)
-    voxels, lo, hi, divisor, meta = call(
+    voxels, near, far, divisor, meta = call(
         voxel_kernel,
         (cells, FACE, FACE, sds((CELLS, C), F32), sds((KINDS, SLOTS), F32)),
-        (got,),
-    )
-    faces = halo(voxels, lo, hi)
+        (core, got),
+        smem=1,
+    )
+    near, far = swap(near), chips(far)
+    faces = (near, far) + edges(core, near, voxels, far)
     matrix, grad_out = call(
         spread_kernel, (sds((CELLS, SLOTS), BF), sds((CELLS, C), F32)), (got, meta)
     )
     wide = pltpu.VMEM((VX + 2, VY + 2, Z, 3 * C), BF)
     block = sds((GY, ROWS, C), BF)
     rows = sds((GY, CAP, C), BF)
-    keep, send, act, grad_hidden, lo, hi = call(
+    keep, send, act, grad_hidden, near, far = call(
         conv_kernel,
         (sds((HALF, C, C), F32), sds((HALF, C, C), BF), sds((CELLS, C), BF), cells, FACE, FACE),
         (core, voxels) + faces + (conv_weight, grad_out, mlp_grad),
@@ -374,14 +386,16 @@
     filled = call(sample_kernel, rows, (matrix, act))
     joined = call(join_kernel, block, (keep, arrived, filled))
     first = exchange(joined)
-    grad_faces = halo(grad_hidden, lo, hi)
+    near, far = swap(near), chips(far)
+    grad_faces = (near, far) + edges(core, near, grad_hidden, far)
+    first, grad_faces = lax.optimization_barrier((first, grad_faces))
     filled = call(
         back_kernel,
         rows,
-        (grad_hidden,) + grad_faces + (conv_weight, meta, divisor),
+        (core, grad_hidden) + grad_faces + (conv_weight, meta, divisor),
         scratch=(wide,),
-    )
-    first, filled = lax.optimization_barrier((first, filled))
+        smem=1,
+    )
     shares = call(share_kernel, sds((4, SHARE, C), BF), (first,), mib=4)
     shares = lax.all_to_all(shares, "y", split_axis=0, concat_axis=0, tiled=True)
     joined = call(spread_share_kernel, block, (shares, filled))

time: 139 us -> 136 us (0.978)
  blocking collectives: 8.16 us -> 0 us
  waiting for transfers between devices: 53.2 us -> 55.9 us
  starting transfers between devices: 59.8 us -> 62.1 us
    all_to_all x1 -> x0, blocking collectives: 8.16 us -> none  [body(): lax.all_to_all(shares, 'y', split_axis=0, concat_axis=0, tiled=True)]
    ppermute x8 -> x6, starting transfers between devices: 25.1 us -> 16.9 us  [the longest x2 7.51 us: chips(): return lax.ppermute(face, ('y', 'c'), pairs + [(j, i) for i, j in pairs])]
    ppermute x2 -> x4, starting transfers between devices: 7.43 us -> 13.5 us  [swap(): return lax.ppermute(half, 'c', [(0, 1), (1, 0)])]
    all_to_all x0 -> x1, starting transfers between devices: none -> 5.02 us  [body(): lax.all_to_all(shares, 'y', split_axis=0, concat_axis=0, tiled=True)]
    all_to_all x0 -> x1, waiting for transfers between devices: none -> 2.5 us  [body(): lax.all_to_all(shares, 'y', split_axis=0, concat_axis=0, tiled=True)]
    all_to_all x3, waiting for transfers between devices: 36.4 us -> 37.9 us  [exchange(): lax.all_to_all(rows, ('x', 'z'), split_axis=0, concat_axis=0, tiled=True)]
    ppermute x8 -> x6, waiting for transfers between devices: 15.4 us -> 14.2 us  [the longest x2 5.49 us: edges(): lax.ppermute(tail, ('x', 'z'), up)]
  transfers between devices with their start and end apart: 13 -> 14, of which waited for: 9 -> 11; matrix products, arithmetic and copies ran while one was open for 0% -> 0% of each run, Pallas kernels for 5% -> 5%
where the time goes in v3:
time: 136 us
  starting transfers between devices  62.1 us (46%)
  waiting for transfers between devices  55.9 us (41%)
  Pallas kernels  16.7 us (12%)
    all_to_all x3, waiting for transfers between devices, exchange(): lax.all_to_all(rows, ('x', 'z'), split_axis=0, concat_axis=0, tiled=True)  37.9 us
    all_to_all x3, starting transfers between devices, exchange(): lax.all_to_all(rows, ('x', 'z'), split_axis=0, concat_axis=0, tiled=True)  26.7 us
    pallas_call x16, Pallas kernels, call(): pl.pallas_call(kernel, out_shape=out_shape, in_specs=[SMEM] * smem + [HBM...  16.7 us
    ppermute x4, starting transfers between devices, swap(): return lax.ppermute(half, 'c', [(0, 1), (1, 0)])  13.5 us
    ppermute x2, starting transfers between devices, chips(): return lax.ppermute(face, ('y', 'c'), pairs + [(j, i) for i, j in pairs])  7.51 us
    ppermute x2, starting transfers between devices, edges(): lax.ppermute(tail, ('x', 'z'), up)  6.82 us
    ppermute x2, waiting for transfers between devices, edges(): lax.ppermute(tail, ('x', 'z'), up)  5.49 us
    all_to_all x1, starting transfers between devices, body(): lax.all_to_all(shares, 'y', split_axis=0, concat_axis=0, tiled=True)  5.02 us
  transfers between devices with their start and end apart: 14, of which 11 were waited for; matrix products, arithmetic and copies ran while one was open for 0% of the time, Pallas kernels for 5%

profile of v3, /device:TPU:1, one launch (start us, length us, event | category | flops | bytes accessed | tf_op | source)
XLA Modules:
  0.0 135.5 jit_solution(376141545920351953)
XLA Ops:
  0.7 3.0 %shard_map.111 = bf16[32,104,128]{2,1,0:T(8,128)(2,1)} custom-call(bf16[512,128]{1,0:T(8,128)(2,1)} %feat_ref.3, bf16[512,128]{1,0:T(8,128)(2,1)} %cot_ref.3, s32[1,512]{1,0:T(1,128)} %bitcast.4, s32[1,512]{1,0:T(1,128)} %bitcast.6, s32[1,512]{1,0:T(1,128)} %bitcast.7, bf16[3,512]{1,0:T(4,128)(2,1)} %off_hbm.1), custom_call_target="tpu_custom_call" | custom-call | tf_op jit(solution)/shard_map/pallas_call | solution.py:38
  3.6 12.0 %all-to-all-start = ((bf16[32,104,128]{2,1,0:T(8,128)(2,1)}), bf16[32,104,128]{2,1,0:T(8,128)(2,1)S(1)}, u32[]{:S(2)}, u32[]{:S(2)}) async-start(bf16[32,104,128]{2,1,0:T(8,128)(2,1)} %shard_map.111), calls=%async_computation | async-start | bytes 1703936 | tf_op jit(solution)/shard_map/all_to_all | solution.py:330
  16.1 19.9 %all-to-all-done.got_ref = bf16[32,104,128]{2,1,0:T(8,128)(2,1)S(1)} async-done(((bf16[32,104,128]{2,1,0:T(8,128)(2,1)}), bf16[32,104,128]{2,1,0:T(8,128)(2,1)S(1)}, u32[]{:S(2)}, u32[]{:S(2)}) %all-to-all-start) | async-done | bytes 852000 | tf_op jit(solution)/shard_map/all_to_all | solution.py:330
  36.7 5.5 %collective-permute-start = (bf16[1,8,16,128]{3,2,1,0:T(8,128)(2,1)S(1)}, bf16[1,8,16,128]{3,2,1,0:T(8,128)(2,1)S(1)}, u32[]{:S(2)}, u32[]{:S(2)}) collective-permute-start(bf16[1,8,16,128]{3,2,1,0:T(8,128)(2,1)S(1)} %get-tuple-element.41), channel_id=1, source_target_pairs={{0,32},{32,0},{1,33},{33,1},{2,34},{34,2},{3,35},{35,3},{4,36},{36... | collective-permute-start | bytes 98312 | tf_op jit(solution)/shard_map/ppermute | solution.py:334
  42.2 3.1 %collective-permute-start.1 = (bf16[1,8,16,128]{3,2,1,0:T(8,128)(2,1)S(1)}, bf16[1,8,16,128]{3,2,1,0:T(8,128)(2,1)S(1)}, u32[]{:S(2)}, u32[]{:S(2)}) collective-permute-start(bf16[1,8,16,128]{3,2,1,0:T(8,128)(2,1)S(1)} %get-tuple-element.42), channel_id=1, source_target_pairs={{32,64},{96,128},{160,192},{64,32},{128,96},{192,160},{33,65},{97,... | collective-permute-start | bytes 98312 | tf_op jit(solution)/shard_map/ppermute | solution.py:319
  45.3 2.1 %collective-permute-done.1.far_ref = bf16[1,8,16,128]{3,2,1,0:T(8,128)(2,1)S(1)} collective-permute-done((bf16[1,8,16,128]{3,2,1,0:T(8,128)(2,1)S(1)}, bf16[1,8,16,128]{3,2,1,0:T(8,128)(2,1)S(1)}, u32[]{:S(2)}, u32[]{:S(2)}) %collective-permute-start.1) | collective-permute-done | bytes 32800 | tf_op jit(solution)/shard_map/ppermute | solution.py:319
  47.4 3.1 %collective-permute-start.2 = (bf16[6,1,16,128]{3,2,1,0:T(8,128)(2,1)S(1)}, bf16[6,1,16,128]{3,2,1,0:T(8,128)(2,1)S(1)}, u32[]{:S(2)}, u32[]{:S(2)}) collective-permute-start(bf16[6,1,16,128]{3,2,1,0:T(8,128)(2,1)S(1)} %get-tuple-element.43), channel_id=1, source_target_pairs={{0,1},{1,2},{2,3},{3,4},{4,5},{5,6},{6,7},{7,8},{8,9},{9,10},{10,1... | collective-permute-start | bytes 73736 | tf_op jit(solution)/shard_map/ppermute | solution.py:326
  52.7 2.4 %collective-permute-done.3.yhi_ref = bf16[6,1,16,128]{3,2,1,0:T(8,128)(2,1)S(1)} collective-permute-done((bf16[6,1,16,128]{3,2,1,0:T(8,128)(2,1)S(1)}, bf16[6,1,16,128]{3,2,1,0:T(8,128)(2,1)S(1)}, u32[]{:S(2)}, u32[]{:S(2)}) %collective-permute-start.3) | collective-permute-done | bytes 24608 | tf_op jit(solution)/shard_map/ppermute | solution.py:326
  55.1 2.2 %shard_map.116 = (f32[14,128,128]{2,1,0:T(8,128)S(1)}, bf16[14,128,128]{2,1,0:T(8,128)(2,1)S(1)}, bf16[512,128]{1,0:T(8,128)(2,1)S(1)}, bf16[4,8,16,128]{3,2,1,0...) custom-call(s32[1]{0:T(128)} %bitcast.core_ref, ...), custom_call_target="tpu_custom_call" | custom-call | tf_op jit(solution)/shard_map/pallas_call | solution.py:38
  60.3 6.4 %all-to-all-start.1 = ((bf16[32,104,128]{2,1,0:T(8,128)(2,1)}), bf16[32,104,128]{2,1,0:T(8,128)(2,1)S(1)}, u32[]{:S(2)}, u32[]{:S(2)}) async-start(bf16[32,104,128]{2,1,0:T(8,128)(2,1)} %shard_map.118), calls=%async_computation.1 | async-start | bytes 1703936 | tf_op jit(solution)/shard_map/all_to_all | solution.py:330
  67.1 4.4 %collective-permute-start.6 = (bf16[1,8,16,128]{3,2,1,0:T(8,128)(2,1)S(1)}, bf16[1,8,16,128]{3,2,1,0:T(8,128)(2,1)S(1)}, u32[]{:S(2)}, u32[]{:S(2)}) collective-permute-start(bf16[1,8,16,128]{3,2,1,0:T(8,128)(2,1)S(1)} %get-tuple-element.53), channel_id=1, source_target_pairs={{32,64},{96,128},{160,192},{64,32},{128,96},{192,160},{33,65},{97,... | collective-permute-start | bytes 98312 | tf_op jit(solution)/shard_map/ppermute | solution.py:319
  71.6 1.6 %collective-permute-done.6.far_ref = bf16[1,8,16,128]{3,2,1,0:T(8,128)(2,1)S(1)} collective-permute-done((bf16[1,8,16,128]{3,2,1,0:T(8,128)(2,1)S(1)}, bf16[1,8,16,128]{3,2,1,0:T(8,128)(2,1)S(1)}, u32[]{:S(2)}, u32[]{:S(2)}) %collective-permute-start.6) | collective-permute-done | bytes 32800 | tf_op jit(solution)/shard_map/ppermute | solution.py:319
  73.1 3.7 %collective-permute-start.7 = (bf16[6,1,16,128]{3,2,1,0:T(8,128)(2,1)S(1)}, bf16[6,1,16,128]{3,2,1,0:T(8,128)(2,1)S(1)}, u32[]{:S(2)}, u32[]{:S(2)}) collective-permute-start(bf16[6,1,16,128]{3,2,1,0:T(8,128)(2,1)S(1)} %get-tuple-element.55), channel_id=1, source_target_pairs={{0,1},{1,2},{2,3},{3,4},{4,5},{5,6},{6,7},{7,8},{8,9},{9,10},{10,1... | collective-permute-start | bytes 73736 | tf_op jit(solution)/shard_map/ppermute | solution.py:326
  78.1 5.5 %collective-permute-done.7.ylo_ref = bf16[6,1,16,128]{3,2,1,0:T(8,128)(2,1)S(1)} collective-permute-done((bf16[6,1,16,128]{3,2,1,0:T(8,128)(2,1)S(1)}, bf16[6,1,16,128]{3,2,1,0:T(8,128)(2,1)S(1)}, u32[]{:S(2)}, u32[]{:S(2)}) %collective-permute-start.7) | collective-permute-done | bytes 24608 | tf_op jit(solution)/shard_map/ppermute | solution.py:326
  83.6 2.6 %collective-permute-done.8.yhi_ref = bf16[6,1,16,128]{3,2,1,0:T(8,128)(2,1)S(1)} collective-permute-done((bf16[6,1,16,128]{3,2,1,0:T(8,128)(2,1)S(1)}, bf16[6,1,16,128]{3,2,1,0:T(8,128)(2,1)S(1)}, u32[]{:S(2)}, u32[]{:S(2)}) %collective-permute-start.8) | collective-permute-done | bytes 24608 | tf_op jit(solution)/shard_map/ppermute | solution.py:326
  86.2 1.6 %all-to-all-done.1.got_ref = bf16[32,104,128]{2,1,0:T(8,128)(2,1)S(1)} async-done(((bf16[32,104,128]{2,1,0:T(8,128)(2,1)}), bf16[32,104,128]{2,1,0:T(8,128)(2,1)S(1)}, u32[]{:S(2)}, u32[]{:S(2)}) %all-to-all-start.1) | async-done | bytes 852000 | tf_op jit(solution)/shard_map/all_to_all | solution.py:330
  88.5 5.0 %all-to-all-start.2 = ((bf16[4,56,128]{2,1,0:T(8,128)(2,1)}), bf16[4,56,128]{2,1,0:T(8,128)(2,1)S(1)}, u32[]{:S(2)}, u32[]{:S(2)}) async-start(bf16[4,56,128]{2,1,0:T(8,128)(2,1)} %shard_map.121), calls=%async_computation.2 | async-start | bytes 114688 | tf_op jit(solution)/shard_map/all_to_all | solution.py:400
  93.5 1.9 %shard_map.122.filled_ref = bf16[32,48,128]{2,1,0:T(8,128)(2,1)S(1)} custom-call(s32[1]{0:T(128)} %bitcast.core_ref, bf16[4,8,16,128]{3,2,1,0:T(8,128)(2,1)S(1)} %get-tuple-element.54.own_ref.hid_ref, bf16[1,8,16,128]{3,2,1,0:T(8,128)(2,1)S(1)} %collective-permute-done.5.near_ref, bf16[1,8,16,128]{3,2,1,0:T(8,128)(2,1)S(1)} %collective-permute-done.6.far_ref, ...), custom_call_target="tpu_custom_call" | custom-call | tf_op jit(solution)/shard_map/pallas_call | solution.py:38
  95.5 2.5 %all-to-all-done.2.got_ref = bf16[4,56,128]{2,1,0:T(8,128)(2,1)S(1)} async-done(((bf16[4,56,128]{2,1,0:T(8,128)(2,1)}), bf16[4,56,128]{2,1,0:T(8,128)(2,1)S(1)}, u32[]{:S(2)}, u32[]{:S(2)}) %all-to-all-start.2) | async-done | bytes 57376 | tf_op jit(solution)/shard_map/all_to_all | solution.py:400
  98.9 8.3 %all-to-all-start.3 = ((bf16[32,104,128]{2,1,0:T(8,128)(2,1)}), bf16[32,104,128]{2,1,0:T(8,128)(2,1)S(1)}, u32[]{:S(2)}, u32[]{:S(2)}) async-start(bf16[32,104,128]{2,1,0:T(8,128)(2,1)} %shard_map.123), calls=%async_computation.3 | async-start | bytes 1703936 | tf_op jit(solution)/shard_map/all_to_all | solution.py:330
  107.2 1.5 %shard_map.120 = (bf16[512,128]{1,0:T(8,128)(2,1)}, s32[512,128]{1,0:T(8,128)S(1)}, f32[512,128]{1,0:T(8,128)S(1)}) custom-call(bf16[32,104,128]{2,1,0:T(8,128)(2,1)S(1)} %all-to-all-done.1.got_ref, s32[1,512]{1,0:T(1,128)S(1)} %bitcast.5, bf16[512,128]{1,0:T(8,128)(2,1)S(1)} %copy-done.1, bf16[512,128]{1,0:T(8,128)(2,1)S(1)} %copy-done.2, ...), custom_call_target="tpu_custom_call" | custom-call | tf_op jit(solution)/shard_map/pallas_call | solution.py:38
  108.8 16.4 %all-to-all-done.3.got_ref = bf16[32,104,128]{2,1,0:T(8,128)(2,1)S(1)} async-done(((bf16[32,104,128]{2,1,0:T(8,128)(2,1)}), bf16[32,104,128]{2,1,0:T(8,128)(2,1)S(1)}, u32[]{:S(2)}, u32[]{:S(2)}) %all-to-all-start.3) | async-done | bytes 852000 | tf_op jit(solution)/shard_map/all_to_all | solution.py:330
  125.2 7.4 %collective-permute-start.9 = (bf16[14,128,128]{2,1,0:T(8,128)(2,1)S(1)}, bf16[14,128,128]{2,1,0:T(8,128)(2,1)S(1)}, u32[]{:S(2)}, u32[]{:S(2)}) collective-permute-start(bf16[14,128,128]{2,1,0:T(8,128)(2,1)S(1)} %shard_map.125.mine_ref), channel_id=1, source_target_pairs={{0,32},{32,0},{1,33},{33,1},{2,34},{34,2},{3,35},{35,3},{4,36},{36... | collective-permute-start | bytes 1376264 | tf_op jit(solution)/shard_map/ppermute | solution.py:334
  134.0 1.5 %shard_map.126 = (f32[27,128,128]{2,1,0:T(8,128)}, f32[128,128]{1,0:T(8,128)}) custom-call(s32[1]{0:T(128)} %bitcast.core_ref, bf16[14,128,128]{2,1,0:T(8,128)(2,1)S(1)} %shard_map.125.mine_ref, bf16[14,128,128]{2,1,0:T(8,128)(2,1)S(1)} %collective-permute-done.9.other_ref), custom_call_target="tpu_custom_call" | custom-call | tf_op jit(solution)/shard_map/pallas_call | solution.py:38
  (30 shorter events, 11.1 us)
Async XLA Ops:
  0.6 15.0 %copy-start.2 = (bf16[512,128]{1,0:T(8,128)(2,1)S(1)}, bf16[512,128]{1,0:T(8,128)(2,1)}, u32[]{:S(2)}) copy-start(bf16[512,128]{1,0:T(8,128)(2,1)} %cot_ref.3) | copy-start | bytes 393220
  0.6 15.0 %copy-start.1 = (bf16[512,128]{1,0:T(8,128)(2,1)S(1)}, bf16[512,128]{1,0:T(8,128)(2,1)}, u32[]{:S(2)}) copy-start(bf16[512,128]{1,0:T(8,128)(2,1)} %feat_ref.3) | copy-start | bytes 393220
  0.7 15.0 %copy-start.3 = (bf16[128,128]{1,0:T(8,128)(2,1)S(1)}, bf16[128,128]{1,0:T(8,128)(2,1)}, u32[]{:S(2)}) copy-start(bf16[128,128]{1,0:T(8,128)(2,1)} %mlp_ref.3) | copy-start | bytes 98308
  3.6 51.5 %copy-start = (bf16[27,128,128]{2,1,0:T(8,128)(2,1)S(1)}, bf16[27,128,128]{2,1,0:T(8,128)(2,1)}, u32[]{:S(2)}) copy-start(bf16[27,128,128]{2,1,0:T(8,128)(2,1)} %weight_ref.3) | copy-start | bytes 2654212
  3.6 32.4 %all-to-all-start = ((bf16[32,104,128]{2,1,0:T(8,128)(2,1)}), bf16[32,104,128]{2,1,0:T(8,128)(2,1)S(1)}, u32[]{:S(2)}, u32[]{:S(2)}) async-start(bf16[32,104,128]{2,1,0:T(8,128)(2,1)} %shard_map.111), calls=%async_computation | async-start | bytes 1703936 | tf_op jit(solution)/shard_map/all_to_all | solution.py:330
  36.7 8.6 %collective-permute-start = (bf16[1,8,16,128]{3,2,1,0:T(8,128)(2,1)S(1)}, bf16[1,8,16,128]{3,2,1,0:T(8,128)(2,1)S(1)}, u32[]{:S(2)}, u32[]{:S(2)}) collective-permute-start(bf16[1,8,16,128]{3,2,1,0:T(8,128)(2,1)S(1)} %get-tuple-element.41), channel_id=1, source_target_pairs={{0,32},{32,0},{1,33},{33,1},{2,34},{34,2},{3,35},{35,3},{4,36},{36... | collective-permute-start | bytes 98312 | tf_op jit(solution)/shard_map/ppermute | solution.py:334
  42.2 5.2 %collective-permute-start.1 = (bf16[1,8,16,128]{3,2,1,0:T(8,128)(2,1)S(1)}, bf16[1,8,16,128]{3,2,1,0:T(8,128)(2,1)S(1)}, u32[]{:S(2)}, u32[]{:S(2)}) collective-permute-start(bf16[1,8,16,128]{3,2,1,0:T(8,128)(2,1)S(1)} %get-tuple-element.42), channel_id=1, source_target_pairs={{32,64},{96,128},{160,192},{64,32},{128,96},{192,160},{33,65},{97,... | collective-permute-start | bytes 98312 | tf_op jit(solution)/shard_map/ppermute | solution.py:319
  47.4 5.3 %collective-permute-start.2 = (bf16[6,1,16,128]{3,2,1,0:T(8,128)(2,1)S(1)}, bf16[6,1,16,128]{3,2,1,0:T(8,128)(2,1)S(1)}, u32[]{:S(2)}, u32[]{:S(2)}) collective-permute-start(bf16[6,1,16,128]{3,2,1,0:T(8,128)(2,1)S(1)} %get-tuple-element.43), channel_id=1, source_target_pairs={{0,1},{1,2},{2,3},{3,4},{4,5},{5,6},{6,7},{7,8},{8,9},{9,10},{10,1... | collective-permute-start | bytes 73736 | tf_op jit(solution)/shard_map/ppermute | solution.py:326
  50.5 4.6 %collective-permute-start.3 = (bf16[6,1,16,128]{3,2,1,0:T(8,128)(2,1)S(1)}, bf16[6,1,16,128]{3,2,1,0:T(8,128)(2,1)S(1)}, u32[]{:S(2)}, u32[]{:S(2)}) collective-permute-start(bf16[6,1,16,128]{3,2,1,0:T(8,128)(2,1)S(1)} %get-tuple-element.44), channel_id=1, source_target_pairs={{1,0},{2,1},{3,2},{4,3},{5,4},{6,5},{7,6},{8,7},{9,8},{10,9},{11,1... | collective-permute-start | bytes 73736 | tf_op jit(solution)/shard_map/ppermute | solution.py:326
  57.3 1.9 %collective-permute-start.4 = (bf16[14,128,128]{2,1,0:T(8,128)(2,1)S(1)}, bf16[14,128,128]{2,1,0:T(8,128)(2,1)S(1)}, u32[]{:S(2)}, u32[]{:S(2)}) collective-permute-start(bf16[14,128,128]{2,1,0:T(8,128)(2,1)S(1)} %get-tuple-element.49), channel_id=1, source_target_pairs={{0,32},{32,0},{1,33},{33,1},{2,34},{34,2},{3,35},{35,3},{4,36},{36... | collective-permute-start | bytes 1376264 | tf_op jit(solution)/shard_map/ppermute | solution.py:334
  60.3 27.5 %all-to-all-start.1 = ((bf16[32,104,128]{2,1,0:T(8,128)(2,1)}), bf16[32,104,128]{2,1,0:T(8,128)(2,1)S(1)}, u32[]{:S(2)}, u32[]{:S(2)}) async-start(bf16[32,104,128]{2,1,0:T(8,128)(2,1)} %shard_map.118), calls=%async_computation.1 | async-start | bytes 1703936 | tf_op jit(solution)/shard_map/all_to_all | solution.py:330
  66.6 4.9 %collective-permute-start.5 = (bf16[1,8,16,128]{3,2,1,0:T(8,128)(2,1)S(1)}, bf16[1,8,16,128]{3,2,1,0:T(8,128)(2,1)S(1)}, u32[]{:S(2)}, u32[]{:S(2)}) collective-permute-start(bf16[1,8,16,128]{3,2,1,0:T(8,128)(2,1)S(1)} %get-tuple-element.52), channel_id=1, source_target_pairs={{0,32},{32,0},{1,33},{33,1},{2,34},{34,2},{3,35},{35,3},{4,36},{36... | collective-permute-start | bytes 98312 | tf_op jit(solution)/shard_map/ppermute | solution.py:334
  67.1 6.0 %collective-permute-start.6 = (bf16[1,8,16,128]{3,2,1,0:T(8,128)(2,1)S(1)}, bf16[1,8,16,128]{3,2,1,0:T(8,128)(2,1)S(1)}, u32[]{:S(2)}, u32[]{:S(2)}) collective-permute-start(bf16[1,8,16,128]{3,2,1,0:T(8,128)(2,1)S(1)} %get-tuple-element.53), channel_id=1, source_target_pairs={{32,64},{96,128},{160,192},{64,32},{128,96},{192,160},{33,65},{97,... | collective-permute-start | bytes 98312 | tf_op jit(solution)/shard_map/ppermute | solution.py:319
  73.1 10.5 %collective-permute-start.7 = (bf16[6,1,16,128]{3,2,1,0:T(8,128)(2,1)S(1)}, bf16[6,1,16,128]{3,2,1,0:T(8,128)(2,1)S(1)}, u32[]{:S(2)}, u32[]{:S(2)}) collective-permute-start(bf16[6,1,16,128]{3,2,1,0:T(8,128)(2,1)S(1)} %get-tuple-element.55), channel_id=1, source_target_pairs={{0,1},{1,2},{2,3},{3,4},{4,5},{5,6},{6,7},{7,8},{8,9},{9,10},{10,1... | collective-permute-start | bytes 73736 | tf_op jit(solution)/shard_map/ppermute | solution.py:326
  76.8 9.4 %collective-permute-start.8 = (bf16[6,1,16,128]{3,2,1,0:T(8,128)(2,1)S(1)}, bf16[6,1,16,128]{3,2,1,0:T(8,128)(2,1)S(1)}, u32[]{:S(2)}, u32[]{:S(2)}) collective-permute-start(bf16[6,1,16,128]{3,2,1,0:T(8,128)(2,1)S(1)} %get-tuple-element.56), channel_id=1, source_target_pairs={{1,0},{2,1},{3,2},{4,3},{5,4},{6,5},{7,6},{8,7},{9,8},{10,9},{11,1... | collective-permute-start | bytes 73736 | tf_op jit(solution)/shard_map/ppermute | solution.py:326
  88.5 9.5 %all-to-all-start.2 = ((bf16[4,56,128]{2,1,0:T(8,128)(2,1)}), bf16[4,56,128]{2,1,0:T(8,128)(2,1)S(1)}, u32[]{:S(2)}, u32[]{:S(2)}) async-start(bf16[4,56,128]{2,1,0:T(8,128)(2,1)} %shard_map.121), calls=%async_computation.2 | async-start | bytes 114688 | tf_op jit(solution)/shard_map/all_to_all | solution.py:400
  95.4 11.8 %copy-start.4 = (s32[512,1]{0,1:T(1,128)S(1)}, s32[512,1]{0,1:T(1,128)}, u32[]{:S(2)}) copy-start(s32[512,1]{0,1:T(1,128)} %param.9) | copy-start | bytes 6148
  98.9 26.2 %all-to-all-start.3 = ((bf16[32,104,128]{2,1,0:T(8,128)(2,1)}), bf16[32,104,128]{2,1,0:T(8,128)(2,1)S(1)}, u32[]{:S(2)}, u32[]{:S(2)}) async-start(bf16[32,104,128]{2,1,0:T(8,128)(2,1)} %shard_map.123), calls=%async_computation.3 | async-start | bytes 1703936 | tf_op jit(solution)/shard_map/all_to_all | solution.py:330
  125.2 8.8 %collective-permute-start.9 = (bf16[14,128,128]{2,1,0:T(8,128)(2,1)S(1)}, bf16[14,128,128]{2,1,0:T(8,128)(2,1)S(1)}, u32[]{:S(2)}, u32[]{:S(2)}) collective-permute-start(bf16[14,128,128]{2,1,0:T(8,128)(2,1)S(1)} %shard_map.125.mine_ref), channel_id=1, source_target_pairs={{0,32},{32,0},{1,33},{33,1},{2,34},{34,2},{3,35},{35,3},{4,36},{36... | collective-permute-start | bytes 1376264 | tf_op jit(solution)/shard_map/ppermute | solution.py:334

commit v4 on v3

--- a/solution.py
+++ b/solution.py
@@ -141,7 +141,7 @@
     return onehot(iota((CELLS, SLOTS), 0) == own)
 
 
-def voxel_kernel(core_ref, got_ref, vox_ref, near_ref, far_ref, div_ref, meta_ref):
+def voxel_kernel(spot_ref, got_ref, vox_ref, near_ref, far_ref, div_ref, meta_ref):
     meta = arrived_meta(got_ref)
     meta_ref[...] = meta
     own_hot = own_matrix(meta)
@@ -151,7 +151,7 @@
     divisor = jnp.maximum(total[:, C:], 1.0)
     div_ref[...] = divisor
     vox_ref[...] = (total[:, :C] / divisor).astype(BF).reshape(VX, VY, Z, C)
-    core = core_ref[0]
+    core = spot_ref[0] % 2
     near_ref[...] = vox_ref[pl.ds((VX - 1) * (1 - core), 1)]
     far_ref[...] = vox_ref[pl.ds((VX - 1) * core, 1)]
 
@@ -175,17 +175,26 @@
     grad_ref[...] = dot(matrix_ref[...], cots)
 
 
-def edge_kernel(core_ref, near_ref, own_ref, far_ref, tail_ref, head_ref):
-    core = core_ref[0]
+def flag(spot_ref, bit):
+    return (spot_ref[0] // 2**bit % 2).astype(F32).astype(BF)
+
+
+def edge_kernel(spot_ref, near_ref, own_ref, far_ref, tail_ref, head_ref):
+    core = spot_ref[0] % 2
+    inside = flag(spot_ref, 1)
     for ref, y in ((tail_ref, VY - 1), (head_ref, 0)):
         ref[pl.ds((VX + 1) * (1 - core), 1)] = near_ref[:, y : y + 1]
         ref[1 : VX + 1] = own_ref[:, y : y + 1]
-        ref[pl.ds((VX + 1) * core, 1)] = far_ref[:, y : y + 1]
-
-
-def assemble(core, wide_ref, own_ref, near_ref, far_ref, ylo_ref, yhi_ref):
-    def put(x, y, block):
+        ref[pl.ds((VX + 1) * core, 1)] = far_ref[:, y : y + 1] * inside
+
+
+def assemble(spot_ref, wide_ref, own_ref, near_ref, far_ref, ylo_ref, yhi_ref):
+    core = spot_ref[0] % 2
+
+    def put(x, y, block, inside=None):
         nx, ny = block.shape[0], block.shape[1]
+        if inside is not None:
+            block = block * flag(spot_ref, inside)
         flat = block.reshape(nx * ny * Z, C).astype(F32)
         z = iota(flat.shape, 0) % Z
         blank = jnp.zeros((8, C), F32)
@@ -201,19 +210,19 @@
 
     put(1, 1, own_ref[...])
     put((VX + 1) * (1 - core), 1, near_ref[...])
-    put((VX + 1) * core, 1, far_ref[...])
-    put(0, 0, ylo_ref[...])
-    put(0, VY + 1, yhi_ref[...])
+    put((VX + 1) * core, 1, far_ref[...], 1)
+    put(0, 0, ylo_ref[...], 2)
+    put(0, VY + 1, yhi_ref[...], 3)
 
 
 def window(wide_ref, x, y):
     return wide_ref[x : x + VX, y : y + VY, :, :].reshape(CELLS, 3 * C)
 
 
-def conv_kernel(core_ref, vox_ref, near_ref, far_ref, ylo_ref, yhi_ref, weight_ref, gout_ref,
+def conv_kernel(spot_ref, vox_ref, near_ref, far_ref, ylo_ref, yhi_ref, weight_ref, gout_ref,
                 mlp_ref, keep_ref, send_ref, act_ref, hid_ref, in_ref, out_ref, wide_ref, all_ref):
-    core = core_ref[0]
-    assemble(core, wide_ref, vox_ref, near_ref, far_ref, ylo_ref, yhi_ref)
+    core = spot_ref[0] % 2
+    assemble(spot_ref, wide_ref, vox_ref, near_ref, far_ref, ylo_ref, yhi_ref)
     hidden = jnp.zeros((CELLS, C), F32)
     for k in range(9):
         taps = weight_ref[3 * k : 3 * k + 3].reshape(3 * C, C)
@@ -249,8 +258,8 @@
     out_ref[...] = jnp.broadcast_to(total.astype(BF)[None], out_ref.shape)
 
 
-def back_kernel(core_ref, hid_ref, near_ref, far_ref, ylo_ref, yhi_ref, weight_ref, meta_ref, div_ref, out_ref, wide_ref):
-    assemble(core_ref[0], wide_ref, hid_ref, near_ref, far_ref, ylo_ref, yhi_ref)
+def back_kernel(spot_ref, hid_ref, near_ref, far_ref, ylo_ref, yhi_ref, weight_ref, meta_ref, div_ref, out_ref, wide_ref):
+    assemble(spot_ref, wide_ref, hid_ref, near_ref, far_ref, ylo_ref, yhi_ref)
     total = jnp.zeros((CELLS, C), F32)
     for k in range(9):
         taps = jnp.concatenate([weight_ref[3 * k + 2 - j] for j in range(3)], axis=1)
@@ -294,18 +303,18 @@
     out_ref[...] = (unpack(pos_ref[...], got_ref) + back_ref[...]).astype(BF)
 
 
-def weights_kernel(core_ref, mine_ref, other_ref, conv_ref, mlp_ref):
+def weights_kernel(spot_ref, mine_ref, other_ref, conv_ref, mlp_ref):
     def fill(first_ref, second_ref):
         for o in range(27):
             half = first_ref[o] if o < HALF else second_ref[o - HALF]
             conv_ref[o] = half.astype(F32).T * (1.0 / math.sqrt(GX * GY * CELLS))
         mlp_ref[...] = second_ref[HALF - 1].astype(F32).T * (1.0 / math.sqrt(GX * GY * PTS))
 
-    @pl.when(core_ref[0] == 0)
+    @pl.when(spot_ref[0] % 2 == 0)
     def _():
         fill(mine_ref, other_ref)
 
-    @pl.when(core_ref[0] == 1)
+    @pl.when(spot_ref[0] % 2 == 1)
     def _():
         fill(other_ref, mine_ref)
 
@@ -315,14 +324,14 @@
 
 
 def chips(face):
-    pairs = [(i, i + 1) for i in range(1, GX - 1, 2)]
+    pairs = [(i, (i + 1) % GX) for i in range(1, GX, 2)]
     return lax.ppermute(face, ("y", "c"), pairs + [(j, i) for i, j in pairs])
 
 
 def edges(core, near, cells, far):
     tail, head = call(edge_kernel, (EDGE, EDGE), (core, near, cells, far), smem=1, mib=2)
-    up = [(i, i + 1) for i in range(GY - 1)]
-    down = [(i + 1, i) for i in range(GY - 1)]
+    up = [(i, (i + 1) % GY) for i in range(GY)]
+    down = [((i + 1) % GY, i) for i in range(GY)]
     return lax.ppermute(tail, ("x", "z"), up), lax.ppermute(head, ("x", "z"), down)
 
 
@@ -335,8 +344,12 @@
 
 
 def body(features, point_slab, base_cell, nearest, offsets, conv_weight, mlp_weight, cotangent):
-    core = lax.axis_index("c").reshape(1)
-    point_slab, core = lax.optimization_barrier((point_slab, core))
+    strip = lax.axis_index(("y", "c"))
+    slab_here = lax.axis_index(("x", "z"))
+    core = lax.axis_index("c")
+    core = core + 2 * (strip % (GX - 1) != 0) + 4 * (slab_here != 0) + 8 * (slab_here != GY - 1)
+    spot = core.reshape(1)
+    point_slab, spot = lax.optimization_barrier((point_slab, spot))
     slab = point_slab.reshape(1, PTS)
     line = pltpu.VMEM((1, PTS), jnp.int32)
     sent = call(
@@ -364,11 +377,11 @@
     voxels, near, far, divisor, meta = call(
         voxel_kernel,
         (cells, FACE, FACE, sds((CELLS, C), F32), sds((KINDS, SLOTS), F32)),
-        (core, got),
+        (spot, got),
         smem=1,
     )
     near, far = swap(near), chips(far)
-    faces = (near, far) + edges(core, near, voxels, far)
+    faces = (near, far) + edges(spot, near, voxels, far)
     matrix, grad_out = call(
         spread_kernel, (sds((CELLS, SLOTS), BF), sds((CELLS, C), F32)), (got, meta)
     )
@@ -378,7 +391,7 @@
     keep, send, act, grad_hidden, near, far = call(
         conv_kernel,
         (sds((HALF, C, C), F32), sds((HALF, C, C), BF), sds((CELLS, C), BF), cells, FACE, FACE),
-        (core, voxels) + faces + (conv_weight, grad_out, mlp_grad),
+        (spot, voxels) + faces + (conv_weight, grad_out, mlp_grad),
         scratch=(wide, pltpu.VMEM((2 * HALF, C, C), F32)),
         smem=1,
     )
@@ -387,12 +400,12 @@
     joined = call(join_kernel, block, (keep, arrived, filled))
     first = exchange(joined)
     near, far = swap(near), chips(far)
-    grad_faces = (near, far) + edges(core, near, grad_hidden, far)
+    grad_faces = (near, far) + edges(spot, near, grad_hidden, far)
     first, grad_faces = lax.optimization_barrier((first, grad_faces))
     filled = call(
         back_kernel,
         rows,
-        (core, grad_hidden) + grad_faces + (conv_weight, meta, divisor),
+        (spot, grad_hidden) + grad_faces + (conv_weight, meta, divisor),
         scratch=(wide,),
         smem=1,
     )
@@ -410,7 +423,7 @@
     other = swap(mine)
     grad_features = call(backward_kernel, sds((PTS, C), BF), (second, position, back))
     grad_conv, grad_mlp = call(
-        weights_kernel, (sds((27, C, C), F32), sds((C, C), F32)), (core, mine, other), smem=1
+        weights_kernel, (sds((27, C, C), F32), sds((C, C), F32)), (spot, mine, other), smem=1
     )
     return (output, grad_features, grad_conv, grad_mlp)
 

time: 136 us -> 133 us (0.978)
  starting transfers between devices: 62.1 us -> 57.7 us
  waiting for transfers between devices: 55.9 us -> 57.4 us
    ppermute x2, starting transfers between devices: 7.51 us -> 1.28 us  [chips(): return lax.ppermute(face, ('y', 'c'), pairs + [(j, i) for i, j in pairs])]
    ppermute x2, waiting for transfers between devices: 5.49 us -> 10.9 us  [edges(): lax.ppermute(tail, ('x', 'z'), up)]
    ppermute x2, waiting for transfers between devices: 5 us -> 0.01 us  [edges(): lax.ppermute(head, ('x', 'z'), down)]
    ppermute x2, starting transfers between devices: 2.58 us -> 7.06 us  [edges(): lax.ppermute(head, ('x', 'z'), down)]
    ppermute x2, starting transfers between devices: 6.82 us -> 3.06 us  [edges(): lax.ppermute(tail, ('x', 'z'), up)]
    ppermute x4, starting transfers between devices: 13.5 us -> 16.2 us  [swap(): return lax.ppermute(half, 'c', [(0, 1), (1, 0)])]
    all_to_all x1, starting transfers between devices: 5.02 us -> 3.28 us  [body(): lax.all_to_all(shares, 'y', split_axis=0, concat_axis=0, tiled=True)]
where the time goes in v4:
time: 133 us
  starting transfers between devices  57.7 us (43%)
  waiting for transfers between devices  57.4 us (43%)
  Pallas kernels  16.7 us (13%)
    all_to_all x3, waiting for transfers between devices, exchange(): lax.all_to_all(rows, ('x', 'z'), split_axis=0, concat_axis=0, tiled=True)  37.5 us
    all_to_all x3, starting transfers between devices, exchange(): lax.all_to_all(rows, ('x', 'z'), split_axis=0, concat_axis=0, tiled=True)  26.9 us
    pallas_call x16, Pallas kernels, call(): pl.pallas_call(kernel, out_shape=out_shape, in_specs=[SMEM] * smem + [HBM...  16.7 us
    ppermute x4, starting transfers between devices, swap(): return lax.ppermute(half, 'c', [(0, 1), (1, 0)])  16.2 us
    ppermute x2, waiting for transfers between devices, edges(): lax.ppermute(tail, ('x', 'z'), up)  10.9 us
    ppermute x2, starting transfers between devices, edges(): lax.ppermute(head, ('x', 'z'), down)  7.06 us
    ppermute x2, waiting for transfers between devices, chips(): return lax.ppermute(face, ('y', 'c'), pairs + [(j, i) for i, j in pairs])  4.54 us
    all_to_all x1, starting transfers between devices, body(): lax.all_to_all(shares, 'y', split_axis=0, concat_axis=0, tiled=True)  3.28 us
  transfers between devices with their start and end apart: 14, of which 11 were waited for; matrix products, arithmetic and copies ran while one was open for 0% of the time, Pallas kernels for 5%

profile of v4, /device:TPU:1, one launch (start us, length us, event | category | flops | bytes accessed | tf_op | source)
XLA Modules:
  0.0 132.7 jit_solution(11117653487388235633)
XLA Ops:
  0.7 3.0 %shard_map.111 = bf16[32,104,128]{2,1,0:T(8,128)(2,1)} custom-call(bf16[512,128]{1,0:T(8,128)(2,1)} %feat_ref.3, bf16[512,128]{1,0:T(8,128)(2,1)} %cot_ref.3, s32[1,512]{1,0:T(1,128)} %bitcast.4, s32[1,512]{1,0:T(1,128)} %bitcast.6, s32[1,512]{1,0:T(1,128)} %bitcast.7, bf16[3,512]{1,0:T(4,128)(2,1)} %off_hbm.1), custom_call_target="tpu_custom_call" | custom-call | tf_op jit(solution)/shard_map/pallas_call | solution.py:38
  3.7 12.0 %all-to-all-start = ((bf16[32,104,128]{2,1,0:T(8,128)(2,1)}), bf16[32,104,128]{2,1,0:T(8,128)(2,1)S(1)}, u32[]{:S(2)}, u32[]{:S(2)}) async-start(bf16[32,104,128]{2,1,0:T(8,128)(2,1)} %shard_map.111), calls=%async_computation | async-start | bytes 1703936 | tf_op jit(solution)/shard_map/all_to_all | solution.py:339
  16.2 19.9 %all-to-all-done.got_ref = bf16[32,104,128]{2,1,0:T(8,128)(2,1)S(1)} async-done(((bf16[32,104,128]{2,1,0:T(8,128)(2,1)}), bf16[32,104,128]{2,1,0:T(8,128)(2,1)S(1)}, u32[]{:S(2)}, u32[]{:S(2)}) %all-to-all-start) | async-done | bytes 852000 | tf_op jit(solution)/shard_map/all_to_all | solution.py:339
  36.8 5.5 %collective-permute-start = (bf16[1,8,16,128]{3,2,1,0:T(8,128)(2,1)S(1)}, bf16[1,8,16,128]{3,2,1,0:T(8,128)(2,1)S(1)}, u32[]{:S(2)}, u32[]{:S(2)}) collective-permute-start(bf16[1,8,16,128]{3,2,1,0:T(8,128)(2,1)S(1)} %get-tuple-element.41), channel_id=1, source_target_pairs={{0,32},{32,0},{1,33},{33,1},{2,34},{34,2},{3,35},{35,3},{4,36},{36... | collective-permute-start | bytes 98312 | tf_op jit(solution)/shard_map/ppermute | solution.py:343
  42.2 1.3 collective-permute-start.1
  43.5 2.1 %collective-permute-done.1.far_ref = bf16[1,8,16,128]{3,2,1,0:T(8,128)(2,1)S(1)} collective-permute-done((bf16[1,8,16,128]{3,2,1,0:T(8,128)(2,1)S(1)}, bf16[1,8,16,128]{3,2,1,0:T(8,128)(2,1)S(1)}, u32[]{:S(2)}, u32[]{:S(2)}) %collective-permute-start.1) | collective-permute-done | bytes 32800 | tf_op jit(solution)/shard_map/ppermute | solution.py:328
  45.6 1.3 collective-permute-start.2
  46.9 3.6 %collective-permute-start.3 = (bf16[6,1,16,128]{3,2,1,0:T(8,128)(2,1)S(1)}, bf16[6,1,16,128]{3,2,1,0:T(8,128)(2,1)S(1)}, u32[]{:S(2)}, u32[]{:S(2)}) collective-permute-start(bf16[6,1,16,128]{3,2,1,0:T(8,128)(2,1)S(1)} %get-tuple-element.44), channel_id=1, source_target_pairs={{1,0},{2,1},{3,2},{4,3},{5,4},{6,5},{7,6},{8,7},{9,8},{10,9},{11,1... | collective-permute-start | bytes 73736 | tf_op jit(solution)/shard_map/ppermute | solution.py:335
  51.6 2.3 %shard_map.116 = (f32[14,128,128]{2,1,0:T(8,128)S(1)}, bf16[14,128,128]{2,1,0:T(8,128)(2,1)S(1)}, bf16[512,128]{1,0:T(8,128)(2,1)S(1)}, bf16[4,8,16,128]{3,2,1,0...) custom-call(s32[1]{0:T(128)} %bitcast.spot_ref, ...), custom_call_target="tpu_custom_call" | custom-call | tf_op jit(solution)/shard_map/pallas_call | solution.py:38
  54.0 2.6 %collective-permute-start.4 = (bf16[14,128,128]{2,1,0:T(8,128)(2,1)S(1)}, bf16[14,128,128]{2,1,0:T(8,128)(2,1)S(1)}, u32[]{:S(2)}, u32[]{:S(2)}) collective-permute-start(bf16[14,128,128]{2,1,0:T(8,128)(2,1)S(1)} %get-tuple-element.49), channel_id=1, source_target_pairs={{0,32},{32,0},{1,33},{33,1},{2,34},{34,2},{3,35},{35,3},{4,36},{36... | collective-permute-start | bytes 1376264 | tf_op jit(solution)/shard_map/ppermute | solution.py:343
  59.1 6.7 %all-to-all-start.1 = ((bf16[32,104,128]{2,1,0:T(8,128)(2,1)}), bf16[32,104,128]{2,1,0:T(8,128)(2,1)S(1)}, u32[]{:S(2)}, u32[]{:S(2)}) async-start(bf16[32,104,128]{2,1,0:T(8,128)(2,1)} %shard_map.118), calls=%async_computation.1 | async-start | bytes 1703936 | tf_op jit(solution)/shard_map/all_to_all | solution.py:339
  67.4 2.5 %collective-permute-done.6.far_ref = bf16[1,8,16,128]{3,2,1,0:T(8,128)(2,1)S(1)} collective-permute-done((bf16[1,8,16,128]{3,2,1,0:T(8,128)(2,1)S(1)}, bf16[1,8,16,128]{3,2,1,0:T(8,128)(2,1)S(1)}, u32[]{:S(2)}, u32[]{:S(2)}) %collective-permute-start.6) | collective-permute-done | bytes 32800 | tf_op jit(solution)/shard_map/ppermute | solution.py:328
  69.9 1.8 %collective-permute-start.7 = (bf16[6,1,16,128]{3,2,1,0:T(8,128)(2,1)S(1)}, bf16[6,1,16,128]{3,2,1,0:T(8,128)(2,1)S(1)}, u32[]{:S(2)}, u32[]{:S(2)}) collective-permute-start(bf16[6,1,16,128]{3,2,1,0:T(8,128)(2,1)S(1)} %get-tuple-element.55), channel_id=1, source_target_pairs={{0,1},{1,2},{2,3},{3,4},{4,5},{5,6},{6,7},{7,8},{8,9},{9,10},{10,1... | collective-permute-start | bytes 73736 | tf_op jit(solution)/shard_map/ppermute | solution.py:335
  71.6 3.5 %collective-permute-start.8 = (bf16[6,1,16,128]{3,2,1,0:T(8,128)(2,1)S(1)}, bf16[6,1,16,128]{3,2,1,0:T(8,128)(2,1)S(1)}, u32[]{:S(2)}, u32[]{:S(2)}) collective-permute-start(bf16[6,1,16,128]{3,2,1,0:T(8,128)(2,1)S(1)} %get-tuple-element.56), channel_id=1, source_target_pairs={{1,0},{2,1},{3,2},{4,3},{5,4},{6,5},{7,6},{8,7},{9,8},{10,9},{11,1... | collective-permute-start | bytes 73736 | tf_op jit(solution)/shard_map/ppermute | solution.py:335
  75.1 10.5 %collective-permute-done.7.ylo_ref = bf16[6,1,16,128]{3,2,1,0:T(8,128)(2,1)S(1)} collective-permute-done((bf16[6,1,16,128]{3,2,1,0:T(8,128)(2,1)S(1)}, bf16[6,1,16,128]{3,2,1,0:T(8,128)(2,1)S(1)}, u32[]{:S(2)}, u32[]{:S(2)}) %collective-permute-start.7) | collective-permute-done | bytes 24608 | tf_op jit(solution)/shard_map/ppermute | solution.py:335
  87.4 3.3 %all-to-all-start.2 = ((bf16[4,56,128]{2,1,0:T(8,128)(2,1)}), bf16[4,56,128]{2,1,0:T(8,128)(2,1)S(1)}, u32[]{:S(2)}, u32[]{:S(2)}) async-start(bf16[4,56,128]{2,1,0:T(8,128)(2,1)} %shard_map.121), calls=%async_computation.2 | async-start | bytes 114688 | tf_op jit(solution)/shard_map/all_to_all | solution.py:413
  90.7 1.8 %shard_map.122.filled_ref = bf16[32,48,128]{2,1,0:T(8,128)(2,1)S(1)} custom-call(s32[1]{0:T(128)} %bitcast.spot_ref, bf16[4,8,16,128]{3,2,1,0:T(8,128)(2,1)S(1)} %get-tuple-element.54.own_ref.hid_ref, bf16[1,8,16,128]{3,2,1,0:T(8,128)(2,1)S(1)} %collective-permute-done.5.near_ref, bf16[1,8,16,128]{3,2,1,0:T(8,128)(2,1)S(1)} %collective-permute-done.6.far_ref, ...), custom_call_target="tpu_custom_call" | custom-call | tf_op jit(solution)/shard_map/pallas_call | solution.py:38
  92.6 2.6 %all-to-all-done.2.got_ref = bf16[4,56,128]{2,1,0:T(8,128)(2,1)S(1)} async-done(((bf16[4,56,128]{2,1,0:T(8,128)(2,1)}), bf16[4,56,128]{2,1,0:T(8,128)(2,1)S(1)}, u32[]{:S(2)}, u32[]{:S(2)}) %all-to-all-start.2) | async-done | bytes 57376 | tf_op jit(solution)/shard_map/all_to_all | solution.py:413
  96.1 8.1 %all-to-all-start.3 = ((bf16[32,104,128]{2,1,0:T(8,128)(2,1)}), bf16[32,104,128]{2,1,0:T(8,128)(2,1)S(1)}, u32[]{:S(2)}, u32[]{:S(2)}) async-start(bf16[32,104,128]{2,1,0:T(8,128)(2,1)} %shard_map.123), calls=%async_computation.3 | async-start | bytes 1703936 | tf_op jit(solution)/shard_map/all_to_all | solution.py:339
  104.2 1.5 %shard_map.120 = (bf16[512,128]{1,0:T(8,128)(2,1)}, s32[512,128]{1,0:T(8,128)S(1)}, f32[512,128]{1,0:T(8,128)S(1)}) custom-call(bf16[32,104,128]{2,1,0:T(8,128)(2,1)S(1)} %all-to-all-done.1.got_ref, s32[1,512]{1,0:T(1,128)S(1)} %bitcast.5, bf16[512,128]{1,0:T(8,128)(2,1)S(1)} %copy-done.1, bf16[512,128]{1,0:T(8,128)(2,1)S(1)} %copy-done.2, ...), custom_call_target="tpu_custom_call" | custom-call | tf_op jit(solution)/shard_map/pallas_call | solution.py:38
  105.7 16.6 %all-to-all-done.3.got_ref = bf16[32,104,128]{2,1,0:T(8,128)(2,1)S(1)} async-done(((bf16[32,104,128]{2,1,0:T(8,128)(2,1)}), bf16[32,104,128]{2,1,0:T(8,128)(2,1)S(1)}, u32[]{:S(2)}, u32[]{:S(2)}) %all-to-all-start.3) | async-done | bytes 852000 | tf_op jit(solution)/shard_map/all_to_all | solution.py:339
  122.4 7.4 %collective-permute-start.9 = (bf16[14,128,128]{2,1,0:T(8,128)(2,1)S(1)}, bf16[14,128,128]{2,1,0:T(8,128)(2,1)S(1)}, u32[]{:S(2)}, u32[]{:S(2)}) collective-permute-start(bf16[14,128,128]{2,1,0:T(8,128)(2,1)S(1)} %shard_map.125.mine_ref), channel_id=1, source_target_pairs={{0,32},{32,0},{1,33},{33,1},{2,34},{34,2},{3,35},{35,3},{4,36},{36... | collective-permute-start | bytes 1376264 | tf_op jit(solution)/shard_map/ppermute | solution.py:343
  129.8 1.2 shard_map.124
  131.2 1.5 %shard_map.126 = (f32[27,128,128]{2,1,0:T(8,128)}, f32[128,128]{1,0:T(8,128)}) custom-call(s32[1]{0:T(128)} %bitcast.spot_ref, bf16[14,128,128]{2,1,0:T(8,128)(2,1)S(1)} %shard_map.125.mine_ref, bf16[14,128,128]{2,1,0:T(8,128)(2,1)S(1)} %collective-permute-done.9.other_ref), custom_call_target="tpu_custom_call" | custom-call | tf_op jit(solution)/shard_map/pallas_call | solution.py:38
  (30 shorter events, 9.5 us)
Async XLA Ops:
  0.6 15.1 %copy-start.2 = (bf16[512,128]{1,0:T(8,128)(2,1)S(1)}, bf16[512,128]{1,0:T(8,128)(2,1)}, u32[]{:S(2)}) copy-start(bf16[512,128]{1,0:T(8,128)(2,1)} %cot_ref.3) | copy-start | bytes 393220
  0.6 15.1 %copy-start.1 = (bf16[512,128]{1,0:T(8,128)(2,1)S(1)}, bf16[512,128]{1,0:T(8,128)(2,1)}, u32[]{:S(2)}) copy-start(bf16[512,128]{1,0:T(8,128)(2,1)} %feat_ref.3) | copy-start | bytes 393220
  0.7 15.1 %copy-start.3 = (bf16[128,128]{1,0:T(8,128)(2,1)S(1)}, bf16[128,128]{1,0:T(8,128)(2,1)}, u32[]{:S(2)}) copy-start(bf16[128,128]{1,0:T(8,128)(2,1)} %mlp_ref.3) | copy-start | bytes 98308
  3.7 48.0 %copy-start = (bf16[27,128,128]{2,1,0:T(8,128)(2,1)S(1)}, bf16[27,128,128]{2,1,0:T(8,128)(2,1)}, u32[]{:S(2)}) copy-start(bf16[27,128,128]{2,1,0:T(8,128)(2,1)} %weight_ref.3) | copy-start | bytes 2654212
  3.7 32.4 %all-to-all-start = ((bf16[32,104,128]{2,1,0:T(8,128)(2,1)}), bf16[32,104,128]{2,1,0:T(8,128)(2,1)S(1)}, u32[]{:S(2)}, u32[]{:S(2)}) async-start(bf16[32,104,128]{2,1,0:T(8,128)(2,1)} %shard_map.111), calls=%async_computation | async-start | bytes 1703936 | tf_op jit(solution)/shard_map/all_to_all | solution.py:339
  36.8 6.7 %collective-permute-start = (bf16[1,8,16,128]{3,2,1,0:T(8,128)(2,1)S(1)}, bf16[1,8,16,128]{3,2,1,0:T(8,128)(2,1)S(1)}, u32[]{:S(2)}, u32[]{:S(2)}) collective-permute-start(bf16[1,8,16,128]{3,2,1,0:T(8,128)(2,1)S(1)} %get-tuple-element.41), channel_id=1, source_target_pairs={{0,32},{32,0},{1,33},{33,1},{2,34},{34,2},{3,35},{35,3},{4,36},{36... | collective-permute-start | bytes 98312 | tf_op jit(solution)/shard_map/ppermute | solution.py:343
  42.2 3.3 %collective-permute-start.1 = (bf16[1,8,16,128]{3,2,1,0:T(8,128)(2,1)S(1)}, bf16[1,8,16,128]{3,2,1,0:T(8,128)(2,1)S(1)}, u32[]{:S(2)}, u32[]{:S(2)}) collective-permute-start(bf16[1,8,16,128]{3,2,1,0:T(8,128)(2,1)S(1)} %get-tuple-element.42), channel_id=1, source_target_pairs={{32,64},{96,128},{160,192},{224,0},{64,32},{128,96},{192,160},{0,2... | collective-permute-start | bytes 98312 | tf_op jit(solution)/shard_map/ppermute | solution.py:328
  45.6 6.1 %collective-permute-start.2 = (bf16[6,1,16,128]{3,2,1,0:T(8,128)(2,1)S(1)}, bf16[6,1,16,128]{3,2,1,0:T(8,128)(2,1)S(1)}, u32[]{:S(2)}, u32[]{:S(2)}) collective-permute-start(bf16[6,1,16,128]{3,2,1,0:T(8,128)(2,1)S(1)} %get-tuple-element.43), channel_id=1, source_target_pairs={{0,1},{1,2},{2,3},{3,4},{4,5},{5,6},{6,7},{7,8},{8,9},{9,10},{10,1... | collective-permute-start | bytes 73736 | tf_op jit(solution)/shard_map/ppermute | solution.py:335
  46.9 4.8 %collective-permute-start.3 = (bf16[6,1,16,128]{3,2,1,0:T(8,128)(2,1)S(1)}, bf16[6,1,16,128]{3,2,1,0:T(8,128)(2,1)S(1)}, u32[]{:S(2)}, u32[]{:S(2)}) collective-permute-start(bf16[6,1,16,128]{3,2,1,0:T(8,128)(2,1)S(1)} %get-tuple-element.44), channel_id=1, source_target_pairs={{1,0},{2,1},{3,2},{4,3},{5,4},{6,5},{7,6},{8,7},{9,8},{10,9},{11,1... | collective-permute-start | bytes 73736 | tf_op jit(solution)/shard_map/ppermute | solution.py:335
  54.0 4.1 %collective-permute-start.4 = (bf16[14,128,128]{2,1,0:T(8,128)(2,1)S(1)}, bf16[14,128,128]{2,1,0:T(8,128)(2,1)S(1)}, u32[]{:S(2)}, u32[]{:S(2)}) collective-permute-start(bf16[14,128,128]{2,1,0:T(8,128)(2,1)S(1)} %get-tuple-element.49), channel_id=1, source_target_pairs={{0,32},{32,0},{1,33},{33,1},{2,34},{34,2},{3,35},{35,3},{4,36},{36... | collective-permute-start | bytes 1376264 | tf_op jit(solution)/shard_map/ppermute | solution.py:343
  59.1 27.7 %all-to-all-start.1 = ((bf16[32,104,128]{2,1,0:T(8,128)(2,1)}), bf16[32,104,128]{2,1,0:T(8,128)(2,1)S(1)}, u32[]{:S(2)}, u32[]{:S(2)}) async-start(bf16[32,104,128]{2,1,0:T(8,128)(2,1)} %shard_map.118), calls=%async_computation.1 | async-start | bytes 1703936 | tf_op jit(solution)/shard_map/all_to_all | solution.py:339
  65.8 1.6 %collective-permute-start.5 = (bf16[1,8,16,128]{3,2,1,0:T(8,128)(2,1)S(1)}, bf16[1,8,16,128]{3,2,1,0:T(8,128)(2,1)S(1)}, u32[]{:S(2)}, u32[]{:S(2)}) collective-permute-start(bf16[1,8,16,128]{3,2,1,0:T(8,128)(2,1)S(1)} %get-tuple-element.52), channel_id=1, source_target_pairs={{0,32},{32,0},{1,33},{33,1},{2,34},{34,2},{3,35},{35,3},{4,36},{36... | collective-permute-start | bytes 98312 | tf_op jit(solution)/shard_map/ppermute | solution.py:343
  66.5 3.3 %collective-permute-start.6 = (bf16[1,8,16,128]{3,2,1,0:T(8,128)(2,1)S(1)}, bf16[1,8,16,128]{3,2,1,0:T(8,128)(2,1)S(1)}, u32[]{:S(2)}, u32[]{:S(2)}) collective-permute-start(bf16[1,8,16,128]{3,2,1,0:T(8,128)(2,1)S(1)} %get-tuple-element.53), channel_id=1, source_target_pairs={{32,64},{96,128},{160,192},{224,0},{64,32},{128,96},{192,160},{0,2... | collective-permute-start | bytes 98312 | tf_op jit(solution)/shard_map/ppermute | solution.py:328
  69.9 15.7 %collective-permute-start.7 = (bf16[6,1,16,128]{3,2,1,0:T(8,128)(2,1)S(1)}, bf16[6,1,16,128]{3,2,1,0:T(8,128)(2,1)S(1)}, u32[]{:S(2)}, u32[]{:S(2)}) collective-permute-start(bf16[6,1,16,128]{3,2,1,0:T(8,128)(2,1)S(1)} %get-tuple-element.55), channel_id=1, source_target_pairs={{0,1},{1,2},{2,3},{3,4},{4,5},{5,6},{6,7},{7,8},{8,9},{9,10},{10,1... | collective-permute-start | bytes 73736 | tf_op jit(solution)/shard_map/ppermute | solution.py:335
  71.6 14.0 %collective-permute-start.8 = (bf16[6,1,16,128]{3,2,1,0:T(8,128)(2,1)S(1)}, bf16[6,1,16,128]{3,2,1,0:T(8,128)(2,1)S(1)}, u32[]{:S(2)}, u32[]{:S(2)}) collective-permute-start(bf16[6,1,16,128]{3,2,1,0:T(8,128)(2,1)S(1)} %get-tuple-element.56), channel_id=1, source_target_pairs={{1,0},{2,1},{3,2},{4,3},{5,4},{6,5},{7,6},{8,7},{9,8},{10,9},{11,1... | collective-permute-start | bytes 73736 | tf_op jit(solution)/shard_map/ppermute | solution.py:335
  87.4 7.7 %all-to-all-start.2 = ((bf16[4,56,128]{2,1,0:T(8,128)(2,1)}), bf16[4,56,128]{2,1,0:T(8,128)(2,1)S(1)}, u32[]{:S(2)}, u32[]{:S(2)}) async-start(bf16[4,56,128]{2,1,0:T(8,128)(2,1)} %shard_map.121), calls=%async_computation.2 | async-start | bytes 114688 | tf_op jit(solution)/shard_map/all_to_all | solution.py:413
  92.5 11.7 %copy-start.4 = (s32[512,1]{0,1:T(1,128)S(1)}, s32[512,1]{0,1:T(1,128)}, u32[]{:S(2)}) copy-start(s32[512,1]{0,1:T(1,128)} %param.9) | copy-start | bytes 6148
  96.1 26.2 %all-to-all-start.3 = ((bf16[32,104,128]{2,1,0:T(8,128)(2,1)}), bf16[32,104,128]{2,1,0:T(8,128)(2,1)S(1)}, u32[]{:S(2)}, u32[]{:S(2)}) async-start(bf16[32,104,128]{2,1,0:T(8,128)(2,1)} %shard_map.123), calls=%async_computation.3 | async-start | bytes 1703936 | tf_op jit(solution)/shard_map/all_to_all | solution.py:339
  122.4 8.8 %collective-permute-start.9 = (bf16[14,128,128]{2,1,0:T(8,128)(2,1)S(1)}, bf16[14,128,128]{2,1,0:T(8,128)(2,1)S(1)}, u32[]{:S(2)}, u32[]{:S(2)}) collective-permute-start(bf16[14,128,128]{2,1,0:T(8,128)(2,1)S(1)} %shard_map.125.mine_ref), channel_id=1, source_target_pairs={{0,32},{32,0},{1,33},{33,1},{2,34},{34,2},{3,35},{35,3},{4,36},{36... | collective-permute-start | bytes 1376264 | tf_op jit(solution)/shard_map/ppermute | solution.py:343

commit v5 on v4

--- a/solution.py
+++ b/solution.py
@@ -179,17 +179,20 @@
     return (spot_ref[0] // 2**bit % 2).astype(F32).astype(BF)
 
 
-def edge_kernel(spot_ref, near_ref, own_ref, far_ref, tail_ref, head_ref):
+def edge_kernel(spot_ref, near_ref, own_ref, far_ref, even_ref, odd_ref):
     core = spot_ref[0] % 2
+    turn = spot_ref[0] // 4 % 2
     inside = flag(spot_ref, 1)
-    for ref, y in ((tail_ref, VY - 1), (head_ref, 0)):
-        ref[pl.ds((VX + 1) * (1 - core), 1)] = near_ref[:, y : y + 1]
-        ref[1 : VX + 1] = own_ref[:, y : y + 1]
-        ref[pl.ds((VX + 1) * core, 1)] = far_ref[:, y : y + 1] * inside
-
-
-def assemble(spot_ref, wide_ref, own_ref, near_ref, far_ref, ylo_ref, yhi_ref):
+    for ref, y in ((even_ref, (VY - 1) * (1 - turn)), (odd_ref, (VY - 1) * turn)):
+        row = pl.ds(y, 1)
+        ref[pl.ds((VX + 1) * (1 - core), 1)] = near_ref[:, row]
+        ref[1 : VX + 1] = own_ref[:, row]
+        ref[pl.ds((VX + 1) * core, 1)] = far_ref[:, row] * inside
+
+
+def assemble(spot_ref, wide_ref, own_ref, near_ref, far_ref, even_ref, odd_ref):
     core = spot_ref[0] % 2
+    turn = spot_ref[0] // 4 % 2
 
     def put(x, y, block, inside=None):
         nx, ny = block.shape[0], block.shape[1]
@@ -203,26 +206,26 @@
         down = jnp.where(z == 0, 0.0, down)
         up = jnp.where(z == Z - 1, 0.0, up)
         shape = (nx, ny, Z, C)
-        planes = pl.ds(x, nx)
-        wide_ref[planes, y : y + ny, :, 0:C] = down.astype(BF).reshape(shape)
-        wide_ref[planes, y : y + ny, :, C : 2 * C] = block
-        wide_ref[planes, y : y + ny, :, 2 * C :] = up.astype(BF).reshape(shape)
+        planes, rows = pl.ds(x, nx), pl.ds(y, ny)
+        wide_ref[planes, rows, :, 0:C] = down.astype(BF).reshape(shape)
+        wide_ref[planes, rows, :, C : 2 * C] = block
+        wide_ref[planes, rows, :, 2 * C :] = up.astype(BF).reshape(shape)
 
     put(1, 1, own_ref[...])
     put((VX + 1) * (1 - core), 1, near_ref[...])
     put((VX + 1) * core, 1, far_ref[...], 1)
-    put(0, 0, ylo_ref[...], 2)
-    put(0, VY + 1, yhi_ref[...], 3)
+    put(0, (VY + 1) * (1 - turn), even_ref[...])
+    put(0, (VY + 1) * turn, odd_ref[...], 3)
 
 
 def window(wide_ref, x, y):
     return wide_ref[x : x + VX, y : y + VY, :, :].reshape(CELLS, 3 * C)
 
 
-def conv_kernel(spot_ref, vox_ref, near_ref, far_ref, ylo_ref, yhi_ref, weight_ref, gout_ref,
+def conv_kernel(spot_ref, vox_ref, near_ref, far_ref, even_ref, odd_ref, weight_ref, gout_ref,
                 mlp_ref, keep_ref, send_ref, act_ref, hid_ref, in_ref, out_ref, wide_ref, all_ref):
     core = spot_ref[0] % 2
-    assemble(spot_ref, wide_ref, vox_ref, near_ref, far_ref, ylo_ref, yhi_ref)
+    assemble(spot_ref, wide_ref, vox_ref, near_ref, far_ref, even_ref, odd_ref)
     hidden = jnp.zeros((CELLS, C), F32)
     for k in range(9):
         taps = weight_ref[3 * k : 3 * k + 3].reshape(3 * C, C)
@@ -258,8 +261,8 @@
     out_ref[...] = jnp.broadcast_to(total.astype(BF)[None], out_ref.shape)
 
 
-def back_kernel(spot_ref, hid_ref, near_ref, far_ref, ylo_ref, yhi_ref, weight_ref, meta_ref, div_ref, out_ref, wide_ref):
-    assemble(spot_ref, wide_ref, hid_ref, near_ref, far_ref, ylo_ref, yhi_ref)
+def back_kernel(spot_ref, hid_ref, near_ref, far_ref, even_ref, odd_ref, weight_ref, meta_ref, div_ref, out_ref, wide_ref):
+    assemble(spot_ref, wide_ref, hid_ref, near_ref, far_ref, even_ref, odd_ref)
     total = jnp.zeros((CELLS, C), F32)
     for k in range(9):
         taps = jnp.concatenate([weight_ref[3 * k + 2 - j] for j in range(3)], axis=1)
@@ -323,16 +326,23 @@
 EDGE = sds((VX + 2, 1, Z, C), BF)
 
 
+def pairs(count, start):
+    swaps = [(i, (i + 1) % count) for i in range(start, count, 2)]
+    return swaps + [(j, i) for i, j in swaps]
+
+
 def chips(face):
-    pairs = [(i, (i + 1) % GX) for i in range(1, GX, 2)]
-    return lax.ppermute(face, ("y", "c"), pairs + [(j, i) for i, j in pairs])
-
-
-def edges(core, near, cells, far):
-    tail, head = call(edge_kernel, (EDGE, EDGE), (core, near, cells, far), smem=1, mib=2)
-    up = [(i, (i + 1) % GY) for i in range(GY)]
-    down = [((i + 1) % GY, i) for i in range(GY)]
-    return lax.ppermute(tail, ("x", "z"), up), lax.ppermute(head, ("x", "z"), down)
+    return lax.ppermute(face, ("y", "c"), pairs(GX, 1))
+
+
+def edges(spot, near, cells, far):
+    even, odd = call(edge_kernel, (EDGE, EDGE), (spot, near, cells, far), smem=1, mib=2)
+    odds = [(s * GY + i, s * GY + j) for s in range(GX) for i, j in pairs(GY, 1) if abs(i - j) == 1]
+    ends = [(s * GY + i, (s ^ 1) * GY + i) for s in range(GX) for i in (0, GY - 1)]
+    return (
+        lax.ppermute(even, ("x", "z"), pairs(GY, 0)),
+        lax.ppermute(odd, ("y", "c", "x", "z"), odds + ends),
+    )
 
 
 def exchange(rows):
@@ -347,7 +357,7 @@
     strip = lax.axis_index(("y", "c"))
     slab_here = lax.axis_index(("x", "z"))
     core = lax.axis_index("c")
-    core = core + 2 * (strip % (GX - 1) != 0) + 4 * (slab_here != 0) + 8 * (slab_here != GY - 1)
+    core = core + 2 * (strip % (GX - 1) != 0) + 4 * (slab_here % 2) + 8 * (slab_here % (GY - 1) != 0)
     spot = core.reshape(1)
     point_slab, spot = lax.optimization_barrier((point_slab, spot))
     slab = point_slab.reshape(1, PTS)

time: 133 us -> 130 us (0.977)
  starting transfers between devices: 57.7 us -> 52.7 us
  waiting for transfers between devices: 57.4 us -> 58.9 us
    ppermute x6, starting transfers between devices: 11.4 us -> 7.47 us  [the longest x2 3.1 us: edges(): lax.ppermute(even, ('x', 'z'), pairs(GY, 0))]
  transfers between devices with their start and end apart: 14 -> 14, of which waited for: 11 -> 10; matrix products, arithmetic and copies ran while one was open for 0% -> 0% of each run, Pallas kernels for 5% -> 5%
where the time goes in v5:
time: 130 us; the launch traced here: 129 us
  waiting for transfers between devices  58.9 us (45%)
  starting transfers between devices  52.7 us (41%)
  Pallas kernels  16.8 us (13%)
    all_to_all x3, waiting for transfers between devices, exchange(): lax.all_to_all(rows, ('x', 'z'), split_axis=0, concat_axis=0, tiled=True)  38.1 us
    all_to_all x3, starting transfers between devices, exchange(): lax.all_to_all(rows, ('x', 'z'), split_axis=0, concat_axis=0, tiled=True)  26.7 us
    pallas_call x16, Pallas kernels, call(): pl.pallas_call(kernel, out_shape=out_shape, in_specs=[SMEM] * smem + [HBM...  16.8 us
    ppermute x4, starting transfers between devices, swap(): return lax.ppermute(half, 'c', [(0, 1), (1, 0)])  15.1 us
    ppermute x2, waiting for transfers between devices, edges(): lax.ppermute(even, ('x', 'z'), pairs(GY, 0))  12 us
    ppermute x2, waiting for transfers between devices, chips(): return lax.ppermute(face, ('y', 'c'), pairs(GX, 1))  4.53 us
    all_to_all x1, starting transfers between devices, body(): lax.all_to_all(shares, 'y', split_axis=0, concat_axis=0, tiled=True)  3.46 us
    ppermute x2, starting transfers between devices, edges(): lax.ppermute(even, ('x', 'z'), pairs(GY, 0))  3.1 us
  transfers between devices with their start and end apart: 14, of which 10 were waited for; matrix products, arithmetic and copies ran while one was open for 0% of the time, Pallas kernels for 5%

profile of v5, /device:TPU:1, one launch (start us, length us, event | category | flops | bytes accessed | tf_op | source)
XLA Modules:
  0.0 129.3 jit_solution(2754229475852596381)
XLA Ops:
  0.7 3.0 %shard_map.111 = bf16[32,104,128]{2,1,0:T(8,128)(2,1)} custom-call(bf16[512,128]{1,0:T(8,128)(2,1)} %feat_ref.3, bf16[512,128]{1,0:T(8,128)(2,1)} %cot_ref.3, s32[1,512]{1,0:T(1,128)} %bitcast.4, s32[1,512]{1,0:T(1,128)} %bitcast.6, s32[1,512]{1,0:T(1,128)} %bitcast.7, bf16[3,512]{1,0:T(4,128)(2,1)} %off_hbm.1), custom_call_target="tpu_custom_call" | custom-call | tf_op jit(solution)/shard_map/pallas_call | solution.py:38
  3.7 12.0 %all-to-all-start = ((bf16[32,104,128]{2,1,0:T(8,128)(2,1)}), bf16[32,104,128]{2,1,0:T(8,128)(2,1)S(1)}, u32[]{:S(2)}, u32[]{:S(2)}) async-start(bf16[32,104,128]{2,1,0:T(8,128)(2,1)} %shard_map.111), calls=%async_computation | async-start | bytes 1703936 | tf_op jit(solution)/shard_map/all_to_all | solution.py:349
  16.2 19.9 %all-to-all-done.got_ref = bf16[32,104,128]{2,1,0:T(8,128)(2,1)S(1)} async-done(((bf16[32,104,128]{2,1,0:T(8,128)(2,1)}), bf16[32,104,128]{2,1,0:T(8,128)(2,1)S(1)}, u32[]{:S(2)}, u32[]{:S(2)}) %all-to-all-start) | async-done | bytes 852000 | tf_op jit(solution)/shard_map/all_to_all | solution.py:349
  36.8 5.5 %collective-permute-start = (bf16[1,8,16,128]{3,2,1,0:T(8,128)(2,1)S(1)}, bf16[1,8,16,128]{3,2,1,0:T(8,128)(2,1)S(1)}, u32[]{:S(2)}, u32[]{:S(2)}) collective-permute-start(bf16[1,8,16,128]{3,2,1,0:T(8,128)(2,1)S(1)} %get-tuple-element.41), channel_id=1, source_target_pairs={{0,32},{32,0},{1,33},{33,1},{2,34},{34,2},{3,35},{35,3},{4,36},{36... | collective-permute-start | bytes 98312 | tf_op jit(solution)/shard_map/ppermute | solution.py:353
  42.2 1.3 collective-permute-start.1
  43.5 2.1 %collective-permute-done.1.far_ref = bf16[1,8,16,128]{3,2,1,0:T(8,128)(2,1)S(1)} collective-permute-done((bf16[1,8,16,128]{3,2,1,0:T(8,128)(2,1)S(1)}, bf16[1,8,16,128]{3,2,1,0:T(8,128)(2,1)S(1)}, u32[]{:S(2)}, u32[]{:S(2)}) %collective-permute-start.1) | collective-permute-done | bytes 32800 | tf_op jit(solution)/shard_map/ppermute | solution.py:335
  45.6 1.3 %collective-permute-start.2 = (bf16[6,1,16,128]{3,2,1,0:T(8,128)(2,1)S(1)}, bf16[6,1,16,128]{3,2,1,0:T(8,128)(2,1)S(1)}, u32[]{:S(2)}, u32[]{:S(2)}) collective-permute-start(bf16[6,1,16,128]{3,2,1,0:T(8,128)(2,1)S(1)} %get-tuple-element.43), channel_id=1, source_target_pairs={{0,1},{2,3},{4,5},{6,7},{8,9},{10,11},{12,13},{14,15},{16,17},{18,... | collective-permute-start | bytes 73736 | tf_op jit(solution)/shard_map/ppermute | solution.py:343
  46.9 1.7 %collective-permute-start.3 = (bf16[6,1,16,128]{3,2,1,0:T(8,128)(2,1)S(1)}, bf16[6,1,16,128]{3,2,1,0:T(8,128)(2,1)S(1)}, u32[]{:S(2)}, u32[]{:S(2)}) collective-permute-start(bf16[6,1,16,128]{3,2,1,0:T(8,128)(2,1)S(1)} %get-tuple-element.44), channel_id=1, source_target_pairs={{1,2},{3,4},{5,6},{7,8},{9,10},{11,12},{13,14},{15,16},{17,18},{19... | collective-permute-start | bytes 73736 | tf_op jit(solution)/shard_map/ppermute | solution.py:344
  49.4 2.4 %shard_map.116 = (f32[14,128,128]{2,1,0:T(8,128)S(1)}, bf16[14,128,128]{2,1,0:T(8,128)(2,1)S(1)}, bf16[512,128]{1,0:T(8,128)(2,1)S(1)}, bf16[4,8,16,128]{3,2,1,0...) custom-call(s32[1]{0:T(128)} %bitcast.spot_ref, ...), custom_call_target="tpu_custom_call" | custom-call | tf_op jit(solution)/shard_map/pallas_call | solution.py:38
  51.8 1.5 %collective-permute-start.4 = (bf16[14,128,128]{2,1,0:T(8,128)(2,1)S(1)}, bf16[14,128,128]{2,1,0:T(8,128)(2,1)S(1)}, u32[]{:S(2)}, u32[]{:S(2)}) collective-permute-start(bf16[14,128,128]{2,1,0:T(8,128)(2,1)S(1)} %get-tuple-element.49), channel_id=1, source_target_pairs={{0,32},{32,0},{1,33},{33,1},{2,34},{34,2},{3,35},{35,3},{4,36},{36... | collective-permute-start | bytes 1376264 | tf_op jit(solution)/shard_map/ppermute | solution.py:353
  55.8 6.6 %all-to-all-start.1 = ((bf16[32,104,128]{2,1,0:T(8,128)(2,1)}), bf16[32,104,128]{2,1,0:T(8,128)(2,1)S(1)}, u32[]{:S(2)}, u32[]{:S(2)}) async-start(bf16[32,104,128]{2,1,0:T(8,128)(2,1)} %shard_map.118), calls=%async_computation.1 | async-start | bytes 1703936 | tf_op jit(solution)/shard_map/all_to_all | solution.py:349
  64.0 2.5 %collective-permute-done.6.far_ref = bf16[1,8,16,128]{3,2,1,0:T(8,128)(2,1)S(1)} collective-permute-done((bf16[1,8,16,128]{3,2,1,0:T(8,128)(2,1)S(1)}, bf16[1,8,16,128]{3,2,1,0:T(8,128)(2,1)S(1)}, u32[]{:S(2)}, u32[]{:S(2)}) %collective-permute-start.6) | collective-permute-done | bytes 32800 | tf_op jit(solution)/shard_map/ppermute | solution.py:335
  66.5 1.8 %collective-permute-start.7 = (bf16[6,1,16,128]{3,2,1,0:T(8,128)(2,1)S(1)}, bf16[6,1,16,128]{3,2,1,0:T(8,128)(2,1)S(1)}, u32[]{:S(2)}, u32[]{:S(2)}) collective-permute-start(bf16[6,1,16,128]{3,2,1,0:T(8,128)(2,1)S(1)} %get-tuple-element.55), channel_id=1, source_target_pairs={{0,1},{2,3},{4,5},{6,7},{8,9},{10,11},{12,13},{14,15},{16,17},{18,... | collective-permute-start | bytes 73736 | tf_op jit(solution)/shard_map/ppermute | solution.py:343
  68.3 1.4 %collective-permute-start.8 = (bf16[6,1,16,128]{3,2,1,0:T(8,128)(2,1)S(1)}, bf16[6,1,16,128]{3,2,1,0:T(8,128)(2,1)S(1)}, u32[]{:S(2)}, u32[]{:S(2)}) collective-permute-start(bf16[6,1,16,128]{3,2,1,0:T(8,128)(2,1)S(1)} %get-tuple-element.56), channel_id=1, source_target_pairs={{1,2},{3,4},{5,6},{7,8},{9,10},{11,12},{13,14},{15,16},{17,18},{19... | collective-permute-start | bytes 73736 | tf_op jit(solution)/shard_map/ppermute | solution.py:344
  69.7 12.0 %collective-permute-done.7.even_ref = bf16[6,1,16,128]{3,2,1,0:T(8,128)(2,1)S(1)} collective-permute-done((bf16[6,1,16,128]{3,2,1,0:T(8,128)(2,1)S(1)}, bf16[6,1,16,128]{3,2,1,0:T(8,128)(2,1)S(1)}, u32[]{:S(2)}, u32[]{:S(2)}) %collective-permute-start.7) | collective-permute-done | bytes 24608 | tf_op jit(solution)/shard_map/ppermute | solution.py:343
  81.7 1.7 %all-to-all-done.1.got_ref = bf16[32,104,128]{2,1,0:T(8,128)(2,1)S(1)} async-done(((bf16[32,104,128]{2,1,0:T(8,128)(2,1)}), bf16[32,104,128]{2,1,0:T(8,128)(2,1)S(1)}, u32[]{:S(2)}, u32[]{:S(2)}) %all-to-all-start.1) | async-done | bytes 852000 | tf_op jit(solution)/shard_map/all_to_all | solution.py:349
  84.0 3.5 %all-to-all-start.2 = ((bf16[4,56,128]{2,1,0:T(8,128)(2,1)}), bf16[4,56,128]{2,1,0:T(8,128)(2,1)S(1)}, u32[]{:S(2)}, u32[]{:S(2)}) async-start(bf16[4,56,128]{2,1,0:T(8,128)(2,1)} %shard_map.121), calls=%async_computation.2 | async-start | bytes 114688 | tf_op jit(solution)/shard_map/all_to_all | solution.py:423
  87.5 1.9 %shard_map.122.filled_ref = bf16[32,48,128]{2,1,0:T(8,128)(2,1)S(1)} custom-call(s32[1]{0:T(128)} %bitcast.spot_ref, bf16[4,8,16,128]{3,2,1,0:T(8,128)(2,1)S(1)} %get-tuple-element.54.own_ref.hid_ref, bf16[1,8,16,128]{3,2,1,0:T(8,128)(2,1)S(1)} %collective-permute-done.5.near_ref, bf16[1,8,16,128]{3,2,1,0:T(8,128)(2,1)S(1)} %collective-permute-done.6.far_ref, ...), custom_call_target="tpu_custom_call" | custom-call | tf_op jit(solution)/shard_map/pallas_call | solution.py:38
  89.4 2.3 %all-to-all-done.2.got_ref = bf16[4,56,128]{2,1,0:T(8,128)(2,1)S(1)} async-done(((bf16[4,56,128]{2,1,0:T(8,128)(2,1)}), bf16[4,56,128]{2,1,0:T(8,128)(2,1)S(1)}, u32[]{:S(2)}, u32[]{:S(2)}) %all-to-all-start.2) | async-done | bytes 57376 | tf_op jit(solution)/shard_map/all_to_all | solution.py:423
  92.7 8.1 %all-to-all-start.3 = ((bf16[32,104,128]{2,1,0:T(8,128)(2,1)}), bf16[32,104,128]{2,1,0:T(8,128)(2,1)S(1)}, u32[]{:S(2)}, u32[]{:S(2)}) async-start(bf16[32,104,128]{2,1,0:T(8,128)(2,1)} %shard_map.123), calls=%async_computation.3 | async-start | bytes 1703936 | tf_op jit(solution)/shard_map/all_to_all | solution.py:349
  100.8 1.5 %shard_map.120 = (bf16[512,128]{1,0:T(8,128)(2,1)}, s32[512,128]{1,0:T(8,128)S(1)}, f32[512,128]{1,0:T(8,128)S(1)}) custom-call(bf16[32,104,128]{2,1,0:T(8,128)(2,1)S(1)} %all-to-all-done.1.got_ref, s32[1,512]{1,0:T(1,128)S(1)} %bitcast.5, bf16[512,128]{1,0:T(8,128)(2,1)S(1)} %copy-done.1, bf16[512,128]{1,0:T(8,128)(2,1)S(1)} %copy-done.2, ...), custom_call_target="tpu_custom_call" | custom-call | tf_op jit(solution)/shard_map/pallas_call | solution.py:38
  102.4 16.6 %all-to-all-done.3.got_ref = bf16[32,104,128]{2,1,0:T(8,128)(2,1)S(1)} async-done(((bf16[32,104,128]{2,1,0:T(8,128)(2,1)}), bf16[32,104,128]{2,1,0:T(8,128)(2,1)S(1)}, u32[]{:S(2)}, u32[]{:S(2)}) %all-to-all-start.3) | async-done | bytes 852000 | tf_op jit(solution)/shard_map/all_to_all | solution.py:349
  119.0 7.4 %collective-permute-start.9 = (bf16[14,128,128]{2,1,0:T(8,128)(2,1)S(1)}, bf16[14,128,128]{2,1,0:T(8,128)(2,1)S(1)}, u32[]{:S(2)}, u32[]{:S(2)}) collective-permute-start(bf16[14,128,128]{2,1,0:T(8,128)(2,1)S(1)} %shard_map.125.mine_ref), channel_id=1, source_target_pairs={{0,32},{32,0},{1,33},{33,1},{2,34},{34,2},{3,35},{35,3},{4,36},{36... | collective-permute-start | bytes 1376264 | tf_op jit(solution)/shard_map/ppermute | solution.py:353
  127.8 1.5 %shard_map.126 = (f32[27,128,128]{2,1,0:T(8,128)}, f32[128,128]{1,0:T(8,128)}) custom-call(s32[1]{0:T(128)} %bitcast.spot_ref, bf16[14,128,128]{2,1,0:T(8,128)(2,1)S(1)} %shard_map.125.mine_ref, bf16[14,128,128]{2,1,0:T(8,128)(2,1)S(1)} %collective-permute-done.9.other_ref), custom_call_target="tpu_custom_call" | custom-call | tf_op jit(solution)/shard_map/pallas_call | solution.py:38
  (30 shorter events, 9.2 us)
Async XLA Ops:
  0.6 15.1 %copy-start.2 = (bf16[512,128]{1,0:T(8,128)(2,1)S(1)}, bf16[512,128]{1,0:T(8,128)(2,1)}, u32[]{:S(2)}) copy-start(bf16[512,128]{1,0:T(8,128)(2,1)} %cot_ref.3) | copy-start | bytes 393220
  0.6 15.1 %copy-start.1 = (bf16[512,128]{1,0:T(8,128)(2,1)S(1)}, bf16[512,128]{1,0:T(8,128)(2,1)}, u32[]{:S(2)}) copy-start(bf16[512,128]{1,0:T(8,128)(2,1)} %feat_ref.3) | copy-start | bytes 393220
  0.7 15.1 %copy-start.3 = (bf16[128,128]{1,0:T(8,128)(2,1)S(1)}, bf16[128,128]{1,0:T(8,128)(2,1)}, u32[]{:S(2)}) copy-start(bf16[128,128]{1,0:T(8,128)(2,1)} %mlp_ref.3) | copy-start | bytes 98308
  3.7 45.7 %copy-start = (bf16[27,128,128]{2,1,0:T(8,128)(2,1)S(1)}, bf16[27,128,128]{2,1,0:T(8,128)(2,1)}, u32[]{:S(2)}) copy-start(bf16[27,128,128]{2,1,0:T(8,128)(2,1)} %weight_ref.3) | copy-start | bytes 2654212
  3.7 32.4 %all-to-all-start = ((bf16[32,104,128]{2,1,0:T(8,128)(2,1)}), bf16[32,104,128]{2,1,0:T(8,128)(2,1)S(1)}, u32[]{:S(2)}, u32[]{:S(2)}) async-start(bf16[32,104,128]{2,1,0:T(8,128)(2,1)} %shard_map.111), calls=%async_computation | async-start | bytes 1703936 | tf_op jit(solution)/shard_map/all_to_all | solution.py:349
  36.8 6.7 %collective-permute-start = (bf16[1,8,16,128]{3,2,1,0:T(8,128)(2,1)S(1)}, bf16[1,8,16,128]{3,2,1,0:T(8,128)(2,1)S(1)}, u32[]{:S(2)}, u32[]{:S(2)}) collective-permute-start(bf16[1,8,16,128]{3,2,1,0:T(8,128)(2,1)S(1)} %get-tuple-element.41), channel_id=1, source_target_pairs={{0,32},{32,0},{1,33},{33,1},{2,34},{34,2},{3,35},{35,3},{4,36},{36... | collective-permute-start | bytes 98312 | tf_op jit(solution)/shard_map/ppermute | solution.py:353
  42.2 3.3 %collective-permute-start.1 = (bf16[1,8,16,128]{3,2,1,0:T(8,128)(2,1)S(1)}, bf16[1,8,16,128]{3,2,1,0:T(8,128)(2,1)S(1)}, u32[]{:S(2)}, u32[]{:S(2)}) collective-permute-start(bf16[1,8,16,128]{3,2,1,0:T(8,128)(2,1)S(1)} %get-tuple-element.42), channel_id=1, source_target_pairs={{32,64},{96,128},{160,192},{224,0},{64,32},{128,96},{192,160},{0,2... | collective-permute-start | bytes 98312 | tf_op jit(solution)/shard_map/ppermute | solution.py:335
  45.6 3.8 %collective-permute-start.2 = (bf16[6,1,16,128]{3,2,1,0:T(8,128)(2,1)S(1)}, bf16[6,1,16,128]{3,2,1,0:T(8,128)(2,1)S(1)}, u32[]{:S(2)}, u32[]{:S(2)}) collective-permute-start(bf16[6,1,16,128]{3,2,1,0:T(8,128)(2,1)S(1)} %get-tuple-element.43), channel_id=1, source_target_pairs={{0,1},{2,3},{4,5},{6,7},{8,9},{10,11},{12,13},{14,15},{16,17},{18,... | collective-permute-start | bytes 73736 | tf_op jit(solution)/shard_map/ppermute | solution.py:343
  46.9 2.5 %collective-permute-start.3 = (bf16[6,1,16,128]{3,2,1,0:T(8,128)(2,1)S(1)}, bf16[6,1,16,128]{3,2,1,0:T(8,128)(2,1)S(1)}, u32[]{:S(2)}, u32[]{:S(2)}) collective-permute-start(bf16[6,1,16,128]{3,2,1,0:T(8,128)(2,1)S(1)} %get-tuple-element.44), channel_id=1, source_target_pairs={{1,2},{3,4},{5,6},{7,8},{9,10},{11,12},{13,14},{15,16},{17,18},{19... | collective-permute-start | bytes 73736 | tf_op jit(solution)/shard_map/ppermute | solution.py:344
  51.8 3.0 %collective-permute-start.4 = (bf16[14,128,128]{2,1,0:T(8,128)(2,1)S(1)}, bf16[14,128,128]{2,1,0:T(8,128)(2,1)S(1)}, u32[]{:S(2)}, u32[]{:S(2)}) collective-permute-start(bf16[14,128,128]{2,1,0:T(8,128)(2,1)S(1)} %get-tuple-element.49), channel_id=1, source_target_pairs={{0,32},{32,0},{1,33},{33,1},{2,34},{34,2},{3,35},{35,3},{4,36},{36... | collective-permute-start | bytes 1376264 | tf_op jit(solution)/shard_map/ppermute | solution.py:353
  55.8 27.5 %all-to-all-start.1 = ((bf16[32,104,128]{2,1,0:T(8,128)(2,1)}), bf16[32,104,128]{2,1,0:T(8,128)(2,1)S(1)}, u32[]{:S(2)}, u32[]{:S(2)}) async-start(bf16[32,104,128]{2,1,0:T(8,128)(2,1)} %shard_map.118), calls=%async_computation.1 | async-start | bytes 1703936 | tf_op jit(solution)/shard_map/all_to_all | solution.py:349
  62.4 1.6 %collective-permute-start.5 = (bf16[1,8,16,128]{3,2,1,0:T(8,128)(2,1)S(1)}, bf16[1,8,16,128]{3,2,1,0:T(8,128)(2,1)S(1)}, u32[]{:S(2)}, u32[]{:S(2)}) collective-permute-start(bf16[1,8,16,128]{3,2,1,0:T(8,128)(2,1)S(1)} %get-tuple-element.52), channel_id=1, source_target_pairs={{0,32},{32,0},{1,33},{33,1},{2,34},{34,2},{3,35},{35,3},{4,36},{36... | collective-permute-start | bytes 98312 | tf_op jit(solution)/shard_map/ppermute | solution.py:353
  63.1 3.3 %collective-permute-start.6 = (bf16[1,8,16,128]{3,2,1,0:T(8,128)(2,1)S(1)}, bf16[1,8,16,128]{3,2,1,0:T(8,128)(2,1)S(1)}, u32[]{:S(2)}, u32[]{:S(2)}) collective-permute-start(bf16[1,8,16,128]{3,2,1,0:T(8,128)(2,1)S(1)} %get-tuple-element.53), channel_id=1, source_target_pairs={{32,64},{96,128},{160,192},{224,0},{64,32},{128,96},{192,160},{0,2... | collective-permute-start | bytes 98312 | tf_op jit(solution)/shard_map/ppermute | solution.py:335
  66.5 15.2 %collective-permute-start.7 = (bf16[6,1,16,128]{3,2,1,0:T(8,128)(2,1)S(1)}, bf16[6,1,16,128]{3,2,1,0:T(8,128)(2,1)S(1)}, u32[]{:S(2)}, u32[]{:S(2)}) collective-permute-start(bf16[6,1,16,128]{3,2,1,0:T(8,128)(2,1)S(1)} %get-tuple-element.55), channel_id=1, source_target_pairs={{0,1},{2,3},{4,5},{6,7},{8,9},{10,11},{12,13},{14,15},{16,17},{18,... | collective-permute-start | bytes 73736 | tf_op jit(solution)/shard_map/ppermute | solution.py:343
  68.3 13.4 %collective-permute-start.8 = (bf16[6,1,16,128]{3,2,1,0:T(8,128)(2,1)S(1)}, bf16[6,1,16,128]{3,2,1,0:T(8,128)(2,1)S(1)}, u32[]{:S(2)}, u32[]{:S(2)}) collective-permute-start(bf16[6,1,16,128]{3,2,1,0:T(8,128)(2,1)S(1)} %get-tuple-element.56), channel_id=1, source_target_pairs={{1,2},{3,4},{5,6},{7,8},{9,10},{11,12},{13,14},{15,16},{17,18},{19... | collective-permute-start | bytes 73736 | tf_op jit(solution)/shard_map/ppermute | solution.py:344
  84.0 7.7 %all-to-all-start.2 = ((bf16[4,56,128]{2,1,0:T(8,128)(2,1)}), bf16[4,56,128]{2,1,0:T(8,128)(2,1)S(1)}, u32[]{:S(2)}, u32[]{:S(2)}) async-start(bf16[4,56,128]{2,1,0:T(8,128)(2,1)} %shard_map.121), calls=%async_computation.2 | async-start | bytes 114688 | tf_op jit(solution)/shard_map/all_to_all | solution.py:423
  89.4 11.4 %copy-start.4 = (s32[512,1]{0,1:T(1,128)S(1)}, s32[512,1]{0,1:T(1,128)}, u32[]{:S(2)}) copy-start(s32[512,1]{0,1:T(1,128)} %param.9) | copy-start | bytes 6148
  92.7 26.2 %all-to-all-start.3 = ((bf16[32,104,128]{2,1,0:T(8,128)(2,1)}), bf16[32,104,128]{2,1,0:T(8,128)(2,1)S(1)}, u32[]{:S(2)}, u32[]{:S(2)}) async-start(bf16[32,104,128]{2,1,0:T(8,128)(2,1)} %shard_map.123), calls=%async_computation.3 | async-start | bytes 1703936 | tf_op jit(solution)/shard_map/all_to_all | solution.py:349
  119.0 8.8 %collective-permute-start.9 = (bf16[14,128,128]{2,1,0:T(8,128)(2,1)S(1)}, bf16[14,128,128]{2,1,0:T(8,128)(2,1)S(1)}, u32[]{:S(2)}, u32[]{:S(2)}) collective-permute-start(bf16[14,128,128]{2,1,0:T(8,128)(2,1)S(1)} %shard_map.125.mine_ref), channel_id=1, source_target_pairs={{0,32},{32,0},{1,33},{33,1},{2,34},{34,2},{3,35},{35,3},{4,36},{36... | collective-permute-start | bytes 1376264 | tf_op jit(solution)/shard_map/ppermute | solution.py:353

commit v6 on v5

--- a/solution.py
+++ b/solution.py
@@ -257,8 +257,11 @@
 
 
 def share_kernel(got_ref, out_ref):
-    total = jnp.sum(got_ref[:, CAP:, :].astype(F32), axis=0)
-    out_ref[...] = jnp.broadcast_to(total.astype(BF)[None], out_ref.shape)
+    out_ref[...] = jnp.sum(got_ref[:, CAP:, :].astype(F32), axis=0).astype(BF)
+
+
+def pair_kernel(own_ref, got_ref, out_ref):
+    out_ref[...] = own_ref[...].astype(F32) + got_ref[...].astype(F32)
 
 
 def back_kernel(spot_ref, hid_ref, near_ref, far_ref, even_ref, odd_ref, weight_ref, meta_ref, div_ref, out_ref, wide_ref):
@@ -271,9 +274,9 @@
     out_ref[...] = dot(own_matrix(meta_ref[...]), mean, LEFT).astype(BF).reshape(GY, CAP, C)
 
 
-def spread_share_kernel(got_ref, filled_ref, out_ref):
-    total = jnp.sum(got_ref[...].astype(F32), axis=0)
-    out_ref[:, CAP:, :] = jnp.broadcast_to(total.astype(BF)[None], (GY, SHARE, C))
+def deal_kernel(own_ref, got_ref, filled_ref, out_ref):
+    total = (own_ref[...] + got_ref[...]).astype(BF)
+    out_ref[:, CAP:, :] = jnp.broadcast_to(total[None], (GY, SHARE, C))
     out_ref[:, 0:CAP, :] = filled_ref[...]
 
 
@@ -347,6 +350,10 @@
 
 def exchange(rows):
     return lax.all_to_all(rows, ("x", "z"), split_axis=0, concat_axis=0, tiled=True)
+
+
+def across(share, partner):
+    return lax.ppermute(share, "y", list(enumerate(partner)))
 
 
 def swap(half):
@@ -419,9 +426,9 @@
         scratch=(wide,),
         smem=1,
     )
-    shares = call(share_kernel, sds((4, SHARE, C), BF), (first,), mib=4)
-    shares = lax.all_to_all(shares, "y", split_axis=0, concat_axis=0, tiled=True)
-    joined = call(spread_share_kernel, block, (shares, filled))
+    share = call(share_kernel, sds((SHARE, C), BF), (first,), mib=4)
+    pair = call(pair_kernel, sds((SHARE, C), F32), (share, across(share, (1, 0, 3, 2))), mib=1)
+    joined = call(deal_kernel, block, (pair, across(pair, (3, 2, 1, 0)), filled))
     second = exchange(joined)
     output, position, back = call(
         forward_kernel,

time: 130 us -> 128 us (0.985)
    ppermute x0 -> x2, waiting for transfers between devices: none -> 3.46 us  [across(): return lax.ppermute(share, 'y', list(enumerate(partner)))]
    all_to_all x1 -> x0, starting transfers between devices: 3.46 us -> none  [body(): lax.all_to_all(shares, 'y', split_axis=0, concat_axis=0, tiled=True)]
    all_to_all x1 -> x0, waiting for transfers between devices: 2.33 us -> none  [body(): lax.all_to_all(shares, 'y', split_axis=0, concat_axis=0, tiled=True)]
    ppermute x0 -> x2, starting transfers between devices: none -> 1.71 us  [across(): return lax.ppermute(share, 'y', list(enumerate(partner)))]
    pallas_call x16 -> x17, Pallas kernels: 16.8 us -> 16.2 us  [call(): pl.pallas_call(kernel, out_shape=out_shape, in_specs=[SMEM] * smem + [HBM...]
  transfers between devices with their start and end apart: 14 -> 15, of which waited for: 10 -> 11; matrix products, arithmetic and copies ran while one was open for 0% -> 0% of each run, Pallas kernels for 5% -> 5%
where the time goes in v6:
time: 128 us
  waiting for transfers between devices  58.7 us (46%)
  starting transfers between devices  51.8 us (40%)
  Pallas kernels  16.2 us (13%)
    all_to_all x3, waiting for transfers between devices, exchange(): lax.all_to_all(rows, ('x', 'z'), split_axis=0, concat_axis=0, tiled=True)  36.9 us
    all_to_all x3, starting transfers between devices, exchange(): lax.all_to_all(rows, ('x', 'z'), split_axis=0, concat_axis=0, tiled=True)  26.4 us
    pallas_call x17, Pallas kernels, call(): pl.pallas_call(kernel, out_shape=out_shape, in_specs=[SMEM] * smem + [HBM...  16.2 us
    ppermute x4, starting transfers between devices, swap(): return lax.ppermute(half, 'c', [(0, 1), (1, 0)])  16.2 us
    ppermute x2, waiting for transfers between devices, edges(): lax.ppermute(even, ('x', 'z'), pairs(GY, 0))  12 us
    ppermute x2, waiting for transfers between devices, chips(): return lax.ppermute(face, ('y', 'c'), pairs(GX, 1))  4.53 us
    ppermute x2, waiting for transfers between devices, across(): return lax.ppermute(share, 'y', list(enumerate(partner)))  3.46 us
    ppermute x2, starting transfers between devices, edges(): lax.ppermute(even, ('x', 'z'), pairs(GY, 0))  3.1 us
  transfers between devices with their start and end apart: 15, of which 11 were waited for; matrix products, arithmetic and copies ran while one was open for 0% of the time, Pallas kernels for 5%

profile of v6, /device:TPU:1, one launch (start us, length us, event | category | flops | bytes accessed | tf_op | source)
XLA Modules:
  0.0 127.6 jit_solution(17672699235081295391)
XLA Ops:
  0.7 3.0 %shard_map.111 = bf16[32,104,128]{2,1,0:T(8,128)(2,1)} custom-call(bf16[512,128]{1,0:T(8,128)(2,1)} %feat_ref.3, bf16[512,128]{1,0:T(8,128)(2,1)} %cot_ref.3, s32[1,512]{1,0:T(1,128)} %bitcast.4, s32[1,512]{1,0:T(1,128)} %bitcast.6, s32[1,512]{1,0:T(1,128)} %bitcast.7, bf16[3,512]{1,0:T(4,128)(2,1)} %off_hbm.1), custom_call_target="tpu_custom_call" | custom-call | tf_op jit(solution)/shard_map/pallas_call | solution.py:38
  3.7 12.0 %all-to-all-start = ((bf16[32,104,128]{2,1,0:T(8,128)(2,1)}), bf16[32,104,128]{2,1,0:T(8,128)(2,1)S(1)}, u32[]{:S(2)}, u32[]{:S(2)}) async-start(bf16[32,104,128]{2,1,0:T(8,128)(2,1)} %shard_map.111), calls=%async_computation | async-start | bytes 1703936 | tf_op jit(solution)/shard_map/all_to_all | solution.py:352
  16.2 19.9 %all-to-all-done.got_ref = bf16[32,104,128]{2,1,0:T(8,128)(2,1)S(1)} async-done(((bf16[32,104,128]{2,1,0:T(8,128)(2,1)}), bf16[32,104,128]{2,1,0:T(8,128)(2,1)S(1)}, u32[]{:S(2)}, u32[]{:S(2)}) %all-to-all-start) | async-done | bytes 852000 | tf_op jit(solution)/shard_map/all_to_all | solution.py:352
  36.8 5.5 %collective-permute-start = (bf16[1,8,16,128]{3,2,1,0:T(8,128)(2,1)S(1)}, bf16[1,8,16,128]{3,2,1,0:T(8,128)(2,1)S(1)}, u32[]{:S(2)}, u32[]{:S(2)}) collective-permute-start(bf16[1,8,16,128]{3,2,1,0:T(8,128)(2,1)S(1)} %get-tuple-element.41), channel_id=1, source_target_pairs={{0,32},{32,0},{1,33},{33,1},{2,34},{34,2},{3,35},{35,3},{4,36},{36... | collective-permute-start | bytes 98312 | tf_op jit(solution)/shard_map/ppermute | solution.py:360
  42.2 1.3 %collective-permute-start.1 = (bf16[1,8,16,128]{3,2,1,0:T(8,128)(2,1)S(1)}, bf16[1,8,16,128]{3,2,1,0:T(8,128)(2,1)S(1)}, u32[]{:S(2)}, u32[]{:S(2)}) collective-permute-start(bf16[1,8,16,128]{3,2,1,0:T(8,128)(2,1)S(1)} %get-tuple-element.42), channel_id=1, source_target_pairs={{32,64},{96,128},{160,192},{224,0},{64,32},{128,96},{192,160},{0,2... | collective-permute-start | bytes 98312 | tf_op jit(solution)/shard_map/ppermute | solution.py:338
  43.5 2.1 %collective-permute-done.1.far_ref = bf16[1,8,16,128]{3,2,1,0:T(8,128)(2,1)S(1)} collective-permute-done((bf16[1,8,16,128]{3,2,1,0:T(8,128)(2,1)S(1)}, bf16[1,8,16,128]{3,2,1,0:T(8,128)(2,1)S(1)}, u32[]{:S(2)}, u32[]{:S(2)}) %collective-permute-start.1) | collective-permute-done | bytes 32800 | tf_op jit(solution)/shard_map/ppermute | solution.py:338
  45.6 1.3 %collective-permute-start.2 = (bf16[6,1,16,128]{3,2,1,0:T(8,128)(2,1)S(1)}, bf16[6,1,16,128]{3,2,1,0:T(8,128)(2,1)S(1)}, u32[]{:S(2)}, u32[]{:S(2)}) collective-permute-start(bf16[6,1,16,128]{3,2,1,0:T(8,128)(2,1)S(1)} %get-tuple-element.43), channel_id=1, source_target_pairs={{0,1},{2,3},{4,5},{6,7},{8,9},{10,11},{12,13},{14,15},{16,17},{18,... | collective-permute-start | bytes 73736 | tf_op jit(solution)/shard_map/ppermute | solution.py:346
  46.9 1.7 %collective-permute-start.3 = (bf16[6,1,16,128]{3,2,1,0:T(8,128)(2,1)S(1)}, bf16[6,1,16,128]{3,2,1,0:T(8,128)(2,1)S(1)}, u32[]{:S(2)}, u32[]{:S(2)}) collective-permute-start(bf16[6,1,16,128]{3,2,1,0:T(8,128)(2,1)S(1)} %get-tuple-element.44), channel_id=1, source_target_pairs={{1,2},{3,4},{5,6},{7,8},{9,10},{11,12},{13,14},{15,16},{17,18},{19... | collective-permute-start | bytes 73736 | tf_op jit(solution)/shard_map/ppermute | solution.py:347
  49.4 2.4 %shard_map.116 = (f32[14,128,128]{2,1,0:T(8,128)S(1)}, bf16[14,128,128]{2,1,0:T(8,128)(2,1)S(1)}, bf16[512,128]{1,0:T(8,128)(2,1)S(1)}, bf16[4,8,16,128]{3,2,1,0...) custom-call(s32[1]{0:T(128)} %bitcast.spot_ref, ...), custom_call_target="tpu_custom_call" | custom-call | tf_op jit(solution)/shard_map/pallas_call | solution.py:38
  51.8 1.5 %collective-permute-start.4 = (bf16[14,128,128]{2,1,0:T(8,128)(2,1)S(1)}, bf16[14,128,128]{2,1,0:T(8,128)(2,1)S(1)}, u32[]{:S(2)}, u32[]{:S(2)}) collective-permute-start(bf16[14,128,128]{2,1,0:T(8,128)(2,1)S(1)} %get-tuple-element.49), channel_id=1, source_target_pairs={{0,32},{32,0},{1,33},{33,1},{2,34},{34,2},{3,35},{35,3},{4,36},{36... | collective-permute-start | bytes 1376264 | tf_op jit(solution)/shard_map/ppermute | solution.py:360
  55.8 6.6 %all-to-all-start.1 = ((bf16[32,104,128]{2,1,0:T(8,128)(2,1)}), bf16[32,104,128]{2,1,0:T(8,128)(2,1)S(1)}, u32[]{:S(2)}, u32[]{:S(2)}) async-start(bf16[32,104,128]{2,1,0:T(8,128)(2,1)} %shard_map.118), calls=%async_computation.1 | async-start | bytes 1703936 | tf_op jit(solution)/shard_map/all_to_all | solution.py:352
  64.0 2.5 %collective-permute-done.6.far_ref = bf16[1,8,16,128]{3,2,1,0:T(8,128)(2,1)S(1)} collective-permute-done((bf16[1,8,16,128]{3,2,1,0:T(8,128)(2,1)S(1)}, bf16[1,8,16,128]{3,2,1,0:T(8,128)(2,1)S(1)}, u32[]{:S(2)}, u32[]{:S(2)}) %collective-permute-start.6) | collective-permute-done | bytes 32800 | tf_op jit(solution)/shard_map/ppermute | solution.py:338
  66.5 1.8 %collective-permute-start.7 = (bf16[6,1,16,128]{3,2,1,0:T(8,128)(2,1)S(1)}, bf16[6,1,16,128]{3,2,1,0:T(8,128)(2,1)S(1)}, u32[]{:S(2)}, u32[]{:S(2)}) collective-permute-start(bf16[6,1,16,128]{3,2,1,0:T(8,128)(2,1)S(1)} %get-tuple-element.55), channel_id=1, source_target_pairs={{0,1},{2,3},{4,5},{6,7},{8,9},{10,11},{12,13},{14,15},{16,17},{18,... | collective-permute-start | bytes 73736 | tf_op jit(solution)/shard_map/ppermute | solution.py:346
  68.3 1.4 %collective-permute-start.8 = (bf16[6,1,16,128]{3,2,1,0:T(8,128)(2,1)S(1)}, bf16[6,1,16,128]{3,2,1,0:T(8,128)(2,1)S(1)}, u32[]{:S(2)}, u32[]{:S(2)}) collective-permute-start(bf16[6,1,16,128]{3,2,1,0:T(8,128)(2,1)S(1)} %get-tuple-element.56), channel_id=1, source_target_pairs={{1,2},{3,4},{5,6},{7,8},{9,10},{11,12},{13,14},{15,16},{17,18},{19... | collective-permute-start | bytes 73736 | tf_op jit(solution)/shard_map/ppermute | solution.py:347
  69.7 12.0 %collective-permute-done.7.even_ref = bf16[6,1,16,128]{3,2,1,0:T(8,128)(2,1)S(1)} collective-permute-done((bf16[6,1,16,128]{3,2,1,0:T(8,128)(2,1)S(1)}, bf16[6,1,16,128]{3,2,1,0:T(8,128)(2,1)S(1)}, u32[]{:S(2)}, u32[]{:S(2)}) %collective-permute-start.7) | collective-permute-done | bytes 24608 | tf_op jit(solution)/shard_map/ppermute | solution.py:346
  81.7 1.7 %all-to-all-done.1.got_ref = bf16[32,104,128]{2,1,0:T(8,128)(2,1)S(1)} async-done(((bf16[32,104,128]{2,1,0:T(8,128)(2,1)}), bf16[32,104,128]{2,1,0:T(8,128)(2,1)S(1)}, u32[]{:S(2)}, u32[]{:S(2)}) %all-to-all-start.1) | async-done | bytes 852000 | tf_op jit(solution)/shard_map/all_to_all | solution.py:352
  83.7 2.8 %collective-permute-done.9.got_ref = bf16[56,128]{1,0:T(8,128)(2,1)S(1)} collective-permute-done((bf16[56,128]{1,0:T(8,128)(2,1)S(1)}, bf16[56,128]{1,0:T(8,128)(2,1)S(1)}, u32[]{:S(2)}, u32[]{:S(2)}) %collective-permute-start.9) | collective-permute-done | bytes 14368 | tf_op jit(solution)/shard_map/ppermute | solution.py:356
  86.6 1.4 %collective-permute-start.10 = (f32[56,128]{1,0:T(8,128)S(1)}, f32[56,128]{1,0:T(8,128)S(1)}, u32[]{:S(2)}, u32[]{:S(2)}) collective-permute-start(f32[56,128]{1,0:T(8,128)S(1)} %shard_map.122.own_ref), channel_id=1, source_target_pairs={{0,192},{64,128},{128,64},{192,0},{1,193},{65,129},{129,65},{193,1... | collective-permute-start | bytes 86024 | tf_op jit(solution)/shard_map/ppermute | solution.py:356
  88.0 1.9 %shard_map.123.filled_ref = bf16[32,48,128]{2,1,0:T(8,128)(2,1)S(1)} custom-call(s32[1]{0:T(128)} %bitcast.spot_ref, bf16[4,8,16,128]{3,2,1,0:T(8,128)(2,1)S(1)} %get-tuple-element.54.own_ref.hid_ref, bf16[1,8,16,128]{3,2,1,0:T(8,128)(2,1)S(1)} %collective-permute-done.5.near_ref, bf16[1,8,16,128]{3,2,1,0:T(8,128)(2,1)S(1)} %collective-permute-done.6.far_ref, ...), custom_call_target="tpu_custom_call" | custom-call | tf_op jit(solution)/shard_map/pallas_call | solution.py:38
  91.4 7.8 %all-to-all-start.2 = ((bf16[32,104,128]{2,1,0:T(8,128)(2,1)}), bf16[32,104,128]{2,1,0:T(8,128)(2,1)S(1)}, u32[]{:S(2)}, u32[]{:S(2)}) async-start(bf16[32,104,128]{2,1,0:T(8,128)(2,1)} %shard_map.124), calls=%async_computation.2 | async-start | bytes 1703936 | tf_op jit(solution)/shard_map/all_to_all | solution.py:352
  99.3 1.5 %shard_map.120 = (bf16[512,128]{1,0:T(8,128)(2,1)}, s32[512,128]{1,0:T(8,128)S(1)}, f32[512,128]{1,0:T(8,128)S(1)}) custom-call(bf16[32,104,128]{2,1,0:T(8,128)(2,1)S(1)} %all-to-all-done.1.got_ref, s32[1,512]{1,0:T(1,128)S(1)} %bitcast.5, bf16[512,128]{1,0:T(8,128)(2,1)S(1)} %copy-done.1, bf16[512,128]{1,0:T(8,128)(2,1)S(1)} %copy-done.2, ...), custom_call_target="tpu_custom_call" | custom-call | tf_op jit(solution)/shard_map/pallas_call | solution.py:38
  100.8 15.3 %all-to-all-done.2.got_ref = bf16[32,104,128]{2,1,0:T(8,128)(2,1)S(1)} async-done(((bf16[32,104,128]{2,1,0:T(8,128)(2,1)}), bf16[32,104,128]{2,1,0:T(8,128)(2,1)S(1)}, u32[]{:S(2)}, u32[]{:S(2)}) %all-to-all-start.2) | async-done | bytes 852000 | tf_op jit(solution)/shard_map/all_to_all | solution.py:352
  116.2 8.4 %collective-permute-start.11 = (bf16[14,128,128]{2,1,0:T(8,128)(2,1)S(1)}, bf16[14,128,128]{2,1,0:T(8,128)(2,1)S(1)}, u32[]{:S(2)}, u32[]{:S(2)}) collective-permute-start(bf16[14,128,128]{2,1,0:T(8,128)(2,1)S(1)} %shard_map.126.mine_ref), channel_id=1, source_target_pairs={{0,32},{32,0},{1,33},{33,1},{2,34},{34,2},{3,35},{35,3},{4,36},{36... | collective-permute-start | bytes 1376264 | tf_op jit(solution)/shard_map/ppermute | solution.py:360
  126.1 1.5 %shard_map.127 = (f32[27,128,128]{2,1,0:T(8,128)}, f32[128,128]{1,0:T(8,128)}) custom-call(s32[1]{0:T(128)} %bitcast.spot_ref, bf16[14,128,128]{2,1,0:T(8,128)(2,1)S(1)} %shard_map.126.mine_ref, bf16[14,128,128]{2,1,0:T(8,128)(2,1)S(1)} %collective-permute-done.11.other_ref), custom_call_target="tpu_custom_call" | custom-call | tf_op jit(solution)/shard_map/pallas_call | solution.py:38
  (33 shorter events, 9.5 us)
Async XLA Ops:
  0.6 15.1 %copy-start.2 = (bf16[512,128]{1,0:T(8,128)(2,1)S(1)}, bf16[512,128]{1,0:T(8,128)(2,1)}, u32[]{:S(2)}) copy-start(bf16[512,128]{1,0:T(8,128)(2,1)} %cot_ref.3) | copy-start | bytes 393220
  0.6 15.1 %copy-start.1 = (bf16[512,128]{1,0:T(8,128)(2,1)S(1)}, bf16[512,128]{1,0:T(8,128)(2,1)}, u32[]{:S(2)}) copy-start(bf16[512,128]{1,0:T(8,128)(2,1)} %feat_ref.3) | copy-start | bytes 393220
  0.7 15.1 %copy-start.3 = (bf16[128,128]{1,0:T(8,128)(2,1)S(1)}, bf16[128,128]{1,0:T(8,128)(2,1)}, u32[]{:S(2)}) copy-start(bf16[128,128]{1,0:T(8,128)(2,1)} %mlp_ref.3) | copy-start | bytes 98308
  3.7 45.7 %copy-start = (bf16[27,128,128]{2,1,0:T(8,128)(2,1)S(1)}, bf16[27,128,128]{2,1,0:T(8,128)(2,1)}, u32[]{:S(2)}) copy-start(bf16[27,128,128]{2,1,0:T(8,128)(2,1)} %weight_ref.3) | copy-start | bytes 2654212
  3.7 32.4 %all-to-all-start = ((bf16[32,104,128]{2,1,0:T(8,128)(2,1)}), bf16[32,104,128]{2,1,0:T(8,128)(2,1)S(1)}, u32[]{:S(2)}, u32[]{:S(2)}) async-start(bf16[32,104,128]{2,1,0:T(8,128)(2,1)} %shard_map.111), calls=%async_computation | async-start | bytes 1703936 | tf_op jit(solution)/shard_map/all_to_all | solution.py:352
  36.8 6.7 %collective-permute-start = (bf16[1,8,16,128]{3,2,1,0:T(8,128)(2,1)S(1)}, bf16[1,8,16,128]{3,2,1,0:T(8,128)(2,1)S(1)}, u32[]{:S(2)}, u32[]{:S(2)}) collective-permute-start(bf16[1,8,16,128]{3,2,1,0:T(8,128)(2,1)S(1)} %get-tuple-element.41), channel_id=1, source_target_pairs={{0,32},{32,0},{1,33},{33,1},{2,34},{34,2},{3,35},{35,3},{4,36},{36... | collective-permute-start | bytes 98312 | tf_op jit(solution)/shard_map/ppermute | solution.py:360
  42.2 3.3 %collective-permute-start.1 = (bf16[1,8,16,128]{3,2,1,0:T(8,128)(2,1)S(1)}, bf16[1,8,16,128]{3,2,1,0:T(8,128)(2,1)S(1)}, u32[]{:S(2)}, u32[]{:S(2)}) collective-permute-start(bf16[1,8,16,128]{3,2,1,0:T(8,128)(2,1)S(1)} %get-tuple-element.42), channel_id=1, source_target_pairs={{32,64},{96,128},{160,192},{224,0},{64,32},{128,96},{192,160},{0,2... | collective-permute-start | bytes 98312 | tf_op jit(solution)/shard_map/ppermute | solution.py:338
  45.6 3.8 %collective-permute-start.2 = (bf16[6,1,16,128]{3,2,1,0:T(8,128)(2,1)S(1)}, bf16[6,1,16,128]{3,2,1,0:T(8,128)(2,1)S(1)}, u32[]{:S(2)}, u32[]{:S(2)}) collective-permute-start(bf16[6,1,16,128]{3,2,1,0:T(8,128)(2,1)S(1)} %get-tuple-element.43), channel_id=1, source_target_pairs={{0,1},{2,3},{4,5},{6,7},{8,9},{10,11},{12,13},{14,15},{16,17},{18,... | collective-permute-start | bytes 73736 | tf_op jit(solution)/shard_map/ppermute | solution.py:346
  46.9 2.5 %collective-permute-start.3 = (bf16[6,1,16,128]{3,2,1,0:T(8,128)(2,1)S(1)}, bf16[6,1,16,128]{3,2,1,0:T(8,128)(2,1)S(1)}, u32[]{:S(2)}, u32[]{:S(2)}) collective-permute-start(bf16[6,1,16,128]{3,2,1,0:T(8,128)(2,1)S(1)} %get-tuple-element.44), channel_id=1, source_target_pairs={{1,2},{3,4},{5,6},{7,8},{9,10},{11,12},{13,14},{15,16},{17,18},{19... | collective-permute-start | bytes 73736 | tf_op jit(solution)/shard_map/ppermute | solution.py:347
  51.8 3.0 %collective-permute-start.4 = (bf16[14,128,128]{2,1,0:T(8,128)(2,1)S(1)}, bf16[14,128,128]{2,1,0:T(8,128)(2,1)S(1)}, u32[]{:S(2)}, u32[]{:S(2)}) collective-permute-start(bf16[14,128,128]{2,1,0:T(8,128)(2,1)S(1)} %get-tuple-element.49), channel_id=1, source_target_pairs={{0,32},{32,0},{1,33},{33,1},{2,34},{34,2},{3,35},{35,3},{4,36},{36... | collective-permute-start | bytes 1376264 | tf_op jit(solution)/shard_map/ppermute | solution.py:360
  55.8 27.5 %all-to-all-start.1 = ((bf16[32,104,128]{2,1,0:T(8,128)(2,1)}), bf16[32,104,128]{2,1,0:T(8,128)(2,1)S(1)}, u32[]{:S(2)}, u32[]{:S(2)}) async-start(bf16[32,104,128]{2,1,0:T(8,128)(2,1)} %shard_map.118), calls=%async_computation.1 | async-start | bytes 1703936 | tf_op jit(solution)/shard_map/all_to_all | solution.py:352
  62.4 1.6 %collective-permute-start.5 = (bf16[1,8,16,128]{3,2,1,0:T(8,128)(2,1)S(1)}, bf16[1,8,16,128]{3,2,1,0:T(8,128)(2,1)S(1)}, u32[]{:S(2)}, u32[]{:S(2)}) collective-permute-start(bf16[1,8,16,128]{3,2,1,0:T(8,128)(2,1)S(1)} %get-tuple-element.52), channel_id=1, source_target_pairs={{0,32},{32,0},{1,33},{33,1},{2,34},{34,2},{3,35},{35,3},{4,36},{36... | collective-permute-start | bytes 98312 | tf_op jit(solution)/shard_map/ppermute | solution.py:360
  63.1 3.3 %collective-permute-start.6 = (bf16[1,8,16,128]{3,2,1,0:T(8,128)(2,1)S(1)}, bf16[1,8,16,128]{3,2,1,0:T(8,128)(2,1)S(1)}, u32[]{:S(2)}, u32[]{:S(2)}) collective-permute-start(bf16[1,8,16,128]{3,2,1,0:T(8,128)(2,1)S(1)} %get-tuple-element.53), channel_id=1, source_target_pairs={{32,64},{96,128},{160,192},{224,0},{64,32},{128,96},{192,160},{0,2... | collective-permute-start | bytes 98312 | tf_op jit(solution)/shard_map/ppermute | solution.py:338
  66.5 15.2 %collective-permute-start.7 = (bf16[6,1,16,128]{3,2,1,0:T(8,128)(2,1)S(1)}, bf16[6,1,16,128]{3,2,1,0:T(8,128)(2,1)S(1)}, u32[]{:S(2)}, u32[]{:S(2)}) collective-permute-start(bf16[6,1,16,128]{3,2,1,0:T(8,128)(2,1)S(1)} %get-tuple-element.55), channel_id=1, source_target_pairs={{0,1},{2,3},{4,5},{6,7},{8,9},{10,11},{12,13},{14,15},{16,17},{18,... | collective-permute-start | bytes 73736 | tf_op jit(solution)/shard_map/ppermute | solution.py:346
  68.3 13.4 %collective-permute-start.8 = (bf16[6,1,16,128]{3,2,1,0:T(8,128)(2,1)S(1)}, bf16[6,1,16,128]{3,2,1,0:T(8,128)(2,1)S(1)}, u32[]{:S(2)}, u32[]{:S(2)}) collective-permute-start(bf16[6,1,16,128]{3,2,1,0:T(8,128)(2,1)S(1)} %get-tuple-element.56), channel_id=1, source_target_pairs={{1,2},{3,4},{5,6},{7,8},{9,10},{11,12},{13,14},{15,16},{17,18},{19... | collective-permute-start | bytes 73736 | tf_op jit(solution)/shard_map/ppermute | solution.py:347
  83.4 3.1 %collective-permute-start.9 = (bf16[56,128]{1,0:T(8,128)(2,1)S(1)}, bf16[56,128]{1,0:T(8,128)(2,1)S(1)}, u32[]{:S(2)}, u32[]{:S(2)}) collective-permute-start(bf16[56,128]{1,0:T(8,128)(2,1)S(1)} %shard_map.121.own_ref), channel_id=1, source_target_pairs={{0,64},{64,0},{128,192},{192,128},{1,65},{65,1},{129,193},{193,129... | collective-permute-start | bytes 43016 | tf_op jit(solution)/shard_map/ppermute | solution.py:356
  86.6 3.9 %collective-permute-start.10 = (f32[56,128]{1,0:T(8,128)S(1)}, f32[56,128]{1,0:T(8,128)S(1)}, u32[]{:S(2)}, u32[]{:S(2)}) collective-permute-start(f32[56,128]{1,0:T(8,128)S(1)} %shard_map.122.own_ref), channel_id=1, source_target_pairs={{0,192},{64,128},{128,64},{192,0},{1,193},{65,129},{129,65},{193,1... | collective-permute-start | bytes 86024 | tf_op jit(solution)/shard_map/ppermute | solution.py:356
  89.9 9.4 %copy-start.4 = (s32[512,1]{0,1:T(1,128)S(1)}, s32[512,1]{0,1:T(1,128)}, u32[]{:S(2)}) copy-start(s32[512,1]{0,1:T(1,128)} %param.9) | copy-start | bytes 6148
  91.4 24.6 %all-to-all-start.2 = ((bf16[32,104,128]{2,1,0:T(8,128)(2,1)}), bf16[32,104,128]{2,1,0:T(8,128)(2,1)S(1)}, u32[]{:S(2)}, u32[]{:S(2)}) async-start(bf16[32,104,128]{2,1,0:T(8,128)(2,1)} %shard_map.124), calls=%async_computation.2 | async-start | bytes 1703936 | tf_op jit(solution)/shard_map/all_to_all | solution.py:352
  116.2 9.9 %collective-permute-start.11 = (bf16[14,128,128]{2,1,0:T(8,128)(2,1)S(1)}, bf16[14,128,128]{2,1,0:T(8,128)(2,1)S(1)}, u32[]{:S(2)}, u32[]{:S(2)}) collective-permute-start(bf16[14,128,128]{2,1,0:T(8,128)(2,1)S(1)} %shard_map.126.mine_ref), channel_id=1, source_target_pairs={{0,32},{32,0},{1,33},{33,1},{2,34},{34,2},{3,35},{35,3},{4,36},{36... | collective-permute-start | bytes 1376264 | tf_op jit(solution)/shard_map/ppermute | solution.py:360

commit v7 on v6

--- a/solution.py
+++ b/solution.py
@@ -190,10 +190,7 @@
         ref[pl.ds((VX + 1) * core, 1)] = far_ref[:, row] * inside
 
 
-def assemble(spot_ref, wide_ref, own_ref, near_ref, far_ref, even_ref, odd_ref):
-    core = spot_ref[0] % 2
-    turn = spot_ref[0] // 4 % 2
-
+def placer(spot_ref, wide_ref):
     def put(x, y, block, inside=None):
         nx, ny = block.shape[0], block.shape[1]
         if inside is not None:
@@ -211,9 +208,20 @@
         wide_ref[planes, rows, :, C : 2 * C] = block
         wide_ref[planes, rows, :, 2 * C :] = up.astype(BF).reshape(shape)
 
+    return put
+
+
+def assemble(spot_ref, wide_ref, own_ref, near_ref, far_ref):
+    core = spot_ref[0] % 2
+    put = placer(spot_ref, wide_ref)
     put(1, 1, own_ref[...])
     put((VX + 1) * (1 - core), 1, near_ref[...])
     put((VX + 1) * core, 1, far_ref[...], 1)
+
+
+def add_rows(spot_ref, wide_ref, even_ref, odd_ref):
+    turn = spot_ref[0] // 4 % 2
+    put = placer(spot_ref, wide_ref)
     put(0, (VY + 1) * (1 - turn), even_ref[...])
     put(0, (VY + 1) * turn, odd_ref[...], 3)
 
@@ -222,28 +230,68 @@
     return wide_ref[x : x + VX, y : y + VY, :, :].reshape(CELLS, 3 * C)
 
 
-def conv_kernel(spot_ref, vox_ref, near_ref, far_ref, even_ref, odd_ref, weight_ref, gout_ref,
-                mlp_ref, keep_ref, send_ref, act_ref, hid_ref, in_ref, out_ref, wide_ref, all_ref):
-    core = spot_ref[0] % 2
-    assemble(spot_ref, wide_ref, vox_ref, near_ref, far_ref, even_ref, odd_ref)
+def taps(weight_ref, k):
+    return weight_ref[3 * k : 3 * k + 3].reshape(3 * C, C)
+
+
+def inner_kernel(spot_ref, vox_ref, near_ref, far_ref, weight_ref, wide_ref, hidden_ref):
+    assemble(spot_ref, wide_ref, vox_ref, near_ref, far_ref)
+    blank = jnp.zeros((VX + 2, 1, Z, 3 * C), BF)
+    wide_ref[:, 0:1] = blank
+    wide_ref[:, VY + 1 :] = blank
     hidden = jnp.zeros((CELLS, C), F32)
     for k in range(9):
-        taps = weight_ref[3 * k : 3 * k + 3].reshape(3 * C, C)
-        hidden = hidden + dot(window(wide_ref, k // 3, k % 3), taps)
+        hidden = hidden + dot(window(wide_ref, k // 3, k % 3), taps(weight_ref, k))
+    hidden_ref[...] = hidden.reshape(VX, VY, Z, C)
+
+
+def half_blocks(half, wide_ref, turned, mlp_ref, out_ref):
+    def part(k):
+        return dot(turned, wide_ref[pl.ds(k // 3, VX), pl.ds(k % 3, VY)].reshape(CELLS, 3 * C)).astype(out_ref.dtype)
+
+    for i in range(4):
+        blocks = part(5 * half + i)
+        for j in range(3):
+            out_ref[3 * i + half + j] = blocks[:, j * C : (j + 1) * C]
+    blocks = part(4)
+
+    @pl.when(half == 0)
+    def _():
+        out_ref[12] = blocks[:, 0:C]
+        out_ref[13] = blocks[:, C : 2 * C]
+
+    @pl.when(half == 1)
+    def _():
+        out_ref[0] = blocks[:, 2 * C :]
+        out_ref[13] = mlp_ref[...].astype(out_ref.dtype)
+
+
+def conv_kernel(spot_ref, inner_ref, hidden_ref, even_ref, odd_ref, weight_ref, gout_ref, mlp_ref,
+                send_ref, wide_ref, turned_ref, act_ref, hid_ref, in_ref, out_ref, sum_ref):
+    wide_ref[...] = inner_ref[...]
+    add_rows(spot_ref, wide_ref, even_ref, odd_ref)
+    sum_ref[...] = hidden_ref[...]
+    for y, at, dy in ((0, 0, 0), (VY - 1, VY + 1, 2)):
+        more = jnp.zeros((VX * Z, C), F32)
+        for dx in range(3):
+            row = wide_ref[dx : dx + VX, at].reshape(VX * Z, 3 * C)
+            more = more + dot(row, taps(weight_ref, 3 * dx + dy))
+        sum_ref[:, y] += more.reshape(VX, Z, C)
+    hidden = sum_ref[...].reshape(CELLS, C)
     s = sigmoid(hidden)
     act_ref[...] = (hidden * s).astype(BF)
     grad_hidden = (gout_ref[...] * slope(hidden, s)).astype(BF)
+    core = spot_ref[0] % 2
     hid_ref[...] = grad_hidden.reshape(VX, VY, Z, C)
     in_ref[...] = hid_ref[pl.ds((VX - 1) * (1 - core), 1)]
     out_ref[...] = hid_ref[pl.ds((VX - 1) * core, 1)]
     turned = grad_hidden.astype(F32).T.astype(BF)
-    for k in range(9):
-        part = dot(turned, window(wide_ref, k // 3, k % 3))
-        for j in range(3):
-            all_ref[3 * k + j] = part[:, j * C : (j + 1) * C]
-    all_ref[27] = mlp_ref[...]
-    keep_ref[...] = all_ref[pl.ds(core * HALF, HALF)]
-    send_ref[...] = all_ref[pl.ds((1 - core) * HALF, HALF)].astype(BF)
+    turned_ref[...] = turned
+    half_blocks(1 - core, wide_ref, turned, mlp_ref, send_ref)
+
+
+def keep_kernel(spot_ref, wide_ref, turned_ref, mlp_ref, keep_ref):
+    half_blocks(spot_ref[0] % 2, wide_ref, turned_ref[...], mlp_ref, keep_ref)
 
 
 def sample_kernel(matrix_ref, act_ref, out_ref):
@@ -260,12 +308,9 @@
     out_ref[...] = jnp.sum(got_ref[:, CAP:, :].astype(F32), axis=0).astype(BF)
 
 
-def pair_kernel(own_ref, got_ref, out_ref):
-    out_ref[...] = own_ref[...].astype(F32) + got_ref[...].astype(F32)
-
-
 def back_kernel(spot_ref, hid_ref, near_ref, far_ref, even_ref, odd_ref, weight_ref, meta_ref, div_ref, out_ref, wide_ref):
-    assemble(spot_ref, wide_ref, hid_ref, near_ref, far_ref, even_ref, odd_ref)
+    assemble(spot_ref, wide_ref, hid_ref, near_ref, far_ref)
+    add_rows(spot_ref, wide_ref, even_ref, odd_ref)
     total = jnp.zeros((CELLS, C), F32)
     for k in range(9):
         taps = jnp.concatenate([weight_ref[3 * k + 2 - j] for j in range(3)], axis=1)
@@ -274,8 +319,11 @@
     out_ref[...] = dot(own_matrix(meta_ref[...]), mean, LEFT).astype(BF).reshape(GY, CAP, C)
 
 
-def deal_kernel(own_ref, got_ref, filled_ref, out_ref):
-    total = (own_ref[...] + got_ref[...]).astype(BF)
+def deal_kernel(spot_ref, own_ref, one_ref, two_ref, three_ref, filled_ref, out_ref, part_ref):
+    y = spot_ref[0] // 16
+    for k, ref in enumerate((own_ref, one_ref, two_ref, three_ref)):
+        part_ref[y ^ k] = ref[...].astype(F32)
+    total = jnp.sum(part_ref[...], axis=0).astype(BF)
     out_ref[:, CAP:, :] = jnp.broadcast_to(total[None], (GY, SHARE, C))
     out_ref[:, 0:CAP, :] = filled_ref[...]
 
@@ -364,7 +412,7 @@
     strip = lax.axis_index(("y", "c"))
     slab_here = lax.axis_index(("x", "z"))
     core = lax.axis_index("c")
-    core = core + 2 * (strip % (GX - 1) != 0) + 4 * (slab_here % 2) + 8 * (slab_here % (GY - 1) != 0)
+    core = core + 16 * (strip // 2) + 2 * (strip % (GX - 1) != 0) + 4 * (slab_here % 2) + 8 * (slab_here % (GY - 1) != 0)
     spot = core.reshape(1)
     point_slab, spot = lax.optimization_barrier((point_slab, spot))
     slab = point_slab.reshape(1, PTS)
@@ -398,21 +446,30 @@
         smem=1,
     )
     near, far = swap(near), chips(far)
-    faces = (near, far) + edges(spot, near, voxels, far)
+    even, odd = edges(spot, near, voxels, far)
+    spread = sds((VX + 2, VY + 2, Z, 3 * C), BF)
+    inner, hidden = call(
+        inner_kernel,
+        (spread, sds((VX, VY, Z, C), F32)),
+        (spot, voxels, near, far, conv_weight),
+        smem=1,
+    )
     matrix, grad_out = call(
         spread_kernel, (sds((CELLS, SLOTS), BF), sds((CELLS, C), F32)), (got, meta)
     )
     wide = pltpu.VMEM((VX + 2, VY + 2, Z, 3 * C), BF)
     block = sds((GY, ROWS, C), BF)
     rows = sds((GY, CAP, C), BF)
-    keep, send, act, grad_hidden, near, far = call(
+    half = sds((HALF, C, C), BF)
+    send, full, turned, act, grad_hidden, near, far = call(
         conv_kernel,
-        (sds((HALF, C, C), F32), sds((HALF, C, C), BF), sds((CELLS, C), BF), cells, FACE, FACE),
-        (spot, voxels) + faces + (conv_weight, grad_out, mlp_grad),
-        scratch=(wide, pltpu.VMEM((2 * HALF, C, C), F32)),
+        (half, spread, sds((C, CELLS), BF), sds((CELLS, C), BF), cells, FACE, FACE),
+        (spot, inner, hidden, even, odd, conv_weight, grad_out, mlp_grad),
+        scratch=(pltpu.VMEM((VX, VY, Z, C), F32),),
         smem=1,
     )
     arrived = swap(send)
+    keep = call(keep_kernel, sds((HALF, C, C), F32), (spot, full, turned, mlp_grad), smem=1)
     filled = call(sample_kernel, rows, (matrix, act))
     joined = call(join_kernel, block, (keep, arrived, filled))
     first = exchange(joined)
@@ -427,8 +484,14 @@
         smem=1,
     )
     share = call(share_kernel, sds((SHARE, C), BF), (first,), mib=4)
-    pair = call(pair_kernel, sds((SHARE, C), F32), (share, across(share, (1, 0, 3, 2))), mib=1)
-    joined = call(deal_kernel, block, (pair, across(pair, (3, 2, 1, 0)), filled))
+    others = tuple(across(share, [y ^ k for y in range(4)]) for k in (1, 2, 3))
+    joined = call(
+        deal_kernel,
+        block,
+        (spot, share) + others + (filled,),
+        scratch=(pltpu.VMEM((4, SHARE, C), F32),),
+        smem=1,
+    )
     second = exchange(joined)
     output, position, back = call(
         forward_kernel,

time: 128 us -> 126 us (0.984)
  waiting for transfers between devices: 58.7 us -> 57 us
    ppermute x2 -> x3, waiting for transfers between devices: 3.46 us -> 1 us  [across(): return lax.ppermute(share, 'y', list(enumerate(partner)))]
    ppermute x4, starting transfers between devices: 16.2 us -> 14.1 us  [swap(): return lax.ppermute(half, 'c', [(0, 1), (1, 0)])]
    ppermute x2 -> x3, starting transfers between devices: 1.71 us -> 3.52 us  [across(): return lax.ppermute(share, 'y', list(enumerate(partner)))]
    pallas_call x17 -> x18, Pallas kernels: 16.2 us -> 16.4 us  [call(): pl.pallas_call(kernel, out_shape=out_shape, in_specs=[SMEM] * smem + [HBM...]
  transfers between devices with their start and end apart: 15 -> 16, of which waited for: 11 -> 10; matrix products, arithmetic and copies ran while one was open for 0% -> 0% of each run, Pallas kernels for 5% -> 6%
where the time goes in v7:
time: 126 us
  waiting for transfers between devices  57 us (45%)
  starting transfers between devices  51.6 us (41%)
  Pallas kernels  16.4 us (13%)
    all_to_all x3, waiting for transfers between devices, exchange(): lax.all_to_all(rows, ('x', 'z'), split_axis=0, concat_axis=0, tiled=True)  38 us
    all_to_all x3, starting transfers between devices, exchange(): lax.all_to_all(rows, ('x', 'z'), split_axis=0, concat_axis=0, tiled=True)  26.6 us
    pallas_call x18, Pallas kernels, call(): pl.pallas_call(kernel, out_shape=out_shape, in_specs=[SMEM] * smem + [HBM...  16.4 us
    ppermute x4, starting transfers between devices, swap(): return lax.ppermute(half, 'c', [(0, 1), (1, 0)])  14.1 us
    ppermute x2, waiting for transfers between devices, edges(): lax.ppermute(even, ('x', 'z'), pairs(GY, 0))  12 us
    ppermute x2, waiting for transfers between devices, chips(): return lax.ppermute(face, ('y', 'c'), pairs(GX, 1))  4.53 us
    ppermute x3, starting transfers between devices, across(): return lax.ppermute(share, 'y', list(enumerate(partner)))  3.52 us
    ppermute x2, starting transfers between devices, edges(): lax.ppermute(even, ('x', 'z'), pairs(GY, 0))  3.09 us
  transfers between devices with their start and end apart: 16, of which 10 were waited for; matrix products, arithmetic and copies ran while one was open for 0% of the time, Pallas kernels for 6%

profile of v7, /device:TPU:1, one launch (start us, length us, event | category | flops | bytes accessed | tf_op | source)
XLA Modules:
  0.0 125.9 jit_solution(7984148523281444936)
XLA Ops:
  0.7 3.0 %shard_map.111 = bf16[32,104,128]{2,1,0:T(8,128)(2,1)} custom-call(bf16[512,128]{1,0:T(8,128)(2,1)} %feat_ref.3, bf16[512,128]{1,0:T(8,128)(2,1)} %cot_ref.3, s32[1,512]{1,0:T(1,128)} %bitcast.4, s32[1,512]{1,0:T(1,128)} %bitcast.6, s32[1,512]{1,0:T(1,128)} %bitcast.7, bf16[3,512]{1,0:T(4,128)(2,1)} %off_hbm.1), custom_call_target="tpu_custom_call" | custom-call | tf_op jit(solution)/shard_map/pallas_call | solution.py:38
  3.7 12.0 %all-to-all-start = ((bf16[32,104,128]{2,1,0:T(8,128)(2,1)}), bf16[32,104,128]{2,1,0:T(8,128)(2,1)S(1)}, u32[]{:S(2)}, u32[]{:S(2)}) async-start(bf16[32,104,128]{2,1,0:T(8,128)(2,1)} %shard_map.111), calls=%async_computation | async-start | bytes 1703936 | tf_op jit(solution)/shard_map/all_to_all | solution.py:400
  16.2 19.9 %all-to-all-done.got_ref = bf16[32,104,128]{2,1,0:T(8,128)(2,1)S(1)} async-done(((bf16[32,104,128]{2,1,0:T(8,128)(2,1)}), bf16[32,104,128]{2,1,0:T(8,128)(2,1)S(1)}, u32[]{:S(2)}, u32[]{:S(2)}) %all-to-all-start) | async-done | bytes 852000 | tf_op jit(solution)/shard_map/all_to_all | solution.py:400
  36.8 5.5 %collective-permute-start = (bf16[1,8,16,128]{3,2,1,0:T(8,128)(2,1)S(1)}, bf16[1,8,16,128]{3,2,1,0:T(8,128)(2,1)S(1)}, u32[]{:S(2)}, u32[]{:S(2)}) collective-permute-start(bf16[1,8,16,128]{3,2,1,0:T(8,128)(2,1)S(1)} %get-tuple-element.44), channel_id=1, source_target_pairs={{0,32},{32,0},{1,33},{33,1},{2,34},{34,2},{3,35},{35,3},{4,36},{36... | collective-permute-start | bytes 98312 | tf_op jit(solution)/shard_map/ppermute | solution.py:408
  42.2 1.3 %collective-permute-start.1 = (bf16[1,8,16,128]{3,2,1,0:T(8,128)(2,1)S(1)}, bf16[1,8,16,128]{3,2,1,0:T(8,128)(2,1)S(1)}, u32[]{:S(2)}, u32[]{:S(2)}) collective-permute-start(bf16[1,8,16,128]{3,2,1,0:T(8,128)(2,1)S(1)} %get-tuple-element.45), channel_id=1, source_target_pairs={{32,64},{96,128},{160,192},{224,0},{64,32},{128,96},{192,160},{0,2... | collective-permute-start | bytes 98312 | tf_op jit(solution)/shard_map/ppermute | solution.py:386
  43.5 2.1 %collective-permute-done.1.far_ref = bf16[1,8,16,128]{3,2,1,0:T(8,128)(2,1)S(1)} collective-permute-done((bf16[1,8,16,128]{3,2,1,0:T(8,128)(2,1)S(1)}, bf16[1,8,16,128]{3,2,1,0:T(8,128)(2,1)S(1)}, u32[]{:S(2)}, u32[]{:S(2)}) %collective-permute-start.1) | collective-permute-done | bytes 32800 | tf_op jit(solution)/shard_map/ppermute | solution.py:386
  45.6 1.3 %collective-permute-start.2 = (bf16[6,1,16,128]{3,2,1,0:T(8,128)(2,1)S(1)}, bf16[6,1,16,128]{3,2,1,0:T(8,128)(2,1)S(1)}, u32[]{:S(2)}, u32[]{:S(2)}) collective-permute-start(bf16[6,1,16,128]{3,2,1,0:T(8,128)(2,1)S(1)} %get-tuple-element.48), channel_id=1, source_target_pairs={{0,1},{2,3},{4,5},{6,7},{8,9},{10,11},{12,13},{14,15},{16,17},{18,... | collective-permute-start | bytes 73736 | tf_op jit(solution)/shard_map/ppermute | solution.py:394
  46.9 1.7 %collective-permute-start.3 = (bf16[6,1,16,128]{3,2,1,0:T(8,128)(2,1)S(1)}, bf16[6,1,16,128]{3,2,1,0:T(8,128)(2,1)S(1)}, u32[]{:S(2)}, u32[]{:S(2)}) collective-permute-start(bf16[6,1,16,128]{3,2,1,0:T(8,128)(2,1)S(1)} %get-tuple-element.49), channel_id=1, source_target_pairs={{1,2},{3,4},{5,6},{7,8},{9,10},{11,12},{13,14},{15,16},{17,18},{19... | collective-permute-start | bytes 73736 | tf_op jit(solution)/shard_map/ppermute | solution.py:395
  49.4 1.2 shard_map.114
  54.4 6.5 %all-to-all-start.1 = ((bf16[32,104,128]{2,1,0:T(8,128)(2,1)}), bf16[32,104,128]{2,1,0:T(8,128)(2,1)S(1)}, u32[]{:S(2)}, u32[]{:S(2)}) async-start(bf16[32,104,128]{2,1,0:T(8,128)(2,1)} %shard_map.120), calls=%async_computation.1 | async-start | bytes 1703936 | tf_op jit(solution)/shard_map/all_to_all | solution.py:400
  62.5 2.5 %collective-permute-done.6.far_ref = bf16[1,8,16,128]{3,2,1,0:T(8,128)(2,1)S(1)} collective-permute-done((bf16[1,8,16,128]{3,2,1,0:T(8,128)(2,1)S(1)}, bf16[1,8,16,128]{3,2,1,0:T(8,128)(2,1)S(1)}, u32[]{:S(2)}, u32[]{:S(2)}) %collective-permute-start.6) | collective-permute-done | bytes 32800 | tf_op jit(solution)/shard_map/ppermute | solution.py:386
  65.0 1.8 %collective-permute-start.7 = (bf16[6,1,16,128]{3,2,1,0:T(8,128)(2,1)S(1)}, bf16[6,1,16,128]{3,2,1,0:T(8,128)(2,1)S(1)}, u32[]{:S(2)}, u32[]{:S(2)}) collective-permute-start(bf16[6,1,16,128]{3,2,1,0:T(8,128)(2,1)S(1)} %get-tuple-element.61), channel_id=1, source_target_pairs={{0,1},{2,3},{4,5},{6,7},{8,9},{10,11},{12,13},{14,15},{16,17},{18,... | collective-permute-start | bytes 73736 | tf_op jit(solution)/shard_map/ppermute | solution.py:394
  66.8 1.4 %collective-permute-start.8 = (bf16[6,1,16,128]{3,2,1,0:T(8,128)(2,1)S(1)}, bf16[6,1,16,128]{3,2,1,0:T(8,128)(2,1)S(1)}, u32[]{:S(2)}, u32[]{:S(2)}) collective-permute-start(bf16[6,1,16,128]{3,2,1,0:T(8,128)(2,1)S(1)} %get-tuple-element.62), channel_id=1, source_target_pairs={{1,2},{3,4},{5,6},{7,8},{9,10},{11,12},{13,14},{15,16},{17,18},{19... | collective-permute-start | bytes 73736 | tf_op jit(solution)/shard_map/ppermute | solution.py:395
  68.2 12.0 %collective-permute-done.7.even_ref = bf16[6,1,16,128]{3,2,1,0:T(8,128)(2,1)S(1)} collective-permute-done((bf16[6,1,16,128]{3,2,1,0:T(8,128)(2,1)S(1)}, bf16[6,1,16,128]{3,2,1,0:T(8,128)(2,1)S(1)}, u32[]{:S(2)}, u32[]{:S(2)}) %collective-permute-start.7) | collective-permute-done | bytes 24608 | tf_op jit(solution)/shard_map/ppermute | solution.py:394
  80.1 1.7 %all-to-all-done.1.got_ref = bf16[32,104,128]{2,1,0:T(8,128)(2,1)S(1)} async-done(((bf16[32,104,128]{2,1,0:T(8,128)(2,1)}), bf16[32,104,128]{2,1,0:T(8,128)(2,1)S(1)}, u32[]{:S(2)}, u32[]{:S(2)}) %all-to-all-start.1) | async-done | bytes 852000 | tf_op jit(solution)/shard_map/all_to_all | solution.py:400
  81.9 2.3 %collective-permute-start.11 = (bf16[56,128]{1,0:T(8,128)(2,1)S(1)}, bf16[56,128]{1,0:T(8,128)(2,1)S(1)}, u32[]{:S(2)}, u32[]{:S(2)}) collective-permute-start(bf16[56,128]{1,0:T(8,128)(2,1)S(1)} %shard_map.123.own_ref), channel_id=1, source_target_pairs={{0,192},{64,128},{128,64},{192,0},{1,193},{65,129},{129,65},{193,1... | collective-permute-start | bytes 43016 | tf_op jit(solution)/shard_map/ppermute | solution.py:404
  84.2 1.2 collective-permute-start.9
  85.4 1.9 %shard_map.124.filled_ref = bf16[32,48,128]{2,1,0:T(8,128)(2,1)S(1)} custom-call(s32[1]{0:T(128)} %bitcast.spot_ref, bf16[4,8,16,128]{3,2,1,0:T(8,128)(2,1)S(1)} %get-tuple-element.60.own_ref.hid_ref, bf16[1,8,16,128]{3,2,1,0:T(8,128)(2,1)S(1)} %collective-permute-done.5.near_ref, bf16[1,8,16,128]{3,2,1,0:T(8,128)(2,1)S(1)} %collective-permute-done.6.far_ref, ...), custom_call_target="tpu_custom_call" | custom-call | tf_op jit(solution)/shard_map/pallas_call | solution.py:38
  89.3 8.1 %all-to-all-start.2 = ((bf16[32,104,128]{2,1,0:T(8,128)(2,1)}), bf16[32,104,128]{2,1,0:T(8,128)(2,1)S(1)}, u32[]{:S(2)}, u32[]{:S(2)}) async-start(bf16[32,104,128]{2,1,0:T(8,128)(2,1)} %shard_map.125), calls=%async_computation.2 | async-start | bytes 1703936 | tf_op jit(solution)/shard_map/all_to_all | solution.py:400
  97.4 1.5 %shard_map.122 = (bf16[512,128]{1,0:T(8,128)(2,1)}, s32[512,128]{1,0:T(8,128)S(1)}, f32[512,128]{1,0:T(8,128)S(1)}) custom-call(bf16[32,104,128]{2,1,0:T(8,128)(2,1)S(1)} %all-to-all-done.1.got_ref, s32[1,512]{1,0:T(1,128)S(1)} %bitcast.5, bf16[512,128]{1,0:T(8,128)(2,1)S(1)} %copy-done.1, bf16[512,128]{1,0:T(8,128)(2,1)S(1)} %copy-done.2, ...), custom_call_target="tpu_custom_call" | custom-call | tf_op jit(solution)/shard_map/pallas_call | solution.py:38
  98.9 16.5 %all-to-all-done.2.got_ref = bf16[32,104,128]{2,1,0:T(8,128)(2,1)S(1)} async-done(((bf16[32,104,128]{2,1,0:T(8,128)(2,1)}), bf16[32,104,128]{2,1,0:T(8,128)(2,1)S(1)}, u32[]{:S(2)}, u32[]{:S(2)}) %all-to-all-start.2) | async-done | bytes 852000 | tf_op jit(solution)/shard_map/all_to_all | solution.py:400
  115.4 7.5 %collective-permute-start.12 = (bf16[14,128,128]{2,1,0:T(8,128)(2,1)S(1)}, bf16[14,128,128]{2,1,0:T(8,128)(2,1)S(1)}, u32[]{:S(2)}, u32[]{:S(2)}) collective-permute-start(bf16[14,128,128]{2,1,0:T(8,128)(2,1)S(1)} %shard_map.127.mine_ref), channel_id=1, source_target_pairs={{0,32},{32,0},{1,33},{33,1},{2,34},{34,2},{3,35},{35,3},{4,36},{36... | collective-permute-start | bytes 1376264 | tf_op jit(solution)/shard_map/ppermute | solution.py:408
  122.9 1.2 shard_map.126
  124.4 1.5 %shard_map.128 = (f32[27,128,128]{2,1,0:T(8,128)}, f32[128,128]{1,0:T(8,128)}) custom-call(s32[1]{0:T(128)} %bitcast.spot_ref, bf16[14,128,128]{2,1,0:T(8,128)(2,1)S(1)} %shard_map.127.mine_ref, bf16[14,128,128]{2,1,0:T(8,128)(2,1)S(1)} %collective-permute-done.12.other_ref), custom_call_target="tpu_custom_call" | custom-call | tf_op jit(solution)/shard_map/pallas_call | solution.py:38
  (36 shorter events, 9.7 us)
Async XLA Ops:
  0.6 15.1 %copy-start.2 = (bf16[512,128]{1,0:T(8,128)(2,1)S(1)}, bf16[512,128]{1,0:T(8,128)(2,1)}, u32[]{:S(2)}) copy-start(bf16[512,128]{1,0:T(8,128)(2,1)} %cot_ref.3) | copy-start | bytes 393220
  0.6 15.1 %copy-start.1 = (bf16[512,128]{1,0:T(8,128)(2,1)S(1)}, bf16[512,128]{1,0:T(8,128)(2,1)}, u32[]{:S(2)}) copy-start(bf16[512,128]{1,0:T(8,128)(2,1)} %feat_ref.3) | copy-start | bytes 393220
  0.7 15.1 %copy-start.3 = (bf16[128,128]{1,0:T(8,128)(2,1)S(1)}, bf16[128,128]{1,0:T(8,128)(2,1)}, u32[]{:S(2)}) copy-start(bf16[128,128]{1,0:T(8,128)(2,1)} %mlp_ref.3) | copy-start | bytes 98308
  3.7 45.7 %copy-start = (bf16[27,128,128]{2,1,0:T(8,128)(2,1)S(1)}, bf16[27,128,128]{2,1,0:T(8,128)(2,1)}, u32[]{:S(2)}) copy-start(bf16[27,128,128]{2,1,0:T(8,128)(2,1)} %weight_ref.5) | copy-start | bytes 2654212
  3.7 32.4 %all-to-all-start = ((bf16[32,104,128]{2,1,0:T(8,128)(2,1)}), bf16[32,104,128]{2,1,0:T(8,128)(2,1)S(1)}, u32[]{:S(2)}, u32[]{:S(2)}) async-start(bf16[32,104,128]{2,1,0:T(8,128)(2,1)} %shard_map.111), calls=%async_computation | async-start | bytes 1703936 | tf_op jit(solution)/shard_map/all_to_all | solution.py:400
  36.8 6.8 %collective-permute-start = (bf16[1,8,16,128]{3,2,1,0:T(8,128)(2,1)S(1)}, bf16[1,8,16,128]{3,2,1,0:T(8,128)(2,1)S(1)}, u32[]{:S(2)}, u32[]{:S(2)}) collective-permute-start(bf16[1,8,16,128]{3,2,1,0:T(8,128)(2,1)S(1)} %get-tuple-element.44), channel_id=1, source_target_pairs={{0,32},{32,0},{1,33},{33,1},{2,34},{34,2},{3,35},{35,3},{4,36},{36... | collective-permute-start | bytes 98312 | tf_op jit(solution)/shard_map/ppermute | solution.py:408
  42.2 3.3 %collective-permute-start.1 = (bf16[1,8,16,128]{3,2,1,0:T(8,128)(2,1)S(1)}, bf16[1,8,16,128]{3,2,1,0:T(8,128)(2,1)S(1)}, u32[]{:S(2)}, u32[]{:S(2)}) collective-permute-start(bf16[1,8,16,128]{3,2,1,0:T(8,128)(2,1)S(1)} %get-tuple-element.45), channel_id=1, source_target_pairs={{32,64},{96,128},{160,192},{224,0},{64,32},{128,96},{192,160},{0,2... | collective-permute-start | bytes 98312 | tf_op jit(solution)/shard_map/ppermute | solution.py:386
  45.6 5.0 %collective-permute-start.2 = (bf16[6,1,16,128]{3,2,1,0:T(8,128)(2,1)S(1)}, bf16[6,1,16,128]{3,2,1,0:T(8,128)(2,1)S(1)}, u32[]{:S(2)}, u32[]{:S(2)}) collective-permute-start(bf16[6,1,16,128]{3,2,1,0:T(8,128)(2,1)S(1)} %get-tuple-element.48), channel_id=1, source_target_pairs={{0,1},{2,3},{4,5},{6,7},{8,9},{10,11},{12,13},{14,15},{16,17},{18,... | collective-permute-start | bytes 73736 | tf_op jit(solution)/shard_map/ppermute | solution.py:394
  46.9 3.7 %collective-permute-start.3 = (bf16[6,1,16,128]{3,2,1,0:T(8,128)(2,1)S(1)}, bf16[6,1,16,128]{3,2,1,0:T(8,128)(2,1)S(1)}, u32[]{:S(2)}, u32[]{:S(2)}) collective-permute-start(bf16[6,1,16,128]{3,2,1,0:T(8,128)(2,1)S(1)} %get-tuple-element.49), channel_id=1, source_target_pairs={{1,2},{3,4},{5,6},{7,8},{9,10},{11,12},{13,14},{15,16},{17,18},{19... | collective-permute-start | bytes 73736 | tf_op jit(solution)/shard_map/ppermute | solution.py:395
  51.5 1.9 %collective-permute-start.4 = (bf16[14,128,128]{2,1,0:T(8,128)(2,1)S(1)}, bf16[14,128,128]{2,1,0:T(8,128)(2,1)S(1)}, u32[]{:S(2)}, u32[]{:S(2)}) collective-permute-start(bf16[14,128,128]{2,1,0:T(8,128)(2,1)S(1)} %get-tuple-element.55), channel_id=1, source_target_pairs={{0,32},{32,0},{1,33},{33,1},{2,34},{34,2},{3,35},{35,3},{4,36},{36... | collective-permute-start | bytes 1376264 | tf_op jit(solution)/shard_map/ppermute | solution.py:408
  54.4 27.4 %all-to-all-start.1 = ((bf16[32,104,128]{2,1,0:T(8,128)(2,1)}), bf16[32,104,128]{2,1,0:T(8,128)(2,1)S(1)}, u32[]{:S(2)}, u32[]{:S(2)}) async-start(bf16[32,104,128]{2,1,0:T(8,128)(2,1)} %shard_map.120), calls=%async_computation.1 | async-start | bytes 1703936 | tf_op jit(solution)/shard_map/all_to_all | solution.py:400
  60.9 1.6 %collective-permute-start.5 = (bf16[1,8,16,128]{3,2,1,0:T(8,128)(2,1)S(1)}, bf16[1,8,16,128]{3,2,1,0:T(8,128)(2,1)S(1)}, u32[]{:S(2)}, u32[]{:S(2)}) collective-permute-start(bf16[1,8,16,128]{3,2,1,0:T(8,128)(2,1)S(1)} %get-tuple-element.58), channel_id=1, source_target_pairs={{0,32},{32,0},{1,33},{33,1},{2,34},{34,2},{3,35},{35,3},{4,36},{36... | collective-permute-start | bytes 98312 | tf_op jit(solution)/shard_map/ppermute | solution.py:408
  61.6 3.3 %collective-permute-start.6 = (bf16[1,8,16,128]{3,2,1,0:T(8,128)(2,1)S(1)}, bf16[1,8,16,128]{3,2,1,0:T(8,128)(2,1)S(1)}, u32[]{:S(2)}, u32[]{:S(2)}) collective-permute-start(bf16[1,8,16,128]{3,2,1,0:T(8,128)(2,1)S(1)} %get-tuple-element.59), channel_id=1, source_target_pairs={{32,64},{96,128},{160,192},{224,0},{64,32},{128,96},{192,160},{0,2... | collective-permute-start | bytes 98312 | tf_op jit(solution)/shard_map/ppermute | solution.py:386
  65.0 15.2 %collective-permute-start.7 = (bf16[6,1,16,128]{3,2,1,0:T(8,128)(2,1)S(1)}, bf16[6,1,16,128]{3,2,1,0:T(8,128)(2,1)S(1)}, u32[]{:S(2)}, u32[]{:S(2)}) collective-permute-start(bf16[6,1,16,128]{3,2,1,0:T(8,128)(2,1)S(1)} %get-tuple-element.61), channel_id=1, source_target_pairs={{0,1},{2,3},{4,5},{6,7},{8,9},{10,11},{12,13},{14,15},{16,17},{18,... | collective-permute-start | bytes 73736 | tf_op jit(solution)/shard_map/ppermute | solution.py:394
  66.8 13.4 %collective-permute-start.8 = (bf16[6,1,16,128]{3,2,1,0:T(8,128)(2,1)S(1)}, bf16[6,1,16,128]{3,2,1,0:T(8,128)(2,1)S(1)}, u32[]{:S(2)}, u32[]{:S(2)}) collective-permute-start(bf16[6,1,16,128]{3,2,1,0:T(8,128)(2,1)S(1)} %get-tuple-element.62), channel_id=1, source_target_pairs={{1,2},{3,4},{5,6},{7,8},{9,10},{11,12},{13,14},{15,16},{17,18},{19... | collective-permute-start | bytes 73736 | tf_op jit(solution)/shard_map/ppermute | solution.py:395
  81.9 5.4 %collective-permute-start.11 = (bf16[56,128]{1,0:T(8,128)(2,1)S(1)}, bf16[56,128]{1,0:T(8,128)(2,1)S(1)}, u32[]{:S(2)}, u32[]{:S(2)}) collective-permute-start(bf16[56,128]{1,0:T(8,128)(2,1)S(1)} %shard_map.123.own_ref), channel_id=1, source_target_pairs={{0,192},{64,128},{128,64},{192,0},{1,193},{65,129},{129,65},{193,1... | collective-permute-start | bytes 43016 | tf_op jit(solution)/shard_map/ppermute | solution.py:404
  84.2 4.1 %collective-permute-start.10 = (bf16[56,128]{1,0:T(8,128)(2,1)S(1)}, bf16[56,128]{1,0:T(8,128)(2,1)S(1)}, u32[]{:S(2)}, u32[]{:S(2)}) collective-permute-start(bf16[56,128]{1,0:T(8,128)(2,1)S(1)} %shard_map.123.own_ref), channel_id=1, source_target_pairs={{0,128},{64,192},{128,0},{192,64},{1,129},{65,193},{129,1},{193,65... | collective-permute-start | bytes 43016 | tf_op jit(solution)/shard_map/ppermute | solution.py:404
  84.2 4.1 %collective-permute-start.9 = (bf16[56,128]{1,0:T(8,128)(2,1)S(1)}, bf16[56,128]{1,0:T(8,128)(2,1)S(1)}, u32[]{:S(2)}, u32[]{:S(2)}) collective-permute-start(bf16[56,128]{1,0:T(8,128)(2,1)S(1)} %shard_map.123.own_ref), channel_id=1, source_target_pairs={{0,64},{64,0},{128,192},{192,128},{1,65},{65,1},{129,193},{193,129... | collective-permute-start | bytes 43016 | tf_op jit(solution)/shard_map/ppermute | solution.py:404
  87.3 10.1 %copy-start.4 = (s32[512,1]{0,1:T(1,128)S(1)}, s32[512,1]{0,1:T(1,128)}, u32[]{:S(2)}) copy-start(s32[512,1]{0,1:T(1,128)} %param.9) | copy-start | bytes 6148
  89.3 26.1 %all-to-all-start.2 = ((bf16[32,104,128]{2,1,0:T(8,128)(2,1)}), bf16[32,104,128]{2,1,0:T(8,128)(2,1)S(1)}, u32[]{:S(2)}, u32[]{:S(2)}) async-start(bf16[32,104,128]{2,1,0:T(8,128)(2,1)} %shard_map.125), calls=%async_computation.2 | async-start | bytes 1703936 | tf_op jit(solution)/shard_map/all_to_all | solution.py:400
  115.4 8.9 %collective-permute-start.12 = (bf16[14,128,128]{2,1,0:T(8,128)(2,1)S(1)}, bf16[14,128,128]{2,1,0:T(8,128)(2,1)S(1)}, u32[]{:S(2)}, u32[]{:S(2)}) collective-permute-start(bf16[14,128,128]{2,1,0:T(8,128)(2,1)S(1)} %shard_map.127.mine_ref), channel_id=1, source_target_pairs={{0,32},{32,0},{1,33},{33,1},{2,34},{34,2},{3,35},{35,3},{4,36},{36... | collective-permute-start | bytes 1376264 | tf_op jit(solution)/shard_map/ppermute | solution.py:408

commit v8 on v7

--- a/solution.py
+++ b/solution.py
@@ -70,14 +70,14 @@
 
 
 def pack_kernel(feat_hbm, cot_hbm, slab_hbm, base_hbm, near_hbm, off_hbm, sent_hbm,
-                both_ref, slab_ref, base_ref, near_ref, off_ref, sent_ref, sems, out_sems):
+                feat_ref, cot_ref, slab_ref, base_ref, near_ref, off_ref, sent_ref, sems, out_sems):
     moves = [
         pltpu.make_async_copy(slab_hbm, slab_ref, sems.at[0]),
         pltpu.make_async_copy(base_hbm, base_ref, sems.at[1]),
         pltpu.make_async_copy(near_hbm, near_ref, sems.at[2]),
         pltpu.make_async_copy(off_hbm, off_ref, sems.at[3]),
-        pltpu.make_async_copy(feat_hbm, both_ref.at[:, 0:C], sems.at[4]),
-        pltpu.make_async_copy(cot_hbm, both_ref.at[:, C : 2 * C], sems.at[5]),
+        pltpu.make_async_copy(feat_hbm, feat_ref, sems.at[4]),
+        pltpu.make_async_copy(cot_hbm, cot_ref, sems.at[5]),
     ]
     for move in moves:
         move.start()
@@ -96,8 +96,8 @@
     ).astype(BF)
     moves[4].wait()
     moves[5].wait()
-    both = both_ref[...]
-    group = 8
+    both = jnp.concatenate([feat_ref[...], cot_ref[...]], axis=1)
+    group = 4
     sends = []
     for g in range(GY // group):
         span = group * CAP
@@ -422,14 +422,15 @@
         sds((GY, 2 * CAP + KINDS, C), BF),
         (features, cotangent, slab, base_cell.reshape(1, PTS), nearest.reshape(1, PTS), offsets),
         scratch=(
-            pltpu.VMEM((PTS, 2 * C), BF),
+            pltpu.VMEM((PTS, C), BF),
+            pltpu.VMEM((PTS, C), BF),
             line,
             line,
             line,
             pltpu.VMEM((3, PTS), BF),
             pltpu.VMEM((GY, 2 * CAP + KINDS, C), BF),
             pltpu.SemaphoreType.DMA((6,)),
-            pltpu.SemaphoreType.DMA((4,)),
+            pltpu.SemaphoreType.DMA((8,)),
         ),
         hbm=6,
         mib=60,

time: 126 us -> 126 us (level)
  transfers between devices with their start and end apart: 16 -> 16, of which waited for: 10 -> 10; matrix products, arithmetic and copies ran while one was open for 0% -> 0% of each run, Pallas kernels for 6% -> 7%
where the time goes in v8:
time: 126 us
  waiting for transfers between devices  57 us (45%)
  starting transfers between devices  51.4 us (41%)
  Pallas kernels  16.3 us (13%)
    all_to_all x3, waiting for transfers between devices, exchange(): lax.all_to_all(rows, ('x', 'z'), split_axis=0, concat_axis=0, tiled=True)  38 us
    all_to_all x3, starting transfers between devices, exchange(): lax.all_to_all(rows, ('x', 'z'), split_axis=0, concat_axis=0, tiled=True)  26.6 us
    pallas_call x18, Pallas kernels, call(): pl.pallas_call(kernel, out_shape=out_shape, in_specs=[SMEM] * smem + [HBM...  16.3 us
    ppermute x4, starting transfers between devices, swap(): return lax.ppermute(half, 'c', [(0, 1), (1, 0)])  14.1 us
    ppermute x2, waiting for transfers between devices, edges(): lax.ppermute(even, ('x', 'z'), pairs(GY, 0))  12 us
    ppermute x2, waiting for transfers between devices, chips(): return lax.ppermute(face, ('y', 'c'), pairs(GX, 1))  4.54 us
    ppermute x3, starting transfers between devices, across(): return lax.ppermute(share, 'y', list(enumerate(partner)))  3.34 us
    ppermute x2, starting transfers between devices, edges(): lax.ppermute(even, ('x', 'z'), pairs(GY, 0))  3.09 us
  transfers between devices with their start and end apart: 16, of which 10 were waited for; matrix products, arithmetic and copies ran while one was open for 0% of the time, Pallas kernels for 7%

profile of v8, /device:TPU:1, one launch (start us, length us, event | category | flops | bytes accessed | tf_op | source)
XLA Modules:
  0.0 125.7 jit_solution(15542035623960399856)
XLA Ops:
  0.7 2.9 %shard_map.111 = bf16[32,104,128]{2,1,0:T(8,128)(2,1)} custom-call(bf16[512,128]{1,0:T(8,128)(2,1)} %feat_ref.3, bf16[512,128]{1,0:T(8,128)(2,1)} %cot_ref.3, s32[1,512]{1,0:T(1,128)} %bitcast.4, s32[1,512]{1,0:T(1,128)} %bitcast.6, s32[1,512]{1,0:T(1,128)} %bitcast.7, bf16[3,512]{1,0:T(4,128)(2,1)} %off_hbm.1), custom_call_target="tpu_custom_call" | custom-call | tf_op jit(solution)/shard_map/pallas_call | solution.py:38
  3.7 12.0 %all-to-all-start = ((bf16[32,104,128]{2,1,0:T(8,128)(2,1)}), bf16[32,104,128]{2,1,0:T(8,128)(2,1)S(1)}, u32[]{:S(2)}, u32[]{:S(2)}) async-start(bf16[32,104,128]{2,1,0:T(8,128)(2,1)} %shard_map.111), calls=%async_computation | async-start | bytes 1703936 | tf_op jit(solution)/shard_map/all_to_all | solution.py:400
  16.1 19.9 %all-to-all-done.got_ref = bf16[32,104,128]{2,1,0:T(8,128)(2,1)S(1)} async-done(((bf16[32,104,128]{2,1,0:T(8,128)(2,1)}), bf16[32,104,128]{2,1,0:T(8,128)(2,1)S(1)}, u32[]{:S(2)}, u32[]{:S(2)}) %all-to-all-start) | async-done | bytes 852000 | tf_op jit(solution)/shard_map/all_to_all | solution.py:400
  36.7 5.5 %collective-permute-start = (bf16[1,8,16,128]{3,2,1,0:T(8,128)(2,1)S(1)}, bf16[1,8,16,128]{3,2,1,0:T(8,128)(2,1)S(1)}, u32[]{:S(2)}, u32[]{:S(2)}) collective-permute-start(bf16[1,8,16,128]{3,2,1,0:T(8,128)(2,1)S(1)} %get-tuple-element.44), channel_id=1, source_target_pairs={{0,32},{32,0},{1,33},{33,1},{2,34},{34,2},{3,35},{35,3},{4,36},{36... | collective-permute-start | bytes 98312 | tf_op jit(solution)/shard_map/ppermute | solution.py:408
  42.2 1.3 %collective-permute-start.1 = (bf16[1,8,16,128]{3,2,1,0:T(8,128)(2,1)S(1)}, bf16[1,8,16,128]{3,2,1,0:T(8,128)(2,1)S(1)}, u32[]{:S(2)}, u32[]{:S(2)}) collective-permute-start(bf16[1,8,16,128]{3,2,1,0:T(8,128)(2,1)S(1)} %get-tuple-element.45), channel_id=1, source_target_pairs={{32,64},{96,128},{160,192},{224,0},{64,32},{128,96},{192,160},{0,2... | collective-permute-start | bytes 98312 | tf_op jit(solution)/shard_map/ppermute | solution.py:386
  43.5 2.1 %collective-permute-done.1.far_ref = bf16[1,8,16,128]{3,2,1,0:T(8,128)(2,1)S(1)} collective-permute-done((bf16[1,8,16,128]{3,2,1,0:T(8,128)(2,1)S(1)}, bf16[1,8,16,128]{3,2,1,0:T(8,128)(2,1)S(1)}, u32[]{:S(2)}, u32[]{:S(2)}) %collective-permute-start.1) | collective-permute-done | bytes 32800 | tf_op jit(solution)/shard_map/ppermute | solution.py:386
  45.5 1.3 %collective-permute-start.2 = (bf16[6,1,16,128]{3,2,1,0:T(8,128)(2,1)S(1)}, bf16[6,1,16,128]{3,2,1,0:T(8,128)(2,1)S(1)}, u32[]{:S(2)}, u32[]{:S(2)}) collective-permute-start(bf16[6,1,16,128]{3,2,1,0:T(8,128)(2,1)S(1)} %get-tuple-element.48), channel_id=1, source_target_pairs={{0,1},{2,3},{4,5},{6,7},{8,9},{10,11},{12,13},{14,15},{16,17},{18,... | collective-permute-start | bytes 73736 | tf_op jit(solution)/shard_map/ppermute | solution.py:394
  46.9 1.7 %collective-permute-start.3 = (bf16[6,1,16,128]{3,2,1,0:T(8,128)(2,1)S(1)}, bf16[6,1,16,128]{3,2,1,0:T(8,128)(2,1)S(1)}, u32[]{:S(2)}, u32[]{:S(2)}) collective-permute-start(bf16[6,1,16,128]{3,2,1,0:T(8,128)(2,1)S(1)} %get-tuple-element.49), channel_id=1, source_target_pairs={{1,2},{3,4},{5,6},{7,8},{9,10},{11,12},{13,14},{15,16},{17,18},{19... | collective-permute-start | bytes 73736 | tf_op jit(solution)/shard_map/ppermute | solution.py:395
  49.4 1.2 shard_map.114
  54.4 6.5 %all-to-all-start.1 = ((bf16[32,104,128]{2,1,0:T(8,128)(2,1)}), bf16[32,104,128]{2,1,0:T(8,128)(2,1)S(1)}, u32[]{:S(2)}, u32[]{:S(2)}) async-start(bf16[32,104,128]{2,1,0:T(8,128)(2,1)} %shard_map.120), calls=%async_computation.1 | async-start | bytes 1703936 | tf_op jit(solution)/shard_map/all_to_all | solution.py:400
  62.5 2.5 %collective-permute-done.6.far_ref = bf16[1,8,16,128]{3,2,1,0:T(8,128)(2,1)S(1)} collective-permute-done((bf16[1,8,16,128]{3,2,1,0:T(8,128)(2,1)S(1)}, bf16[1,8,16,128]{3,2,1,0:T(8,128)(2,1)S(1)}, u32[]{:S(2)}, u32[]{:S(2)}) %collective-permute-start.6) | collective-permute-done | bytes 32800 | tf_op jit(solution)/shard_map/ppermute | solution.py:386
  65.0 1.8 %collective-permute-start.7 = (bf16[6,1,16,128]{3,2,1,0:T(8,128)(2,1)S(1)}, bf16[6,1,16,128]{3,2,1,0:T(8,128)(2,1)S(1)}, u32[]{:S(2)}, u32[]{:S(2)}) collective-permute-start(bf16[6,1,16,128]{3,2,1,0:T(8,128)(2,1)S(1)} %get-tuple-element.61), channel_id=1, source_target_pairs={{0,1},{2,3},{4,5},{6,7},{8,9},{10,11},{12,13},{14,15},{16,17},{18,... | collective-permute-start | bytes 73736 | tf_op jit(solution)/shard_map/ppermute | solution.py:394
  66.7 1.4 %collective-permute-start.8 = (bf16[6,1,16,128]{3,2,1,0:T(8,128)(2,1)S(1)}, bf16[6,1,16,128]{3,2,1,0:T(8,128)(2,1)S(1)}, u32[]{:S(2)}, u32[]{:S(2)}) collective-permute-start(bf16[6,1,16,128]{3,2,1,0:T(8,128)(2,1)S(1)} %get-tuple-element.62), channel_id=1, source_target_pairs={{1,2},{3,4},{5,6},{7,8},{9,10},{11,12},{13,14},{15,16},{17,18},{19... | collective-permute-start | bytes 73736 | tf_op jit(solution)/shard_map/ppermute | solution.py:395
  68.1 12.0 %collective-permute-done.7.even_ref = bf16[6,1,16,128]{3,2,1,0:T(8,128)(2,1)S(1)} collective-permute-done((bf16[6,1,16,128]{3,2,1,0:T(8,128)(2,1)S(1)}, bf16[6,1,16,128]{3,2,1,0:T(8,128)(2,1)S(1)}, u32[]{:S(2)}, u32[]{:S(2)}) %collective-permute-start.7) | collective-permute-done | bytes 24608 | tf_op jit(solution)/shard_map/ppermute | solution.py:394
  80.1 1.7 %all-to-all-done.1.got_ref = bf16[32,104,128]{2,1,0:T(8,128)(2,1)S(1)} async-done(((bf16[32,104,128]{2,1,0:T(8,128)(2,1)}), bf16[32,104,128]{2,1,0:T(8,128)(2,1)S(1)}, u32[]{:S(2)}, u32[]{:S(2)}) %all-to-all-start.1) | async-done | bytes 852000 | tf_op jit(solution)/shard_map/all_to_all | solution.py:400
  81.9 2.1 %collective-permute-start.11 = (bf16[56,128]{1,0:T(8,128)(2,1)S(1)}, bf16[56,128]{1,0:T(8,128)(2,1)S(1)}, u32[]{:S(2)}, u32[]{:S(2)}) collective-permute-start(bf16[56,128]{1,0:T(8,128)(2,1)S(1)} %shard_map.123.own_ref), channel_id=1, source_target_pairs={{0,192},{64,128},{128,64},{192,0},{1,193},{65,129},{129,65},{193,1... | collective-permute-start | bytes 43016 | tf_op jit(solution)/shard_map/ppermute | solution.py:404
  84.0 1.2 collective-permute-start.9
  85.2 1.9 %shard_map.124.filled_ref = bf16[32,48,128]{2,1,0:T(8,128)(2,1)S(1)} custom-call(s32[1]{0:T(128)} %bitcast.spot_ref, bf16[4,8,16,128]{3,2,1,0:T(8,128)(2,1)S(1)} %get-tuple-element.60.own_ref.hid_ref, bf16[1,8,16,128]{3,2,1,0:T(8,128)(2,1)S(1)} %collective-permute-done.5.near_ref, bf16[1,8,16,128]{3,2,1,0:T(8,128)(2,1)S(1)} %collective-permute-done.6.far_ref, ...), custom_call_target="tpu_custom_call" | custom-call | tf_op jit(solution)/shard_map/pallas_call | solution.py:38
  89.1 8.1 %all-to-all-start.2 = ((bf16[32,104,128]{2,1,0:T(8,128)(2,1)}), bf16[32,104,128]{2,1,0:T(8,128)(2,1)S(1)}, u32[]{:S(2)}, u32[]{:S(2)}) async-start(bf16[32,104,128]{2,1,0:T(8,128)(2,1)} %shard_map.125), calls=%async_computation.2 | async-start | bytes 1703936 | tf_op jit(solution)/shard_map/all_to_all | solution.py:400
  97.2 1.5 %shard_map.122 = (bf16[512,128]{1,0:T(8,128)(2,1)}, s32[512,128]{1,0:T(8,128)S(1)}, f32[512,128]{1,0:T(8,128)S(1)}) custom-call(bf16[32,104,128]{2,1,0:T(8,128)(2,1)S(1)} %all-to-all-done.1.got_ref, s32[1,512]{1,0:T(1,128)S(1)} %bitcast.5, bf16[512,128]{1,0:T(8,128)(2,1)S(1)} %copy-done.1, bf16[512,128]{1,0:T(8,128)(2,1)S(1)} %copy-done.2, ...), custom_call_target="tpu_custom_call" | custom-call | tf_op jit(solution)/shard_map/pallas_call | solution.py:38
  98.7 16.5 %all-to-all-done.2.got_ref = bf16[32,104,128]{2,1,0:T(8,128)(2,1)S(1)} async-done(((bf16[32,104,128]{2,1,0:T(8,128)(2,1)}), bf16[32,104,128]{2,1,0:T(8,128)(2,1)S(1)}, u32[]{:S(2)}, u32[]{:S(2)}) %all-to-all-start.2) | async-done | bytes 852000 | tf_op jit(solution)/shard_map/all_to_all | solution.py:400
  115.2 7.5 %collective-permute-start.12 = (bf16[14,128,128]{2,1,0:T(8,128)(2,1)S(1)}, bf16[14,128,128]{2,1,0:T(8,128)(2,1)S(1)}, u32[]{:S(2)}, u32[]{:S(2)}) collective-permute-start(bf16[14,128,128]{2,1,0:T(8,128)(2,1)S(1)} %shard_map.127.mine_ref), channel_id=1, source_target_pairs={{0,32},{32,0},{1,33},{33,1},{2,34},{34,2},{3,35},{35,3},{4,36},{36... | collective-permute-start | bytes 1376264 | tf_op jit(solution)/shard_map/ppermute | solution.py:408
  122.7 1.2 shard_map.126
  124.1 1.5 %shard_map.128 = (f32[27,128,128]{2,1,0:T(8,128)}, f32[128,128]{1,0:T(8,128)}) custom-call(s32[1]{0:T(128)} %bitcast.spot_ref, bf16[14,128,128]{2,1,0:T(8,128)(2,1)S(1)} %shard_map.127.mine_ref, bf16[14,128,128]{2,1,0:T(8,128)(2,1)S(1)} %collective-permute-done.12.other_ref), custom_call_target="tpu_custom_call" | custom-call | tf_op jit(solution)/shard_map/pallas_call | solution.py:38
  (36 shorter events, 9.7 us)
Async XLA Ops:
  0.6 15.0 %copy-start.2 = (bf16[512,128]{1,0:T(8,128)(2,1)S(1)}, bf16[512,128]{1,0:T(8,128)(2,1)}, u32[]{:S(2)}) copy-start(bf16[512,128]{1,0:T(8,128)(2,1)} %cot_ref.3) | copy-start | bytes 393220
  0.6 15.0 %copy-start.1 = (bf16[512,128]{1,0:T(8,128)(2,1)S(1)}, bf16[512,128]{1,0:T(8,128)(2,1)}, u32[]{:S(2)}) copy-start(bf16[512,128]{1,0:T(8,128)(2,1)} %feat_ref.3) | copy-start | bytes 393220
  0.7 15.0 %copy-start.3 = (bf16[128,128]{1,0:T(8,128)(2,1)S(1)}, bf16[128,128]{1,0:T(8,128)(2,1)}, u32[]{:S(2)}) copy-start(bf16[128,128]{1,0:T(8,128)(2,1)} %mlp_ref.3) | copy-start | bytes 98308
  3.6 45.7 %copy-start = (bf16[27,128,128]{2,1,0:T(8,128)(2,1)S(1)}, bf16[27,128,128]{2,1,0:T(8,128)(2,1)}, u32[]{:S(2)}) copy-start(bf16[27,128,128]{2,1,0:T(8,128)(2,1)} %weight_ref.5) | copy-start | bytes 2654212
  3.7 32.4 %all-to-all-start = ((bf16[32,104,128]{2,1,0:T(8,128)(2,1)}), bf16[32,104,128]{2,1,0:T(8,128)(2,1)S(1)}, u32[]{:S(2)}, u32[]{:S(2)}) async-start(bf16[32,104,128]{2,1,0:T(8,128)(2,1)} %shard_map.111), calls=%async_computation | async-start | bytes 1703936 | tf_op jit(solution)/shard_map/all_to_all | solution.py:400
  36.7 6.7 %collective-permute-start = (bf16[1,8,16,128]{3,2,1,0:T(8,128)(2,1)S(1)}, bf16[1,8,16,128]{3,2,1,0:T(8,128)(2,1)S(1)}, u32[]{:S(2)}, u32[]{:S(2)}) collective-permute-start(bf16[1,8,16,128]{3,2,1,0:T(8,128)(2,1)S(1)} %get-tuple-element.44), channel_id=1, source_target_pairs={{0,32},{32,0},{1,33},{33,1},{2,34},{34,2},{3,35},{35,3},{4,36},{36... | collective-permute-start | bytes 98312 | tf_op jit(solution)/shard_map/ppermute | solution.py:408
  42.2 3.3 %collective-permute-start.1 = (bf16[1,8,16,128]{3,2,1,0:T(8,128)(2,1)S(1)}, bf16[1,8,16,128]{3,2,1,0:T(8,128)(2,1)S(1)}, u32[]{:S(2)}, u32[]{:S(2)}) collective-permute-start(bf16[1,8,16,128]{3,2,1,0:T(8,128)(2,1)S(1)} %get-tuple-element.45), channel_id=1, source_target_pairs={{32,64},{96,128},{160,192},{224,0},{64,32},{128,96},{192,160},{0,2... | collective-permute-start | bytes 98312 | tf_op jit(solution)/shard_map/ppermute | solution.py:386
  45.5 5.0 %collective-permute-start.2 = (bf16[6,1,16,128]{3,2,1,0:T(8,128)(2,1)S(1)}, bf16[6,1,16,128]{3,2,1,0:T(8,128)(2,1)S(1)}, u32[]{:S(2)}, u32[]{:S(2)}) collective-permute-start(bf16[6,1,16,128]{3,2,1,0:T(8,128)(2,1)S(1)} %get-tuple-element.48), channel_id=1, source_target_pairs={{0,1},{2,3},{4,5},{6,7},{8,9},{10,11},{12,13},{14,15},{16,17},{18,... | collective-permute-start | bytes 73736 | tf_op jit(solution)/shard_map/ppermute | solution.py:394
  46.9 3.7 %collective-permute-start.3 = (bf16[6,1,16,128]{3,2,1,0:T(8,128)(2,1)S(1)}, bf16[6,1,16,128]{3,2,1,0:T(8,128)(2,1)S(1)}, u32[]{:S(2)}, u32[]{:S(2)}) collective-permute-start(bf16[6,1,16,128]{3,2,1,0:T(8,128)(2,1)S(1)} %get-tuple-element.49), channel_id=1, source_target_pairs={{1,2},{3,4},{5,6},{7,8},{9,10},{11,12},{13,14},{15,16},{17,18},{19... | collective-permute-start | bytes 73736 | tf_op jit(solution)/shard_map/ppermute | solution.py:395
  51.5 1.9 %collective-permute-start.4 = (bf16[14,128,128]{2,1,0:T(8,128)(2,1)S(1)}, bf16[14,128,128]{2,1,0:T(8,128)(2,1)S(1)}, u32[]{:S(2)}, u32[]{:S(2)}) collective-permute-start(bf16[14,128,128]{2,1,0:T(8,128)(2,1)S(1)} %get-tuple-element.55), channel_id=1, source_target_pairs={{0,32},{32,0},{1,33},{33,1},{2,34},{34,2},{3,35},{35,3},{4,36},{36... | collective-permute-start | bytes 1376264 | tf_op jit(solution)/shard_map/ppermute | solution.py:408
  54.4 27.4 %all-to-all-start.1 = ((bf16[32,104,128]{2,1,0:T(8,128)(2,1)}), bf16[32,104,128]{2,1,0:T(8,128)(2,1)S(1)}, u32[]{:S(2)}, u32[]{:S(2)}) async-start(bf16[32,104,128]{2,1,0:T(8,128)(2,1)} %shard_map.120), calls=%async_computation.1 | async-start | bytes 1703936 | tf_op jit(solution)/shard_map/all_to_all | solution.py:400
  60.9 1.6 %collective-permute-start.5 = (bf16[1,8,16,128]{3,2,1,0:T(8,128)(2,1)S(1)}, bf16[1,8,16,128]{3,2,1,0:T(8,128)(2,1)S(1)}, u32[]{:S(2)}, u32[]{:S(2)}) collective-permute-start(bf16[1,8,16,128]{3,2,1,0:T(8,128)(2,1)S(1)} %get-tuple-element.58), channel_id=1, source_target_pairs={{0,32},{32,0},{1,33},{33,1},{2,34},{34,2},{3,35},{35,3},{4,36},{36... | collective-permute-start | bytes 98312 | tf_op jit(solution)/shard_map/ppermute | solution.py:408
  61.6 3.3 %collective-permute-start.6 = (bf16[1,8,16,128]{3,2,1,0:T(8,128)(2,1)S(1)}, bf16[1,8,16,128]{3,2,1,0:T(8,128)(2,1)S(1)}, u32[]{:S(2)}, u32[]{:S(2)}) collective-permute-start(bf16[1,8,16,128]{3,2,1,0:T(8,128)(2,1)S(1)} %get-tuple-element.59), channel_id=1, source_target_pairs={{32,64},{96,128},{160,192},{224,0},{64,32},{128,96},{192,160},{0,2... | collective-permute-start | bytes 98312 | tf_op jit(solution)/shard_map/ppermute | solution.py:386
  65.0 15.2 %collective-permute-start.7 = (bf16[6,1,16,128]{3,2,1,0:T(8,128)(2,1)S(1)}, bf16[6,1,16,128]{3,2,1,0:T(8,128)(2,1)S(1)}, u32[]{:S(2)}, u32[]{:S(2)}) collective-permute-start(bf16[6,1,16,128]{3,2,1,0:T(8,128)(2,1)S(1)} %get-tuple-element.61), channel_id=1, source_target_pairs={{0,1},{2,3},{4,5},{6,7},{8,9},{10,11},{12,13},{14,15},{16,17},{18,... | collective-permute-start | bytes 73736 | tf_op jit(solution)/shard_map/ppermute | solution.py:394
  66.7 13.4 %collective-permute-start.8 = (bf16[6,1,16,128]{3,2,1,0:T(8,128)(2,1)S(1)}, bf16[6,1,16,128]{3,2,1,0:T(8,128)(2,1)S(1)}, u32[]{:S(2)}, u32[]{:S(2)}) collective-permute-start(bf16[6,1,16,128]{3,2,1,0:T(8,128)(2,1)S(1)} %get-tuple-element.62), channel_id=1, source_target_pairs={{1,2},{3,4},{5,6},{7,8},{9,10},{11,12},{13,14},{15,16},{17,18},{19... | collective-permute-start | bytes 73736 | tf_op jit(solution)/shard_map/ppermute | solution.py:395
  81.9 5.2 %collective-permute-start.11 = (bf16[56,128]{1,0:T(8,128)(2,1)S(1)}, bf16[56,128]{1,0:T(8,128)(2,1)S(1)}, u32[]{:S(2)}, u32[]{:S(2)}) collective-permute-start(bf16[56,128]{1,0:T(8,128)(2,1)S(1)} %shard_map.123.own_ref), channel_id=1, source_target_pairs={{0,192},{64,128},{128,64},{192,0},{1,193},{65,129},{129,65},{193,1... | collective-permute-start | bytes 43016 | tf_op jit(solution)/shard_map/ppermute | solution.py:404
  84.0 4.1 %collective-permute-start.10 = (bf16[56,128]{1,0:T(8,128)(2,1)S(1)}, bf16[56,128]{1,0:T(8,128)(2,1)S(1)}, u32[]{:S(2)}, u32[]{:S(2)}) collective-permute-start(bf16[56,128]{1,0:T(8,128)(2,1)S(1)} %shard_map.123.own_ref), channel_id=1, source_target_pairs={{0,128},{64,192},{128,0},{192,64},{1,129},{65,193},{129,1},{193,65... | collective-permute-start | bytes 43016 | tf_op jit(solution)/shard_map/ppermute | solution.py:404
  84.0 4.1 %collective-permute-start.9 = (bf16[56,128]{1,0:T(8,128)(2,1)S(1)}, bf16[56,128]{1,0:T(8,128)(2,1)S(1)}, u32[]{:S(2)}, u32[]{:S(2)}) collective-permute-start(bf16[56,128]{1,0:T(8,128)(2,1)S(1)} %shard_map.123.own_ref), channel_id=1, source_target_pairs={{0,64},{64,0},{128,192},{192,128},{1,65},{65,1},{129,193},{193,129... | collective-permute-start | bytes 43016 | tf_op jit(solution)/shard_map/ppermute | solution.py:404
  87.1 10.1 %copy-start.4 = (s32[512,1]{0,1:T(1,128)S(1)}, s32[512,1]{0,1:T(1,128)}, u32[]{:S(2)}) copy-start(s32[512,1]{0,1:T(1,128)} %param.9) | copy-start | bytes 6148
  89.1 26.1 %all-to-all-start.2 = ((bf16[32,104,128]{2,1,0:T(8,128)(2,1)}), bf16[32,104,128]{2,1,0:T(8,128)(2,1)S(1)}, u32[]{:S(2)}, u32[]{:S(2)}) async-start(bf16[32,104,128]{2,1,0:T(8,128)(2,1)} %shard_map.125), calls=%async_computation.2 | async-start | bytes 1703936 | tf_op jit(solution)/shard_map/all_to_all | solution.py:400
  115.2 8.9 %collective-permute-start.12 = (bf16[14,128,128]{2,1,0:T(8,128)(2,1)S(1)}, bf16[14,128,128]{2,1,0:T(8,128)(2,1)S(1)}, u32[]{:S(2)}, u32[]{:S(2)}) collective-permute-start(bf16[14,128,128]{2,1,0:T(8,128)(2,1)S(1)} %shard_map.127.mine_ref), channel_id=1, source_target_pairs={{0,32},{32,0},{1,33},{33,1},{2,34},{34,2},{3,35},{35,3},{4,36},{36... | collective-permute-start | bytes 1376264 | tf_op jit(solution)/shard_map/ppermute | solution.py:408

commit v9 on v8

--- a/solution.py
+++ b/solution.py
@@ -447,6 +447,10 @@
         smem=1,
     )
     near, far = swap(near), chips(far)
+    matrix, grad_out = call(
+        spread_kernel, (sds((CELLS, SLOTS), BF), sds((CELLS, C), F32)), (got, meta)
+    )
+    near, far, matrix, grad_out = lax.optimization_barrier((near, far, matrix, grad_out))
     even, odd = edges(spot, near, voxels, far)
     spread = sds((VX + 2, VY + 2, Z, 3 * C), BF)
     inner, hidden = call(
@@ -454,9 +458,6 @@
         (spread, sds((VX, VY, Z, C), F32)),
         (spot, voxels, near, far, conv_weight),
         smem=1,
-    )
-    matrix, grad_out = call(
-        spread_kernel, (sds((CELLS, SLOTS), BF), sds((CELLS, C), F32)), (got, meta)
     )
     wide = pltpu.VMEM((VX + 2, VY + 2, Z, 3 * C), BF)
     block = sds((GY, ROWS, C), BF)

time: 126 us -> 126 us (level)
  waiting for transfers between devices: 57 us -> 55.5 us
where the time goes in v9:
time: 126 us; the launch traced here: 125 us
  waiting for transfers between devices  55.5 us (44%)
  starting transfers between devices  52.4 us (42%)
  Pallas kernels  16.3 us (13%)
    all_to_all x3, waiting for transfers between devices, exchange(): lax.all_to_all(rows, ('x', 'z'), split_axis=0, concat_axis=0, tiled=True)  38.1 us
    all_to_all x3, starting transfers between devices, exchange(): lax.all_to_all(rows, ('x', 'z'), split_axis=0, concat_axis=0, tiled=True)  26.8 us
    pallas_call x18, Pallas kernels, call(): pl.pallas_call(kernel, out_shape=out_shape, in_specs=[SMEM] * smem + [HBM...  16.3 us
    ppermute x4, starting transfers between devices, swap(): return lax.ppermute(half, 'c', [(0, 1), (1, 0)])  14.8 us
    ppermute x2, waiting for transfers between devices, edges(): lax.ppermute(even, ('x', 'z'), pairs(GY, 0))  12 us
    ppermute x2, waiting for transfers between devices, chips(): return lax.ppermute(face, ('y', 'c'), pairs(GX, 1))  3.71 us
    ppermute x3, starting transfers between devices, across(): return lax.ppermute(share, 'y', list(enumerate(partner)))  3.34 us
    ppermute x2, starting transfers between devices, edges(): lax.ppermute(even, ('x', 'z'), pairs(GY, 0))  3.09 us
  transfers between devices with their start and end apart: 16, of which 10 were waited for; matrix products, arithmetic and copies ran while one was open for 0% of the time, Pallas kernels for 7%

profile of v9, /device:TPU:1, one launch (start us, length us, event | category | flops | bytes accessed | tf_op | source)
XLA Modules:
  0.0 125.1 jit_solution(9659951222173641871)
XLA Ops:
  0.7 2.9 %shard_map.111 = bf16[32,104,128]{2,1,0:T(8,128)(2,1)} custom-call(bf16[512,128]{1,0:T(8,128)(2,1)} %feat_ref.3, bf16[512,128]{1,0:T(8,128)(2,1)} %cot_ref.3, s32[1,512]{1,0:T(1,128)} %bitcast.4, s32[1,512]{1,0:T(1,128)} %bitcast.6, s32[1,512]{1,0:T(1,128)} %bitcast.7, bf16[3,512]{1,0:T(4,128)(2,1)} %off_hbm.1), custom_call_target="tpu_custom_call" | custom-call | tf_op jit(solution)/shard_map/pallas_call | solution.py:38
  3.7 12.0 %all-to-all-start = ((bf16[32,104,128]{2,1,0:T(8,128)(2,1)}), bf16[32,104,128]{2,1,0:T(8,128)(2,1)S(1)}, u32[]{:S(2)}, u32[]{:S(2)}) async-start(bf16[32,104,128]{2,1,0:T(8,128)(2,1)} %shard_map.111), calls=%async_computation | async-start | bytes 1703936 | tf_op jit(solution)/shard_map/all_to_all | solution.py:400
  16.1 19.9 %all-to-all-done.got_ref = bf16[32,104,128]{2,1,0:T(8,128)(2,1)S(1)} async-done(((bf16[32,104,128]{2,1,0:T(8,128)(2,1)}), bf16[32,104,128]{2,1,0:T(8,128)(2,1)S(1)}, u32[]{:S(2)}, u32[]{:S(2)}) %all-to-all-start) | async-done | bytes 852000 | tf_op jit(solution)/shard_map/all_to_all | solution.py:400
  36.7 5.5 %collective-permute-start = (bf16[1,8,16,128]{3,2,1,0:T(8,128)(2,1)S(1)}, bf16[1,8,16,128]{3,2,1,0:T(8,128)(2,1)S(1)}, u32[]{:S(2)}, u32[]{:S(2)}) collective-permute-start(bf16[1,8,16,128]{3,2,1,0:T(8,128)(2,1)S(1)} %get-tuple-element.48), channel_id=1, source_target_pairs={{0,32},{32,0},{1,33},{33,1},{2,34},{34,2},{3,35},{35,3},{4,36},{36... | collective-permute-start | bytes 98312 | tf_op jit(solution)/shard_map/ppermute | solution.py:408
  42.2 1.3 %collective-permute-start.1 = (bf16[1,8,16,128]{3,2,1,0:T(8,128)(2,1)S(1)}, bf16[1,8,16,128]{3,2,1,0:T(8,128)(2,1)S(1)}, u32[]{:S(2)}, u32[]{:S(2)}) collective-permute-start(bf16[1,8,16,128]{3,2,1,0:T(8,128)(2,1)S(1)} %get-tuple-element.49), channel_id=1, source_target_pairs={{32,64},{96,128},{160,192},{224,0},{64,32},{128,96},{192,160},{0,2... | collective-permute-start | bytes 98312 | tf_op jit(solution)/shard_map/ppermute | solution.py:386
  44.3 1.2 collective-permute-done.1.far_ref
  45.5 1.3 %collective-permute-start.2 = (bf16[6,1,16,128]{3,2,1,0:T(8,128)(2,1)S(1)}, bf16[6,1,16,128]{3,2,1,0:T(8,128)(2,1)S(1)}, u32[]{:S(2)}, u32[]{:S(2)}) collective-permute-start(bf16[6,1,16,128]{3,2,1,0:T(8,128)(2,1)S(1)} %get-tuple-element.57), channel_id=1, source_target_pairs={{0,1},{2,3},{4,5},{6,7},{8,9},{10,11},{12,13},{14,15},{16,17},{18,... | collective-permute-start | bytes 73736 | tf_op jit(solution)/shard_map/ppermute | solution.py:394
  46.9 1.7 %collective-permute-start.3 = (bf16[6,1,16,128]{3,2,1,0:T(8,128)(2,1)S(1)}, bf16[6,1,16,128]{3,2,1,0:T(8,128)(2,1)S(1)}, u32[]{:S(2)}, u32[]{:S(2)}) collective-permute-start(bf16[6,1,16,128]{3,2,1,0:T(8,128)(2,1)S(1)} %get-tuple-element.58), channel_id=1, source_target_pairs={{1,2},{3,4},{5,6},{7,8},{9,10},{11,12},{13,14},{15,16},{17,18},{19... | collective-permute-start | bytes 73736 | tf_op jit(solution)/shard_map/ppermute | solution.py:395
  50.6 1.2 collective-permute-start.4
  54.3 6.6 %all-to-all-start.1 = ((bf16[32,104,128]{2,1,0:T(8,128)(2,1)}), bf16[32,104,128]{2,1,0:T(8,128)(2,1)S(1)}, u32[]{:S(2)}, u32[]{:S(2)}) async-start(bf16[32,104,128]{2,1,0:T(8,128)(2,1)} %shard_map.120), calls=%async_computation.1 | async-start | bytes 1703936 | tf_op jit(solution)/shard_map/all_to_all | solution.py:400
  62.5 2.5 %collective-permute-done.6.far_ref = bf16[1,8,16,128]{3,2,1,0:T(8,128)(2,1)S(1)} collective-permute-done((bf16[1,8,16,128]{3,2,1,0:T(8,128)(2,1)S(1)}, bf16[1,8,16,128]{3,2,1,0:T(8,128)(2,1)S(1)}, u32[]{:S(2)}, u32[]{:S(2)}) %collective-permute-start.6) | collective-permute-done | bytes 32800 | tf_op jit(solution)/shard_map/ppermute | solution.py:386
  64.9 1.8 %collective-permute-start.7 = (bf16[6,1,16,128]{3,2,1,0:T(8,128)(2,1)S(1)}, bf16[6,1,16,128]{3,2,1,0:T(8,128)(2,1)S(1)}, u32[]{:S(2)}, u32[]{:S(2)}) collective-permute-start(bf16[6,1,16,128]{3,2,1,0:T(8,128)(2,1)S(1)} %get-tuple-element.69), channel_id=1, source_target_pairs={{0,1},{2,3},{4,5},{6,7},{8,9},{10,11},{12,13},{14,15},{16,17},{18,... | collective-permute-start | bytes 73736 | tf_op jit(solution)/shard_map/ppermute | solution.py:394
  66.7 1.4 %collective-permute-start.8 = (bf16[6,1,16,128]{3,2,1,0:T(8,128)(2,1)S(1)}, bf16[6,1,16,128]{3,2,1,0:T(8,128)(2,1)S(1)}, u32[]{:S(2)}, u32[]{:S(2)}) collective-permute-start(bf16[6,1,16,128]{3,2,1,0:T(8,128)(2,1)S(1)} %get-tuple-element.70), channel_id=1, source_target_pairs={{1,2},{3,4},{5,6},{7,8},{9,10},{11,12},{13,14},{15,16},{17,18},{19... | collective-permute-start | bytes 73736 | tf_op jit(solution)/shard_map/ppermute | solution.py:395
  68.1 12.0 %collective-permute-done.7.even_ref = bf16[6,1,16,128]{3,2,1,0:T(8,128)(2,1)S(1)} collective-permute-done((bf16[6,1,16,128]{3,2,1,0:T(8,128)(2,1)S(1)}, bf16[6,1,16,128]{3,2,1,0:T(8,128)(2,1)S(1)}, u32[]{:S(2)}, u32[]{:S(2)}) %collective-permute-start.7) | collective-permute-done | bytes 24608 | tf_op jit(solution)/shard_map/ppermute | solution.py:394
  80.1 1.7 %all-to-all-done.1.got_ref = bf16[32,104,128]{2,1,0:T(8,128)(2,1)S(1)} async-done(((bf16[32,104,128]{2,1,0:T(8,128)(2,1)}), bf16[32,104,128]{2,1,0:T(8,128)(2,1)S(1)}, u32[]{:S(2)}, u32[]{:S(2)}) %all-to-all-start.1) | async-done | bytes 852000 | tf_op jit(solution)/shard_map/all_to_all | solution.py:400
  81.9 1.5 %collective-permute-start.11 = (bf16[56,128]{1,0:T(8,128)(2,1)S(1)}, bf16[56,128]{1,0:T(8,128)(2,1)S(1)}, u32[]{:S(2)}, u32[]{:S(2)}) collective-permute-start(bf16[56,128]{1,0:T(8,128)(2,1)S(1)} %shard_map.123.own_ref), channel_id=1, source_target_pairs={{0,192},{64,128},{128,64},{192,0},{1,193},{65,129},{129,65},{193,1... | collective-permute-start | bytes 43016 | tf_op jit(solution)/shard_map/ppermute | solution.py:404
  83.8 1.5 %collective-permute-start.9 = (bf16[56,128]{1,0:T(8,128)(2,1)S(1)}, bf16[56,128]{1,0:T(8,128)(2,1)S(1)}, u32[]{:S(2)}, u32[]{:S(2)}) collective-permute-start(bf16[56,128]{1,0:T(8,128)(2,1)S(1)} %shard_map.123.own_ref), channel_id=1, source_target_pairs={{0,64},{64,0},{128,192},{192,128},{1,65},{65,1},{129,193},{193,129... | collective-permute-start | bytes 43016 | tf_op jit(solution)/shard_map/ppermute | solution.py:404
  85.2 1.9 %shard_map.124.filled_ref = bf16[32,48,128]{2,1,0:T(8,128)(2,1)S(1)} custom-call(s32[1]{0:T(128)} %bitcast.spot_ref, bf16[4,8,16,128]{3,2,1,0:T(8,128)(2,1)S(1)} %get-tuple-element.68.own_ref.hid_ref, bf16[1,8,16,128]{3,2,1,0:T(8,128)(2,1)S(1)} %collective-permute-done.5.near_ref, bf16[1,8,16,128]{3,2,1,0:T(8,128)(2,1)S(1)} %collective-permute-done.6.far_ref, ...), custom_call_target="tpu_custom_call" | custom-call | tf_op jit(solution)/shard_map/pallas_call | solution.py:38
  88.4 8.2 %all-to-all-start.2 = ((bf16[32,104,128]{2,1,0:T(8,128)(2,1)}), bf16[32,104,128]{2,1,0:T(8,128)(2,1)S(1)}, u32[]{:S(2)}, u32[]{:S(2)}) async-start(bf16[32,104,128]{2,1,0:T(8,128)(2,1)} %shard_map.125), calls=%async_computation.2 | async-start | bytes 1703936 | tf_op jit(solution)/shard_map/all_to_all | solution.py:400
  96.7 1.5 %shard_map.122 = (bf16[512,128]{1,0:T(8,128)(2,1)}, s32[512,128]{1,0:T(8,128)S(1)}, f32[512,128]{1,0:T(8,128)S(1)}) custom-call(bf16[32,104,128]{2,1,0:T(8,128)(2,1)S(1)} %all-to-all-done.1.got_ref, s32[1,512]{1,0:T(1,128)S(1)} %bitcast.5, bf16[512,128]{1,0:T(8,128)(2,1)S(1)} %copy-done.1, bf16[512,128]{1,0:T(8,128)(2,1)S(1)} %copy-done.2, ...), custom_call_target="tpu_custom_call" | custom-call | tf_op jit(solution)/shard_map/pallas_call | solution.py:38
  98.2 16.5 %all-to-all-done.2.got_ref = bf16[32,104,128]{2,1,0:T(8,128)(2,1)S(1)} async-done(((bf16[32,104,128]{2,1,0:T(8,128)(2,1)}), bf16[32,104,128]{2,1,0:T(8,128)(2,1)S(1)}, u32[]{:S(2)}, u32[]{:S(2)}) %all-to-all-start.2) | async-done | bytes 852000 | tf_op jit(solution)/shard_map/all_to_all | solution.py:400
  114.8 7.4 %collective-permute-start.12 = (bf16[14,128,128]{2,1,0:T(8,128)(2,1)S(1)}, bf16[14,128,128]{2,1,0:T(8,128)(2,1)S(1)}, u32[]{:S(2)}, u32[]{:S(2)}) collective-permute-start(bf16[14,128,128]{2,1,0:T(8,128)(2,1)S(1)} %shard_map.127.mine_ref), channel_id=1, source_target_pairs={{0,32},{32,0},{1,33},{33,1},{2,34},{34,2},{3,35},{35,3},{4,36},{36... | collective-permute-start | bytes 1376264 | tf_op jit(solution)/shard_map/ppermute | solution.py:408
  122.2 1.2 shard_map.126
  123.6 1.5 %shard_map.128 = (f32[27,128,128]{2,1,0:T(8,128)}, f32[128,128]{1,0:T(8,128)}) custom-call(s32[1]{0:T(128)} %bitcast.spot_ref, bf16[14,128,128]{2,1,0:T(8,128)(2,1)S(1)} %shard_map.127.mine_ref, bf16[14,128,128]{2,1,0:T(8,128)(2,1)S(1)} %collective-permute-done.12.other_ref), custom_call_target="tpu_custom_call" | custom-call | tf_op jit(solution)/shard_map/pallas_call | solution.py:38
  (36 shorter events, 10.1 us)
Async XLA Ops:
  0.6 15.0 %copy-start.2 = (bf16[512,128]{1,0:T(8,128)(2,1)S(1)}, bf16[512,128]{1,0:T(8,128)(2,1)}, u32[]{:S(2)}) copy-start(bf16[512,128]{1,0:T(8,128)(2,1)} %cot_ref.3) | copy-start | bytes 393220
  0.6 15.0 %copy-start.1 = (bf16[512,128]{1,0:T(8,128)(2,1)S(1)}, bf16[512,128]{1,0:T(8,128)(2,1)}, u32[]{:S(2)}) copy-start(bf16[512,128]{1,0:T(8,128)(2,1)} %feat_ref.3) | copy-start | bytes 393220
  0.7 15.0 %copy-start.3 = (bf16[128,128]{1,0:T(8,128)(2,1)S(1)}, bf16[128,128]{1,0:T(8,128)(2,1)}, u32[]{:S(2)}) copy-start(bf16[128,128]{1,0:T(8,128)(2,1)} %mlp_ref.3) | copy-start | bytes 98308
  3.6 44.9 %copy-start = (bf16[27,128,128]{2,1,0:T(8,128)(2,1)S(1)}, bf16[27,128,128]{2,1,0:T(8,128)(2,1)}, u32[]{:S(2)}) copy-start(bf16[27,128,128]{2,1,0:T(8,128)(2,1)} %weight_ref.5) | copy-start | bytes 2654212
  3.7 32.4 %all-to-all-start = ((bf16[32,104,128]{2,1,0:T(8,128)(2,1)}), bf16[32,104,128]{2,1,0:T(8,128)(2,1)S(1)}, u32[]{:S(2)}, u32[]{:S(2)}) async-start(bf16[32,104,128]{2,1,0:T(8,128)(2,1)} %shard_map.111), calls=%async_computation | async-start | bytes 1703936 | tf_op jit(solution)/shard_map/all_to_all | solution.py:400
  36.7 7.6 %collective-permute-start = (bf16[1,8,16,128]{3,2,1,0:T(8,128)(2,1)S(1)}, bf16[1,8,16,128]{3,2,1,0:T(8,128)(2,1)S(1)}, u32[]{:S(2)}, u32[]{:S(2)}) collective-permute-start(bf16[1,8,16,128]{3,2,1,0:T(8,128)(2,1)S(1)} %get-tuple-element.48), channel_id=1, source_target_pairs={{0,32},{32,0},{1,33},{33,1},{2,34},{34,2},{3,35},{35,3},{4,36},{36... | collective-permute-start | bytes 98312 | tf_op jit(solution)/shard_map/ppermute | solution.py:408
  42.2 3.3 %collective-permute-start.1 = (bf16[1,8,16,128]{3,2,1,0:T(8,128)(2,1)S(1)}, bf16[1,8,16,128]{3,2,1,0:T(8,128)(2,1)S(1)}, u32[]{:S(2)}, u32[]{:S(2)}) collective-permute-start(bf16[1,8,16,128]{3,2,1,0:T(8,128)(2,1)S(1)} %get-tuple-element.49), channel_id=1, source_target_pairs={{32,64},{96,128},{160,192},{224,0},{64,32},{128,96},{192,160},{0,2... | collective-permute-start | bytes 98312 | tf_op jit(solution)/shard_map/ppermute | solution.py:386
  45.5 4.2 %collective-permute-start.2 = (bf16[6,1,16,128]{3,2,1,0:T(8,128)(2,1)S(1)}, bf16[6,1,16,128]{3,2,1,0:T(8,128)(2,1)S(1)}, u32[]{:S(2)}, u32[]{:S(2)}) collective-permute-start(bf16[6,1,16,128]{3,2,1,0:T(8,128)(2,1)S(1)} %get-tuple-element.57), channel_id=1, source_target_pairs={{0,1},{2,3},{4,5},{6,7},{8,9},{10,11},{12,13},{14,15},{16,17},{18,... | collective-permute-start | bytes 73736 | tf_op jit(solution)/shard_map/ppermute | solution.py:394
  46.9 2.8 %collective-permute-start.3 = (bf16[6,1,16,128]{3,2,1,0:T(8,128)(2,1)S(1)}, bf16[6,1,16,128]{3,2,1,0:T(8,128)(2,1)S(1)}, u32[]{:S(2)}, u32[]{:S(2)}) collective-permute-start(bf16[6,1,16,128]{3,2,1,0:T(8,128)(2,1)S(1)} %get-tuple-element.58), channel_id=1, source_target_pairs={{1,2},{3,4},{5,6},{7,8},{9,10},{11,12},{13,14},{15,16},{17,18},{19... | collective-permute-start | bytes 73736 | tf_op jit(solution)/shard_map/ppermute | solution.py:395
  50.6 2.7 %collective-permute-start.4 = (bf16[14,128,128]{2,1,0:T(8,128)(2,1)S(1)}, bf16[14,128,128]{2,1,0:T(8,128)(2,1)S(1)}, u32[]{:S(2)}, u32[]{:S(2)}) collective-permute-start(bf16[14,128,128]{2,1,0:T(8,128)(2,1)S(1)} %get-tuple-element.63), channel_id=1, source_target_pairs={{0,32},{32,0},{1,33},{33,1},{2,34},{34,2},{3,35},{35,3},{4,36},{36... | collective-permute-start | bytes 1376264 | tf_op jit(solution)/shard_map/ppermute | solution.py:408
  54.3 27.5 %all-to-all-start.1 = ((bf16[32,104,128]{2,1,0:T(8,128)(2,1)}), bf16[32,104,128]{2,1,0:T(8,128)(2,1)S(1)}, u32[]{:S(2)}, u32[]{:S(2)}) async-start(bf16[32,104,128]{2,1,0:T(8,128)(2,1)} %shard_map.120), calls=%async_computation.1 | async-start | bytes 1703936 | tf_op jit(solution)/shard_map/all_to_all | solution.py:400
  60.9 1.6 %collective-permute-start.5 = (bf16[1,8,16,128]{3,2,1,0:T(8,128)(2,1)S(1)}, bf16[1,8,16,128]{3,2,1,0:T(8,128)(2,1)S(1)}, u32[]{:S(2)}, u32[]{:S(2)}) collective-permute-start(bf16[1,8,16,128]{3,2,1,0:T(8,128)(2,1)S(1)} %get-tuple-element.66), channel_id=1, source_target_pairs={{0,32},{32,0},{1,33},{33,1},{2,34},{34,2},{3,35},{35,3},{4,36},{36... | collective-permute-start | bytes 98312 | tf_op jit(solution)/shard_map/ppermute | solution.py:408
  61.6 3.3 %collective-permute-start.6 = (bf16[1,8,16,128]{3,2,1,0:T(8,128)(2,1)S(1)}, bf16[1,8,16,128]{3,2,1,0:T(8,128)(2,1)S(1)}, u32[]{:S(2)}, u32[]{:S(2)}) collective-permute-start(bf16[1,8,16,128]{3,2,1,0:T(8,128)(2,1)S(1)} %get-tuple-element.67), channel_id=1, source_target_pairs={{32,64},{96,128},{160,192},{224,0},{64,32},{128,96},{192,160},{0,2... | collective-permute-start | bytes 98312 | tf_op jit(solution)/shard_map/ppermute | solution.py:386
  64.9 15.2 %collective-permute-start.7 = (bf16[6,1,16,128]{3,2,1,0:T(8,128)(2,1)S(1)}, bf16[6,1,16,128]{3,2,1,0:T(8,128)(2,1)S(1)}, u32[]{:S(2)}, u32[]{:S(2)}) collective-permute-start(bf16[6,1,16,128]{3,2,1,0:T(8,128)(2,1)S(1)} %get-tuple-element.69), channel_id=1, source_target_pairs={{0,1},{2,3},{4,5},{6,7},{8,9},{10,11},{12,13},{14,15},{16,17},{18,... | collective-permute-start | bytes 73736 | tf_op jit(solution)/shard_map/ppermute | solution.py:394
  66.7 13.4 %collective-permute-start.8 = (bf16[6,1,16,128]{3,2,1,0:T(8,128)(2,1)S(1)}, bf16[6,1,16,128]{3,2,1,0:T(8,128)(2,1)S(1)}, u32[]{:S(2)}, u32[]{:S(2)}) collective-permute-start(bf16[6,1,16,128]{3,2,1,0:T(8,128)(2,1)S(1)} %get-tuple-element.70), channel_id=1, source_target_pairs={{1,2},{3,4},{5,6},{7,8},{9,10},{11,12},{13,14},{15,16},{17,18},{19... | collective-permute-start | bytes 73736 | tf_op jit(solution)/shard_map/ppermute | solution.py:395
  81.9 5.2 %collective-permute-start.11 = (bf16[56,128]{1,0:T(8,128)(2,1)S(1)}, bf16[56,128]{1,0:T(8,128)(2,1)S(1)}, u32[]{:S(2)}, u32[]{:S(2)}) collective-permute-start(bf16[56,128]{1,0:T(8,128)(2,1)S(1)} %shard_map.123.own_ref), channel_id=1, source_target_pairs={{0,192},{64,128},{128,64},{192,0},{1,193},{65,129},{129,65},{193,1... | collective-permute-start | bytes 43016 | tf_op jit(solution)/shard_map/ppermute | solution.py:404
  83.4 4.1 %collective-permute-start.10 = (bf16[56,128]{1,0:T(8,128)(2,1)S(1)}, bf16[56,128]{1,0:T(8,128)(2,1)S(1)}, u32[]{:S(2)}, u32[]{:S(2)}) collective-permute-start(bf16[56,128]{1,0:T(8,128)(2,1)S(1)} %shard_map.123.own_ref), channel_id=1, source_target_pairs={{0,128},{64,192},{128,0},{192,64},{1,129},{65,193},{129,1},{193,65... | collective-permute-start | bytes 43016 | tf_op jit(solution)/shard_map/ppermute | solution.py:404
  83.8 3.7 %collective-permute-start.9 = (bf16[56,128]{1,0:T(8,128)(2,1)S(1)}, bf16[56,128]{1,0:T(8,128)(2,1)S(1)}, u32[]{:S(2)}, u32[]{:S(2)}) collective-permute-start(bf16[56,128]{1,0:T(8,128)(2,1)S(1)} %shard_map.123.own_ref), channel_id=1, source_target_pairs={{0,64},{64,0},{128,192},{192,128},{1,65},{65,1},{129,193},{193,129... | collective-permute-start | bytes 43016 | tf_op jit(solution)/shard_map/ppermute | solution.py:404
  87.1 9.6 %copy-start.4 = (s32[512,1]{0,1:T(1,128)S(1)}, s32[512,1]{0,1:T(1,128)}, u32[]{:S(2)}) copy-start(s32[512,1]{0,1:T(1,128)} %param.9) | copy-start | bytes 6148
  88.4 26.3 %all-to-all-start.2 = ((bf16[32,104,128]{2,1,0:T(8,128)(2,1)}), bf16[32,104,128]{2,1,0:T(8,128)(2,1)S(1)}, u32[]{:S(2)}, u32[]{:S(2)}) async-start(bf16[32,104,128]{2,1,0:T(8,128)(2,1)} %shard_map.125), calls=%async_computation.2 | async-start | bytes 1703936 | tf_op jit(solution)/shard_map/all_to_all | solution.py:400
  114.8 8.8 %collective-permute-start.12 = (bf16[14,128,128]{2,1,0:T(8,128)(2,1)S(1)}, bf16[14,128,128]{2,1,0:T(8,128)(2,1)S(1)}, u32[]{:S(2)}, u32[]{:S(2)}) collective-permute-start(bf16[14,128,128]{2,1,0:T(8,128)(2,1)S(1)} %shard_map.127.mine_ref), channel_id=1, source_target_pairs={{0,32},{32,0},{1,33},{33,1},{2,34},{34,2},{3,35},{35,3},{4,36},{36... | collective-permute-start | bytes 1376264 | tf_op jit(solution)/shard_map/ppermute | solution.py:408

commit v10 on v9

--- a/solution.py
+++ b/solution.py
@@ -357,20 +357,34 @@
     out_ref[...] = (unpack(pos_ref[...], got_ref) + back_ref[...]).astype(BF)
 
 
-def weights_kernel(spot_ref, mine_ref, other_ref, conv_ref, mlp_ref):
-    def fill(first_ref, second_ref):
-        for o in range(27):
+def weights_kernel(spot_ref, mine_ref, other_ref, conv_hbm, mlp_hbm, conv_ref, mlp_ref, sems):
+    moves = [
+        pltpu.make_async_copy(conv_ref.at[pl.ds(9 * k, 9)], conv_hbm.at[pl.ds(9 * k, 9)], sems.at[k])
+        for k in range(3)
+    ]
+    moves.append(pltpu.make_async_copy(mlp_ref, mlp_hbm, sems.at[3]))
+
+    def fill(first_ref, second_ref, k):
+        for o in range(9 * k, 9 * k + 9):
             half = first_ref[o] if o < HALF else second_ref[o - HALF]
             conv_ref[o] = half.astype(F32).T * (1.0 / math.sqrt(GX * GY * CELLS))
-        mlp_ref[...] = second_ref[HALF - 1].astype(F32).T * (1.0 / math.sqrt(GX * GY * PTS))
-
-    @pl.when(spot_ref[0] % 2 == 0)
-    def _():
-        fill(mine_ref, other_ref)
-
-    @pl.when(spot_ref[0] % 2 == 1)
-    def _():
-        fill(other_ref, mine_ref)
+        if k == 2:
+            mlp_ref[...] = second_ref[HALF - 1].astype(F32).T * (1.0 / math.sqrt(GX * GY * PTS))
+
+    for k in range(3):
+
+        @pl.when(spot_ref[0] % 2 == 0)
+        def _():
+            fill(mine_ref, other_ref, k)
+
+        @pl.when(spot_ref[0] % 2 == 1)
+        def _():
+            fill(other_ref, mine_ref, k)
+
+        moves[k].start()
+    moves[3].start()
+    for move in moves:
+        move.wait()
 
 
 FACE = sds((1, VY, Z, C), BF)
@@ -446,7 +460,8 @@
         (spot, got),
         smem=1,
     )
-    near, far = swap(near), chips(far)
+    far = chips(far)
+    near = swap(near)
     matrix, grad_out = call(
         spread_kernel, (sds((CELLS, SLOTS), BF), sds((CELLS, C), F32)), (got, meta)
     )
@@ -475,7 +490,8 @@
     filled = call(sample_kernel, rows, (matrix, act))
     joined = call(join_kernel, block, (keep, arrived, filled))
     first = exchange(joined)
-    near, far = swap(near), chips(far)
+    far = chips(far)
+    near = swap(near)
     grad_faces = (near, far) + edges(spot, near, grad_hidden, far)
     first, grad_faces = lax.optimization_barrier((first, grad_faces))
     filled = call(
@@ -505,7 +521,16 @@
     other = swap(mine)
     grad_features = call(backward_kernel, sds((PTS, C), BF), (second, position, back))
     grad_conv, grad_mlp = call(
-        weights_kernel, (sds((27, C, C), F32), sds((C, C), F32)), (spot, mine, other), smem=1
+        weights_kernel,
+        (sds((27, C, C), F32), sds((C, C), F32)),
+        (spot, mine, other),
+        scratch=(
+            pltpu.VMEM((27, C, C), F32),
+            pltpu.VMEM((C, C), F32),
+            pltpu.SemaphoreType.DMA((4,)),
+        ),
+        smem=1,
+        out=HBM,
     )
     return (output, grad_features, grad_conv, grad_mlp)
 

time: 126 us -> 126 us (level)
  no operation moved by 1% of the time
where the time goes in v10:
time: 126 us; the launch traced here: 125 us
  waiting for transfers between devices  55.5 us (44%)
  starting transfers between devices  52.4 us (42%)
  Pallas kernels  16.2 us (13%)
    all_to_all x3, waiting for transfers between devices, exchange(): lax.all_to_all(rows, ('x', 'z'), split_axis=0, concat_axis=0, tiled=True)  38.1 us
    all_to_all x3, starting transfers between devices, exchange(): lax.all_to_all(rows, ('x', 'z'), split_axis=0, concat_axis=0, tiled=True)  26.8 us
    pallas_call x18, Pallas kernels, call(): pl.pallas_call(kernel, out_shape=out_shape, in_specs=[SMEM] * smem + [HBM...  16.2 us
    ppermute x4, starting transfers between devices, swap(): return lax.ppermute(half, 'c', [(0, 1), (1, 0)])  14.8 us
    ppermute x2, waiting for transfers between devices, edges(): lax.ppermute(even, ('x', 'z'), pairs(GY, 0))  12 us
    ppermute x2, waiting for transfers between devices, chips(): return lax.ppermute(face, ('y', 'c'), pairs(GX, 1))  3.71 us
    ppermute x3, starting transfers between devices, across(): return lax.ppermute(share, 'y', list(enumerate(partner)))  3.34 us
    ppermute x2, starting transfers between devices, edges(): lax.ppermute(even, ('x', 'z'), pairs(GY, 0))  3.09 us
  transfers between devices with their start and end apart: 16, of which 10 were waited for; matrix products, arithmetic and copies ran while one was open for 0% of the time, Pallas kernels for 7%

profile of v10, /device:TPU:1, one launch (start us, length us, event | category | flops | bytes accessed | tf_op | source)
XLA Modules:
  0.0 125.2 jit_solution(7845377825127273971)
XLA Ops:
  0.7 2.9 %shard_map.111 = bf16[32,104,128]{2,1,0:T(8,128)(2,1)} custom-call(bf16[512,128]{1,0:T(8,128)(2,1)} %feat_ref.3, bf16[512,128]{1,0:T(8,128)(2,1)} %cot_ref.3, s32[1,512]{1,0:T(1,128)} %bitcast.4, s32[1,512]{1,0:T(1,128)} %bitcast.6, s32[1,512]{1,0:T(1,128)} %bitcast.7, bf16[3,512]{1,0:T(4,128)(2,1)} %off_hbm.1), custom_call_target="tpu_custom_call" | custom-call | tf_op jit(solution)/shard_map/pallas_call | solution.py:38
  3.7 12.0 %all-to-all-start = ((bf16[32,104,128]{2,1,0:T(8,128)(2,1)}), bf16[32,104,128]{2,1,0:T(8,128)(2,1)S(1)}, u32[]{:S(2)}, u32[]{:S(2)}) async-start(bf16[32,104,128]{2,1,0:T(8,128)(2,1)} %shard_map.111), calls=%async_computation | async-start | bytes 1703936 | tf_op jit(solution)/shard_map/all_to_all | solution.py:414
  16.1 19.9 %all-to-all-done.got_ref = bf16[32,104,128]{2,1,0:T(8,128)(2,1)S(1)} async-done(((bf16[32,104,128]{2,1,0:T(8,128)(2,1)}), bf16[32,104,128]{2,1,0:T(8,128)(2,1)S(1)}, u32[]{:S(2)}, u32[]{:S(2)}) %all-to-all-start) | async-done | bytes 852000 | tf_op jit(solution)/shard_map/all_to_all | solution.py:414
  36.7 5.5 %collective-permute-start = (bf16[1,8,16,128]{3,2,1,0:T(8,128)(2,1)S(1)}, bf16[1,8,16,128]{3,2,1,0:T(8,128)(2,1)S(1)}, u32[]{:S(2)}, u32[]{:S(2)}) collective-permute-start(bf16[1,8,16,128]{3,2,1,0:T(8,128)(2,1)S(1)} %get-tuple-element.48), channel_id=1, source_target_pairs={{0,32},{32,0},{1,33},{33,1},{2,34},{34,2},{3,35},{35,3},{4,36},{36... | collective-permute-start | bytes 98312 | tf_op jit(solution)/shard_map/ppermute | solution.py:422
  42.2 1.3 %collective-permute-start.1 = (bf16[1,8,16,128]{3,2,1,0:T(8,128)(2,1)S(1)}, bf16[1,8,16,128]{3,2,1,0:T(8,128)(2,1)S(1)}, u32[]{:S(2)}, u32[]{:S(2)}) collective-permute-start(bf16[1,8,16,128]{3,2,1,0:T(8,128)(2,1)S(1)} %get-tuple-element.49), channel_id=1, source_target_pairs={{32,64},{96,128},{160,192},{224,0},{64,32},{128,96},{192,160},{0,2... | collective-permute-start | bytes 98312 | tf_op jit(solution)/shard_map/ppermute | solution.py:400
  44.3 1.2 collective-permute-done.1.far_ref
  45.5 1.3 %collective-permute-start.2 = (bf16[6,1,16,128]{3,2,1,0:T(8,128)(2,1)S(1)}, bf16[6,1,16,128]{3,2,1,0:T(8,128)(2,1)S(1)}, u32[]{:S(2)}, u32[]{:S(2)}) collective-permute-start(bf16[6,1,16,128]{3,2,1,0:T(8,128)(2,1)S(1)} %get-tuple-element.57), channel_id=1, source_target_pairs={{0,1},{2,3},{4,5},{6,7},{8,9},{10,11},{12,13},{14,15},{16,17},{18,... | collective-permute-start | bytes 73736 | tf_op jit(solution)/shard_map/ppermute | solution.py:408
  46.9 1.7 %collective-permute-start.3 = (bf16[6,1,16,128]{3,2,1,0:T(8,128)(2,1)S(1)}, bf16[6,1,16,128]{3,2,1,0:T(8,128)(2,1)S(1)}, u32[]{:S(2)}, u32[]{:S(2)}) collective-permute-start(bf16[6,1,16,128]{3,2,1,0:T(8,128)(2,1)S(1)} %get-tuple-element.58), channel_id=1, source_target_pairs={{1,2},{3,4},{5,6},{7,8},{9,10},{11,12},{13,14},{15,16},{17,18},{19... | collective-permute-start | bytes 73736 | tf_op jit(solution)/shard_map/ppermute | solution.py:409
  50.6 1.2 collective-permute-start.4
  54.3 6.6 %all-to-all-start.1 = ((bf16[32,104,128]{2,1,0:T(8,128)(2,1)}), bf16[32,104,128]{2,1,0:T(8,128)(2,1)S(1)}, u32[]{:S(2)}, u32[]{:S(2)}) async-start(bf16[32,104,128]{2,1,0:T(8,128)(2,1)} %shard_map.120), calls=%async_computation.1 | async-start | bytes 1703936 | tf_op jit(solution)/shard_map/all_to_all | solution.py:414
  62.5 2.5 %collective-permute-done.6.far_ref = bf16[1,8,16,128]{3,2,1,0:T(8,128)(2,1)S(1)} collective-permute-done((bf16[1,8,16,128]{3,2,1,0:T(8,128)(2,1)S(1)}, bf16[1,8,16,128]{3,2,1,0:T(8,128)(2,1)S(1)}, u32[]{:S(2)}, u32[]{:S(2)}) %collective-permute-start.6) | collective-permute-done | bytes 32800 | tf_op jit(solution)/shard_map/ppermute | solution.py:400
  64.9 1.8 %collective-permute-start.7 = (bf16[6,1,16,128]{3,2,1,0:T(8,128)(2,1)S(1)}, bf16[6,1,16,128]{3,2,1,0:T(8,128)(2,1)S(1)}, u32[]{:S(2)}, u32[]{:S(2)}) collective-permute-start(bf16[6,1,16,128]{3,2,1,0:T(8,128)(2,1)S(1)} %get-tuple-element.69), channel_id=1, source_target_pairs={{0,1},{2,3},{4,5},{6,7},{8,9},{10,11},{12,13},{14,15},{16,17},{18,... | collective-permute-start | bytes 73736 | tf_op jit(solution)/shard_map/ppermute | solution.py:408
  66.7 1.4 %collective-permute-start.8 = (bf16[6,1,16,128]{3,2,1,0:T(8,128)(2,1)S(1)}, bf16[6,1,16,128]{3,2,1,0:T(8,128)(2,1)S(1)}, u32[]{:S(2)}, u32[]{:S(2)}) collective-permute-start(bf16[6,1,16,128]{3,2,1,0:T(8,128)(2,1)S(1)} %get-tuple-element.70), channel_id=1, source_target_pairs={{1,2},{3,4},{5,6},{7,8},{9,10},{11,12},{13,14},{15,16},{17,18},{19... | collective-permute-start | bytes 73736 | tf_op jit(solution)/shard_map/ppermute | solution.py:409
  68.1 12.0 %collective-permute-done.7.even_ref = bf16[6,1,16,128]{3,2,1,0:T(8,128)(2,1)S(1)} collective-permute-done((bf16[6,1,16,128]{3,2,1,0:T(8,128)(2,1)S(1)}, bf16[6,1,16,128]{3,2,1,0:T(8,128)(2,1)S(1)}, u32[]{:S(2)}, u32[]{:S(2)}) %collective-permute-start.7) | collective-permute-done | bytes 24608 | tf_op jit(solution)/shard_map/ppermute | solution.py:408
  80.1 1.7 %all-to-all-done.1.got_ref = bf16[32,104,128]{2,1,0:T(8,128)(2,1)S(1)} async-done(((bf16[32,104,128]{2,1,0:T(8,128)(2,1)}), bf16[32,104,128]{2,1,0:T(8,128)(2,1)S(1)}, u32[]{:S(2)}, u32[]{:S(2)}) %all-to-all-start.1) | async-done | bytes 852000 | tf_op jit(solution)/shard_map/all_to_all | solution.py:414
  81.9 1.5 %collective-permute-start.11 = (bf16[56,128]{1,0:T(8,128)(2,1)S(1)}, bf16[56,128]{1,0:T(8,128)(2,1)S(1)}, u32[]{:S(2)}, u32[]{:S(2)}) collective-permute-start(bf16[56,128]{1,0:T(8,128)(2,1)S(1)} %shard_map.123.own_ref), channel_id=1, source_target_pairs={{0,192},{64,128},{128,64},{192,0},{1,193},{65,129},{129,65},{193,1... | collective-permute-start | bytes 43016 | tf_op jit(solution)/shard_map/ppermute | solution.py:418
  83.8 1.5 %collective-permute-start.9 = (bf16[56,128]{1,0:T(8,128)(2,1)S(1)}, bf16[56,128]{1,0:T(8,128)(2,1)S(1)}, u32[]{:S(2)}, u32[]{:S(2)}) collective-permute-start(bf16[56,128]{1,0:T(8,128)(2,1)S(1)} %shard_map.123.own_ref), channel_id=1, source_target_pairs={{0,64},{64,0},{128,192},{192,128},{1,65},{65,1},{129,193},{193,129... | collective-permute-start | bytes 43016 | tf_op jit(solution)/shard_map/ppermute | solution.py:418
  85.2 1.9 %shard_map.124.filled_ref = bf16[32,48,128]{2,1,0:T(8,128)(2,1)S(1)} custom-call(s32[1]{0:T(128)} %bitcast.spot_ref, bf16[4,8,16,128]{3,2,1,0:T(8,128)(2,1)S(1)} %get-tuple-element.68.own_ref.hid_ref, bf16[1,8,16,128]{3,2,1,0:T(8,128)(2,1)S(1)} %collective-permute-done.5.near_ref, bf16[1,8,16,128]{3,2,1,0:T(8,128)(2,1)S(1)} %collective-permute-done.6.far_ref, ...), custom_call_target="tpu_custom_call" | custom-call | tf_op jit(solution)/shard_map/pallas_call | solution.py:38
  88.4 8.2 %all-to-all-start.2 = ((bf16[32,104,128]{2,1,0:T(8,128)(2,1)}), bf16[32,104,128]{2,1,0:T(8,128)(2,1)S(1)}, u32[]{:S(2)}, u32[]{:S(2)}) async-start(bf16[32,104,128]{2,1,0:T(8,128)(2,1)} %shard_map.125), calls=%async_computation.2 | async-start | bytes 1703936 | tf_op jit(solution)/shard_map/all_to_all | solution.py:414
  96.7 1.5 %shard_map.122 = (bf16[512,128]{1,0:T(8,128)(2,1)}, s32[512,128]{1,0:T(8,128)S(1)}, f32[512,128]{1,0:T(8,128)S(1)}) custom-call(bf16[32,104,128]{2,1,0:T(8,128)(2,1)S(1)} %all-to-all-done.1.got_ref, s32[1,512]{1,0:T(1,128)S(1)} %bitcast.5, bf16[512,128]{1,0:T(8,128)(2,1)S(1)} %copy-done.1, bf16[512,128]{1,0:T(8,128)(2,1)S(1)} %copy-done.2, ...), custom_call_target="tpu_custom_call" | custom-call | tf_op jit(solution)/shard_map/pallas_call | solution.py:38
  98.2 16.5 %all-to-all-done.2.got_ref = bf16[32,104,128]{2,1,0:T(8,128)(2,1)S(1)} async-done(((bf16[32,104,128]{2,1,0:T(8,128)(2,1)}), bf16[32,104,128]{2,1,0:T(8,128)(2,1)S(1)}, u32[]{:S(2)}, u32[]{:S(2)}) %all-to-all-start.2) | async-done | bytes 852000 | tf_op jit(solution)/shard_map/all_to_all | solution.py:414
  114.8 7.4 %collective-permute-start.12 = (bf16[14,128,128]{2,1,0:T(8,128)(2,1)S(1)}, bf16[14,128,128]{2,1,0:T(8,128)(2,1)S(1)}, u32[]{:S(2)}, u32[]{:S(2)}) collective-permute-start(bf16[14,128,128]{2,1,0:T(8,128)(2,1)S(1)} %shard_map.127.mine_ref), channel_id=1, source_target_pairs={{0,32},{32,0},{1,33},{33,1},{2,34},{34,2},{3,35},{35,3},{4,36},{36... | collective-permute-start | bytes 1376264 | tf_op jit(solution)/shard_map/ppermute | solution.py:422
  122.2 1.2 shard_map.126
  123.6 1.4 %shard_map.128 = (f32[27,128,128]{2,1,0:T(8,128)}, f32[128,128]{1,0:T(8,128)}) custom-call(s32[1]{0:T(128)} %bitcast.spot_ref, bf16[14,128,128]{2,1,0:T(8,128)(2,1)S(1)} %shard_map.127.mine_ref, bf16[14,128,128]{2,1,0:T(8,128)(2,1)S(1)} %collective-permute-done.12.other_ref), custom_call_target="tpu_custom_call" | custom-call | tf_op jit(solution)/shard_map/pallas_call | solution.py:38
  (36 shorter events, 10.1 us)
Async XLA Ops:
  0.6 15.0 %copy-start.2 = (bf16[512,128]{1,0:T(8,128)(2,1)S(1)}, bf16[512,128]{1,0:T(8,128)(2,1)}, u32[]{:S(2)}) copy-start(bf16[512,128]{1,0:T(8,128)(2,1)} %cot_ref.3) | copy-start | bytes 393220
  0.6 15.0 %copy-start.1 = (bf16[512,128]{1,0:T(8,128)(2,1)S(1)}, bf16[512,128]{1,0:T(8,128)(2,1)}, u32[]{:S(2)}) copy-start(bf16[512,128]{1,0:T(8,128)(2,1)} %feat_ref.3) | copy-start | bytes 393220
  0.7 15.0 %copy-start.3 = (bf16[128,128]{1,0:T(8,128)(2,1)S(1)}, bf16[128,128]{1,0:T(8,128)(2,1)}, u32[]{:S(2)}) copy-start(bf16[128,128]{1,0:T(8,128)(2,1)} %mlp_ref.3) | copy-start | bytes 98308
  3.6 44.9 %copy-start = (bf16[27,128,128]{2,1,0:T(8,128)(2,1)S(1)}, bf16[27,128,128]{2,1,0:T(8,128)(2,1)}, u32[]{:S(2)}) copy-start(bf16[27,128,128]{2,1,0:T(8,128)(2,1)} %weight_ref.5) | copy-start | bytes 2654212
  3.7 32.4 %all-to-all-start = ((bf16[32,104,128]{2,1,0:T(8,128)(2,1)}), bf16[32,104,128]{2,1,0:T(8,128)(2,1)S(1)}, u32[]{:S(2)}, u32[]{:S(2)}) async-start(bf16[32,104,128]{2,1,0:T(8,128)(2,1)} %shard_map.111), calls=%async_computation | async-start | bytes 1703936 | tf_op jit(solution)/shard_map/all_to_all | solution.py:414
  36.7 7.6 %collective-permute-start = (bf16[1,8,16,128]{3,2,1,0:T(8,128)(2,1)S(1)}, bf16[1,8,16,128]{3,2,1,0:T(8,128)(2,1)S(1)}, u32[]{:S(2)}, u32[]{:S(2)}) collective-permute-start(bf16[1,8,16,128]{3,2,1,0:T(8,128)(2,1)S(1)} %get-tuple-element.48), channel_id=1, source_target_pairs={{0,32},{32,0},{1,33},{33,1},{2,34},{34,2},{3,35},{35,3},{4,36},{36... | collective-permute-start | bytes 98312 | tf_op jit(solution)/shard_map/ppermute | solution.py:422
  42.2 3.3 %collective-permute-start.1 = (bf16[1,8,16,128]{3,2,1,0:T(8,128)(2,1)S(1)}, bf16[1,8,16,128]{3,2,1,0:T(8,128)(2,1)S(1)}, u32[]{:S(2)}, u32[]{:S(2)}) collective-permute-start(bf16[1,8,16,128]{3,2,1,0:T(8,128)(2,1)S(1)} %get-tuple-element.49), channel_id=1, source_target_pairs={{32,64},{96,128},{160,192},{224,0},{64,32},{128,96},{192,160},{0,2... | collective-permute-start | bytes 98312 | tf_op jit(solution)/shard_map/ppermute | solution.py:400
  45.5 4.2 %collective-permute-start.2 = (bf16[6,1,16,128]{3,2,1,0:T(8,128)(2,1)S(1)}, bf16[6,1,16,128]{3,2,1,0:T(8,128)(2,1)S(1)}, u32[]{:S(2)}, u32[]{:S(2)}) collective-permute-start(bf16[6,1,16,128]{3,2,1,0:T(8,128)(2,1)S(1)} %get-tuple-element.57), channel_id=1, source_target_pairs={{0,1},{2,3},{4,5},{6,7},{8,9},{10,11},{12,13},{14,15},{16,17},{18,... | collective-permute-start | bytes 73736 | tf_op jit(solution)/shard_map/ppermute | solution.py:408
  46.9 2.8 %collective-permute-start.3 = (bf16[6,1,16,128]{3,2,1,0:T(8,128)(2,1)S(1)}, bf16[6,1,16,128]{3,2,1,0:T(8,128)(2,1)S(1)}, u32[]{:S(2)}, u32[]{:S(2)}) collective-permute-start(bf16[6,1,16,128]{3,2,1,0:T(8,128)(2,1)S(1)} %get-tuple-element.58), channel_id=1, source_target_pairs={{1,2},{3,4},{5,6},{7,8},{9,10},{11,12},{13,14},{15,16},{17,18},{19... | collective-permute-start | bytes 73736 | tf_op jit(solution)/shard_map/ppermute | solution.py:409
  50.6 2.7 %collective-permute-start.4 = (bf16[14,128,128]{2,1,0:T(8,128)(2,1)S(1)}, bf16[14,128,128]{2,1,0:T(8,128)(2,1)S(1)}, u32[]{:S(2)}, u32[]{:S(2)}) collective-permute-start(bf16[14,128,128]{2,1,0:T(8,128)(2,1)S(1)} %get-tuple-element.63), channel_id=1, source_target_pairs={{0,32},{32,0},{1,33},{33,1},{2,34},{34,2},{3,35},{35,3},{4,36},{36... | collective-permute-start | bytes 1376264 | tf_op jit(solution)/shard_map/ppermute | solution.py:422
  54.3 27.5 %all-to-all-start.1 = ((bf16[32,104,128]{2,1,0:T(8,128)(2,1)}), bf16[32,104,128]{2,1,0:T(8,128)(2,1)S(1)}, u32[]{:S(2)}, u32[]{:S(2)}) async-start(bf16[32,104,128]{2,1,0:T(8,128)(2,1)} %shard_map.120), calls=%async_computation.1 | async-start | bytes 1703936 | tf_op jit(solution)/shard_map/all_to_all | solution.py:414
  60.9 1.6 %collective-permute-start.5 = (bf16[1,8,16,128]{3,2,1,0:T(8,128)(2,1)S(1)}, bf16[1,8,16,128]{3,2,1,0:T(8,128)(2,1)S(1)}, u32[]{:S(2)}, u32[]{:S(2)}) collective-permute-start(bf16[1,8,16,128]{3,2,1,0:T(8,128)(2,1)S(1)} %get-tuple-element.66), channel_id=1, source_target_pairs={{0,32},{32,0},{1,33},{33,1},{2,34},{34,2},{3,35},{35,3},{4,36},{36... | collective-permute-start | bytes 98312 | tf_op jit(solution)/shard_map/ppermute | solution.py:422
  61.6 3.3 %collective-permute-start.6 = (bf16[1,8,16,128]{3,2,1,0:T(8,128)(2,1)S(1)}, bf16[1,8,16,128]{3,2,1,0:T(8,128)(2,1)S(1)}, u32[]{:S(2)}, u32[]{:S(2)}) collective-permute-start(bf16[1,8,16,128]{3,2,1,0:T(8,128)(2,1)S(1)} %get-tuple-element.67), channel_id=1, source_target_pairs={{32,64},{96,128},{160,192},{224,0},{64,32},{128,96},{192,160},{0,2... | collective-permute-start | bytes 98312 | tf_op jit(solution)/shard_map/ppermute | solution.py:400
  64.9 15.2 %collective-permute-start.7 = (bf16[6,1,16,128]{3,2,1,0:T(8,128)(2,1)S(1)}, bf16[6,1,16,128]{3,2,1,0:T(8,128)(2,1)S(1)}, u32[]{:S(2)}, u32[]{:S(2)}) collective-permute-start(bf16[6,1,16,128]{3,2,1,0:T(8,128)(2,1)S(1)} %get-tuple-element.69), channel_id=1, source_target_pairs={{0,1},{2,3},{4,5},{6,7},{8,9},{10,11},{12,13},{14,15},{16,17},{18,... | collective-permute-start | bytes 73736 | tf_op jit(solution)/shard_map/ppermute | solution.py:408
  66.7 13.4 %collective-permute-start.8 = (bf16[6,1,16,128]{3,2,1,0:T(8,128)(2,1)S(1)}, bf16[6,1,16,128]{3,2,1,0:T(8,128)(2,1)S(1)}, u32[]{:S(2)}, u32[]{:S(2)}) collective-permute-start(bf16[6,1,16,128]{3,2,1,0:T(8,128)(2,1)S(1)} %get-tuple-element.70), channel_id=1, source_target_pairs={{1,2},{3,4},{5,6},{7,8},{9,10},{11,12},{13,14},{15,16},{17,18},{19... | collective-permute-start | bytes 73736 | tf_op jit(solution)/shard_map/ppermute | solution.py:409
  81.9 5.2 %collective-permute-start.11 = (bf16[56,128]{1,0:T(8,128)(2,1)S(1)}, bf16[56,128]{1,0:T(8,128)(2,1)S(1)}, u32[]{:S(2)}, u32[]{:S(2)}) collective-permute-start(bf16[56,128]{1,0:T(8,128)(2,1)S(1)} %shard_map.123.own_ref), channel_id=1, source_target_pairs={{0,192},{64,128},{128,64},{192,0},{1,193},{65,129},{129,65},{193,1... | collective-permute-start | bytes 43016 | tf_op jit(solution)/shard_map/ppermute | solution.py:418
  83.4 4.1 %collective-permute-start.10 = (bf16[56,128]{1,0:T(8,128)(2,1)S(1)}, bf16[56,128]{1,0:T(8,128)(2,1)S(1)}, u32[]{:S(2)}, u32[]{:S(2)}) collective-permute-start(bf16[56,128]{1,0:T(8,128)(2,1)S(1)} %shard_map.123.own_ref), channel_id=1, source_target_pairs={{0,128},{64,192},{128,0},{192,64},{1,129},{65,193},{129,1},{193,65... | collective-permute-start | bytes 43016 | tf_op jit(solution)/shard_map/ppermute | solution.py:418
  83.8 3.7 %collective-permute-start.9 = (bf16[56,128]{1,0:T(8,128)(2,1)S(1)}, bf16[56,128]{1,0:T(8,128)(2,1)S(1)}, u32[]{:S(2)}, u32[]{:S(2)}) collective-permute-start(bf16[56,128]{1,0:T(8,128)(2,1)S(1)} %shard_map.123.own_ref), channel_id=1, source_target_pairs={{0,64},{64,0},{128,192},{192,128},{1,65},{65,1},{129,193},{193,129... | collective-permute-start | bytes 43016 | tf_op jit(solution)/shard_map/ppermute | solution.py:418
  87.1 9.6 %copy-start.4 = (s32[512,1]{0,1:T(1,128)S(1)}, s32[512,1]{0,1:T(1,128)}, u32[]{:S(2)}) copy-start(s32[512,1]{0,1:T(1,128)} %param.9) | copy-start | bytes 6148
  88.4 26.3 %all-to-all-start.2 = ((bf16[32,104,128]{2,1,0:T(8,128)(2,1)}), bf16[32,104,128]{2,1,0:T(8,128)(2,1)S(1)}, u32[]{:S(2)}, u32[]{:S(2)}) async-start(bf16[32,104,128]{2,1,0:T(8,128)(2,1)} %shard_map.125), calls=%async_computation.2 | async-start | bytes 1703936 | tf_op jit(solution)/shard_map/all_to_all | solution.py:414
  114.8 8.8 %collective-permute-start.12 = (bf16[14,128,128]{2,1,0:T(8,128)(2,1)S(1)}, bf16[14,128,128]{2,1,0:T(8,128)(2,1)S(1)}, u32[]{:S(2)}, u32[]{:S(2)}) collective-permute-start(bf16[14,128,128]{2,1,0:T(8,128)(2,1)S(1)} %shard_map.127.mine_ref), channel_id=1, source_target_pairs={{0,32},{32,0},{1,33},{33,1},{2,34},{34,2},{3,35},{35,3},{4,36},{36... | collective-permute-start | bytes 1376264 | tf_op jit(solution)/shard_map/ppermute | solution.py:422

commit v11 on v10

--- a/solution.py
+++ b/solution.py
@@ -298,10 +298,21 @@
     out_ref[...] = dot(matrix_ref[...], act_ref[...], LEFT).astype(BF).reshape(GY, CAP, C)
 
 
-def join_kernel(keep_ref, got_ref, filled_ref, out_ref):
-    total = keep_ref[...] + got_ref[...].astype(F32)
-    out_ref[:, CAP:, :] = total.reshape(GY, SHARE, C).astype(BF)
-    out_ref[:, 0:CAP, :] = filled_ref[...]
+def deliver(filled_ref, share, out_hbm, out_ref, sems):
+    moves = []
+    for g in range(4):
+        here = pl.ds(8 * g, 8)
+        out_ref[here, 0:CAP, :] = filled_ref[here]
+        out_ref[here, CAP:, :] = share(8 * g)
+        moves.append(pltpu.make_async_copy(out_ref.at[here], out_hbm.at[here], sems.at[g]))
+        moves[g].start()
+    for move in moves:
+        move.wait()
+
+
+def join_kernel(keep_ref, got_ref, filled_ref, out_hbm, out_ref, sems):
+    total = (keep_ref[...] + got_ref[...].astype(F32)).reshape(GY, SHARE, C)
+    deliver(filled_ref, lambda t: total[t : t + 8].astype(BF), out_hbm, out_ref, sems)
 
 
 def share_kernel(got_ref, out_ref):
@@ -319,13 +330,13 @@
     out_ref[...] = dot(own_matrix(meta_ref[...]), mean, LEFT).astype(BF).reshape(GY, CAP, C)
 
 
-def deal_kernel(spot_ref, own_ref, one_ref, two_ref, three_ref, filled_ref, out_ref, part_ref):
+def deal_kernel(spot_ref, own_ref, one_ref, two_ref, three_ref, filled_ref, out_hbm, part_ref, out_ref, sems):
     y = spot_ref[0] // 16
     for k, ref in enumerate((own_ref, one_ref, two_ref, three_ref)):
         part_ref[y ^ k] = ref[...].astype(F32)
     total = jnp.sum(part_ref[...], axis=0).astype(BF)
-    out_ref[:, CAP:, :] = jnp.broadcast_to(total[None], (GY, SHARE, C))
-    out_ref[:, 0:CAP, :] = filled_ref[...]
+    spread = jnp.broadcast_to(total[None], (8, SHARE, C))
+    deliver(filled_ref, lambda t: spread, out_hbm, out_ref, sems)
 
 
 def unpack(pos, got_ref):
@@ -488,7 +499,8 @@
     arrived = swap(send)
     keep = call(keep_kernel, sds((HALF, C, C), F32), (spot, full, turned, mlp_grad), smem=1)
     filled = call(sample_kernel, rows, (matrix, act))
-    joined = call(join_kernel, block, (keep, arrived, filled))
+    sending = (pltpu.VMEM(block.shape, BF), pltpu.SemaphoreType.DMA((4,)))
+    joined = call(join_kernel, block, (keep, arrived, filled), scratch=sending, out=HBM)
     first = exchange(joined)
     far = chips(far)
     near = swap(near)
@@ -507,8 +519,9 @@
         deal_kernel,
         block,
         (spot, share) + others + (filled,),
-        scratch=(pltpu.VMEM((4, SHARE, C), F32),),
+        scratch=(pltpu.VMEM((4, SHARE, C), F32),) + sending,
         smem=1,
+        out=HBM,
     )
     second = exchange(joined)
     output, position, back = call(

time: 126 us -> 126 us (level)
  no operation moved by 1% of the time
where the time goes in v11:
time: 126 us; the launch traced here: 125 us
  waiting for transfers between devices  55.5 us (44%)
  starting transfers between devices  52.4 us (42%)
  Pallas kernels  16.2 us (13%)
    all_to_all x3, waiting for transfers between devices, exchange(): lax.all_to_all(rows, ('x', 'z'), split_axis=0, concat_axis=0, tiled=True)  38.1 us
    all_to_all x3, starting transfers between devices, exchange(): lax.all_to_all(rows, ('x', 'z'), split_axis=0, concat_axis=0, tiled=True)  26.8 us
    pallas_call x18, Pallas kernels, call(): pl.pallas_call(kernel, out_shape=out_shape, in_specs=[SMEM] * smem + [HBM...  16.2 us
    ppermute x4, starting transfers between devices, swap(): return lax.ppermute(half, 'c', [(0, 1), (1, 0)])  14.8 us
    ppermute x2, waiting for transfers between devices, edges(): lax.ppermute(even, ('x', 'z'), pairs(GY, 0))  12 us
    ppermute x2, waiting for transfers between devices, chips(): return lax.ppermute(face, ('y', 'c'), pairs(GX, 1))  3.71 us
    ppermute x3, starting transfers between devices, across(): return lax.ppermute(share, 'y', list(enumerate(partner)))  3.34 us
    ppermute x2, starting transfers between devices, edges(): lax.ppermute(even, ('x', 'z'), pairs(GY, 0))  3.09 us
  transfers between devices with their start and end apart: 16, of which 10 were waited for; matrix products, arithmetic and copies ran while one was open for 0% of the time, Pallas kernels for 7%

profile of v11, /device:TPU:1, one launch (start us, length us, event | category | flops | bytes accessed | tf_op | source)
XLA Modules:
  0.0 125.2 jit_solution(4046983280913992577)
XLA Ops:
  0.7 2.9 %shard_map.111 = bf16[32,104,128]{2,1,0:T(8,128)(2,1)} custom-call(bf16[512,128]{1,0:T(8,128)(2,1)} %feat_ref.3, bf16[512,128]{1,0:T(8,128)(2,1)} %cot_ref.3, s32[1,512]{1,0:T(1,128)} %bitcast.4, s32[1,512]{1,0:T(1,128)} %bitcast.6, s32[1,512]{1,0:T(1,128)} %bitcast.7, bf16[3,512]{1,0:T(4,128)(2,1)} %off_hbm.1), custom_call_target="tpu_custom_call" | custom-call | tf_op jit(solution)/shard_map/pallas_call | solution.py:38
  3.7 12.0 %all-to-all-start = ((bf16[32,104,128]{2,1,0:T(8,128)(2,1)}), bf16[32,104,128]{2,1,0:T(8,128)(2,1)S(1)}, u32[]{:S(2)}, u32[]{:S(2)}) async-start(bf16[32,104,128]{2,1,0:T(8,128)(2,1)} %shard_map.111), calls=%async_computation | async-start | bytes 1703936 | tf_op jit(solution)/shard_map/all_to_all | solution.py:425
  16.1 19.9 %all-to-all-done.got_ref = bf16[32,104,128]{2,1,0:T(8,128)(2,1)S(1)} async-done(((bf16[32,104,128]{2,1,0:T(8,128)(2,1)}), bf16[32,104,128]{2,1,0:T(8,128)(2,1)S(1)}, u32[]{:S(2)}, u32[]{:S(2)}) %all-to-all-start) | async-done | bytes 852000 | tf_op jit(solution)/shard_map/all_to_all | solution.py:425
  36.7 5.5 %collective-permute-start = (bf16[1,8,16,128]{3,2,1,0:T(8,128)(2,1)S(1)}, bf16[1,8,16,128]{3,2,1,0:T(8,128)(2,1)S(1)}, u32[]{:S(2)}, u32[]{:S(2)}) collective-permute-start(bf16[1,8,16,128]{3,2,1,0:T(8,128)(2,1)S(1)} %get-tuple-element.48), channel_id=1, source_target_pairs={{0,32},{32,0},{1,33},{33,1},{2,34},{34,2},{3,35},{35,3},{4,36},{36... | collective-permute-start | bytes 98312 | tf_op jit(solution)/shard_map/ppermute | solution.py:433
  42.2 1.3 %collective-permute-start.1 = (bf16[1,8,16,128]{3,2,1,0:T(8,128)(2,1)S(1)}, bf16[1,8,16,128]{3,2,1,0:T(8,128)(2,1)S(1)}, u32[]{:S(2)}, u32[]{:S(2)}) collective-permute-start(bf16[1,8,16,128]{3,2,1,0:T(8,128)(2,1)S(1)} %get-tuple-element.49), channel_id=1, source_target_pairs={{32,64},{96,128},{160,192},{224,0},{64,32},{128,96},{192,160},{0,2... | collective-permute-start | bytes 98312 | tf_op jit(solution)/shard_map/ppermute | solution.py:411
  44.3 1.2 collective-permute-done.1.far_ref
  45.5 1.3 %collective-permute-start.2 = (bf16[6,1,16,128]{3,2,1,0:T(8,128)(2,1)S(1)}, bf16[6,1,16,128]{3,2,1,0:T(8,128)(2,1)S(1)}, u32[]{:S(2)}, u32[]{:S(2)}) collective-permute-start(bf16[6,1,16,128]{3,2,1,0:T(8,128)(2,1)S(1)} %get-tuple-element.57), channel_id=1, source_target_pairs={{0,1},{2,3},{4,5},{6,7},{8,9},{10,11},{12,13},{14,15},{16,17},{18,... | collective-permute-start | bytes 73736 | tf_op jit(solution)/shard_map/ppermute | solution.py:419
  46.9 1.7 %collective-permute-start.3 = (bf16[6,1,16,128]{3,2,1,0:T(8,128)(2,1)S(1)}, bf16[6,1,16,128]{3,2,1,0:T(8,128)(2,1)S(1)}, u32[]{:S(2)}, u32[]{:S(2)}) collective-permute-start(bf16[6,1,16,128]{3,2,1,0:T(8,128)(2,1)S(1)} %get-tuple-element.58), channel_id=1, source_target_pairs={{1,2},{3,4},{5,6},{7,8},{9,10},{11,12},{13,14},{15,16},{17,18},{19... | collective-permute-start | bytes 73736 | tf_op jit(solution)/shard_map/ppermute | solution.py:420
  50.6 1.2 collective-permute-start.4
  54.2 6.6 %all-to-all-start.1 = ((bf16[32,104,128]{2,1,0:T(8,128)(2,1)}), bf16[32,104,128]{2,1,0:T(8,128)(2,1)S(1)}, u32[]{:S(2)}, u32[]{:S(2)}) async-start(bf16[32,104,128]{2,1,0:T(8,128)(2,1)} %shard_map.120), calls=%async_computation.1 | async-start | bytes 1703936 | tf_op jit(solution)/shard_map/all_to_all | solution.py:425
  62.4 2.5 %collective-permute-done.6.far_ref = bf16[1,8,16,128]{3,2,1,0:T(8,128)(2,1)S(1)} collective-permute-done((bf16[1,8,16,128]{3,2,1,0:T(8,128)(2,1)S(1)}, bf16[1,8,16,128]{3,2,1,0:T(8,128)(2,1)S(1)}, u32[]{:S(2)}, u32[]{:S(2)}) %collective-permute-start.6) | collective-permute-done | bytes 32800 | tf_op jit(solution)/shard_map/ppermute | solution.py:411
  64.9 1.8 %collective-permute-start.7 = (bf16[6,1,16,128]{3,2,1,0:T(8,128)(2,1)S(1)}, bf16[6,1,16,128]{3,2,1,0:T(8,128)(2,1)S(1)}, u32[]{:S(2)}, u32[]{:S(2)}) collective-permute-start(bf16[6,1,16,128]{3,2,1,0:T(8,128)(2,1)S(1)} %get-tuple-element.69), channel_id=1, source_target_pairs={{0,1},{2,3},{4,5},{6,7},{8,9},{10,11},{12,13},{14,15},{16,17},{18,... | collective-permute-start | bytes 73736 | tf_op jit(solution)/shard_map/ppermute | solution.py:419
  66.7 1.4 %collective-permute-start.8 = (bf16[6,1,16,128]{3,2,1,0:T(8,128)(2,1)S(1)}, bf16[6,1,16,128]{3,2,1,0:T(8,128)(2,1)S(1)}, u32[]{:S(2)}, u32[]{:S(2)}) collective-permute-start(bf16[6,1,16,128]{3,2,1,0:T(8,128)(2,1)S(1)} %get-tuple-element.70), channel_id=1, source_target_pairs={{1,2},{3,4},{5,6},{7,8},{9,10},{11,12},{13,14},{15,16},{17,18},{19... | collective-permute-start | bytes 73736 | tf_op jit(solution)/shard_map/ppermute | solution.py:420
  68.1 12.0 %collective-permute-done.7.even_ref = bf16[6,1,16,128]{3,2,1,0:T(8,128)(2,1)S(1)} collective-permute-done((bf16[6,1,16,128]{3,2,1,0:T(8,128)(2,1)S(1)}, bf16[6,1,16,128]{3,2,1,0:T(8,128)(2,1)S(1)}, u32[]{:S(2)}, u32[]{:S(2)}) %collective-permute-start.7) | collective-permute-done | bytes 24608 | tf_op jit(solution)/shard_map/ppermute | solution.py:419
  80.1 1.7 %all-to-all-done.1.got_ref = bf16[32,104,128]{2,1,0:T(8,128)(2,1)S(1)} async-done(((bf16[32,104,128]{2,1,0:T(8,128)(2,1)}), bf16[32,104,128]{2,1,0:T(8,128)(2,1)S(1)}, u32[]{:S(2)}, u32[]{:S(2)}) %all-to-all-start.1) | async-done | bytes 852000 | tf_op jit(solution)/shard_map/all_to_all | solution.py:425
  81.8 1.5 %collective-permute-start.11 = (bf16[56,128]{1,0:T(8,128)(2,1)S(1)}, bf16[56,128]{1,0:T(8,128)(2,1)S(1)}, u32[]{:S(2)}, u32[]{:S(2)}) collective-permute-start(bf16[56,128]{1,0:T(8,128)(2,1)S(1)} %shard_map.123.own_ref), channel_id=1, source_target_pairs={{0,192},{64,128},{128,64},{192,0},{1,193},{65,129},{129,65},{193,1... | collective-permute-start | bytes 43016 | tf_op jit(solution)/shard_map/ppermute | solution.py:429
  83.7 1.5 %collective-permute-start.9 = (bf16[56,128]{1,0:T(8,128)(2,1)S(1)}, bf16[56,128]{1,0:T(8,128)(2,1)S(1)}, u32[]{:S(2)}, u32[]{:S(2)}) collective-permute-start(bf16[56,128]{1,0:T(8,128)(2,1)S(1)} %shard_map.123.own_ref), channel_id=1, source_target_pairs={{0,64},{64,0},{128,192},{192,128},{1,65},{65,1},{129,193},{193,129... | collective-permute-start | bytes 43016 | tf_op jit(solution)/shard_map/ppermute | solution.py:429
  85.2 1.9 %shard_map.124.filled_ref = bf16[32,48,128]{2,1,0:T(8,128)(2,1)S(1)} custom-call(s32[1]{0:T(128)} %bitcast.spot_ref, bf16[4,8,16,128]{3,2,1,0:T(8,128)(2,1)S(1)} %get-tuple-element.68.own_ref.hid_ref, bf16[1,8,16,128]{3,2,1,0:T(8,128)(2,1)S(1)} %collective-permute-done.5.near_ref, bf16[1,8,16,128]{3,2,1,0:T(8,128)(2,1)S(1)} %collective-permute-done.6.far_ref, ...), custom_call_target="tpu_custom_call" | custom-call | tf_op jit(solution)/shard_map/pallas_call | solution.py:38
  88.4 8.2 %all-to-all-start.2 = ((bf16[32,104,128]{2,1,0:T(8,128)(2,1)}), bf16[32,104,128]{2,1,0:T(8,128)(2,1)S(1)}, u32[]{:S(2)}, u32[]{:S(2)}) async-start(bf16[32,104,128]{2,1,0:T(8,128)(2,1)} %shard_map.125), calls=%async_computation.2 | async-start | bytes 1703936 | tf_op jit(solution)/shard_map/all_to_all | solution.py:425
  96.6 1.5 %shard_map.122 = (bf16[512,128]{1,0:T(8,128)(2,1)}, s32[512,128]{1,0:T(8,128)S(1)}, f32[512,128]{1,0:T(8,128)S(1)}) custom-call(bf16[32,104,128]{2,1,0:T(8,128)(2,1)S(1)} %all-to-all-done.1.got_ref, s32[1,512]{1,0:T(1,128)S(1)} %bitcast.5, bf16[512,128]{1,0:T(8,128)(2,1)S(1)} %copy-done.1, bf16[512,128]{1,0:T(8,128)(2,1)S(1)} %copy-done.2, ...), custom_call_target="tpu_custom_call" | custom-call | tf_op jit(solution)/shard_map/pallas_call | solution.py:38
  98.2 16.5 %all-to-all-done.2.got_ref = bf16[32,104,128]{2,1,0:T(8,128)(2,1)S(1)} async-done(((bf16[32,104,128]{2,1,0:T(8,128)(2,1)}), bf16[32,104,128]{2,1,0:T(8,128)(2,1)S(1)}, u32[]{:S(2)}, u32[]{:S(2)}) %all-to-all-start.2) | async-done | bytes 852000 | tf_op jit(solution)/shard_map/all_to_all | solution.py:425
  114.8 7.4 %collective-permute-start.12 = (bf16[14,128,128]{2,1,0:T(8,128)(2,1)S(1)}, bf16[14,128,128]{2,1,0:T(8,128)(2,1)S(1)}, u32[]{:S(2)}, u32[]{:S(2)}) collective-permute-start(bf16[14,128,128]{2,1,0:T(8,128)(2,1)S(1)} %shard_map.127.mine_ref), channel_id=1, source_target_pairs={{0,32},{32,0},{1,33},{33,1},{2,34},{34,2},{3,35},{35,3},{4,36},{36... | collective-permute-start | bytes 1376264 | tf_op jit(solution)/shard_map/ppermute | solution.py:433
  122.2 1.2 shard_map.126
  123.6 1.4 %shard_map.128 = (f32[27,128,128]{2,1,0:T(8,128)}, f32[128,128]{1,0:T(8,128)}) custom-call(s32[1]{0:T(128)} %bitcast.spot_ref, bf16[14,128,128]{2,1,0:T(8,128)(2,1)S(1)} %shard_map.127.mine_ref, bf16[14,128,128]{2,1,0:T(8,128)(2,1)S(1)} %collective-permute-done.12.other_ref), custom_call_target="tpu_custom_call" | custom-call | tf_op jit(solution)/shard_map/pallas_call | solution.py:38
  (36 shorter events, 10.1 us)
Async XLA Ops:
  0.6 15.0 %copy-start.2 = (bf16[512,128]{1,0:T(8,128)(2,1)S(1)}, bf16[512,128]{1,0:T(8,128)(2,1)}, u32[]{:S(2)}) copy-start(bf16[512,128]{1,0:T(8,128)(2,1)} %cot_ref.3) | copy-start | bytes 393220
  0.6 15.0 %copy-start.1 = (bf16[512,128]{1,0:T(8,128)(2,1)S(1)}, bf16[512,128]{1,0:T(8,128)(2,1)}, u32[]{:S(2)}) copy-start(bf16[512,128]{1,0:T(8,128)(2,1)} %feat_ref.3) | copy-start | bytes 393220
  0.7 15.0 %copy-start.3 = (bf16[128,128]{1,0:T(8,128)(2,1)S(1)}, bf16[128,128]{1,0:T(8,128)(2,1)}, u32[]{:S(2)}) copy-start(bf16[128,128]{1,0:T(8,128)(2,1)} %mlp_ref.3) | copy-start | bytes 98308
  3.6 44.9 %copy-start = (bf16[27,128,128]{2,1,0:T(8,128)(2,1)S(1)}, bf16[27,128,128]{2,1,0:T(8,128)(2,1)}, u32[]{:S(2)}) copy-start(bf16[27,128,128]{2,1,0:T(8,128)(2,1)} %weight_ref.5) | copy-start | bytes 2654212
  3.7 32.4 %all-to-all-start = ((bf16[32,104,128]{2,1,0:T(8,128)(2,1)}), bf16[32,104,128]{2,1,0:T(8,128)(2,1)S(1)}, u32[]{:S(2)}, u32[]{:S(2)}) async-start(bf16[32,104,128]{2,1,0:T(8,128)(2,1)} %shard_map.111), calls=%async_computation | async-start | bytes 1703936 | tf_op jit(solution)/shard_map/all_to_all | solution.py:425
  36.7 7.6 %collective-permute-start = (bf16[1,8,16,128]{3,2,1,0:T(8,128)(2,1)S(1)}, bf16[1,8,16,128]{3,2,1,0:T(8,128)(2,1)S(1)}, u32[]{:S(2)}, u32[]{:S(2)}) collective-permute-start(bf16[1,8,16,128]{3,2,1,0:T(8,128)(2,1)S(1)} %get-tuple-element.48), channel_id=1, source_target_pairs={{0,32},{32,0},{1,33},{33,1},{2,34},{34,2},{3,35},{35,3},{4,36},{36... | collective-permute-start | bytes 98312 | tf_op jit(solution)/shard_map/ppermute | solution.py:433
  42.2 3.3 %collective-permute-start.1 = (bf16[1,8,16,128]{3,2,1,0:T(8,128)(2,1)S(1)}, bf16[1,8,16,128]{3,2,1,0:T(8,128)(2,1)S(1)}, u32[]{:S(2)}, u32[]{:S(2)}) collective-permute-start(bf16[1,8,16,128]{3,2,1,0:T(8,128)(2,1)S(1)} %get-tuple-element.49), channel_id=1, source_target_pairs={{32,64},{96,128},{160,192},{224,0},{64,32},{128,96},{192,160},{0,2... | collective-permute-start | bytes 98312 | tf_op jit(solution)/shard_map/ppermute | solution.py:411
  45.5 4.2 %collective-permute-start.2 = (bf16[6,1,16,128]{3,2,1,0:T(8,128)(2,1)S(1)}, bf16[6,1,16,128]{3,2,1,0:T(8,128)(2,1)S(1)}, u32[]{:S(2)}, u32[]{:S(2)}) collective-permute-start(bf16[6,1,16,128]{3,2,1,0:T(8,128)(2,1)S(1)} %get-tuple-element.57), channel_id=1, source_target_pairs={{0,1},{2,3},{4,5},{6,7},{8,9},{10,11},{12,13},{14,15},{16,17},{18,... | collective-permute-start | bytes 73736 | tf_op jit(solution)/shard_map/ppermute | solution.py:419
  46.9 2.8 %collective-permute-start.3 = (bf16[6,1,16,128]{3,2,1,0:T(8,128)(2,1)S(1)}, bf16[6,1,16,128]{3,2,1,0:T(8,128)(2,1)S(1)}, u32[]{:S(2)}, u32[]{:S(2)}) collective-permute-start(bf16[6,1,16,128]{3,2,1,0:T(8,128)(2,1)S(1)} %get-tuple-element.58), channel_id=1, source_target_pairs={{1,2},{3,4},{5,6},{7,8},{9,10},{11,12},{13,14},{15,16},{17,18},{19... | collective-permute-start | bytes 73736 | tf_op jit(solution)/shard_map/ppermute | solution.py:420
  50.6 2.7 %collective-permute-start.4 = (bf16[14,128,128]{2,1,0:T(8,128)(2,1)S(1)}, bf16[14,128,128]{2,1,0:T(8,128)(2,1)S(1)}, u32[]{:S(2)}, u32[]{:S(2)}) collective-permute-start(bf16[14,128,128]{2,1,0:T(8,128)(2,1)S(1)} %get-tuple-element.63), channel_id=1, source_target_pairs={{0,32},{32,0},{1,33},{33,1},{2,34},{34,2},{3,35},{35,3},{4,36},{36... | collective-permute-start | bytes 1376264 | tf_op jit(solution)/shard_map/ppermute | solution.py:433
  54.2 27.5 %all-to-all-start.1 = ((bf16[32,104,128]{2,1,0:T(8,128)(2,1)}), bf16[32,104,128]{2,1,0:T(8,128)(2,1)S(1)}, u32[]{:S(2)}, u32[]{:S(2)}) async-start(bf16[32,104,128]{2,1,0:T(8,128)(2,1)} %shard_map.120), calls=%async_computation.1 | async-start | bytes 1703936 | tf_op jit(solution)/shard_map/all_to_all | solution.py:425
  60.8 1.6 %collective-permute-start.5 = (bf16[1,8,16,128]{3,2,1,0:T(8,128)(2,1)S(1)}, bf16[1,8,16,128]{3,2,1,0:T(8,128)(2,1)S(1)}, u32[]{:S(2)}, u32[]{:S(2)}) collective-permute-start(bf16[1,8,16,128]{3,2,1,0:T(8,128)(2,1)S(1)} %get-tuple-element.66), channel_id=1, source_target_pairs={{0,32},{32,0},{1,33},{33,1},{2,34},{34,2},{3,35},{35,3},{4,36},{36... | collective-permute-start | bytes 98312 | tf_op jit(solution)/shard_map/ppermute | solution.py:433
  61.6 3.3 %collective-permute-start.6 = (bf16[1,8,16,128]{3,2,1,0:T(8,128)(2,1)S(1)}, bf16[1,8,16,128]{3,2,1,0:T(8,128)(2,1)S(1)}, u32[]{:S(2)}, u32[]{:S(2)}) collective-permute-start(bf16[1,8,16,128]{3,2,1,0:T(8,128)(2,1)S(1)} %get-tuple-element.67), channel_id=1, source_target_pairs={{32,64},{96,128},{160,192},{224,0},{64,32},{128,96},{192,160},{0,2... | collective-permute-start | bytes 98312 | tf_op jit(solution)/shard_map/ppermute | solution.py:411
  64.9 15.2 %collective-permute-start.7 = (bf16[6,1,16,128]{3,2,1,0:T(8,128)(2,1)S(1)}, bf16[6,1,16,128]{3,2,1,0:T(8,128)(2,1)S(1)}, u32[]{:S(2)}, u32[]{:S(2)}) collective-permute-start(bf16[6,1,16,128]{3,2,1,0:T(8,128)(2,1)S(1)} %get-tuple-element.69), channel_id=1, source_target_pairs={{0,1},{2,3},{4,5},{6,7},{8,9},{10,11},{12,13},{14,15},{16,17},{18,... | collective-permute-start | bytes 73736 | tf_op jit(solution)/shard_map/ppermute | solution.py:419
  66.7 13.4 %collective-permute-start.8 = (bf16[6,1,16,128]{3,2,1,0:T(8,128)(2,1)S(1)}, bf16[6,1,16,128]{3,2,1,0:T(8,128)(2,1)S(1)}, u32[]{:S(2)}, u32[]{:S(2)}) collective-permute-start(bf16[6,1,16,128]{3,2,1,0:T(8,128)(2,1)S(1)} %get-tuple-element.70), channel_id=1, source_target_pairs={{1,2},{3,4},{5,6},{7,8},{9,10},{11,12},{13,14},{15,16},{17,18},{19... | collective-permute-start | bytes 73736 | tf_op jit(solution)/shard_map/ppermute | solution.py:420
  81.8 5.2 %collective-permute-start.11 = (bf16[56,128]{1,0:T(8,128)(2,1)S(1)}, bf16[56,128]{1,0:T(8,128)(2,1)S(1)}, u32[]{:S(2)}, u32[]{:S(2)}) collective-permute-start(bf16[56,128]{1,0:T(8,128)(2,1)S(1)} %shard_map.123.own_ref), channel_id=1, source_target_pairs={{0,192},{64,128},{128,64},{192,0},{1,193},{65,129},{129,65},{193,1... | collective-permute-start | bytes 43016 | tf_op jit(solution)/shard_map/ppermute | solution.py:429
  83.4 4.1 %collective-permute-start.10 = (bf16[56,128]{1,0:T(8,128)(2,1)S(1)}, bf16[56,128]{1,0:T(8,128)(2,1)S(1)}, u32[]{:S(2)}, u32[]{:S(2)}) collective-permute-start(bf16[56,128]{1,0:T(8,128)(2,1)S(1)} %shard_map.123.own_ref), channel_id=1, source_target_pairs={{0,128},{64,192},{128,0},{192,64},{1,129},{65,193},{129,1},{193,65... | collective-permute-start | bytes 43016 | tf_op jit(solution)/shard_map/ppermute | solution.py:429
  83.7 3.7 %collective-permute-start.9 = (bf16[56,128]{1,0:T(8,128)(2,1)S(1)}, bf16[56,128]{1,0:T(8,128)(2,1)S(1)}, u32[]{:S(2)}, u32[]{:S(2)}) collective-permute-start(bf16[56,128]{1,0:T(8,128)(2,1)S(1)} %shard_map.123.own_ref), channel_id=1, source_target_pairs={{0,64},{64,0},{128,192},{192,128},{1,65},{65,1},{129,193},{193,129... | collective-permute-start | bytes 43016 | tf_op jit(solution)/shard_map/ppermute | solution.py:429
  87.0 9.6 %copy-start.4 = (s32[512,1]{0,1:T(1,128)S(1)}, s32[512,1]{0,1:T(1,128)}, u32[]{:S(2)}) copy-start(s32[512,1]{0,1:T(1,128)} %param.9) | copy-start | bytes 6148
  88.4 26.3 %all-to-all-start.2 = ((bf16[32,104,128]{2,1,0:T(8,128)(2,1)}), bf16[32,104,128]{2,1,0:T(8,128)(2,1)S(1)}, u32[]{:S(2)}, u32[]{:S(2)}) async-start(bf16[32,104,128]{2,1,0:T(8,128)(2,1)} %shard_map.125), calls=%async_computation.2 | async-start | bytes 1703936 | tf_op jit(solution)/shard_map/all_to_all | solution.py:425
  114.8 8.8 %collective-permute-start.12 = (bf16[14,128,128]{2,1,0:T(8,128)(2,1)S(1)}, bf16[14,128,128]{2,1,0:T(8,128)(2,1)S(1)}, u32[]{:S(2)}, u32[]{:S(2)}) collective-permute-start(bf16[14,128,128]{2,1,0:T(8,128)(2,1)S(1)} %shard_map.127.mine_ref), channel_id=1, source_target_pairs={{0,32},{32,0},{1,33},{33,1},{2,34},{34,2},{3,35},{35,3},{4,36},{36... | collective-permute-start | bytes 1376264 | tf_op jit(solution)/shard_map/ppermute | solution.py:433
